TPU v7x, 32 devices: a whole 2x2x4 slice. The times are simulated.
32 devices in a mesh: prow: 8 (over z, y), pcol: 4 (over x, core).
Axes of the slice: x: 2, y: 2, z: 4, core: 2. Of those that a mesh axis runs over, the one named last changes fastest.
Arguments:
- matrix: float32 [4096, 11, 4, 256], P('prow', None, 'pcol'), may hold values from -6 to 6
Outputs:
- r_factor: float32 [512, 11, 4, 256], P('prow', None, 'pcol')
- remainder: float32 [4096, 11, 4, 256], P('prow', None, 'pcol')
All inputs are finite; a program needn't handle non-finite values.
Results may differ from a plain program's by a relative error of at most 0.0003.
Values sent between devices are 32-bit elements; how exact they have to be, the bound alone decides.
No kernel may reach another device: no remote copies, remote signals or barrier semaphores. Data moves between devices by JAX's collectives and lax.ppermute only.
A program may use at most 192 MiB of HBM per device.

v0:
```python
import functools

import jax
import jax.numpy as jnp
from jax import lax
from jax.experimental import pallas as pl
from jax.experimental.pallas import tpu as pltpu
from jax.sharding import PartitionSpec as P

highest = lax.Precision.HIGHEST
f32 = jnp.float32
bf16 = jnp.bfloat16
TILE = 128
SIZES = (2, 1, 2, 2, 2, 2)
SENDS = ((0,), (1,), (2,), (3,), (4,), (5,))
ORDER = (
    "gram send1 send0 send4", "g1 ~g1 send5 keep1", "g2 send2 keep0 send3", "~keep1 zm1 keep2 g4",
    "keep4 ~zm1 zm0 zm2", "keep3 g5 zo0 keep5", "zm4 zo2 g6 ag0", "ch0 zm3 zo1 zo4",
    "ag2 ~zo1 zm5 ~ag2", "ch1 ag4 zo5 ag1", "~ag0 ch2 zo3 ch3", "ag5 weights fin4 ~zo3",
    "fin1 ag3 fin5 fin2", "fin0 fin3",
)


def dot(a, b):
    return jnp.dot(a, b, precision=highest, preferred_element_type=f32)


def dot_t(a, b):
    return lax.dot_general(a, b, (((0,), (0,)), ((), ())), precision=highest, preferred_element_type=f32)


def dot_nt(a, b):
    return lax.dot_general(a, b, (((1,), (1,)), ((), ())), precision=highest, preferred_element_type=f32)


def split(value):
    high = value.astype(bf16)
    return high, (value - high.astype(f32)).astype(bf16)


def dot3(a, b):
    def product(x, y):
        return jnp.dot(x, y, preferred_element_type=f32)

    return product(a[0], b[0]) + (product(a[0], b[1]) + product(a[1], b[0]))


def flip(value, axis, bit):
    n = lax.axis_size(axis)
    return lax.ppermute(value, axis, [(i, i ^ bit) for i in range(n)])


class Chain:
    def __init__(self):
        self.last = []
        self.waits = []

    def __call__(self, kernel, name, outs, flags, *operands, scratch=()):
        after = self.last + self.waits
        n_in, n_after = len(operands), len(after)
        vmem = pl.BlockSpec(memory_space=pltpu.VMEM)

        def body(*refs):
            skip = 1 + n_in
            kernel(*refs[:skip], *refs[skip + n_after:])

        result = pl.pallas_call(
            body,
            out_shape=[jax.ShapeDtypeStruct(*(o if isinstance(o[0], tuple) else (o, f32))) for o in outs],
            in_specs=[pl.BlockSpec(memory_space=pltpu.SMEM)] + [vmem] * n_in
            + [pl.BlockSpec(memory_space=pl.ANY)] * n_after,
            out_specs=[vmem] * len(outs),
            scratch_shapes=list(scratch),
            name=name,
            compiler_params=pltpu.CompilerParams(vmem_limit_bytes=24 * 2**20),
            cost_estimate=pl.CostEstimate(flops=1000, bytes_accessed=1000, transcendentals=0),
        )(flags, *operands, *after)
        self.last = [result[0]]
        self.waits = []
        return result


def spread_kernel(parts, flags, in_ref, *out_refs):
    part = 0
    for out_ref, high_ref, low_ref in zip(out_refs[::3], out_refs[1::3], out_refs[2::3]):
        rows, columns = out_ref.shape
        for at in range(0, columns, TILE):
            cut = slice(at, at + TILE)
            value = in_ref[pl.ds(part, rows, stride=parts), :]
            out_ref[:, cut] = value
            high_ref[:, cut], low_ref[:, cut] = split(value)
            part += 1


def pick_kernel(which, flags, a_ref, b_ref, out_ref):
    @pl.when(flags[which] != 0)
    def _():
        out_ref[...] = a_ref[...]

    @pl.when(flags[which] == 0)
    def _():
        out_ref[...] = b_ref[...]


def panels_kernel(
    flags, held_ref, other_ref, both_ref, keep_high, keep_low, send_high, send_low, share_ref, stack
):
    width = held_ref.shape[1]
    share = share_ref.shape[0]
    held, other = held_ref[...], other_ref[...]
    low = flags[1] != 0
    p0, p1 = jnp.where(low, held, other), jnp.where(low, other, held)
    both_ref[:, :width] = p0
    both_ref[:, width:] = p1
    t0, t1 = p0.T, p1.T
    first = flags[2] != 0
    keep_high[...], keep_low[...] = split(jnp.where(first, t0, t1))
    send_high[...], send_low[...] = split(jnp.where(first, t1, t0))
    stack[:width] = dot(t0, p0)
    stack[width:2 * width] = dot(t1, p0)
    stack[2 * width:] = dot(t1, p1)
    share_ref[...] = stack[pl.ds(pl.multiple_of(flags[4] * share, 8), share), :]


def product_kernel(flags, panel_high, panel_low, *refs):
    panel = panel_high[...], panel_low[...]
    at, out_ref = 0, refs[-1]
    for high, low in zip(refs[:-1:2], refs[1:-1:2]):
        columns = high.shape[1]
        out_ref[:, at:at + columns] = dot3(panel, (high[...], low[...]))
        at += columns


def product_add_kernel(skip, flags, panel_high, panel_low, a_high, a_low, came_ref, out_ref):
    panel = panel_high[...], panel_low[...]
    came = came_ref[:, skip:skip + out_ref.shape[1]]
    out_ref[...] = dot3(panel, (a_high[...], a_low[...])) + came


def stack_kernel(flags, a_ref, b_ref, out_ref):
    rows = a_ref.shape[0]
    out_ref[:rows] = a_ref[...]
    out_ref[rows:] = b_ref[...]


def gather_kernel(which, flags, a_ref, b_ref, out_ref):
    share = out_ref.shape[0] // len(which)
    half = len(which) // 2
    for place, w in enumerate(which):
        at = pl.multiple_of((flags[4] ^ w) * share, 8)
        ref, here = (a_ref, place) if place < half else (b_ref, place - half)
        out_ref[pl.ds(at, share), :] = ref[here * share:(here + 1) * share]


def add_kernel(flags, a_ref, b_ref, out_ref):
    out_ref[...] = a_ref[...] + b_ref[...]


def eliminate(block, rows_ref, heads_ref):
    size = block.shape[0]
    group = 4
    sub = lax.broadcasted_iota(jnp.int32, (size, size), 0)
    lane = lax.broadcasted_iota(jnp.int32, (size, size), 1)
    left = block
    right = jnp.where(sub == lane, 1.0, 0.0).astype(f32)

    def spread(j):
        return [jnp.broadcast_to(left[:, j + p:j + p + 1], left.shape) for p in range(group)]

    cols = spread(0)
    for j in range(0, size, group):
        at = j % 8
        last = j + group == size
        ahead = [] if last else spread(j + group)
        rows = [left[at + p:at + p + 1] for p in range(group)]
        others = [right[at + p:at + p + 1] for p in range(group)]
        factors = []
        for p in range(group):
            head = cols[p][at + p:at + p + 1]
            factor = cols[p] * (1.0 / head)
            factors.append(factor)
            heads_ref[j + p:j + p + 1, :] = head
            rows_ref[j + p:j + p + 1, :] = others[p]
            for q in range(p + 1, group):
                cols[q] = cols[q] - factor * cols[p][at + q:at + q + 1]
                low = factor[at + q:at + q + 1]
                rows[q] = rows[q] - low * rows[p]
                others[q] = others[q] - low * others[p]
            for q in range(len(ahead)):
                here = at + group + q
                ahead[q] = ahead[q] - factor * cols[p][here:here + 1]
        if last:
            break
        cut = 8 if at + group == 8 else 0
        left, right, cols = left[cut:], right[cut:], [c[cut:] for c in ahead]
        for p in range(group):
            left = left - factors[p][cut:] * rows[p]
            right = right - factors[p][cut:] * others[p]


def factor_kernel(step, flags, *refs):
    if step == 0:
        gram_ref, out_state_ref, out_inv_ref, rows_ref, heads_ref = refs
    else:
        state_ref, inv_ref, out_state_ref, out_inv_ref, rows_ref, heads_ref = refs
    size = out_state_ref.shape[0]
    lo, hi = step * TILE, (step + 1) * TILE
    if step == 0:
        half = size // 2
        out_state_ref[:half, :half] = gram_ref[:half]
        out_state_ref[half:, :half] = gram_ref[half:size]
        out_state_ref[half:, half:] = gram_ref[size:]
        sub = lax.broadcasted_iota(jnp.int32, (size, size), 0)
        lane = lax.broadcasted_iota(jnp.int32, (size, size), 1)
        out_inv_ref[...] = jnp.where(sub == lane, 1.0, 0.0).astype(f32)
    else:
        out_state_ref[...] = state_ref[...]
        out_inv_ref[...] = inv_ref[...]
    eliminate(out_state_ref[lo:hi, lo:hi], rows_ref, heads_ref)
    block_inv = rows_ref[...] * lax.rsqrt(heads_ref[...])
    done = dot(block_inv, out_inv_ref[lo:hi, :hi])
    out_inv_ref[lo:hi, :hi] = done
    if hi < size:
        below = dot_nt(out_state_ref[hi:, lo:hi], block_inv)
        out_state_ref[hi:, hi:] = out_state_ref[hi:, hi:] - dot_nt(below, below)
        out_inv_ref[hi:, :hi] = out_inv_ref[hi:, :hi] - dot(below, done)


def weights_kernel(flags, both_ref, inv_ref, high_ref, low_ref):
    rows = both_ref.shape[0]
    width = both_ref.shape[1] // 2
    per_device = high_ref.shape[0] - rows
    inverse = inv_ref[...]
    high, low = split(inverse)
    ortho = split(dot3(split(both_ref[...]), split(inverse.T)))
    first = flags[2] != 0
    mine = inv_ref[pl.ds(pl.multiple_of(flags[5] * per_device, 8), per_device), :]

    def put(place, left, right):
        high_ref[place, :width], low_ref[place, :width] = split(jnp.where(first, left, right))
        high_ref[place, width:], low_ref[place, width:] = split(jnp.where(first, right, left))

    both = dot3(ortho, (high, low))
    put(slice(0, rows), both[:, :width], both[:, width:])
    put(slice(rows, rows + per_device), mine[:, :width], mine[:, width:])


def finish_kernel(flags, a_ref, high_ref, low_ref, first_ref, second_ref, rest_ref, factor_ref):
    rows, width = a_ref.shape[0], first_ref.shape[0]
    change = dot3((high_ref[:, :width], low_ref[:, :width]), split(first_ref[...]))
    change += dot3((high_ref[:, width:], low_ref[:, width:]), split(second_ref[...]))
    rest_ref[...] = a_ref[...] - change[:rows]
    factor_ref[...] = change[rows:]


def rows_kernel(parts, n, *refs):
    rests, factors, (rest_ref, factor_ref) = refs[:n], refs[n:2 * n], refs[2 * n:]

    def lay(pieces, out_ref):
        part = 0
        for piece in pieces:
            rows = piece.shape[0]
            for at in range(0, piece.shape[1], TILE):
                out_ref[pl.ds(part, rows, stride=parts), :] = piece[:, at:at + TILE]
                part += 1

    lay(rests, rest_ref)

    @pl.when(pl.program_id(0) == 0)
    def _():
        lay(factors, factor_ref)


def in_rows(rests, factors, parts):
    rows, own_rows = rests[0].shape[0], factors[0].shape[0]
    step = min(rows, 64)
    return pl.pallas_call(
        functools.partial(rows_kernel, parts, len(rests)),
        grid=(rows // step,),
        out_shape=[
            jax.ShapeDtypeStruct((rows * parts, TILE), f32),
            jax.ShapeDtypeStruct((own_rows * parts, TILE), f32),
        ],
        in_specs=[pl.BlockSpec((step, v.shape[1]), lambda i: (i, 0)) for v in rests]
        + [pl.BlockSpec(v.shape, lambda i: (0, 0)) for v in factors],
        out_specs=[
            pl.BlockSpec((step * parts, TILE), lambda i: (i, 0)),
            pl.BlockSpec((own_rows * parts, TILE), lambda i: (0, 0)),
        ],
        name="tiles_to_rows",
        compiler_params=pltpu.CompilerParams(vmem_limit_bytes=24 * 2**20),
    )(*rests, *factors)


def local(matrix):
    rows, blocks, _, width = matrix.shape
    parts = blocks * width // TILE
    depth = 2 * width
    n_row, n_col = lax.axis_size("prow"), lax.axis_size("pcol")
    row, col = lax.axis_index("prow"), lax.axis_index("pcol")
    place = row // 2
    line = n_row == 8
    sizes, sends = (SIZES, SENDS) if sum(SIZES) == blocks else ((blocks,), ((0,),))
    flags = jnp.stack([
        col >= 2, col % 2 == 0, row % 2 == 0, (place == 1) | (place == 2), col, row,
    ]).astype(jnp.int32)
    chain = Chain()
    flat = matrix.reshape(rows * parts, TILE)

    held = matrix[:, 0, 0, :]
    reach = 2
    came = lax.ppermute(held, "pcol", [(0, 2), (1, 3)]) if n_col > 2 else held
    shapes = []
    for count in sizes:
        shape = (rows, count * width)
        shapes += [shape, (shape, bf16), (shape, bf16)]
    cuts = chain(functools.partial(spread_kernel, parts), "rows_to_tiles", shapes, flags, flat)
    cuts = [cuts[3 * k:3 * k + 3] for k in range(len(sizes))]
    held, = chain(functools.partial(pick_kernel, 0), "pick", [held.shape], flags, came, held)
    reach = 4
    while reach < n_col:
        came = lax.ppermute(held, "pcol", [(i, i + reach) for i in range(reach) if i + reach < n_col])
        held = jnp.where((col >= reach) & (col < 2 * reach), came, held)
        reach *= 2
    beside = flip(held, "pcol", 1)

    state = {}
    starts = [sum(sizes[:k]) * width for k in range(len(sizes) + 1)]

    def in_hop(value):
        return lax.ppermute(value, "prow", [(0, 2), (1, 3), (6, 4), (7, 5)]) if line else None

    def mid_hop(value):
        return lax.ppermute(value, "prow", [(2, 4), (3, 5), (4, 2), (5, 3)]) if line else None

    def out_hop(value):
        return lax.ppermute(value, "prow", [(2, 0), (3, 1), (4, 6), (5, 7)]) if line else None

    def add(name, a, b):
        if b is None:
            return a
        return chain(add_kernel, name, [a.shape], flags, a, b)[0]

    def pick_inner(name, a, b):
        if b is None:
            bit = 2
            while bit < n_row:
                a = a + flip(a, "prow", bit)
                bit *= 2
            return a
        return chain(functools.partial(pick_kernel, 3), name, [a.shape], flags, a, b)[0]

    def run(task):
        if task == "gram":
            cut = ((width, rows), bf16)
            both, *panels, share = chain(
                panels_kernel, "panels", [(rows, depth)] + [cut] * 4 + [(3 * width // n_col, width)],
                flags, held, beside, scratch=[pltpu.VMEM((3 * width, width), f32)],
            )
            state.update(both=both, keep=panels[:2], send=panels[2:], g=share, gr=flip(share, "prow", 1))
        elif task == "g1" or task == "g2":
            state["g"] = add(task, state["g"], state["gr"])
            state["gr"] = flip(state["g"], "prow", 2 * int(task[1]))
        elif task == "g4":
            state["g"] = add(task, state["g"], state["gr"])
            bit = 8
            while bit < n_row:
                state["g"] = state["g"] + flip(state["g"], "prow", bit)
                bit *= 2
            bit = n_col // 2
            state["gr"] = flip(state["g"], "pcol", bit)
        elif task == "g5":
            bit = n_col // 2
            which = [0, bit]
            joint, = chain(stack_kernel, task, [(2 * state["g"].shape[0], width)], flags, state["g"], state["gr"])
            bit //= 2
            while bit > 1:
                which += [w ^ bit for w in which]
                joint = jnp.concatenate([joint, flip(joint, "pcol", bit)], 0)
                bit //= 2
            state.update(held=joint, which=which + [w ^ 1 for w in which], gr=flip(joint, "pcol", 1))
        elif task == "g6":
            state["gram"], = chain(
                functools.partial(gather_kernel, state["which"]), task, [(3 * width, width)], flags, state["held"], state["gr"]
            )
        elif task.startswith("ch"):
            step = int(task[2:])
            operands = [state["gram"]] if step == 0 else state["factor"]
            state["factor"] = chain(
                functools.partial(factor_kernel, step), f"factor{step}", [(depth, depth)] * 2, flags, *operands,
                scratch=[pltpu.VMEM((TILE, TILE), f32)] * 2,
            )
        elif task == "weights":
            cut = ((rows + depth // n_row, depth), bf16)
            state["weights"] = chain(weights_kernel, task, [cut] * 2, flags, state["both"], state["factor"][1])
        else:
            kind, k = task.rstrip("0123456789"), int(task.lstrip("abcdefghijklmnopqrstuvwxyz"))
            if k >= (len(sends) if kind == "send" else len(sizes)):
                return
            if kind != "send":
                lo, hi = starts[k], starts[k + 1]
            if kind == "send":
                members = sends[k]
                lo, hi = starts[members[0]], starts[members[-1] + 1]
                pieces = [v for member in members for v in cuts[member][1:]]
                out, = chain(product_kernel, task, [(width, hi - lo)], flags, *state["send"], *pieces)
                came = flip(out, "prow", 1)
                for member in members:
                    state["r", member] = came
            elif kind == "keep":
                skip = lo - starts[next(m for m in sends if k in m)[0]]
                out, = chain(functools.partial(product_add_kernel, skip), task, [(width, hi - lo)],
                             flags, *state["keep"], *cuts[k][1:], state["r", k])
                state["s", k], state["r", k] = out, in_hop(out)
            elif kind == "zm":
                out = add(task, state["s", k], state["r", k])
                state["s", k], state["r", k] = out, mid_hop(out)
            elif kind == "zo":
                out = add(task, state["s", k], state["r", k])
                state["s", k], state["r", k] = out, out_hop(out)
            elif kind == "ag":
                out = pick_inner(task, state["s", k], state["r", k])
                state["s", k], state["r", k] = out, flip(out, "prow", 1)
            elif kind == "fin":
                state["out", k] = chain(
                    finish_kernel, task, [(rows, hi - lo), (depth // n_row, hi - lo)],
                    flags, cuts[k][0], *state["weights"], state["s", k], state["r", k],
                )

    for task in " ".join(ORDER).split():
        if task[0] != "~":
            run(task)
        elif task[1] == "g":
            chain.waits.append(state["gr"])
        elif line and ("r", int(task[-1])) in state:
            chain.waits.append(state["r", int(task[-1])])
    outs = [state["out", k] for k in range(len(sizes))]
    rest, factor = in_rows([o[0] for o in outs], [o[1] for o in outs], parts)
    return (
        factor.reshape(depth // n_row, blocks, 1, width),
        rest.reshape(rows, blocks, 1, width),
    )


def solution(mesh):
    placed = P("prow", None, "pcol", None)
    return jax.shard_map(
        local, mesh=mesh, in_specs=(placed,), out_specs=(placed, placed), check_vma=False
    )
```

profile of v0, /device:TPU:0, one launch (start us, length us, event | category | flops | bytes accessed | tf_op | source)
XLA Modules:
  0.0 187.0 jit_solution(17415866125447529570)
XLA Ops:
  0.6 1.4 slice.3
  2.1 4.9 %collective-permute-start = (f32[512,256]{1,0:T(8,128)S(1)}, f32[512,256]{1,0:T(8,128)S(1)}, u32[]{:S(2)}, u32[]{:S(2)}) collective-permute-start(f32[512,256]{1,0:T(8,128)S(1)} %bitcast.13), channel_id=1, source_target_pairs={{0,2},{1,3},{4,6},{5,7},{8,10},{9,11},{12,14},{13,15},{16,18},{17,... | collective-permute-start | bytes 1572872 | tf_op jit(solution)/shard_map/ppermute | solution.py:312
  7.1 2.6 %copy-done = f32[512,11,1,256]{3,2,1,0:T(1,128)S(1)} copy-done((f32[512,11,1,256]{3,2,1,0:T(1,128)S(1)}, f32[512,11,1,256]{3,2,1,0:T(1,128)}, u32[]{:S(2)}) %copy-start) | copy-done | bytes 5767192
  9.7 2.4 %rows_to_tiles.1 = (f32[512,512]{1,0:T(8,128)S(1)}, bf16[512,512]{1,0:T(8,128)(2,1)S(1)}, bf16[512,512]{1,0:T(8,128)(2,1)S(1)}, f32[512,256]{1,0:T(8,128)S(1)}, ...) custom-call(s32[6]{0:T(128)S(1)} %stack.43.refs_0_, ...), custom_call_target="tpu_custom_call" | custom-call | flops 1000 | bytes 1000 | tf_op jit(solution)/shard_map/rows_to_tiles/pallas_call | solution.py:67
  12.1 6.0 %collective-permute-done.refs_1_ = f32[512,256]{1,0:T(8,128)S(1)} collective-permute-done((f32[512,256]{1,0:T(8,128)S(1)}, f32[512,256]{1,0:T(8,128)S(1)}, u32[]{:S(2)}, u32[]{:S(2)}) %collective-permute-start) | collective-permute-done | bytes 524320 | tf_op jit(solution)/shard_map/ppermute | solution.py:312
  18.8 1.9 %collective-permute-done.1.refs_2_ = f32[512,256]{1,0:T(8,128)S(1)} collective-permute-done((f32[512,256]{1,0:T(8,128)S(1)}, f32[512,256]{1,0:T(8,128)S(1)}, u32[]{:S(2)}, u32[]{:S(2)}) %collective-permute-start.1) | collective-permute-done | bytes 524320 | tf_op jit(solution)/shard_map/ppermute | solution.py:50
  20.7 2.3 %panels.1 = (f32[512,512]{1,0:T(8,128)S(1)}, bf16[256,512]{1,0:T(8,128)(2,1)S(1)}, bf16[256,512]{1,0:T(8,128)(2,1)S(1)}, bf16[256,512]{1,0:T(8,128)(2,1)S(1)}, b...) custom-call(s32[6]{0:T(128)S(1)} %stack.43.refs_0_, f32[512,256]{1,0:T(8,128)S(1)} %pick.1.refs_1_.refs_3_, ...), custom_call_target="tpu_custom_call" | custom-call | flops 1000 | bytes 1000 | tf_op jit(solution)/shard_map/panels/pallas_call | solution.py:67
  23.0 1.6 collective-permute-start.2
  27.2 1.6 collective-permute-start.8
  31.4 1.6 collective-permute-start.3
  33.0 4.1 %collective-permute-done.3.refs_6_.refs_2_ = f32[192,256]{1,0:T(8,128)S(1)} collective-permute-done((f32[192,256]{1,0:T(8,128)S(1)}, f32[192,256]{1,0:T(8,128)S(1)}, u32[]{:S(2)}, u32[]{:S(2)}) %collective-permute-start.3) | collective-permute-done | bytes 196640 | tf_op jit(solution)/shard_map/ppermute | solution.py:50
  40.8 1.6 collective-permute-start.6
  42.4 3.5 %collective-permute-start.7 = (f32[256,256]{1,0:T(8,128)S(1)}, f32[256,256]{1,0:T(8,128)S(1)}, u32[]{:S(2)}, u32[]{:S(2)}) collective-permute-start(f32[256,256]{1,0:T(8,128)S(1)} %keep1.1.refs_3_.refs_1_), channel_id=1, source_target_pairs={{0,8},{4,12},{24,16},{28,20},{1,9},{5,13},{25,17},{29,21},{2,10},{... | collective-permute-start | bytes 786440 | tf_op jit(solution)/shard_map/ppermute | solution.py:331
  48.8 3.5 %collective-permute-start.12 = (f32[256,512]{1,0:T(8,128)S(1)}, f32[256,512]{1,0:T(8,128)S(1)}, u32[]{:S(2)}, u32[]{:S(2)}) collective-permute-start(f32[256,512]{1,0:T(8,128)S(1)} %keep0.1.refs_5_.refs_1_), channel_id=1, source_target_pairs={{0,8},{4,12},{24,16},{28,20},{1,9},{5,13},{25,17},{29,21},{2,10},{... | collective-permute-start | bytes 1572872 | tf_op jit(solution)/shard_map/ppermute | solution.py:331
  54.4 4.5 %collective-permute-done.6.refs_5_ = f32[256,512]{1,0:T(8,128)S(1)} collective-permute-done((f32[256,512]{1,0:T(8,128)S(1)}, f32[256,512]{1,0:T(8,128)S(1)}, u32[]{:S(2)}, u32[]{:S(2)}) %collective-permute-start.6) | collective-permute-done | bytes 524320 | tf_op jit(solution)/shard_map/ppermute | solution.py:50
  60.0 3.5 %collective-permute-start.11 = (f32[256,512]{1,0:T(8,128)S(1)}, f32[256,512]{1,0:T(8,128)S(1)}, u32[]{:S(2)}, u32[]{:S(2)}) collective-permute-start(f32[256,512]{1,0:T(8,128)S(1)} %keep2.1.refs_3_.refs_1_), channel_id=1, source_target_pairs={{0,8},{4,12},{24,16},{28,20},{1,9},{5,13},{25,17},{29,21},{2,10},{... | collective-permute-start | bytes 1572872 | tf_op jit(solution)/shard_map/ppermute | solution.py:331
  64.2 4.6 %collective-permute-done.5.refs_2_ = f32[192,256]{1,0:T(8,128)S(1)} collective-permute-done((f32[192,256]{1,0:T(8,128)S(1)}, f32[192,256]{1,0:T(8,128)S(1)}, u32[]{:S(2)}, u32[]{:S(2)}) %collective-permute-start.5) | collective-permute-done | bytes 196640 | tf_op jit(solution)/shard_map/ppermute | solution.py:50
  68.8 1.5 collective-permute-start.10
  74.1 2.5 %collective-permute-start.9 = (f32[192,256]{1,0:T(8,128)S(1)}, f32[192,256]{1,0:T(8,128)S(1)}, u32[]{:S(2)}, u32[]{:S(2)}) collective-permute-start(f32[192,256]{1,0:T(8,128)S(1)} %g4.1.refs_6_.refs_1_), channel_id=1, source_target_pairs={{0,2},{1,3},{2,0},{3,1},{4,6},{5,7},{6,4},{7,5},{8,10},{9,11},{10,... | collective-permute-start | bytes 589832 | tf_op jit(solution)/shard_map/ppermute | solution.py:50
  77.5 6.3 %collective-permute-start.17 = (f32[256,512]{1,0:T(8,128)S(1)}, f32[256,512]{1,0:T(8,128)S(1)}, u32[]{:S(2)}, u32[]{:S(2)}) collective-permute-start(f32[256,512]{1,0:T(8,128)S(1)} %keep4.1.refs_3_.refs_1_), channel_id=1, source_target_pairs={{0,8},{4,12},{24,16},{28,20},{1,9},{5,13},{25,17},{29,21},{2,10},{... | collective-permute-start | bytes 1572872 | tf_op jit(solution)/shard_map/ppermute | solution.py:331
  87.6 1.3 collective-permute-start.20
  88.9 2.9 %collective-permute-done.18.refs_5_ = f32[256,512]{1,0:T(8,128)S(1)} collective-permute-done((f32[256,512]{1,0:T(8,128)S(1)}, f32[256,512]{1,0:T(8,128)S(1)}, u32[]{:S(2)}, u32[]{:S(2)}) %collective-permute-start.18) | collective-permute-done | bytes 524320 | tf_op jit(solution)/shard_map/ppermute | solution.py:50
  91.8 4.2 %collective-permute-start.24 = (f32[256,512]{1,0:T(8,128)S(1)}, f32[256,512]{1,0:T(8,128)S(1)}, u32[]{:S(2)}, u32[]{:S(2)}) collective-permute-start(f32[256,512]{1,0:T(8,128)S(1)} %keep3.1.refs_3_.refs_1_), channel_id=1, source_target_pairs={{0,8},{4,12},{24,16},{28,20},{1,9},{5,13},{25,17},{29,21},{2,10},{... | collective-permute-start | bytes 1572872 | tf_op jit(solution)/shard_map/ppermute | solution.py:331
  99.0 1.3 collective-permute-start.22
  100.3 4.6 %collective-permute-start.21 = (f32[256,512]{1,0:T(8,128)S(1)}, f32[256,512]{1,0:T(8,128)S(1)}, u32[]{:S(2)}, u32[]{:S(2)}) collective-permute-start(f32[256,512]{1,0:T(8,128)S(1)} %keep5.1.refs_3_.refs_1_), channel_id=1, source_target_pairs={{0,8},{4,12},{24,16},{28,20},{1,9},{5,13},{25,17},{29,21},{2,10},{... | collective-permute-start | bytes 1572872 | tf_op jit(solution)/shard_map/ppermute | solution.py:331
  107.5 4.9 %factor0.1 = (f32[512,512]{1,0:T(8,128)S(1)}, f32[512,512]{1,0:T(8,128)S(1)}) custom-call(s32[6]{0:T(128)S(1)} %stack.43.refs_0_, f32[768,256]{1,0:T(8,128)S(1)} %g6.1.refs_3_.refs_1_, f32[256,512]{1,0:T(8,128)S(1)} %ag0.1.refs_2_.refs_4_), custom_call_target="tpu_custom_call" | custom-call | flops 1000 | bytes 1000 | tf_op jit(solution)/shard_map/factor0/pallas_call | solution.py:67
  113.6 1.3 collective-permute-start.25
  115.5 2.2 %collective-permute-done.22.refs_2_ = f32[256,512]{1,0:T(8,128)S(1)} collective-permute-done((f32[256,512]{1,0:T(8,128)S(1)}, f32[256,512]{1,0:T(8,128)S(1)}, u32[]{:S(2)}, u32[]{:S(2)}) %collective-permute-start.22) | collective-permute-done | bytes 524320 | tf_op jit(solution)/shard_map/ppermute | solution.py:337
  118.3 1.4 collective-permute-start.26
  121.0 1.7 collective-permute-done.25.refs_4_.refs_2_
  123.9 2.6 %collective-permute-start.29 = (f32[256,512]{1,0:T(8,128)S(1)}, f32[256,512]{1,0:T(8,128)S(1)}, u32[]{:S(2)}, u32[]{:S(2)}) collective-permute-start(f32[256,512]{1,0:T(8,128)S(1)} %ag0.1.refs_2_.refs_4_), channel_id=1, source_target_pairs={{0,4},{4,0},{8,12},{12,8},{16,20},{20,16},{24,28},{28,24},{1,5},{5... | collective-permute-start | bytes 1572872 | tf_op jit(solution)/shard_map/ppermute | solution.py:50
  127.2 6.0 %collective-permute-done.26.refs_4_.refs_5_ = f32[256,512]{1,0:T(8,128)S(1)} collective-permute-done((f32[256,512]{1,0:T(8,128)S(1)}, f32[256,512]{1,0:T(8,128)S(1)}, u32[]{:S(2)}, u32[]{:S(2)}) %collective-permute-start.26) | collective-permute-done | bytes 524320 | tf_op jit(solution)/shard_map/ppermute | solution.py:50
  133.2 4.7 %factor1.1 = (f32[512,512]{1,0:T(8,128)S(1)}, f32[512,512]{1,0:T(8,128)S(1)}) custom-call(s32[6]{0:T(128)S(1)} %stack.43.refs_0_, f32[512,512]{1,0:T(8,128)S(1)} %get-tuple-element.69.refs_3_.refs_1_, f32[512,512]{1,0:T(8,128)S(1)} %get-tuple-element.70.refs_2_, f32[256,512]{1,0:T(8,128)S(1)} %zm5.1.refs_3_.refs_1_, ...), custom_call_target="tpu_custom_call" | custom-call | flops 1000 | bytes 1000 | tf_op jit(solution)/shard_map/factor1/pallas_call | solution.py:67
  140.5 1.4 collective-permute-start.35
  142.7 1.8 collective-permute-done.29.refs_4_.refs_5_
  144.4 4.7 %factor2.1 = (f32[512,512]{1,0:T(8,128)S(1)}, f32[512,512]{1,0:T(8,128)S(1)}) custom-call(s32[6]{0:T(128)S(1)} %stack.43.refs_0_, f32[512,512]{1,0:T(8,128)S(1)} %get-tuple-element.71.refs_3_.refs_1_, f32[512,512]{1,0:T(8,128)S(1)} %get-tuple-element.72.refs_2_, f32[256,256]{1,0:T(8,128)S(1)} %ag1.1.refs_3_.refs_4_, ...), custom_call_target="tpu_custom_call" | custom-call | flops 1000 | bytes 1000 | tf_op jit(solution)/shard_map/factor2/pallas_call | solution.py:67
  151.1 1.4 collective-permute-start.34
  152.5 4.0 %factor3.1 = (f32[512,512]{1,0:T(8,128)S(1)}, f32[512,512]{1,0:T(8,128)S(1)}) custom-call(s32[6]{0:T(128)S(1)} %stack.43.refs_0_, f32[512,512]{1,0:T(8,128)S(1)} %get-tuple-element.73.refs_3_.refs_1_, f32[512,512]{1,0:T(8,128)S(1)} %get-tuple-element.74.refs_2_, f32[256,512]{1,0:T(8,128)S(1)} %zo3.1.refs_3_.refs_1_), custom_call_target="tpu_custom_call" | custom-call | flops 1000 | bytes 1000 | tf_op jit(solution)/shard_map/factor3/pallas_call | solution.py:67
  157.9 2.6 %weights.1 = (bf16[576,512]{1,0:T(8,128)(2,1)S(1)}, bf16[576,512]{1,0:T(8,128)(2,1)S(1)}) custom-call(s32[6]{0:T(128)S(1)} %stack.43.refs_0_, f32[512,512]{1,0:T(8,128)S(1)} %get-tuple-element.51.refs_5_.refs_1_, f32[512,512]{1,0:T(8,128)S(1)} %get-tuple-element.75.refs_2_, f32[256,512]{1,0:T(8,128)S(1)} %ag5.1.refs_3_.refs_4_), custom_call_target="tpu_custom_call" | custom-call | flops 1000 | bytes 1000 | tf_op jit(solution)/shard_map/weights/pallas_call | solution.py:67
  160.5 1.6 fin4.1
  164.2 1.4 collective-permute-start.36
  165.6 7.0 %collective-permute-done.32.refs_5_ = f32[256,512]{1,0:T(8,128)S(1)} collective-permute-done((f32[256,512]{1,0:T(8,128)S(1)}, f32[256,512]{1,0:T(8,128)S(1)}, u32[]{:S(2)}, u32[]{:S(2)}) %collective-permute-start.32) | collective-permute-done | bytes 524320 | tf_op jit(solution)/shard_map/ppermute | solution.py:50
  172.5 1.6 fin5.1
  174.2 1.6 fin2.1
  175.8 1.6 fin0.1
  177.4 3.8 %collective-permute-done.36.refs_5_ = f32[256,512]{1,0:T(8,128)S(1)} collective-permute-done((f32[256,512]{1,0:T(8,128)S(1)}, f32[256,512]{1,0:T(8,128)S(1)}, u32[]{:S(2)}, u32[]{:S(2)}) %collective-permute-start.36) | collective-permute-done | bytes 524320 | tf_op jit(solution)/shard_map/ppermute | solution.py:50
  181.2 1.6 fin3.1
  182.9 4.2 %tiles_to_rows.1 = (f32[11264,128]{1,0:T(8,128)}, f32[1408,128]{1,0:T(8,128)}) custom-call(f32[512,512]{1,0:T(8,128)S(1)} %get-tuple-element.87.refs_6_.refs_0_, f32[512,256]{1,0:T(8,128)S(1)} %get-tuple-element.84.refs_3_.refs_1_, f32[512,512]{1,0:T(8,128)S(1)} %get-tuple-element.86.refs_6_.refs_2_, f32[512,512]{1,0:T(8,128)S(1)} %get-tuple-element.89.refs_3_, ...), custom_call_target="tpu_custom_call" | custom-call | tf_op jit(solution)/shard_map/tiles_to_rows/pallas_call | solution.py:277
  (81 shorter events, 44.4 us)
Async XLA Ops:
  2.1 16.0 %collective-permute-start = (f32[512,256]{1,0:T(8,128)S(1)}, f32[512,256]{1,0:T(8,128)S(1)}, u32[]{:S(2)}, u32[]{:S(2)}) collective-permute-start(f32[512,256]{1,0:T(8,128)S(1)} %bitcast.13), channel_id=1, source_target_pairs={{0,2},{1,3},{4,6},{5,7},{8,10},{9,11},{12,14},{13,15},{16,18},{17,... | collective-permute-start | bytes 1572872 | tf_op jit(solution)/shard_map/ppermute | solution.py:312
  7.1 2.6 %copy-start = (f32[512,11,1,256]{3,2,1,0:T(1,128)S(1)}, f32[512,11,1,256]{3,2,1,0:T(1,128)}, u32[]{:S(2)}) copy-start(f32[512,11,1,256]{3,2,1,0:T(1,128)} %param.1) | copy-start | bytes 17301508
  18.7 2.0 %collective-permute-start.1 = (f32[512,256]{1,0:T(8,128)S(1)}, f32[512,256]{1,0:T(8,128)S(1)}, u32[]{:S(2)}, u32[]{:S(2)}) collective-permute-start(f32[512,256]{1,0:T(8,128)S(1)} %pick.1.refs_1_.refs_3_), channel_id=1, source_target_pairs={{0,1},{1,0},{2,3},{3,2},{4,5},{5,4},{6,7},{7,6},{8,9},{9,8},{10,11... | collective-permute-start | bytes 1572872 | tf_op jit(solution)/shard_map/ppermute | solution.py:50
  23.0 7.8 %collective-permute-start.2 = (f32[192,256]{1,0:T(8,128)S(1)}, f32[192,256]{1,0:T(8,128)S(1)}, u32[]{:S(2)}, u32[]{:S(2)}) collective-permute-start(f32[192,256]{1,0:T(8,128)S(1)} %get-tuple-element.52.refs_1_), channel_id=1, source_target_pairs={{0,4},{4,0},{8,12},{12,8},{16,20},{20,16},{24,28},{28,24},{1,5},{5... | collective-permute-start | bytes 589832 | tf_op jit(solution)/shard_map/ppermute | solution.py:50
  25.5 12.7 %collective-permute-start.4 = (f32[256,256]{1,0:T(8,128)S(1)}, f32[256,256]{1,0:T(8,128)S(1)}, u32[]{:S(2)}, u32[]{:S(2)}) collective-permute-start(f32[256,256]{1,0:T(8,128)S(1)} %send1.1.refs_5_), channel_id=1, source_target_pairs={{0,4},{4,0},{8,12},{12,8},{16,20},{20,16},{24,28},{28,24},{1,5},{5... | collective-permute-start | bytes 786440 | tf_op jit(solution)/shard_map/ppermute | solution.py:50
  27.2 20.5 %collective-permute-start.8 = (f32[256,512]{1,0:T(8,128)S(1)}, f32[256,512]{1,0:T(8,128)S(1)}, u32[]{:S(2)}, u32[]{:S(2)}) collective-permute-start(f32[256,512]{1,0:T(8,128)S(1)} %send0.1.refs_5_), channel_id=1, source_target_pairs={{0,4},{4,0},{8,12},{12,8},{16,20},{20,16},{24,28},{28,24},{1,5},{5... | collective-permute-start | bytes 1572872 | tf_op jit(solution)/shard_map/ppermute | solution.py:50
  31.4 5.7 %collective-permute-start.3 = (f32[192,256]{1,0:T(8,128)S(1)}, f32[192,256]{1,0:T(8,128)S(1)}, u32[]{:S(2)}, u32[]{:S(2)}) collective-permute-start(f32[192,256]{1,0:T(8,128)S(1)} %g1.1.refs_5_.refs_1_), channel_id=1, source_target_pairs={{0,8},{4,12},{8,0},{12,4},{16,24},{20,28},{24,16},{28,20},{1,9},{5... | collective-permute-start | bytes 589832 | tf_op jit(solution)/shard_map/ppermute | solution.py:50
  40.8 18.1 %collective-permute-start.6 = (f32[256,512]{1,0:T(8,128)S(1)}, f32[256,512]{1,0:T(8,128)S(1)}, u32[]{:S(2)}, u32[]{:S(2)}) collective-permute-start(f32[256,512]{1,0:T(8,128)S(1)} %send2.1.refs_6_), channel_id=1, source_target_pairs={{0,4},{4,0},{8,12},{12,8},{16,20},{20,16},{24,28},{28,24},{1,5},{5... | collective-permute-start | bytes 1572872 | tf_op jit(solution)/shard_map/ppermute | solution.py:50
  42.4 11.4 %collective-permute-start.7 = (f32[256,256]{1,0:T(8,128)S(1)}, f32[256,256]{1,0:T(8,128)S(1)}, u32[]{:S(2)}, u32[]{:S(2)}) collective-permute-start(f32[256,256]{1,0:T(8,128)S(1)} %keep1.1.refs_3_.refs_1_), channel_id=1, source_target_pairs={{0,8},{4,12},{24,16},{28,20},{1,9},{5,13},{25,17},{29,21},{2,10},{... | collective-permute-start | bytes 786440 | tf_op jit(solution)/shard_map/ppermute | solution.py:331
  45.9 25.0 %collective-permute-start.13 = (f32[256,512]{1,0:T(8,128)S(1)}, f32[256,512]{1,0:T(8,128)S(1)}, u32[]{:S(2)}, u32[]{:S(2)}) collective-permute-start(f32[256,512]{1,0:T(8,128)S(1)} %send4.1.refs_3_), channel_id=1, source_target_pairs={{0,4},{4,0},{8,12},{12,8},{16,20},{20,16},{24,28},{28,24},{1,5},{5... | collective-permute-start | bytes 1572872 | tf_op jit(solution)/shard_map/ppermute | solution.py:50
  48.8 23.3 %collective-permute-start.12 = (f32[256,512]{1,0:T(8,128)S(1)}, f32[256,512]{1,0:T(8,128)S(1)}, u32[]{:S(2)}, u32[]{:S(2)}) collective-permute-start(f32[256,512]{1,0:T(8,128)S(1)} %keep0.1.refs_5_.refs_1_), channel_id=1, source_target_pairs={{0,8},{4,12},{24,16},{28,20},{1,9},{5,13},{25,17},{29,21},{2,10},{... | collective-permute-start | bytes 1572872 | tf_op jit(solution)/shard_map/ppermute | solution.py:331
  52.3 16.5 %collective-permute-start.5 = (f32[192,256]{1,0:T(8,128)S(1)}, f32[192,256]{1,0:T(8,128)S(1)}, u32[]{:S(2)}, u32[]{:S(2)}) collective-permute-start(f32[192,256]{1,0:T(8,128)S(1)} %g2.1.refs_5_.refs_1_), channel_id=1, source_target_pairs={{0,16},{4,20},{8,24},{12,28},{16,0},{20,4},{24,8},{28,12},{1,17},{... | collective-permute-start | bytes 589832 | tf_op jit(solution)/shard_map/ppermute | solution.py:50
  60.0 17.5 %collective-permute-start.11 = (f32[256,512]{1,0:T(8,128)S(1)}, f32[256,512]{1,0:T(8,128)S(1)}, u32[]{:S(2)}, u32[]{:S(2)}) collective-permute-start(f32[256,512]{1,0:T(8,128)S(1)} %keep2.1.refs_3_.refs_1_), channel_id=1, source_target_pairs={{0,8},{4,12},{24,16},{28,20},{1,9},{5,13},{25,17},{29,21},{2,10},{... | collective-permute-start | bytes 1572872 | tf_op jit(solution)/shard_map/ppermute | solution.py:331
  63.5 8.5 %collective-permute-start.14 = (f32[256,256]{1,0:T(8,128)S(1)}, f32[256,256]{1,0:T(8,128)S(1)}, u32[]{:S(2)}, u32[]{:S(2)}) collective-permute-start(f32[256,256]{1,0:T(8,128)S(1)} %zm1.1.refs_6_.refs_1_), channel_id=1, source_target_pairs={{8,16},{12,20},{16,8},{20,12},{9,17},{13,21},{17,9},{21,13},{10,18... | collective-permute-start | bytes 786440 | tf_op jit(solution)/shard_map/ppermute | solution.py:334
  68.8 15.6 %collective-permute-start.10 = (f32[256,512]{1,0:T(8,128)S(1)}, f32[256,512]{1,0:T(8,128)S(1)}, u32[]{:S(2)}, u32[]{:S(2)}) collective-permute-start(f32[256,512]{1,0:T(8,128)S(1)} %send3.1.refs_3_), channel_id=1, source_target_pairs={{0,4},{4,0},{8,12},{12,8},{16,20},{20,16},{24,28},{28,24},{1,5},{5... | collective-permute-start | bytes 1572872 | tf_op jit(solution)/shard_map/ppermute | solution.py:50
  72.7 14.3 %collective-permute-start.19 = (f32[256,512]{1,0:T(8,128)S(1)}, f32[256,512]{1,0:T(8,128)S(1)}, u32[]{:S(2)}, u32[]{:S(2)}) collective-permute-start(f32[256,512]{1,0:T(8,128)S(1)} %zm0.1.refs_3_.refs_1_), channel_id=1, source_target_pairs={{8,16},{12,20},{16,8},{20,12},{9,17},{13,21},{17,9},{21,13},{10,18... | collective-permute-start | bytes 1572872 | tf_op jit(solution)/shard_map/ppermute | solution.py:334
  73.4 18.4 %collective-permute-start.18 = (f32[256,512]{1,0:T(8,128)S(1)}, f32[256,512]{1,0:T(8,128)S(1)}, u32[]{:S(2)}, u32[]{:S(2)}) collective-permute-start(f32[256,512]{1,0:T(8,128)S(1)} %send5.1.refs_6_), channel_id=1, source_target_pairs={{0,4},{4,0},{8,12},{12,8},{16,20},{20,16},{24,28},{28,24},{1,5},{5... | collective-permute-start | bytes 1572872 | tf_op jit(solution)/shard_map/ppermute | solution.py:50
  74.1 12.1 %collective-permute-start.9 = (f32[192,256]{1,0:T(8,128)S(1)}, f32[192,256]{1,0:T(8,128)S(1)}, u32[]{:S(2)}, u32[]{:S(2)}) collective-permute-start(f32[192,256]{1,0:T(8,128)S(1)} %g4.1.refs_6_.refs_1_), channel_id=1, source_target_pairs={{0,2},{1,3},{2,0},{3,1},{4,6},{5,7},{6,4},{7,5},{8,10},{9,11},{10,... | collective-permute-start | bytes 589832 | tf_op jit(solution)/shard_map/ppermute | solution.py:50
  77.5 19.6 %collective-permute-start.17 = (f32[256,512]{1,0:T(8,128)S(1)}, f32[256,512]{1,0:T(8,128)S(1)}, u32[]{:S(2)}, u32[]{:S(2)}) collective-permute-start(f32[256,512]{1,0:T(8,128)S(1)} %keep4.1.refs_3_.refs_1_), channel_id=1, source_target_pairs={{0,8},{4,12},{24,16},{28,20},{1,9},{5,13},{25,17},{29,21},{2,10},{... | collective-permute-start | bytes 1572872 | tf_op jit(solution)/shard_map/ppermute | solution.py:331
  84.5 13.9 %collective-permute-start.16 = (f32[256,512]{1,0:T(8,128)S(1)}, f32[256,512]{1,0:T(8,128)S(1)}, u32[]{:S(2)}, u32[]{:S(2)}) collective-permute-start(f32[256,512]{1,0:T(8,128)S(1)} %zm2.1.refs_6_.refs_1_), channel_id=1, source_target_pairs={{8,16},{12,20},{16,8},{20,12},{9,17},{13,21},{17,9},{21,13},{10,18... | collective-permute-start | bytes 1572872 | tf_op jit(solution)/shard_map/ppermute | solution.py:334
  86.9 13.5 %collective-permute-start.15 = (f32[384,256]{1,0:T(8,128)S(1)}, f32[384,256]{1,0:T(8,128)S(1)}, u32[]{:S(2)}, u32[]{:S(2)}) collective-permute-start(f32[384,256]{1,0:T(8,128)S(1)} %g5.1.refs_3_.refs_1_), channel_id=1, source_target_pairs={{0,1},{1,0},{2,3},{3,2},{4,5},{5,4},{6,7},{7,6},{8,9},{9,8},{10,11... | collective-permute-start | bytes 1179656 | tf_op jit(solution)/shard_map/ppermute | solution.py:50
  87.6 19.2 %collective-permute-start.20 = (f32[256,512]{1,0:T(8,128)S(1)}, f32[256,512]{1,0:T(8,128)S(1)}, u32[]{:S(2)}, u32[]{:S(2)}) collective-permute-start(f32[256,512]{1,0:T(8,128)S(1)} %zo0.1.refs_6_.refs_1_), channel_id=1, source_target_pairs={{8,0},{12,4},{16,24},{20,28},{9,1},{13,5},{17,25},{21,29},{10,2},{... | collective-permute-start | bytes 1572872 | tf_op jit(solution)/shard_map/ppermute | solution.py:337
  91.8 20.6 %collective-permute-start.24 = (f32[256,512]{1,0:T(8,128)S(1)}, f32[256,512]{1,0:T(8,128)S(1)}, u32[]{:S(2)}, u32[]{:S(2)}) collective-permute-start(f32[256,512]{1,0:T(8,128)S(1)} %keep3.1.refs_3_.refs_1_), channel_id=1, source_target_pairs={{0,8},{4,12},{24,16},{28,20},{1,9},{5,13},{25,17},{29,21},{2,10},{... | collective-permute-start | bytes 1572872 | tf_op jit(solution)/shard_map/ppermute | solution.py:331
  97.7 17.2 %collective-permute-start.23 = (f32[256,512]{1,0:T(8,128)S(1)}, f32[256,512]{1,0:T(8,128)S(1)}, u32[]{:S(2)}, u32[]{:S(2)}) collective-permute-start(f32[256,512]{1,0:T(8,128)S(1)} %zm4.1.refs_3_.refs_1_), channel_id=1, source_target_pairs={{8,16},{12,20},{16,8},{20,12},{9,17},{13,21},{17,9},{21,13},{10,18... | collective-permute-start | bytes 1572872 | tf_op jit(solution)/shard_map/ppermute | solution.py:334
  99.0 18.7 %collective-permute-start.22 = (f32[256,512]{1,0:T(8,128)S(1)}, f32[256,512]{1,0:T(8,128)S(1)}, u32[]{:S(2)}, u32[]{:S(2)}) collective-permute-start(f32[256,512]{1,0:T(8,128)S(1)} %zo2.1.refs_3_.refs_1_), channel_id=1, source_target_pairs={{8,0},{12,4},{16,24},{20,28},{9,1},{13,5},{17,25},{21,29},{10,2},{... | collective-permute-start | bytes 1572872 | tf_op jit(solution)/shard_map/ppermute | solution.py:337
  100.3 20.6 %collective-permute-start.21 = (f32[256,512]{1,0:T(8,128)S(1)}, f32[256,512]{1,0:T(8,128)S(1)}, u32[]{:S(2)}, u32[]{:S(2)}) collective-permute-start(f32[256,512]{1,0:T(8,128)S(1)} %keep5.1.refs_3_.refs_1_), channel_id=1, source_target_pairs={{0,8},{4,12},{24,16},{28,20},{1,9},{5,13},{25,17},{29,21},{2,10},{... | collective-permute-start | bytes 1572872 | tf_op jit(solution)/shard_map/ppermute | solution.py:331
  113.6 9.1 %collective-permute-start.25 = (f32[256,256]{1,0:T(8,128)S(1)}, f32[256,256]{1,0:T(8,128)S(1)}, u32[]{:S(2)}, u32[]{:S(2)}) collective-permute-start(f32[256,256]{1,0:T(8,128)S(1)} %zo1.1.refs_3_.refs_1_), channel_id=1, source_target_pairs={{8,0},{12,4},{16,24},{20,28},{9,1},{13,5},{17,25},{21,29},{10,2},{... | collective-permute-start | bytes 786440 | tf_op jit(solution)/shard_map/ppermute | solution.py:337
  118.3 14.9 %collective-permute-start.26 = (f32[256,512]{1,0:T(8,128)S(1)}, f32[256,512]{1,0:T(8,128)S(1)}, u32[]{:S(2)}, u32[]{:S(2)}) collective-permute-start(f32[256,512]{1,0:T(8,128)S(1)} %ag2.1.refs_3_.refs_4_), channel_id=1, source_target_pairs={{0,4},{4,0},{8,12},{12,8},{16,20},{20,16},{24,28},{28,24},{1,5},{5... | collective-permute-start | bytes 1572872 | tf_op jit(solution)/shard_map/ppermute | solution.py:50
  119.7 18.3 %collective-permute-start.28 = (f32[256,512]{1,0:T(8,128)S(1)}, f32[256,512]{1,0:T(8,128)S(1)}, u32[]{:S(2)}, u32[]{:S(2)}) collective-permute-start(f32[256,512]{1,0:T(8,128)S(1)} %zo4.1.refs_3_.refs_1_), channel_id=1, source_target_pairs={{8,0},{12,4},{16,24},{20,28},{9,1},{13,5},{17,25},{21,29},{10,2},{... | collective-permute-start | bytes 1572872 | tf_op jit(solution)/shard_map/ppermute | solution.py:337
  123.2 15.3 %collective-permute-start.27 = (f32[256,512]{1,0:T(8,128)S(1)}, f32[256,512]{1,0:T(8,128)S(1)}, u32[]{:S(2)}, u32[]{:S(2)}) collective-permute-start(f32[256,512]{1,0:T(8,128)S(1)} %zm5.1.refs_3_.refs_1_), channel_id=1, source_target_pairs={{8,16},{12,20},{16,8},{20,12},{9,17},{13,21},{17,9},{21,13},{10,18... | collective-permute-start | bytes 1572872 | tf_op jit(solution)/shard_map/ppermute | solution.py:334
  123.9 20.5 %collective-permute-start.29 = (f32[256,512]{1,0:T(8,128)S(1)}, f32[256,512]{1,0:T(8,128)S(1)}, u32[]{:S(2)}, u32[]{:S(2)}) collective-permute-start(f32[256,512]{1,0:T(8,128)S(1)} %ag0.1.refs_2_.refs_4_), channel_id=1, source_target_pairs={{0,4},{4,0},{8,12},{12,8},{16,20},{20,16},{24,28},{28,24},{1,5},{5... | collective-permute-start | bytes 1572872 | tf_op jit(solution)/shard_map/ppermute | solution.py:50
  126.6 22.6 %collective-permute-start.30 = (f32[256,512]{1,0:T(8,128)S(1)}, f32[256,512]{1,0:T(8,128)S(1)}, u32[]{:S(2)}, u32[]{:S(2)}) collective-permute-start(f32[256,512]{1,0:T(8,128)S(1)} %zm3.1.refs_3_.refs_1_), channel_id=1, source_target_pairs={{8,16},{12,20},{16,8},{20,12},{9,17},{13,21},{17,9},{21,13},{10,18... | collective-permute-start | bytes 1572872 | tf_op jit(solution)/shard_map/ppermute | solution.py:334
  139.2 17.4 %collective-permute-start.31 = (f32[256,512]{1,0:T(8,128)S(1)}, f32[256,512]{1,0:T(8,128)S(1)}, u32[]{:S(2)}, u32[]{:S(2)}) collective-permute-start(f32[256,512]{1,0:T(8,128)S(1)} %zo5.1.refs_3_.refs_1_), channel_id=1, source_target_pairs={{8,0},{12,4},{16,24},{20,28},{9,1},{13,5},{17,25},{21,29},{10,2},{... | collective-permute-start | bytes 1572872 | tf_op jit(solution)/shard_map/ppermute | solution.py:337
  140.5 20.0 %collective-permute-start.35 = (f32[256,512]{1,0:T(8,128)S(1)}, f32[256,512]{1,0:T(8,128)S(1)}, u32[]{:S(2)}, u32[]{:S(2)}) collective-permute-start(f32[256,512]{1,0:T(8,128)S(1)} %ag4.1.refs_3_.refs_4_), channel_id=1, source_target_pairs={{0,4},{4,0},{8,12},{12,8},{16,20},{20,16},{24,28},{28,24},{1,5},{5... | collective-permute-start | bytes 1572872 | tf_op jit(solution)/shard_map/ppermute | solution.py:50
  149.8 12.3 %collective-permute-start.33 = (f32[256,512]{1,0:T(8,128)S(1)}, f32[256,512]{1,0:T(8,128)S(1)}, u32[]{:S(2)}, u32[]{:S(2)}) collective-permute-start(f32[256,512]{1,0:T(8,128)S(1)} %zo3.1.refs_3_.refs_1_), channel_id=1, source_target_pairs={{8,0},{12,4},{16,24},{20,28},{9,1},{13,5},{17,25},{21,29},{10,2},{... | collective-permute-start | bytes 1572872 | tf_op jit(solution)/shard_map/ppermute | solution.py:337
  151.1 11.0 %collective-permute-start.34 = (f32[256,256]{1,0:T(8,128)S(1)}, f32[256,256]{1,0:T(8,128)S(1)}, u32[]{:S(2)}, u32[]{:S(2)}) collective-permute-start(f32[256,256]{1,0:T(8,128)S(1)} %ag1.1.refs_3_.refs_4_), channel_id=1, source_target_pairs={{0,4},{4,0},{8,12},{12,8},{16,20},{20,16},{24,28},{28,24},{1,5},{5... | collective-permute-start | bytes 786440 | tf_op jit(solution)/shard_map/ppermute | solution.py:50
  157.1 15.4 %collective-permute-start.32 = (f32[256,512]{1,0:T(8,128)S(1)}, f32[256,512]{1,0:T(8,128)S(1)}, u32[]{:S(2)}, u32[]{:S(2)}) collective-permute-start(f32[256,512]{1,0:T(8,128)S(1)} %ag5.1.refs_3_.refs_4_), channel_id=1, source_target_pairs={{0,4},{4,0},{8,12},{12,8},{16,20},{20,16},{24,28},{28,24},{1,5},{5... | collective-permute-start | bytes 1572872 | tf_op jit(solution)/shard_map/ppermute | solution.py:50
  164.2 17.1 %collective-permute-start.36 = (f32[256,512]{1,0:T(8,128)S(1)}, f32[256,512]{1,0:T(8,128)S(1)}, u32[]{:S(2)}, u32[]{:S(2)}) collective-permute-start(f32[256,512]{1,0:T(8,128)S(1)} %ag3.1.refs_6_.refs_4_), channel_id=1, source_target_pairs={{0,4},{4,0},{8,12},{12,8},{16,20},{20,16},{24,28},{28,24},{1,5},{5... | collective-permute-start | bytes 1572872 | tf_op jit(solution)/shard_map/ppermute | solution.py:50
where the time goes:
time: 188 us; the launch traced here: 187 us
  Pallas kernels  66.7 us (35%)
  starting transfers between devices  64.1 us (34%)
  waiting for transfers between devices  50.6 us (27%)
  local copies, waits for them, and re-layouts  4.16 us (2%)
    pallas_call x49, Pallas kernels, __call__(): pl.pallas_call(body, out_shape=[jax.ShapeDtypeStruct(*(o if isinstance(o[...  62.5 us
    ppermute x18, waiting for transfers between devices, flip(): return lax.ppermute(value, axis, [(i, i ^ bit) for i in range(n)])  38.7 us
    ppermute x6, starting transfers between devices, in_hop(): lax.ppermute(value, 'prow', [(0, 2), (1, 3), (6, 4), (7, 5)])  25.6 us
    ppermute x18, starting transfers between devices, flip(): return lax.ppermute(value, axis, [(i, i ^ bit) for i in range(n)])  21.8 us
    ppermute x6, starting transfers between devices, out_hop(): lax.ppermute(value, 'prow', [(2, 0), (3, 1), (4, 6), (5, 7)])  7.74 us
    ppermute x1, waiting for transfers between devices, local(): came = lax.ppermute(held, 'pcol', [(0, 2), (1, 3)]) if n_col > 2 else held  5.99 us
    ppermute x6, waiting for transfers between devices, out_hop(): lax.ppermute(value, 'prow', [(2, 0), (3, 1), (4, 6), (5, 7)])  5.06 us
    ppermute x1, starting transfers between devices, local(): came = lax.ppermute(held, 'pcol', [(0, 2), (1, 3)]) if n_col > 2 else held  4.88 us
  transfers between devices with their start and end apart: 37, of which 16 were waited for; matrix products, arithmetic and copies ran while one was open for 0% of the time, Pallas kernels for 31%

commit v1 on v0

--- a/solution.py
+++ b/solution.py
@@ -11,13 +11,12 @@
 f32 = jnp.float32
 bf16 = jnp.bfloat16
 TILE = 128
-SIZES = (2, 1, 2, 2, 2, 2)
-SENDS = ((0,), (1,), (2,), (3,), (4,), (5,))
+SIZES = (1, 2, 2, 2, 2, 2)
 ORDER = (
-    "gram send1 send0 send4", "g1 ~g1 send5 keep1", "g2 send2 keep0 send3", "~keep1 zm1 keep2 g4",
-    "keep4 ~zm1 zm0 zm2", "keep3 g5 zo0 keep5", "zm4 zo2 g6 ag0", "ch0 zm3 zo1 zo4",
-    "ag2 ~zo1 zm5 ~ag2", "ch1 ag4 zo5 ag1", "~ag0 ch2 zo3 ch3", "ag5 weights fin4 ~zo3",
-    "fin1 ag3 fin5 fin2", "fin0 fin3",
+    "panels send0 send1 keep0", "send2 keep1 zm0 send3", "keep2 zm1 zo0 send4", "keep3 zm2 ~zo0 zo1",
+    "send5 keep4 zm3 ~zo1", "zo2 ag0 keep5 zm4", "~zo2 zo3 ag1 zm5", "~ag0 g4 ~zo3 zo4",
+    "g6 ag2 ch0 ~zo4", "zo5 ~ag1 ag3 ch1", "~ag2 ag4 ch2 ~zo5", "ag5 ch3 ~ag3 weights",
+    "fin0 fin1 fin2 fin3", "fin4 fin5",
 )
 
 
@@ -103,10 +102,9 @@
 
 
 def panels_kernel(
-    flags, held_ref, other_ref, both_ref, keep_high, keep_low, send_high, send_low, share_ref, stack
+    flags, held_ref, other_ref, both_ref, keep_ref, send_ref, keep_high, keep_low, send_high, send_low
 ):
     width = held_ref.shape[1]
-    share = share_ref.shape[0]
     held, other = held_ref[...], other_ref[...]
     low = flags[1] != 0
     p0, p1 = jnp.where(low, held, other), jnp.where(low, other, held)
@@ -114,42 +112,41 @@
     both_ref[:, width:] = p1
     t0, t1 = p0.T, p1.T
     first = flags[2] != 0
-    keep_high[...], keep_low[...] = split(jnp.where(first, t0, t1))
-    send_high[...], send_low[...] = split(jnp.where(first, t1, t0))
-    stack[:width] = dot(t0, p0)
-    stack[width:2 * width] = dot(t1, p0)
-    stack[2 * width:] = dot(t1, p1)
-    share_ref[...] = stack[pl.ds(pl.multiple_of(flags[4] * share, 8), share), :]
-
-
-def product_kernel(flags, panel_high, panel_low, *refs):
-    panel = panel_high[...], panel_low[...]
-    at, out_ref = 0, refs[-1]
-    for high, low in zip(refs[:-1:2], refs[1:-1:2]):
-        columns = high.shape[1]
-        out_ref[:, at:at + columns] = dot3(panel, (high[...], low[...]))
-        at += columns
-
-
-def product_add_kernel(skip, flags, panel_high, panel_low, a_high, a_low, came_ref, out_ref):
-    panel = panel_high[...], panel_low[...]
-    came = came_ref[:, skip:skip + out_ref.shape[1]]
-    out_ref[...] = dot3(panel, (a_high[...], a_low[...])) + came
-
-
-def stack_kernel(flags, a_ref, b_ref, out_ref):
-    rows = a_ref.shape[0]
-    out_ref[:rows] = a_ref[...]
-    out_ref[rows:] = b_ref[...]
-
-
-def gather_kernel(which, flags, a_ref, b_ref, out_ref):
-    share = out_ref.shape[0] // len(which)
-    half = len(which) // 2
-    for place, w in enumerate(which):
-        at = pl.multiple_of((flags[4] ^ w) * share, 8)
-        ref, here = (a_ref, place) if place < half else (b_ref, place - half)
-        out_ref[pl.ds(at, share), :] = ref[here * share:(here + 1) * share]
+    keep, send = jnp.where(first, t0, t1), jnp.where(first, t1, t0)
+    keep_ref[...], send_ref[...] = keep, send
+    keep_high[...], keep_low[...] = split(keep)
+    send_high[...], send_low[...] = split(send)
+
+
+def product_kernel(flags, panel_high, panel_low, a_high, a_low, *refs):
+    columns, out_ref = a_high.shape[1], refs[-1]
+    out_ref[:, :columns] = dot3((panel_high[...], panel_low[...]), (a_high[...], a_low[...]))
+    if len(refs) > 1:
+        out_ref[:, columns:] = dot(refs[0][...], refs[1][...])
+
+
+def product_add_kernel(flags, panel_high, panel_low, a_high, a_low, came_ref, *refs):
+    columns, out_ref = a_high.shape[1], refs[-1]
+    product = dot3((panel_high[...], panel_low[...]), (a_high[...], a_low[...]))
+    out_ref[:, :columns] = product + came_ref[:, :columns]
+    if len(refs) > 1:
+        out_ref[:, columns:] = dot(refs[0][...], refs[1][...]) + came_ref[:, columns:]
+
+
+def share_kernel(flags, keep_ref, other_ref, out_ref):
+    width = keep_ref.shape[0]
+    first = flags[2] != 0
+    keep, other = keep_ref[:, -width:], other_ref[:, -width:]
+    out_ref[:width] = jnp.where(first, keep, other)
+    out_ref[width:] = jnp.where(first, other, keep)
+
+
+def gather_kernel(flags, own_ref, other_ref, out_ref):
+    width = own_ref.shape[1]
+    low = flags[1] != 0
+    own, other = own_ref[...], other_ref[...]
+    out_ref[:, :width] = jnp.where(low, own, other)
+    out_ref[:, width:] = jnp.where(low, other, own)
 
 
 def add_kernel(flags, a_ref, b_ref, out_ref):
@@ -206,10 +203,7 @@
     size = out_state_ref.shape[0]
     lo, hi = step * TILE, (step + 1) * TILE
     if step == 0:
-        half = size // 2
-        out_state_ref[:half, :half] = gram_ref[:half]
-        out_state_ref[half:, :half] = gram_ref[half:size]
-        out_state_ref[half:, half:] = gram_ref[size:]
+        out_state_ref[...] = gram_ref[...]
         sub = lax.broadcasted_iota(jnp.int32, (size, size), 0)
         lane = lax.broadcasted_iota(jnp.int32, (size, size), 1)
         out_inv_ref[...] = jnp.where(sub == lane, 1.0, 0.0).astype(f32)
@@ -246,9 +240,10 @@
 
 
 def finish_kernel(flags, a_ref, high_ref, low_ref, first_ref, second_ref, rest_ref, factor_ref):
-    rows, width = a_ref.shape[0], first_ref.shape[0]
-    change = dot3((high_ref[:, :width], low_ref[:, :width]), split(first_ref[...]))
-    change += dot3((high_ref[:, width:], low_ref[:, width:]), split(second_ref[...]))
+    rows, columns = a_ref.shape
+    width = first_ref.shape[0]
+    change = dot3((high_ref[:, :width], low_ref[:, :width]), split(first_ref[:, :columns]))
+    change += dot3((high_ref[:, width:], low_ref[:, width:]), split(second_ref[:, :columns]))
     rest_ref[...] = a_ref[...] - change[:rows]
     factor_ref[...] = change[rows:]
 
@@ -273,7 +268,7 @@
 
 def in_rows(rests, factors, parts):
     rows, own_rows = rests[0].shape[0], factors[0].shape[0]
-    step = min(rows, 64)
+    step = min(rows, 128)
     return pl.pallas_call(
         functools.partial(rows_kernel, parts, len(rests)),
         grid=(rows // step,),
@@ -300,7 +295,7 @@
     row, col = lax.axis_index("prow"), lax.axis_index("pcol")
     place = row // 2
     line = n_row == 8
-    sizes, sends = (SIZES, SENDS) if sum(SIZES) == blocks else ((blocks,), ((0,),))
+    sizes = SIZES if sum(SIZES) == blocks else (blocks,)
     flags = jnp.stack([
         col >= 2, col % 2 == 0, row % 2 == 0, (place == 1) | (place == 2), col, row,
     ]).astype(jnp.int32)
@@ -325,7 +320,6 @@
     beside = flip(held, "pcol", 1)
 
     state = {}
-    starts = [sum(sizes[:k]) * width for k in range(len(sizes) + 1)]
 
     def in_hop(value):
         return lax.ppermute(value, "prow", [(0, 2), (1, 3), (6, 4), (7, 5)]) if line else None
@@ -351,38 +345,17 @@
         return chain(functools.partial(pick_kernel, 3), name, [a.shape], flags, a, b)[0]
 
     def run(task):
-        if task == "gram":
-            cut = ((width, rows), bf16)
-            both, *panels, share = chain(
-                panels_kernel, "panels", [(rows, depth)] + [cut] * 4 + [(3 * width // n_col, width)],
-                flags, held, beside, scratch=[pltpu.VMEM((3 * width, width), f32)],
+        if task == "panels":
+            cut = (width, rows)
+            both, keep, send, *parted = chain(
+                panels_kernel, task, [(rows, depth), cut, cut] + [(cut, bf16)] * 4, flags, held, beside
             )
-            state.update(both=both, keep=panels[:2], send=panels[2:], g=share, gr=flip(share, "prow", 1))
-        elif task == "g1" or task == "g2":
-            state["g"] = add(task, state["g"], state["gr"])
-            state["gr"] = flip(state["g"], "prow", 2 * int(task[1]))
+            state.update(both=both, keep=parted[:2], send=parted[2:], keep_more=[keep, held], send_more=[send, held])
         elif task == "g4":
-            state["g"] = add(task, state["g"], state["gr"])
-            bit = 8
-            while bit < n_row:
-                state["g"] = state["g"] + flip(state["g"], "prow", bit)
-                bit *= 2
-            bit = n_col // 2
-            state["gr"] = flip(state["g"], "pcol", bit)
-        elif task == "g5":
-            bit = n_col // 2
-            which = [0, bit]
-            joint, = chain(stack_kernel, task, [(2 * state["g"].shape[0], width)], flags, state["g"], state["gr"])
-            bit //= 2
-            while bit > 1:
-                which += [w ^ bit for w in which]
-                joint = jnp.concatenate([joint, flip(joint, "pcol", bit)], 0)
-                bit //= 2
-            state.update(held=joint, which=which + [w ^ 1 for w in which], gr=flip(joint, "pcol", 1))
+            share, = chain(share_kernel, task, [(depth, width)], flags, state["s", 0], state["r", 0])
+            state["gr"] = share, flip(share, "pcol", 1)
         elif task == "g6":
-            state["gram"], = chain(
-                functools.partial(gather_kernel, state["which"]), task, [(3 * width, width)], flags, state["held"], state["gr"]
-            )
+            state["gram"], = chain(gather_kernel, task, [(depth, depth)], flags, *state["gr"])
         elif task.startswith("ch"):
             step = int(task[2:])
             operands = [state["gram"]] if step == 0 else state["factor"]
@@ -395,22 +368,17 @@
             state["weights"] = chain(weights_kernel, task, [cut] * 2, flags, state["both"], state["factor"][1])
         else:
             kind, k = task.rstrip("0123456789"), int(task.lstrip("abcdefghijklmnopqrstuvwxyz"))
-            if k >= (len(sends) if kind == "send" else len(sizes)):
+            if k >= len(sizes):
                 return
-            if kind != "send":
-                lo, hi = starts[k], starts[k + 1]
+            count = (sizes[k] + (k == 0)) * width
             if kind == "send":
-                members = sends[k]
-                lo, hi = starts[members[0]], starts[members[-1] + 1]
-                pieces = [v for member in members for v in cuts[member][1:]]
-                out, = chain(product_kernel, task, [(width, hi - lo)], flags, *state["send"], *pieces)
-                came = flip(out, "prow", 1)
-                for member in members:
-                    state["r", member] = came
+                more = state["send_more"] if k == 0 else []
+                out, = chain(product_kernel, task, [(width, count)], flags, *state["send"], *cuts[k][1:], *more)
+                state["r", k] = flip(out, "prow", 1)
             elif kind == "keep":
-                skip = lo - starts[next(m for m in sends if k in m)[0]]
-                out, = chain(functools.partial(product_add_kernel, skip), task, [(width, hi - lo)],
-                             flags, *state["keep"], *cuts[k][1:], state["r", k])
+                more = state["keep_more"] if k == 0 else []
+                out, = chain(product_add_kernel, task, [(width, count)],
+                             flags, *state["keep"], *cuts[k][1:], state["r", k], *more)
                 state["s", k], state["r", k] = out, in_hop(out)
             elif kind == "zm":
                 out = add(task, state["s", k], state["r", k])
@@ -423,15 +391,13 @@
                 state["s", k], state["r", k] = out, flip(out, "prow", 1)
             elif kind == "fin":
                 state["out", k] = chain(
-                    finish_kernel, task, [(rows, hi - lo), (depth // n_row, hi - lo)],
+                    finish_kernel, task, [(rows, sizes[k] * width), (depth // n_row, sizes[k] * width)],
                     flags, cuts[k][0], *state["weights"], state["s", k], state["r", k],
                 )
 
     for task in " ".join(ORDER).split():
         if task[0] != "~":
             run(task)
-        elif task[1] == "g":
-            chain.waits.append(state["gr"])
         elif line and ("r", int(task[-1])) in state:
             chain.waits.append(state["r", int(task[-1])])
     outs = [state["out", k] for k in range(len(sizes))]

time: 188 us -> 181 us (0.963)
  starting transfers between devices: 64.1 us -> 58.5 us
  Pallas kernels: 66.7 us -> 63.3 us
  waiting for transfers between devices: 50.6 us -> 52.5 us
    ppermute x6, waiting for transfers between devices: 5.06 us -> 12 us  [out_hop(): lax.ppermute(value, 'prow', [(2, 0), (3, 1), (4, 6), (5, 7)])]
    ppermute x18 -> x14, starting transfers between devices: 21.8 us -> 16 us  [flip(): return lax.ppermute(value, axis, [(i, i ^ bit) for i in range(n)])]
    ppermute x18 -> x14, waiting for transfers between devices: 38.7 us -> 33.1 us  [flip(): return lax.ppermute(value, axis, [(i, i ^ bit) for i in range(n)])]
    pallas_call x49 -> x46, Pallas kernels: 62.5 us -> 60.2 us  [__call__(): pl.pallas_call(body, out_shape=[jax.ShapeDtypeStruct(*(o if isinstance(o[...]
  transfers between devices with their start and end apart: 37 -> 33, of which waited for: 16 -> 17; matrix products, arithmetic and copies ran while one was open for 0% -> 0% of each run, Pallas kernels for 31% -> 31%
where the time goes in v1:
time: 181 us; the launch traced here: 180 us
  Pallas kernels  63.3 us (35%)
  starting transfers between devices  58.5 us (32%)
  waiting for transfers between devices  52.5 us (29%)
  local copies, waits for them, and re-layouts  4.16 us (2%)
    pallas_call x46, Pallas kernels, __call__(): pl.pallas_call(body, out_shape=[jax.ShapeDtypeStruct(*(o if isinstance(o[...  60.2 us
    ppermute x14, waiting for transfers between devices, flip(): return lax.ppermute(value, axis, [(i, i ^ bit) for i in range(n)])  33.1 us
    ppermute x6, starting transfers between devices, in_hop(): lax.ppermute(value, 'prow', [(0, 2), (1, 3), (6, 4), (7, 5)])  25.7 us
    ppermute x14, starting transfers between devices, flip(): return lax.ppermute(value, axis, [(i, i ^ bit) for i in range(n)])  16 us
    ppermute x6, waiting for transfers between devices, out_hop(): lax.ppermute(value, 'prow', [(2, 0), (3, 1), (4, 6), (5, 7)])  12 us
    ppermute x6, starting transfers between devices, out_hop(): lax.ppermute(value, 'prow', [(2, 0), (3, 1), (4, 6), (5, 7)])  7.75 us
    ppermute x1, waiting for transfers between devices, local(): came = lax.ppermute(held, 'pcol', [(0, 2), (1, 3)]) if n_col > 2 else held  6 us
    ppermute x1, starting transfers between devices, local(): came = lax.ppermute(held, 'pcol', [(0, 2), (1, 3)]) if n_col > 2 else held  4.88 us
  transfers between devices with their start and end apart: 33, of which 17 were waited for; matrix products, arithmetic and copies ran while one was open for 0% of the time, Pallas kernels for 31%

profile of v1, /device:TPU:0, one launch (start us, length us, event | category | flops | bytes accessed | tf_op | source)
XLA Modules:
  0.0 179.8 jit_solution(4639498256671114952)
XLA Ops:
  0.6 1.4 slice.3
  2.1 4.9 %collective-permute-start = (f32[512,256]{1,0:T(8,128)S(1)}, f32[512,256]{1,0:T(8,128)S(1)}, u32[]{:S(2)}, u32[]{:S(2)}) collective-permute-start(f32[512,256]{1,0:T(8,128)S(1)} %bitcast.13), channel_id=1, source_target_pairs={{0,2},{1,3},{4,6},{5,7},{8,10},{9,11},{12,14},{13,15},{16,18},{17,... | collective-permute-start | bytes 1572872 | tf_op jit(solution)/shard_map/ppermute | solution.py:307
  7.1 2.6 %copy-done = f32[512,11,1,256]{3,2,1,0:T(1,128)S(1)} copy-done((f32[512,11,1,256]{3,2,1,0:T(1,128)S(1)}, f32[512,11,1,256]{3,2,1,0:T(1,128)}, u32[]{:S(2)}) %copy-start) | copy-done | bytes 5767192
  9.7 2.4 %rows_to_tiles.1 = (f32[512,256]{1,0:T(8,128)S(1)}, bf16[512,256]{1,0:T(8,128)(2,1)S(1)}, bf16[512,256]{1,0:T(8,128)(2,1)S(1)}, f32[512,512]{1,0:T(8,128)S(1)}, ...) custom-call(s32[6]{0:T(128)S(1)} %stack.43.refs_0_, ...), custom_call_target="tpu_custom_call" | custom-call | flops 1000 | bytes 1000 | tf_op jit(solution)/shard_map/rows_to_tiles/pallas_call | solution.py:66
  12.1 6.0 %collective-permute-done.refs_1_ = f32[512,256]{1,0:T(8,128)S(1)} collective-permute-done((f32[512,256]{1,0:T(8,128)S(1)}, f32[512,256]{1,0:T(8,128)S(1)}, u32[]{:S(2)}, u32[]{:S(2)}) %collective-permute-start) | collective-permute-done | bytes 524320 | tf_op jit(solution)/shard_map/ppermute | solution.py:307
  18.8 1.9 %collective-permute-done.1.refs_2_ = f32[512,256]{1,0:T(8,128)S(1)} collective-permute-done((f32[512,256]{1,0:T(8,128)S(1)}, f32[512,256]{1,0:T(8,128)S(1)}, u32[]{:S(2)}, u32[]{:S(2)}) %collective-permute-start.1) | collective-permute-done | bytes 524320 | tf_op jit(solution)/shard_map/ppermute | solution.py:49
  21.6 1.3 send0.1.refs_5_
  23.0 1.6 collective-permute-start.2
  26.3 11.6 %collective-permute-done.2.refs_5_ = f32[256,512]{1,0:T(8,128)S(1)} collective-permute-done((f32[256,512]{1,0:T(8,128)S(1)}, f32[256,512]{1,0:T(8,128)S(1)}, u32[]{:S(2)}, u32[]{:S(2)}) %collective-permute-start.2) | collective-permute-done | bytes 524320 | tf_op jit(solution)/shard_map/ppermute | solution.py:49
  37.8 1.4 keep0.1.refs_5_.refs_1_
  39.2 3.5 %collective-permute-start.3 = (f32[256,512]{1,0:T(8,128)S(1)}, f32[256,512]{1,0:T(8,128)S(1)}, u32[]{:S(2)}, u32[]{:S(2)}) collective-permute-start(f32[256,512]{1,0:T(8,128)S(1)} %keep0.1.refs_5_.refs_1_), channel_id=1, source_target_pairs={{0,8},{4,12},{24,16},{28,20},{1,9},{5,13},{25,17},{29,21},{2,10},{... | collective-permute-start | bytes 1572872 | tf_op jit(solution)/shard_map/ppermute | solution.py:325
  43.8 1.6 collective-permute-start.7
  45.4 3.7 %collective-permute-done.4.refs_5_ = f32[256,512]{1,0:T(8,128)S(1)} collective-permute-done((f32[256,512]{1,0:T(8,128)S(1)}, f32[256,512]{1,0:T(8,128)S(1)}, u32[]{:S(2)}, u32[]{:S(2)}) %collective-permute-start.4) | collective-permute-done | bytes 524320 | tf_op jit(solution)/shard_map/ppermute | solution.py:49
  50.2 3.5 %collective-permute-start.6 = (f32[256,512]{1,0:T(8,128)S(1)}, f32[256,512]{1,0:T(8,128)S(1)}, u32[]{:S(2)}, u32[]{:S(2)}) collective-permute-start(f32[256,512]{1,0:T(8,128)S(1)} %keep1.1.refs_3_.refs_1_), channel_id=1, source_target_pairs={{0,8},{4,12},{24,16},{28,20},{1,9},{5,13},{25,17},{29,21},{2,10},{... | collective-permute-start | bytes 1572872 | tf_op jit(solution)/shard_map/ppermute | solution.py:325
  56.1 1.6 collective-permute-start.10
  57.7 2.6 %collective-permute-done.7.refs_5_ = f32[256,512]{1,0:T(8,128)S(1)} collective-permute-done((f32[256,512]{1,0:T(8,128)S(1)}, f32[256,512]{1,0:T(8,128)S(1)}, u32[]{:S(2)}, u32[]{:S(2)}) %collective-permute-start.7) | collective-permute-done | bytes 524320 | tf_op jit(solution)/shard_map/ppermute | solution.py:49
  61.4 3.6 %collective-permute-start.9 = (f32[256,512]{1,0:T(8,128)S(1)}, f32[256,512]{1,0:T(8,128)S(1)}, u32[]{:S(2)}, u32[]{:S(2)}) collective-permute-start(f32[256,512]{1,0:T(8,128)S(1)} %keep2.1.refs_3_.refs_1_), channel_id=1, source_target_pairs={{0,8},{4,12},{24,16},{28,20},{1,9},{5,13},{25,17},{29,21},{2,10},{... | collective-permute-start | bytes 1572872 | tf_op jit(solution)/shard_map/ppermute | solution.py:325
  66.9 1.3 collective-permute-start.8
  69.4 1.5 collective-permute-start.13
  72.3 5.9 %collective-permute-start.12 = (f32[256,512]{1,0:T(8,128)S(1)}, f32[256,512]{1,0:T(8,128)S(1)}, u32[]{:S(2)}, u32[]{:S(2)}) collective-permute-start(f32[256,512]{1,0:T(8,128)S(1)} %keep3.1.refs_3_.refs_1_), channel_id=1, source_target_pairs={{0,8},{4,12},{24,16},{28,20},{1,9},{5,13},{25,17},{29,21},{2,10},{... | collective-permute-start | bytes 1572872 | tf_op jit(solution)/shard_map/ppermute | solution.py:325
  79.5 2.3 %collective-permute-done.8.refs_4_.refs_2_ = f32[256,512]{1,0:T(8,128)S(1)} collective-permute-done((f32[256,512]{1,0:T(8,128)S(1)}, f32[256,512]{1,0:T(8,128)S(1)}, u32[]{:S(2)}, u32[]{:S(2)}) %collective-permute-start.8) | collective-permute-done | bytes 524320 | tf_op jit(solution)/shard_map/ppermute | solution.py:331
  84.8 1.6 collective-permute-start.17
  87.6 4.6 %collective-permute-start.20 = (f32[256,512]{1,0:T(8,128)S(1)}, f32[256,512]{1,0:T(8,128)S(1)}, u32[]{:S(2)}, u32[]{:S(2)}) collective-permute-start(f32[256,512]{1,0:T(8,128)S(1)} %keep4.1.refs_3_.refs_1_), channel_id=1, source_target_pairs={{0,8},{4,12},{24,16},{28,20},{1,9},{5,13},{25,17},{29,21},{2,10},{... | collective-permute-start | bytes 1572872 | tf_op jit(solution)/shard_map/ppermute | solution.py:325
  93.5 1.4 collective-permute-done.15.refs_4_.refs_2_
  95.5 1.3 collective-permute-start.21
  98.5 4.6 %collective-permute-start.18 = (f32[256,512]{1,0:T(8,128)S(1)}, f32[256,512]{1,0:T(8,128)S(1)}, u32[]{:S(2)}, u32[]{:S(2)}) collective-permute-start(f32[256,512]{1,0:T(8,128)S(1)} %keep5.1.refs_3_.refs_1_), channel_id=1, source_target_pairs={{0,8},{4,12},{24,16},{28,20},{1,9},{5,13},{25,17},{29,21},{2,10},{... | collective-permute-start | bytes 1572872 | tf_op jit(solution)/shard_map/ppermute | solution.py:325
  103.1 1.6 collective-permute-start.16
  109.5 1.3 collective-permute-done.18.refs_2_
  113.8 4.9 %collective-permute-done.24.refs_4_.refs_2_ = f32[256,512]{1,0:T(8,128)S(1)} collective-permute-done((f32[256,512]{1,0:T(8,128)S(1)}, f32[256,512]{1,0:T(8,128)S(1)}, u32[]{:S(2)}, u32[]{:S(2)}) %collective-permute-start.24) | collective-permute-done | bytes 524320 | tf_op jit(solution)/shard_map/ppermute | solution.py:331
  120.6 1.6 collective-permute-start.27
  124.2 4.9 %factor0.1 = (f32[512,512]{1,0:T(8,128)S(1)}, f32[512,512]{1,0:T(8,128)S(1)}) custom-call(s32[6]{0:T(128)S(1)} %stack.43.refs_0_, f32[512,512]{1,0:T(8,128)S(1)} %g6.1.refs_3_.refs_1_, f32[256,512]{1,0:T(8,128)S(1)} %ag2.1.refs_2_.refs_4_), custom_call_target="tpu_custom_call" | custom-call | flops 1000 | bytes 1000 | tf_op jit(solution)/shard_map/factor0/pallas_call | solution.py:66
  129.0 2.3 %collective-permute-done.26.refs_4_.refs_2_ = f32[256,512]{1,0:T(8,128)S(1)} collective-permute-done((f32[256,512]{1,0:T(8,128)S(1)}, f32[256,512]{1,0:T(8,128)S(1)}, u32[]{:S(2)}, u32[]{:S(2)}) %collective-permute-start.26) | collective-permute-done | bytes 524320 | tf_op jit(solution)/shard_map/ppermute | solution.py:331
  133.3 2.3 %collective-permute-done.27.refs_4_.refs_5_ = f32[256,512]{1,0:T(8,128)S(1)} collective-permute-done((f32[256,512]{1,0:T(8,128)S(1)}, f32[256,512]{1,0:T(8,128)S(1)}, u32[]{:S(2)}, u32[]{:S(2)}) %collective-permute-start.27) | collective-permute-done | bytes 524320 | tf_op jit(solution)/shard_map/ppermute | solution.py:49
  136.1 1.6 collective-permute-start.30
  137.7 4.7 %factor1.1 = (f32[512,512]{1,0:T(8,128)S(1)}, f32[512,512]{1,0:T(8,128)S(1)}) custom-call(s32[6]{0:T(128)S(1)} %stack.43.refs_0_, f32[512,512]{1,0:T(8,128)S(1)} %get-tuple-element.71.refs_3_.refs_1_, f32[512,512]{1,0:T(8,128)S(1)} %get-tuple-element.72.refs_2_, f32[256,512]{1,0:T(8,128)S(1)} %ag3.1.refs_3_.refs_4_), custom_call_target="tpu_custom_call" | custom-call | flops 1000 | bytes 1000 | tf_op jit(solution)/shard_map/factor1/pallas_call | solution.py:66
  142.5 4.3 %collective-permute-done.28.refs_4_.refs_5_ = f32[256,512]{1,0:T(8,128)S(1)} collective-permute-done((f32[256,512]{1,0:T(8,128)S(1)}, f32[256,512]{1,0:T(8,128)S(1)}, u32[]{:S(2)}, u32[]{:S(2)}) %collective-permute-start.28) | collective-permute-done | bytes 524320 | tf_op jit(solution)/shard_map/ppermute | solution.py:49
  147.6 1.6 collective-permute-start.31
  149.2 4.7 %factor2.1 = (f32[512,512]{1,0:T(8,128)S(1)}, f32[512,512]{1,0:T(8,128)S(1)}) custom-call(s32[6]{0:T(128)S(1)} %stack.43.refs_0_, f32[512,512]{1,0:T(8,128)S(1)} %get-tuple-element.73.refs_3_.refs_1_, f32[512,512]{1,0:T(8,128)S(1)} %get-tuple-element.74.refs_2_, f32[256,512]{1,0:T(8,128)S(1)} %ag4.1.refs_3_.refs_4_), custom_call_target="tpu_custom_call" | custom-call | flops 1000 | bytes 1000 | tf_op jit(solution)/shard_map/factor2/pallas_call | solution.py:66
  155.1 4.0 %factor3.1 = (f32[512,512]{1,0:T(8,128)S(1)}, f32[512,512]{1,0:T(8,128)S(1)}) custom-call(s32[6]{0:T(128)S(1)} %stack.43.refs_0_, f32[512,512]{1,0:T(8,128)S(1)} %get-tuple-element.75.refs_3_.refs_1_, f32[512,512]{1,0:T(8,128)S(1)} %get-tuple-element.76.refs_2_, f32[256,512]{1,0:T(8,128)S(1)} %ag5.1.refs_3_.refs_4_), custom_call_target="tpu_custom_call" | custom-call | flops 1000 | bytes 1000 | tf_op jit(solution)/shard_map/factor3/pallas_call | solution.py:66
  159.1 2.6 %weights.1 = (bf16[576,512]{1,0:T(8,128)(2,1)S(1)}, bf16[576,512]{1,0:T(8,128)(2,1)S(1)}) custom-call(s32[6]{0:T(128)S(1)} %stack.43.refs_0_, f32[512,512]{1,0:T(8,128)S(1)} %get-tuple-element.52.refs_7_.refs_1_, f32[512,512]{1,0:T(8,128)S(1)} %get-tuple-element.77.refs_2_, f32[512,512]{1,0:T(8,128)S(1)} %get-tuple-element.78.refs_3_, ...), custom_call_target="tpu_custom_call" | custom-call | flops 1000 | bytes 1000 | tf_op jit(solution)/shard_map/weights/pallas_call | solution.py:66
  162.9 1.6 fin1.1
  164.5 1.6 fin2.1
  166.2 1.6 fin3.1
  167.8 1.4 collective-permute-done.31.refs_5_
  169.2 1.6 fin4.1
  170.9 4.1 %collective-permute-done.32.refs_5_ = f32[256,512]{1,0:T(8,128)S(1)} collective-permute-done((f32[256,512]{1,0:T(8,128)S(1)}, f32[256,512]{1,0:T(8,128)S(1)}, u32[]{:S(2)}, u32[]{:S(2)}) %collective-permute-start.32) | collective-permute-done | bytes 524320 | tf_op jit(solution)/shard_map/ppermute | solution.py:49
  175.0 1.6 fin5.1
  176.6 3.1 %tiles_to_rows.1 = (f32[11264,128]{1,0:T(8,128)}, f32[1408,128]{1,0:T(8,128)}) custom-call(f32[512,256]{1,0:T(8,128)S(1)} %get-tuple-element.81.refs_6_.refs_0_, f32[512,512]{1,0:T(8,128)S(1)} %get-tuple-element.83.refs_6_.refs_1_, f32[512,512]{1,0:T(8,128)S(1)} %get-tuple-element.85.refs_6_.refs_2_, f32[512,512]{1,0:T(8,128)S(1)} %get-tuple-element.87.refs_6_.refs_3_, ...), custom_call_target="tpu_custom_call" | custom-call | tf_op jit(solution)/shard_map/tiles_to_rows/pallas_call | solution.py:272
  (70 shorter events, 39.7 us)
Async XLA Ops:
  2.1 16.0 %collective-permute-start = (f32[512,256]{1,0:T(8,128)S(1)}, f32[512,256]{1,0:T(8,128)S(1)}, u32[]{:S(2)}, u32[]{:S(2)}) collective-permute-start(f32[512,256]{1,0:T(8,128)S(1)} %bitcast.13), channel_id=1, source_target_pairs={{0,2},{1,3},{4,6},{5,7},{8,10},{9,11},{12,14},{13,15},{16,18},{17,... | collective-permute-start | bytes 1572872 | tf_op jit(solution)/shard_map/ppermute | solution.py:307
  7.1 2.6 %copy-start = (f32[512,11,1,256]{3,2,1,0:T(1,128)S(1)}, f32[512,11,1,256]{3,2,1,0:T(1,128)}, u32[]{:S(2)}) copy-start(f32[512,11,1,256]{3,2,1,0:T(1,128)} %param.1) | copy-start | bytes 17301508
  18.7 2.0 %collective-permute-start.1 = (f32[512,256]{1,0:T(8,128)S(1)}, f32[512,256]{1,0:T(8,128)S(1)}, u32[]{:S(2)}, u32[]{:S(2)}) collective-permute-start(f32[512,256]{1,0:T(8,128)S(1)} %pick.1.refs_1_.refs_3_.refs_6_.refs_7_), channel_id=1, source_target_pairs={{0,1},{1,0},{2,3},{3,2},{4,5},{5,4},{6,7},{7,6},{8,9},{9,8},{10,11... | collective-permute-start | bytes 1572872 | tf_op jit(solution)/shard_map/ppermute | solution.py:49
  23.0 14.8 %collective-permute-start.2 = (f32[256,512]{1,0:T(8,128)S(1)}, f32[256,512]{1,0:T(8,128)S(1)}, u32[]{:S(2)}, u32[]{:S(2)}) collective-permute-start(f32[256,512]{1,0:T(8,128)S(1)} %send0.1.refs_5_), channel_id=1, source_target_pairs={{0,4},{4,0},{8,12},{12,8},{16,20},{20,16},{24,28},{28,24},{1,5},{5... | collective-permute-start | bytes 1572872 | tf_op jit(solution)/shard_map/ppermute | solution.py:49
  25.7 23.4 %collective-permute-start.4 = (f32[256,512]{1,0:T(8,128)S(1)}, f32[256,512]{1,0:T(8,128)S(1)}, u32[]{:S(2)}, u32[]{:S(2)}) collective-permute-start(f32[256,512]{1,0:T(8,128)S(1)} %send1.1.refs_8_), channel_id=1, source_target_pairs={{0,4},{4,0},{8,12},{12,8},{16,20},{20,16},{24,28},{28,24},{1,5},{5... | collective-permute-start | bytes 1572872 | tf_op jit(solution)/shard_map/ppermute | solution.py:49
  39.2 14.5 %collective-permute-start.3 = (f32[256,512]{1,0:T(8,128)S(1)}, f32[256,512]{1,0:T(8,128)S(1)}, u32[]{:S(2)}, u32[]{:S(2)}) collective-permute-start(f32[256,512]{1,0:T(8,128)S(1)} %keep0.1.refs_5_.refs_1_), channel_id=1, source_target_pairs={{0,8},{4,12},{24,16},{28,20},{1,9},{5,13},{25,17},{29,21},{2,10},{... | collective-permute-start | bytes 1572872 | tf_op jit(solution)/shard_map/ppermute | solution.py:325
  43.8 16.5 %collective-permute-start.7 = (f32[256,512]{1,0:T(8,128)S(1)}, f32[256,512]{1,0:T(8,128)S(1)}, u32[]{:S(2)}, u32[]{:S(2)}) collective-permute-start(f32[256,512]{1,0:T(8,128)S(1)} %send2.1.refs_6_), channel_id=1, source_target_pairs={{0,4},{4,0},{8,12},{12,8},{16,20},{20,16},{24,28},{28,24},{1,5},{5... | collective-permute-start | bytes 1572872 | tf_op jit(solution)/shard_map/ppermute | solution.py:49
  50.2 14.8 %collective-permute-start.6 = (f32[256,512]{1,0:T(8,128)S(1)}, f32[256,512]{1,0:T(8,128)S(1)}, u32[]{:S(2)}, u32[]{:S(2)}) collective-permute-start(f32[256,512]{1,0:T(8,128)S(1)} %keep1.1.refs_3_.refs_1_), channel_id=1, source_target_pairs={{0,8},{4,12},{24,16},{28,20},{1,9},{5,13},{25,17},{29,21},{2,10},{... | collective-permute-start | bytes 1572872 | tf_op jit(solution)/shard_map/ppermute | solution.py:325
  54.3 12.0 %collective-permute-start.5 = (f32[256,512]{1,0:T(8,128)S(1)}, f32[256,512]{1,0:T(8,128)S(1)}, u32[]{:S(2)}, u32[]{:S(2)}) collective-permute-start(f32[256,512]{1,0:T(8,128)S(1)} %zm0.1.refs_5_.refs_1_), channel_id=1, source_target_pairs={{8,16},{12,20},{16,8},{20,12},{9,17},{13,21},{17,9},{21,13},{10,18... | collective-permute-start | bytes 1572872 | tf_op jit(solution)/shard_map/ppermute | solution.py:328
  56.1 15.1 %collective-permute-start.10 = (f32[256,512]{1,0:T(8,128)S(1)}, f32[256,512]{1,0:T(8,128)S(1)}, u32[]{:S(2)}, u32[]{:S(2)}) collective-permute-start(f32[256,512]{1,0:T(8,128)S(1)} %send3.1.refs_6_), channel_id=1, source_target_pairs={{0,4},{4,0},{8,12},{12,8},{16,20},{20,16},{24,28},{28,24},{1,5},{5... | collective-permute-start | bytes 1572872 | tf_op jit(solution)/shard_map/ppermute | solution.py:49
  61.4 16.8 %collective-permute-start.9 = (f32[256,512]{1,0:T(8,128)S(1)}, f32[256,512]{1,0:T(8,128)S(1)}, u32[]{:S(2)}, u32[]{:S(2)}) collective-permute-start(f32[256,512]{1,0:T(8,128)S(1)} %keep2.1.refs_3_.refs_1_), channel_id=1, source_target_pairs={{0,8},{4,12},{24,16},{28,20},{1,9},{5,13},{25,17},{29,21},{2,10},{... | collective-permute-start | bytes 1572872 | tf_op jit(solution)/shard_map/ppermute | solution.py:325
  65.6 13.9 %collective-permute-start.14 = (f32[256,512]{1,0:T(8,128)S(1)}, f32[256,512]{1,0:T(8,128)S(1)}, u32[]{:S(2)}, u32[]{:S(2)}) collective-permute-start(f32[256,512]{1,0:T(8,128)S(1)} %zm1.1.refs_3_.refs_1_), channel_id=1, source_target_pairs={{8,16},{12,20},{16,8},{20,12},{9,17},{13,21},{17,9},{21,13},{10,18... | collective-permute-start | bytes 1572872 | tf_op jit(solution)/shard_map/ppermute | solution.py:328
  66.9 14.9 %collective-permute-start.8 = (f32[256,512]{1,0:T(8,128)S(1)}, f32[256,512]{1,0:T(8,128)S(1)}, u32[]{:S(2)}, u32[]{:S(2)}) collective-permute-start(f32[256,512]{1,0:T(8,128)S(1)} %zo0.1.refs_5_.refs_1_), channel_id=1, source_target_pairs={{8,0},{12,4},{16,24},{20,28},{9,1},{13,5},{17,25},{21,29},{10,2},{... | collective-permute-start | bytes 1572872 | tf_op jit(solution)/shard_map/ppermute | solution.py:331
  69.4 17.1 %collective-permute-start.13 = (f32[256,512]{1,0:T(8,128)S(1)}, f32[256,512]{1,0:T(8,128)S(1)}, u32[]{:S(2)}, u32[]{:S(2)}) collective-permute-start(f32[256,512]{1,0:T(8,128)S(1)} %send4.1.refs_6_), channel_id=1, source_target_pairs={{0,4},{4,0},{8,12},{12,8},{16,20},{20,16},{24,28},{28,24},{1,5},{5... | collective-permute-start | bytes 1572872 | tf_op jit(solution)/shard_map/ppermute | solution.py:49
  72.3 19.8 %collective-permute-start.12 = (f32[256,512]{1,0:T(8,128)S(1)}, f32[256,512]{1,0:T(8,128)S(1)}, u32[]{:S(2)}, u32[]{:S(2)}) collective-permute-start(f32[256,512]{1,0:T(8,128)S(1)} %keep3.1.refs_3_.refs_1_), channel_id=1, source_target_pairs={{0,8},{4,12},{24,16},{28,20},{1,9},{5,13},{25,17},{29,21},{2,10},{... | collective-permute-start | bytes 1572872 | tf_op jit(solution)/shard_map/ppermute | solution.py:325
  78.8 14.7 %collective-permute-start.11 = (f32[256,512]{1,0:T(8,128)S(1)}, f32[256,512]{1,0:T(8,128)S(1)}, u32[]{:S(2)}, u32[]{:S(2)}) collective-permute-start(f32[256,512]{1,0:T(8,128)S(1)} %zm2.1.refs_3_.refs_1_), channel_id=1, source_target_pairs={{8,16},{12,20},{16,8},{20,12},{9,17},{13,21},{17,9},{21,13},{10,18... | collective-permute-start | bytes 1572872 | tf_op jit(solution)/shard_map/ppermute | solution.py:328
  82.4 12.5 %collective-permute-start.15 = (f32[256,512]{1,0:T(8,128)S(1)}, f32[256,512]{1,0:T(8,128)S(1)}, u32[]{:S(2)}, u32[]{:S(2)}) collective-permute-start(f32[256,512]{1,0:T(8,128)S(1)} %zo1.1.refs_5_.refs_1_), channel_id=1, source_target_pairs={{8,0},{12,4},{16,24},{20,28},{9,1},{13,5},{17,25},{21,29},{10,2},{... | collective-permute-start | bytes 1572872 | tf_op jit(solution)/shard_map/ppermute | solution.py:331
  84.8 12.5 %collective-permute-start.17 = (f32[256,512]{1,0:T(8,128)S(1)}, f32[256,512]{1,0:T(8,128)S(1)}, u32[]{:S(2)}, u32[]{:S(2)}) collective-permute-start(f32[256,512]{1,0:T(8,128)S(1)} %send5.1.refs_6_), channel_id=1, source_target_pairs={{0,4},{4,0},{8,12},{12,8},{16,20},{20,16},{24,28},{28,24},{1,5},{5... | collective-permute-start | bytes 1572872 | tf_op jit(solution)/shard_map/ppermute | solution.py:49
  87.6 17.2 %collective-permute-start.20 = (f32[256,512]{1,0:T(8,128)S(1)}, f32[256,512]{1,0:T(8,128)S(1)}, u32[]{:S(2)}, u32[]{:S(2)}) collective-permute-start(f32[256,512]{1,0:T(8,128)S(1)} %keep4.1.refs_3_.refs_1_), channel_id=1, source_target_pairs={{0,8},{4,12},{24,16},{28,20},{1,9},{5,13},{25,17},{29,21},{2,10},{... | collective-permute-start | bytes 1572872 | tf_op jit(solution)/shard_map/ppermute | solution.py:325
  92.8 13.2 %collective-permute-start.19 = (f32[256,512]{1,0:T(8,128)S(1)}, f32[256,512]{1,0:T(8,128)S(1)}, u32[]{:S(2)}, u32[]{:S(2)}) collective-permute-start(f32[256,512]{1,0:T(8,128)S(1)} %zm3.1.refs_3_.refs_1_), channel_id=1, source_target_pairs={{8,16},{12,20},{16,8},{20,12},{9,17},{13,21},{17,9},{21,13},{10,18... | collective-permute-start | bytes 1572872 | tf_op jit(solution)/shard_map/ppermute | solution.py:328
  95.5 11.5 %collective-permute-start.21 = (f32[256,512]{1,0:T(8,128)S(1)}, f32[256,512]{1,0:T(8,128)S(1)}, u32[]{:S(2)}, u32[]{:S(2)}) collective-permute-start(f32[256,512]{1,0:T(8,128)S(1)} %zo2.1.refs_3_.refs_1_), channel_id=1, source_target_pairs={{8,0},{12,4},{16,24},{20,28},{9,1},{13,5},{17,25},{21,29},{10,2},{... | collective-permute-start | bytes 1572872 | tf_op jit(solution)/shard_map/ppermute | solution.py:331
  98.5 12.4 %collective-permute-start.18 = (f32[256,512]{1,0:T(8,128)S(1)}, f32[256,512]{1,0:T(8,128)S(1)}, u32[]{:S(2)}, u32[]{:S(2)}) collective-permute-start(f32[256,512]{1,0:T(8,128)S(1)} %keep5.1.refs_3_.refs_1_), channel_id=1, source_target_pairs={{0,8},{4,12},{24,16},{28,20},{1,9},{5,13},{25,17},{29,21},{2,10},{... | collective-permute-start | bytes 1572872 | tf_op jit(solution)/shard_map/ppermute | solution.py:325
  103.1 9.2 %collective-permute-start.16 = (f32[256,512]{1,0:T(8,128)S(1)}, f32[256,512]{1,0:T(8,128)S(1)}, u32[]{:S(2)}, u32[]{:S(2)}) collective-permute-start(f32[256,512]{1,0:T(8,128)S(1)} %ag0.1.refs_6_.refs_1_.refs_4_), channel_id=1, source_target_pairs={{0,4},{4,0},{8,12},{12,8},{16,20},{20,16},{24,28},{28,24},{1,5},{5... | collective-permute-start | bytes 1572872 | tf_op jit(solution)/shard_map/ppermute | solution.py:49
  105.3 8.4 %collective-permute-start.23 = (f32[256,512]{1,0:T(8,128)S(1)}, f32[256,512]{1,0:T(8,128)S(1)}, u32[]{:S(2)}, u32[]{:S(2)}) collective-permute-start(f32[256,512]{1,0:T(8,128)S(1)} %zm4.1.refs_3_.refs_1_), channel_id=1, source_target_pairs={{8,16},{12,20},{16,8},{20,12},{9,17},{13,21},{17,9},{21,13},{10,18... | collective-permute-start | bytes 1572872 | tf_op jit(solution)/shard_map/ppermute | solution.py:328
  107.6 11.1 %collective-permute-start.24 = (f32[256,512]{1,0:T(8,128)S(1)}, f32[256,512]{1,0:T(8,128)S(1)}, u32[]{:S(2)}, u32[]{:S(2)}) collective-permute-start(f32[256,512]{1,0:T(8,128)S(1)} %zo3.1.refs_3_.refs_1_), channel_id=1, source_target_pairs={{8,0},{12,4},{16,24},{20,28},{9,1},{13,5},{17,25},{21,29},{10,2},{... | collective-permute-start | bytes 1572872 | tf_op jit(solution)/shard_map/ppermute | solution.py:331
  113.0 9.2 %collective-permute-start.22 = (f32[512,256]{1,0:T(8,128)S(1)}, f32[512,256]{1,0:T(8,128)S(1)}, u32[]{:S(2)}, u32[]{:S(2)}) collective-permute-start(f32[512,256]{1,0:T(8,128)S(1)} %g4.1.refs_3_.refs_1_), channel_id=1, source_target_pairs={{0,1},{1,0},{2,3},{3,2},{4,5},{5,4},{6,7},{7,6},{8,9},{9,8},{10,11... | collective-permute-start | bytes 1572872 | tf_op jit(solution)/shard_map/ppermute | solution.py:49
  113.0 16.0 %collective-permute-start.25 = (f32[256,512]{1,0:T(8,128)S(1)}, f32[256,512]{1,0:T(8,128)S(1)}, u32[]{:S(2)}, u32[]{:S(2)}) collective-permute-start(f32[256,512]{1,0:T(8,128)S(1)} %zm5.1.refs_3_.refs_1_), channel_id=1, source_target_pairs={{8,16},{12,20},{16,8},{20,12},{9,17},{13,21},{17,9},{21,13},{10,18... | collective-permute-start | bytes 1572872 | tf_op jit(solution)/shard_map/ppermute | solution.py:328
  119.3 12.1 %collective-permute-start.26 = (f32[256,512]{1,0:T(8,128)S(1)}, f32[256,512]{1,0:T(8,128)S(1)}, u32[]{:S(2)}, u32[]{:S(2)}) collective-permute-start(f32[256,512]{1,0:T(8,128)S(1)} %zo4.1.refs_3_.refs_1_), channel_id=1, source_target_pairs={{8,0},{12,4},{16,24},{20,28},{9,1},{13,5},{17,25},{21,29},{10,2},{... | collective-permute-start | bytes 1572872 | tf_op jit(solution)/shard_map/ppermute | solution.py:331
  120.6 14.9 %collective-permute-start.27 = (f32[256,512]{1,0:T(8,128)S(1)}, f32[256,512]{1,0:T(8,128)S(1)}, u32[]{:S(2)}, u32[]{:S(2)}) collective-permute-start(f32[256,512]{1,0:T(8,128)S(1)} %ag1.1.refs_3_.refs_4_), channel_id=1, source_target_pairs={{0,4},{4,0},{8,12},{12,8},{16,20},{20,16},{24,28},{28,24},{1,5},{5... | collective-permute-start | bytes 1572872 | tf_op jit(solution)/shard_map/ppermute | solution.py:49
  123.6 23.2 %collective-permute-start.28 = (f32[256,512]{1,0:T(8,128)S(1)}, f32[256,512]{1,0:T(8,128)S(1)}, u32[]{:S(2)}, u32[]{:S(2)}) collective-permute-start(f32[256,512]{1,0:T(8,128)S(1)} %ag2.1.refs_2_.refs_4_), channel_id=1, source_target_pairs={{0,4},{4,0},{8,12},{12,8},{16,20},{20,16},{24,28},{28,24},{1,5},{5... | collective-permute-start | bytes 1572872 | tf_op jit(solution)/shard_map/ppermute | solution.py:49
  132.0 21.9 %collective-permute-start.29 = (f32[256,512]{1,0:T(8,128)S(1)}, f32[256,512]{1,0:T(8,128)S(1)}, u32[]{:S(2)}, u32[]{:S(2)}) collective-permute-start(f32[256,512]{1,0:T(8,128)S(1)} %zo5.1.refs_3_.refs_1_), channel_id=1, source_target_pairs={{8,0},{12,4},{16,24},{20,28},{9,1},{13,5},{17,25},{21,29},{10,2},{... | collective-permute-start | bytes 1572872 | tf_op jit(solution)/shard_map/ppermute | solution.py:331
  136.1 23.0 %collective-permute-start.30 = (f32[256,512]{1,0:T(8,128)S(1)}, f32[256,512]{1,0:T(8,128)S(1)}, u32[]{:S(2)}, u32[]{:S(2)}) collective-permute-start(f32[256,512]{1,0:T(8,128)S(1)} %ag3.1.refs_3_.refs_4_), channel_id=1, source_target_pairs={{0,4},{4,0},{8,12},{12,8},{16,20},{20,16},{24,28},{28,24},{1,5},{5... | collective-permute-start | bytes 1572872 | tf_op jit(solution)/shard_map/ppermute | solution.py:49
  147.6 21.7 %collective-permute-start.31 = (f32[256,512]{1,0:T(8,128)S(1)}, f32[256,512]{1,0:T(8,128)S(1)}, u32[]{:S(2)}, u32[]{:S(2)}) collective-permute-start(f32[256,512]{1,0:T(8,128)S(1)} %ag4.1.refs_3_.refs_4_), channel_id=1, source_target_pairs={{0,4},{4,0},{8,12},{12,8},{16,20},{20,16},{24,28},{28,24},{1,5},{5... | collective-permute-start | bytes 1572872 | tf_op jit(solution)/shard_map/ppermute | solution.py:49
  154.5 20.5 %collective-permute-start.32 = (f32[256,512]{1,0:T(8,128)S(1)}, f32[256,512]{1,0:T(8,128)S(1)}, u32[]{:S(2)}, u32[]{:S(2)}) collective-permute-start(f32[256,512]{1,0:T(8,128)S(1)} %ag5.1.refs_3_.refs_4_), channel_id=1, source_target_pairs={{0,4},{4,0},{8,12},{12,8},{16,20},{20,16},{24,28},{28,24},{1,5},{5... | collective-permute-start | bytes 1572872 | tf_op jit(solution)/shard_map/ppermute | solution.py:49

commit v2 on v1

--- a/solution.py
+++ b/solution.py
@@ -13,10 +13,10 @@
 TILE = 128
 SIZES = (1, 2, 2, 2, 2, 2)
 ORDER = (
-    "panels send0 send1 keep0", "send2 keep1 zm0 send3", "keep2 zm1 zo0 send4", "keep3 zm2 ~zo0 zo1",
-    "send5 keep4 zm3 ~zo1", "zo2 ag0 keep5 zm4", "~zo2 zo3 ag1 zm5", "~ag0 g4 ~zo3 zo4",
-    "g6 ag2 ch0 ~zo4", "zo5 ~ag1 ag3 ch1", "~ag2 ag4 ch2 ~zo5", "ag5 ch3 ~ag3 weights",
-    "fin0 fin1 fin2 fin3", "fin4 fin5",
+    "panels send0 send1 send2", "send3 keep0 send4 send5", "keep1 zm0 keep2 zm1", "zo0 keep3 zm2 zo1",
+    "~zo0 keep4 zm3 zo2", "~zo1 ag0 keep5 zm4", "zo3 ~zo2 ag1 g4", "zm5 zo4 ~zo3 ag2",
+    "g6 ch0 ~ag1 zo5", "~zo4 ag3 ch1 ~ag2", "ag4 ~zo5 ag5 ch2", "ch3 ~ag3 weights fin0",
+    "fin1 fin2 fin3 fin4", "fin5",
 )
 
 

time: 181 us -> 175 us (0.967)
  starting transfers between devices: 58.5 us -> 50.8 us
    ppermute x6, starting transfers between devices: 25.7 us -> 20.4 us  [in_hop(): lax.ppermute(value, 'prow', [(0, 2), (1, 3), (6, 4), (7, 5)])]
    ppermute x6, waiting for transfers between devices: 12 us -> 15.8 us  [out_hop(): lax.ppermute(value, 'prow', [(2, 0), (3, 1), (4, 6), (5, 7)])]
    ppermute x14, waiting for transfers between devices: 33.1 us -> 30.4 us  [flip(): return lax.ppermute(value, axis, [(i, i ^ bit) for i in range(n)])]
    ppermute x14, starting transfers between devices: 16 us -> 13.6 us  [flip(): return lax.ppermute(value, axis, [(i, i ^ bit) for i in range(n)])]
  transfers between devices with their start and end apart: 33 -> 33, of which waited for: 17 -> 18; matrix products, arithmetic and copies ran while one was open for 0% -> 0% of each run, Pallas kernels for 31% -> 32%
where the time goes in v2:
time: 175 us; the launch traced here: 173 us
  Pallas kernels  63.3 us (36%)
  waiting for transfers between devices  53.3 us (30%)
  starting transfers between devices  50.8 us (29%)
  local copies, waits for them, and re-layouts  4.16 us (2%)
    pallas_call x46, Pallas kernels, __call__(): pl.pallas_call(body, out_shape=[jax.ShapeDtypeStruct(*(o if isinstance(o[...  60.2 us
    ppermute x14, waiting for transfers between devices, flip(): return lax.ppermute(value, axis, [(i, i ^ bit) for i in range(n)])  30.4 us
    ppermute x6, starting transfers between devices, in_hop(): lax.ppermute(value, 'prow', [(0, 2), (1, 3), (6, 4), (7, 5)])  20.4 us
    ppermute x6, waiting for transfers between devices, out_hop(): lax.ppermute(value, 'prow', [(2, 0), (3, 1), (4, 6), (5, 7)])  15.8 us
    ppermute x14, starting transfers between devices, flip(): return lax.ppermute(value, axis, [(i, i ^ bit) for i in range(n)])  13.6 us
    ppermute x6, starting transfers between devices, out_hop(): lax.ppermute(value, 'prow', [(2, 0), (3, 1), (4, 6), (5, 7)])  7.75 us
    ppermute x1, waiting for transfers between devices, local(): came = lax.ppermute(held, 'pcol', [(0, 2), (1, 3)]) if n_col > 2 else held  6 us
    ppermute x1, starting transfers between devices, local(): came = lax.ppermute(held, 'pcol', [(0, 2), (1, 3)]) if n_col > 2 else held  4.88 us
  transfers between devices with their start and end apart: 33, of which 18 were waited for; matrix products, arithmetic and copies ran while one was open for 0% of the time, Pallas kernels for 32%

profile of v2, /device:TPU:0, one launch (start us, length us, event | category | flops | bytes accessed | tf_op | source)
XLA Modules:
  0.0 173.0 jit_solution(9977295928828747042)
XLA Ops:
  0.6 1.4 slice.3
  2.1 4.9 %collective-permute-start = (f32[512,256]{1,0:T(8,128)S(1)}, f32[512,256]{1,0:T(8,128)S(1)}, u32[]{:S(2)}, u32[]{:S(2)}) collective-permute-start(f32[512,256]{1,0:T(8,128)S(1)} %bitcast.13), channel_id=1, source_target_pairs={{0,2},{1,3},{4,6},{5,7},{8,10},{9,11},{12,14},{13,15},{16,18},{17,... | collective-permute-start | bytes 1572872 | tf_op jit(solution)/shard_map/ppermute | solution.py:307
  7.1 2.6 %copy-done = f32[512,11,1,256]{3,2,1,0:T(1,128)S(1)} copy-done((f32[512,11,1,256]{3,2,1,0:T(1,128)S(1)}, f32[512,11,1,256]{3,2,1,0:T(1,128)}, u32[]{:S(2)}) %copy-start) | copy-done | bytes 5767192
  9.7 2.4 %rows_to_tiles.1 = (f32[512,256]{1,0:T(8,128)S(1)}, bf16[512,256]{1,0:T(8,128)(2,1)S(1)}, bf16[512,256]{1,0:T(8,128)(2,1)S(1)}, f32[512,512]{1,0:T(8,128)S(1)}, ...) custom-call(s32[6]{0:T(128)S(1)} %stack.43.refs_0_, ...), custom_call_target="tpu_custom_call" | custom-call | flops 1000 | bytes 1000 | tf_op jit(solution)/shard_map/rows_to_tiles/pallas_call | solution.py:66
  12.1 6.0 %collective-permute-done.refs_1_ = f32[512,256]{1,0:T(8,128)S(1)} collective-permute-done((f32[512,256]{1,0:T(8,128)S(1)}, f32[512,256]{1,0:T(8,128)S(1)}, u32[]{:S(2)}, u32[]{:S(2)}) %collective-permute-start) | collective-permute-done | bytes 524320 | tf_op jit(solution)/shard_map/ppermute | solution.py:307
  18.8 1.9 %collective-permute-done.1.refs_2_ = f32[512,256]{1,0:T(8,128)S(1)} collective-permute-done((f32[512,256]{1,0:T(8,128)S(1)}, f32[512,256]{1,0:T(8,128)S(1)}, u32[]{:S(2)}, u32[]{:S(2)}) %collective-permute-start.1) | collective-permute-done | bytes 524320 | tf_op jit(solution)/shard_map/ppermute | solution.py:49
  21.6 1.3 send0.1.refs_5_
  23.0 1.6 collective-permute-start.2
  28.5 9.3 %collective-permute-done.2.refs_5_ = f32[256,512]{1,0:T(8,128)S(1)} collective-permute-done((f32[256,512]{1,0:T(8,128)S(1)}, f32[256,512]{1,0:T(8,128)S(1)}, u32[]{:S(2)}, u32[]{:S(2)}) %collective-permute-start.2) | collective-permute-done | bytes 524320 | tf_op jit(solution)/shard_map/ppermute | solution.py:49
  37.8 1.4 keep0.1.refs_5_.refs_1_
  39.2 3.5 %collective-permute-start.3 = (f32[256,512]{1,0:T(8,128)S(1)}, f32[256,512]{1,0:T(8,128)S(1)}, u32[]{:S(2)}, u32[]{:S(2)}) collective-permute-start(f32[256,512]{1,0:T(8,128)S(1)} %keep0.1.refs_5_.refs_1_), channel_id=1, source_target_pairs={{0,8},{4,12},{24,16},{28,20},{1,9},{5,13},{25,17},{29,21},{2,10},{... | collective-permute-start | bytes 1572872 | tf_op jit(solution)/shard_map/ppermute | solution.py:325
  42.7 1.6 collective-permute-start.7
  46.5 2.5 %collective-permute-done.4.refs_5_ = f32[256,512]{1,0:T(8,128)S(1)} collective-permute-done((f32[256,512]{1,0:T(8,128)S(1)}, f32[256,512]{1,0:T(8,128)S(1)}, u32[]{:S(2)}, u32[]{:S(2)}) %collective-permute-start.4) | collective-permute-done | bytes 524320 | tf_op jit(solution)/shard_map/ppermute | solution.py:49
  50.2 3.5 %collective-permute-start.6 = (f32[256,512]{1,0:T(8,128)S(1)}, f32[256,512]{1,0:T(8,128)S(1)}, u32[]{:S(2)}, u32[]{:S(2)}) collective-permute-start(f32[256,512]{1,0:T(8,128)S(1)} %keep1.1.refs_3_.refs_1_), channel_id=1, source_target_pairs={{0,8},{4,12},{24,16},{28,20},{1,9},{5,13},{25,17},{29,21},{2,10},{... | collective-permute-start | bytes 1572872 | tf_op jit(solution)/shard_map/ppermute | solution.py:325
  55.0 1.6 collective-permute-start.10
  56.6 3.7 %collective-permute-done.7.refs_5_ = f32[256,512]{1,0:T(8,128)S(1)} collective-permute-done((f32[256,512]{1,0:T(8,128)S(1)}, f32[256,512]{1,0:T(8,128)S(1)}, u32[]{:S(2)}, u32[]{:S(2)}) %collective-permute-start.7) | collective-permute-done | bytes 524320 | tf_op jit(solution)/shard_map/ppermute | solution.py:49
  61.4 3.5 %collective-permute-start.9 = (f32[256,512]{1,0:T(8,128)S(1)}, f32[256,512]{1,0:T(8,128)S(1)}, u32[]{:S(2)}, u32[]{:S(2)}) collective-permute-start(f32[256,512]{1,0:T(8,128)S(1)} %keep2.1.refs_3_.refs_1_), channel_id=1, source_target_pairs={{0,8},{4,12},{24,16},{28,20},{1,9},{5,13},{25,17},{29,21},{2,10},{... | collective-permute-start | bytes 1572872 | tf_op jit(solution)/shard_map/ppermute | solution.py:325
  66.2 1.6 collective-permute-start.13
  68.4 1.3 collective-permute-start.8
  69.7 1.8 %collective-permute-done.10.refs_5_ = f32[256,512]{1,0:T(8,128)S(1)} collective-permute-done((f32[256,512]{1,0:T(8,128)S(1)}, f32[256,512]{1,0:T(8,128)S(1)}, u32[]{:S(2)}, u32[]{:S(2)}) %collective-permute-start.10) | collective-permute-done | bytes 524320 | tf_op jit(solution)/shard_map/ppermute | solution.py:49
  72.6 4.4 %collective-permute-start.12 = (f32[256,512]{1,0:T(8,128)S(1)}, f32[256,512]{1,0:T(8,128)S(1)}, u32[]{:S(2)}, u32[]{:S(2)}) collective-permute-start(f32[256,512]{1,0:T(8,128)S(1)} %keep3.1.refs_3_.refs_1_), channel_id=1, source_target_pairs={{0,8},{4,12},{24,16},{28,20},{1,9},{5,13},{25,17},{29,21},{2,10},{... | collective-permute-start | bytes 1572872 | tf_op jit(solution)/shard_map/ppermute | solution.py:325
  79.0 1.3 collective-permute-start.15
  80.3 1.6 collective-permute-done.13.refs_5_
  82.0 1.5 collective-permute-start.19
  85.5 2.8 %collective-permute-start.18 = (f32[256,512]{1,0:T(8,128)S(1)}, f32[256,512]{1,0:T(8,128)S(1)}, u32[]{:S(2)}, u32[]{:S(2)}) collective-permute-start(f32[256,512]{1,0:T(8,128)S(1)} %keep4.1.refs_3_.refs_1_), channel_id=1, source_target_pairs={{0,8},{4,12},{24,16},{28,20},{1,9},{5,13},{25,17},{29,21},{2,10},{... | collective-permute-start | bytes 1572872 | tf_op jit(solution)/shard_map/ppermute | solution.py:325
  90.3 1.3 collective-permute-start.20
  91.6 4.0 %collective-permute-done.15.refs_4_.refs_2_ = f32[256,512]{1,0:T(8,128)S(1)} collective-permute-done((f32[256,512]{1,0:T(8,128)S(1)}, f32[256,512]{1,0:T(8,128)S(1)}, u32[]{:S(2)}, u32[]{:S(2)}) %collective-permute-start.15) | collective-permute-done | bytes 524320 | tf_op jit(solution)/shard_map/ppermute | solution.py:331
  97.4 2.6 %collective-permute-start.23 = (f32[256,512]{1,0:T(8,128)S(1)}, f32[256,512]{1,0:T(8,128)S(1)}, u32[]{:S(2)}, u32[]{:S(2)}) collective-permute-start(f32[256,512]{1,0:T(8,128)S(1)} %keep5.1.refs_3_.refs_1_), channel_id=1, source_target_pairs={{0,8},{4,12},{24,16},{28,20},{1,9},{5,13},{25,17},{29,21},{2,10},{... | collective-permute-start | bytes 1572872 | tf_op jit(solution)/shard_map/ppermute | solution.py:325
  101.9 1.3 collective-permute-start.24
  103.2 2.5 %collective-permute-done.20.refs_4_.refs_2_ = f32[256,512]{1,0:T(8,128)S(1)} collective-permute-done((f32[256,512]{1,0:T(8,128)S(1)}, f32[256,512]{1,0:T(8,128)S(1)}, u32[]{:S(2)}, u32[]{:S(2)}) %collective-permute-start.20) | collective-permute-done | bytes 524320 | tf_op jit(solution)/shard_map/ppermute | solution.py:331
  110.0 1.6 collective-permute-start.26
  112.2 1.3 collective-permute-start.27
  113.5 3.4 %collective-permute-done.24.refs_4_.refs_2_ = f32[256,512]{1,0:T(8,128)S(1)} collective-permute-done((f32[256,512]{1,0:T(8,128)S(1)}, f32[256,512]{1,0:T(8,128)S(1)}, u32[]{:S(2)}, u32[]{:S(2)}) %collective-permute-start.24) | collective-permute-done | bytes 524320 | tf_op jit(solution)/shard_map/ppermute | solution.py:331
  118.8 4.9 %factor0.1 = (f32[512,512]{1,0:T(8,128)S(1)}, f32[512,512]{1,0:T(8,128)S(1)}) custom-call(s32[6]{0:T(128)S(1)} %stack.43.refs_0_, f32[512,512]{1,0:T(8,128)S(1)} %g6.1.refs_1_.refs_2_, f32[512,512]{1,0:T(8,128)S(1)} %g6.1.refs_1_.refs_2_), custom_call_target="tpu_custom_call" | custom-call | flops 1000 | bytes 1000 | tf_op jit(solution)/shard_map/factor0/pallas_call | solution.py:66
  126.8 3.1 %collective-permute-done.27.refs_4_.refs_2_ = f32[256,512]{1,0:T(8,128)S(1)} collective-permute-done((f32[256,512]{1,0:T(8,128)S(1)}, f32[256,512]{1,0:T(8,128)S(1)}, u32[]{:S(2)}, u32[]{:S(2)}) %collective-permute-start.27) | collective-permute-done | bytes 524320 | tf_op jit(solution)/shard_map/ppermute | solution.py:331
  130.6 4.7 %factor1.1 = (f32[512,512]{1,0:T(8,128)S(1)}, f32[512,512]{1,0:T(8,128)S(1)}) custom-call(s32[6]{0:T(128)S(1)} %stack.43.refs_0_, f32[512,512]{1,0:T(8,128)S(1)} %get-tuple-element.71.refs_3_.refs_1_, f32[512,512]{1,0:T(8,128)S(1)} %get-tuple-element.72.refs_2_, f32[256,512]{1,0:T(8,128)S(1)} %ag3.1.refs_3_.refs_4_), custom_call_target="tpu_custom_call" | custom-call | flops 1000 | bytes 1000 | tf_op jit(solution)/shard_map/factor1/pallas_call | solution.py:66
  136.7 1.6 collective-permute-start.31
  138.3 1.9 %collective-permute-done.28.refs_2_.refs_4_ = f32[256,512]{1,0:T(8,128)S(1)} collective-permute-done((f32[256,512]{1,0:T(8,128)S(1)}, f32[256,512]{1,0:T(8,128)S(1)}, u32[]{:S(2)}, u32[]{:S(2)}) %collective-permute-start.28) | collective-permute-done | bytes 524320 | tf_op jit(solution)/shard_map/ppermute | solution.py:331
  142.2 4.7 %factor2.1 = (f32[512,512]{1,0:T(8,128)S(1)}, f32[512,512]{1,0:T(8,128)S(1)}) custom-call(s32[6]{0:T(128)S(1)} %stack.43.refs_0_, f32[512,512]{1,0:T(8,128)S(1)} %get-tuple-element.73.refs_3_.refs_1_, f32[512,512]{1,0:T(8,128)S(1)} %get-tuple-element.74.refs_2_, f32[256,512]{1,0:T(8,128)S(1)} %ag5.1.refs_3_.refs_4_), custom_call_target="tpu_custom_call" | custom-call | flops 1000 | bytes 1000 | tf_op jit(solution)/shard_map/factor2/pallas_call | solution.py:66
  146.9 4.0 %factor3.1 = (f32[512,512]{1,0:T(8,128)S(1)}, f32[512,512]{1,0:T(8,128)S(1)}) custom-call(s32[6]{0:T(128)S(1)} %stack.43.refs_0_, f32[512,512]{1,0:T(8,128)S(1)} %get-tuple-element.75.refs_1_.refs_3_, f32[512,512]{1,0:T(8,128)S(1)} %get-tuple-element.76.refs_2_, f32[512,512]{1,0:T(8,128)S(1)} %get-tuple-element.75.refs_1_.refs_3_), custom_call_target="tpu_custom_call" | custom-call | flops 1000 | bytes 1000 | tf_op jit(solution)/shard_map/factor3/pallas_call | solution.py:66
  151.0 2.6 %weights.1 = (bf16[576,512]{1,0:T(8,128)(2,1)S(1)}, bf16[576,512]{1,0:T(8,128)(2,1)S(1)}) custom-call(s32[6]{0:T(128)S(1)} %stack.43.refs_0_, f32[512,512]{1,0:T(8,128)S(1)} %get-tuple-element.52.refs_7_.refs_1_, f32[512,512]{1,0:T(8,128)S(1)} %get-tuple-element.77.refs_2_, f32[512,512]{1,0:T(8,128)S(1)} %get-tuple-element.78.refs_3_, ...), custom_call_target="tpu_custom_call" | custom-call | flops 1000 | bytes 1000 | tf_op jit(solution)/shard_map/weights/pallas_call | solution.py:66
  154.8 1.6 fin1.1
  156.4 1.6 fin2.1
  158.0 1.6 fin3.1
  159.7 1.6 fin4.1
  161.3 6.9 %collective-permute-done.32.refs_5_ = f32[256,512]{1,0:T(8,128)S(1)} collective-permute-done((f32[256,512]{1,0:T(8,128)S(1)}, f32[256,512]{1,0:T(8,128)S(1)}, u32[]{:S(2)}, u32[]{:S(2)}) %collective-permute-start.32) | collective-permute-done | bytes 524320 | tf_op jit(solution)/shard_map/ppermute | solution.py:49
  168.2 1.6 fin5.1
  169.8 3.1 %tiles_to_rows.1 = (f32[11264,128]{1,0:T(8,128)}, f32[1408,128]{1,0:T(8,128)}) custom-call(f32[512,256]{1,0:T(8,128)S(1)} %get-tuple-element.81.refs_6_.refs_0_, f32[512,512]{1,0:T(8,128)S(1)} %get-tuple-element.83.refs_6_.refs_1_, f32[512,512]{1,0:T(8,128)S(1)} %get-tuple-element.85.refs_6_.refs_2_, f32[512,512]{1,0:T(8,128)S(1)} %get-tuple-element.87.refs_6_.refs_3_, ...), custom_call_target="tpu_custom_call" | custom-call | tf_op jit(solution)/shard_map/tiles_to_rows/pallas_call | solution.py:272
  (70 shorter events, 38.9 us)
Async XLA Ops:
  2.1 16.0 %collective-permute-start = (f32[512,256]{1,0:T(8,128)S(1)}, f32[512,256]{1,0:T(8,128)S(1)}, u32[]{:S(2)}, u32[]{:S(2)}) collective-permute-start(f32[512,256]{1,0:T(8,128)S(1)} %bitcast.13), channel_id=1, source_target_pairs={{0,2},{1,3},{4,6},{5,7},{8,10},{9,11},{12,14},{13,15},{16,18},{17,... | collective-permute-start | bytes 1572872 | tf_op jit(solution)/shard_map/ppermute | solution.py:307
  7.1 2.6 %copy-start = (f32[512,11,1,256]{3,2,1,0:T(1,128)S(1)}, f32[512,11,1,256]{3,2,1,0:T(1,128)}, u32[]{:S(2)}) copy-start(f32[512,11,1,256]{3,2,1,0:T(1,128)} %param.1) | copy-start | bytes 17301508
  18.7 2.0 %collective-permute-start.1 = (f32[512,256]{1,0:T(8,128)S(1)}, f32[512,256]{1,0:T(8,128)S(1)}, u32[]{:S(2)}, u32[]{:S(2)}) collective-permute-start(f32[512,256]{1,0:T(8,128)S(1)} %pick.1.refs_1_.refs_3_.refs_6_.refs_7_), channel_id=1, source_target_pairs={{0,1},{1,0},{2,3},{3,2},{4,5},{5,4},{6,7},{7,6},{8,9},{9,8},{10,11... | collective-permute-start | bytes 1572872 | tf_op jit(solution)/shard_map/ppermute | solution.py:49
  23.0 14.8 %collective-permute-start.2 = (f32[256,512]{1,0:T(8,128)S(1)}, f32[256,512]{1,0:T(8,128)S(1)}, u32[]{:S(2)}, u32[]{:S(2)}) collective-permute-start(f32[256,512]{1,0:T(8,128)S(1)} %send0.1.refs_5_), channel_id=1, source_target_pairs={{0,4},{4,0},{8,12},{12,8},{16,20},{20,16},{24,28},{28,24},{1,5},{5... | collective-permute-start | bytes 1572872 | tf_op jit(solution)/shard_map/ppermute | solution.py:49
  25.7 23.4 %collective-permute-start.4 = (f32[256,512]{1,0:T(8,128)S(1)}, f32[256,512]{1,0:T(8,128)S(1)}, u32[]{:S(2)}, u32[]{:S(2)}) collective-permute-start(f32[256,512]{1,0:T(8,128)S(1)} %send1.1.refs_5_), channel_id=1, source_target_pairs={{0,4},{4,0},{8,12},{12,8},{16,20},{20,16},{24,28},{28,24},{1,5},{5... | collective-permute-start | bytes 1572872 | tf_op jit(solution)/shard_map/ppermute | solution.py:49
  39.2 14.5 %collective-permute-start.3 = (f32[256,512]{1,0:T(8,128)S(1)}, f32[256,512]{1,0:T(8,128)S(1)}, u32[]{:S(2)}, u32[]{:S(2)}) collective-permute-start(f32[256,512]{1,0:T(8,128)S(1)} %keep0.1.refs_5_.refs_1_), channel_id=1, source_target_pairs={{0,8},{4,12},{24,16},{28,20},{1,9},{5,13},{25,17},{29,21},{2,10},{... | collective-permute-start | bytes 1572872 | tf_op jit(solution)/shard_map/ppermute | solution.py:325
  42.7 17.6 %collective-permute-start.7 = (f32[256,512]{1,0:T(8,128)S(1)}, f32[256,512]{1,0:T(8,128)S(1)}, u32[]{:S(2)}, u32[]{:S(2)}) collective-permute-start(f32[256,512]{1,0:T(8,128)S(1)} %send2.1.refs_5_), channel_id=1, source_target_pairs={{0,4},{4,0},{8,12},{12,8},{16,20},{20,16},{24,28},{28,24},{1,5},{5... | collective-permute-start | bytes 1572872 | tf_op jit(solution)/shard_map/ppermute | solution.py:49
  50.2 14.8 %collective-permute-start.6 = (f32[256,512]{1,0:T(8,128)S(1)}, f32[256,512]{1,0:T(8,128)S(1)}, u32[]{:S(2)}, u32[]{:S(2)}) collective-permute-start(f32[256,512]{1,0:T(8,128)S(1)} %keep1.1.refs_3_.refs_1_), channel_id=1, source_target_pairs={{0,8},{4,12},{24,16},{28,20},{1,9},{5,13},{25,17},{29,21},{2,10},{... | collective-permute-start | bytes 1572872 | tf_op jit(solution)/shard_map/ppermute | solution.py:325
  54.3 13.5 %collective-permute-start.5 = (f32[256,512]{1,0:T(8,128)S(1)}, f32[256,512]{1,0:T(8,128)S(1)}, u32[]{:S(2)}, u32[]{:S(2)}) collective-permute-start(f32[256,512]{1,0:T(8,128)S(1)} %zm0.1.refs_6_.refs_1_), channel_id=1, source_target_pairs={{8,16},{12,20},{16,8},{20,12},{9,17},{13,21},{17,9},{21,13},{10,18... | collective-permute-start | bytes 1572872 | tf_op jit(solution)/shard_map/ppermute | solution.py:328
  55.0 16.5 %collective-permute-start.10 = (f32[256,512]{1,0:T(8,128)S(1)}, f32[256,512]{1,0:T(8,128)S(1)}, u32[]{:S(2)}, u32[]{:S(2)}) collective-permute-start(f32[256,512]{1,0:T(8,128)S(1)} %send3.1.refs_8_), channel_id=1, source_target_pairs={{0,4},{4,0},{8,12},{12,8},{16,20},{20,16},{24,28},{28,24},{1,5},{5... | collective-permute-start | bytes 1572872 | tf_op jit(solution)/shard_map/ppermute | solution.py:49
  61.4 15.7 %collective-permute-start.9 = (f32[256,512]{1,0:T(8,128)S(1)}, f32[256,512]{1,0:T(8,128)S(1)}, u32[]{:S(2)}, u32[]{:S(2)}) collective-permute-start(f32[256,512]{1,0:T(8,128)S(1)} %keep2.1.refs_3_.refs_1_), channel_id=1, source_target_pairs={{0,8},{4,12},{24,16},{28,20},{1,9},{5,13},{25,17},{29,21},{2,10},{... | collective-permute-start | bytes 1572872 | tf_op jit(solution)/shard_map/ppermute | solution.py:325
  65.5 12.9 %collective-permute-start.14 = (f32[256,512]{1,0:T(8,128)S(1)}, f32[256,512]{1,0:T(8,128)S(1)}, u32[]{:S(2)}, u32[]{:S(2)}) collective-permute-start(f32[256,512]{1,0:T(8,128)S(1)} %zm1.1.refs_3_.refs_1_), channel_id=1, source_target_pairs={{8,16},{12,20},{16,8},{20,12},{9,17},{13,21},{17,9},{21,13},{10,18... | collective-permute-start | bytes 1572872 | tf_op jit(solution)/shard_map/ppermute | solution.py:328
  66.2 15.7 %collective-permute-start.13 = (f32[256,512]{1,0:T(8,128)S(1)}, f32[256,512]{1,0:T(8,128)S(1)}, u32[]{:S(2)}, u32[]{:S(2)}) collective-permute-start(f32[256,512]{1,0:T(8,128)S(1)} %send4.1.refs_5_), channel_id=1, source_target_pairs={{0,4},{4,0},{8,12},{12,8},{16,20},{20,16},{24,28},{28,24},{1,5},{5... | collective-permute-start | bytes 1572872 | tf_op jit(solution)/shard_map/ppermute | solution.py:49
  68.4 15.9 %collective-permute-start.8 = (f32[256,512]{1,0:T(8,128)S(1)}, f32[256,512]{1,0:T(8,128)S(1)}, u32[]{:S(2)}, u32[]{:S(2)}) collective-permute-start(f32[256,512]{1,0:T(8,128)S(1)} %zo0.1.refs_6_.refs_1_), channel_id=1, source_target_pairs={{8,0},{12,4},{16,24},{20,28},{9,1},{13,5},{17,25},{21,29},{10,2},{... | collective-permute-start | bytes 1572872 | tf_op jit(solution)/shard_map/ppermute | solution.py:331
  72.6 15.7 %collective-permute-start.12 = (f32[256,512]{1,0:T(8,128)S(1)}, f32[256,512]{1,0:T(8,128)S(1)}, u32[]{:S(2)}, u32[]{:S(2)}) collective-permute-start(f32[256,512]{1,0:T(8,128)S(1)} %keep3.1.refs_3_.refs_1_), channel_id=1, source_target_pairs={{0,8},{4,12},{24,16},{28,20},{1,9},{5,13},{25,17},{29,21},{2,10},{... | collective-permute-start | bytes 1572872 | tf_op jit(solution)/shard_map/ppermute | solution.py:325
  77.7 11.9 %collective-permute-start.11 = (f32[256,512]{1,0:T(8,128)S(1)}, f32[256,512]{1,0:T(8,128)S(1)}, u32[]{:S(2)}, u32[]{:S(2)}) collective-permute-start(f32[256,512]{1,0:T(8,128)S(1)} %zm2.1.refs_3_.refs_1_), channel_id=1, source_target_pairs={{8,16},{12,20},{16,8},{20,12},{9,17},{13,21},{17,9},{21,13},{10,18... | collective-permute-start | bytes 1572872 | tf_op jit(solution)/shard_map/ppermute | solution.py:328
  79.0 16.6 %collective-permute-start.15 = (f32[256,512]{1,0:T(8,128)S(1)}, f32[256,512]{1,0:T(8,128)S(1)}, u32[]{:S(2)}, u32[]{:S(2)}) collective-permute-start(f32[256,512]{1,0:T(8,128)S(1)} %zo1.1.refs_6_.refs_1_), channel_id=1, source_target_pairs={{8,0},{12,4},{16,24},{20,28},{9,1},{13,5},{17,25},{21,29},{10,2},{... | collective-permute-start | bytes 1572872 | tf_op jit(solution)/shard_map/ppermute | solution.py:331
  82.0 14.3 %collective-permute-start.19 = (f32[256,512]{1,0:T(8,128)S(1)}, f32[256,512]{1,0:T(8,128)S(1)}, u32[]{:S(2)}, u32[]{:S(2)}) collective-permute-start(f32[256,512]{1,0:T(8,128)S(1)} %send5.1.refs_6_), channel_id=1, source_target_pairs={{0,4},{4,0},{8,12},{12,8},{16,20},{20,16},{24,28},{28,24},{1,5},{5... | collective-permute-start | bytes 1572872 | tf_op jit(solution)/shard_map/ppermute | solution.py:49
  85.5 14.5 %collective-permute-start.18 = (f32[256,512]{1,0:T(8,128)S(1)}, f32[256,512]{1,0:T(8,128)S(1)}, u32[]{:S(2)}, u32[]{:S(2)}) collective-permute-start(f32[256,512]{1,0:T(8,128)S(1)} %keep4.1.refs_3_.refs_1_), channel_id=1, source_target_pairs={{0,8},{4,12},{24,16},{28,20},{1,9},{5,13},{25,17},{29,21},{2,10},{... | collective-permute-start | bytes 1572872 | tf_op jit(solution)/shard_map/ppermute | solution.py:325
  88.9 12.4 %collective-permute-start.17 = (f32[256,512]{1,0:T(8,128)S(1)}, f32[256,512]{1,0:T(8,128)S(1)}, u32[]{:S(2)}, u32[]{:S(2)}) collective-permute-start(f32[256,512]{1,0:T(8,128)S(1)} %zm3.1.refs_3_.refs_1_), channel_id=1, source_target_pairs={{8,16},{12,20},{16,8},{20,12},{9,17},{13,21},{17,9},{21,13},{10,18... | collective-permute-start | bytes 1572872 | tf_op jit(solution)/shard_map/ppermute | solution.py:328
  90.3 15.5 %collective-permute-start.20 = (f32[256,512]{1,0:T(8,128)S(1)}, f32[256,512]{1,0:T(8,128)S(1)}, u32[]{:S(2)}, u32[]{:S(2)}) collective-permute-start(f32[256,512]{1,0:T(8,128)S(1)} %zo2.1.refs_3_.refs_1_), channel_id=1, source_target_pairs={{8,0},{12,4},{16,24},{20,28},{9,1},{13,5},{17,25},{21,29},{10,2},{... | collective-permute-start | bytes 1572872 | tf_op jit(solution)/shard_map/ppermute | solution.py:331
  96.2 10.7 %collective-permute-start.16 = (f32[256,512]{1,0:T(8,128)S(1)}, f32[256,512]{1,0:T(8,128)S(1)}, u32[]{:S(2)}, u32[]{:S(2)}) collective-permute-start(f32[256,512]{1,0:T(8,128)S(1)} %ag0.1.refs_6_.refs_1_.refs_4_), channel_id=1, source_target_pairs={{0,4},{4,0},{8,12},{12,8},{16,20},{20,16},{24,28},{28,24},{1,5},{5... | collective-permute-start | bytes 1572872 | tf_op jit(solution)/shard_map/ppermute | solution.py:49
  97.4 11.3 %collective-permute-start.23 = (f32[256,512]{1,0:T(8,128)S(1)}, f32[256,512]{1,0:T(8,128)S(1)}, u32[]{:S(2)}, u32[]{:S(2)}) collective-permute-start(f32[256,512]{1,0:T(8,128)S(1)} %keep5.1.refs_3_.refs_1_), channel_id=1, source_target_pairs={{0,8},{4,12},{24,16},{28,20},{1,9},{5,13},{25,17},{29,21},{2,10},{... | collective-permute-start | bytes 1572872 | tf_op jit(solution)/shard_map/ppermute | solution.py:325
  100.6 11.0 %collective-permute-start.22 = (f32[256,512]{1,0:T(8,128)S(1)}, f32[256,512]{1,0:T(8,128)S(1)}, u32[]{:S(2)}, u32[]{:S(2)}) collective-permute-start(f32[256,512]{1,0:T(8,128)S(1)} %zm4.1.refs_3_.refs_1_), channel_id=1, source_target_pairs={{8,16},{12,20},{16,8},{20,12},{9,17},{13,21},{17,9},{21,13},{10,18... | collective-permute-start | bytes 1572872 | tf_op jit(solution)/shard_map/ppermute | solution.py:328
  101.9 14.9 %collective-permute-start.24 = (f32[256,512]{1,0:T(8,128)S(1)}, f32[256,512]{1,0:T(8,128)S(1)}, u32[]{:S(2)}, u32[]{:S(2)}) collective-permute-start(f32[256,512]{1,0:T(8,128)S(1)} %zo3.1.refs_3_.refs_1_), channel_id=1, source_target_pairs={{8,0},{12,4},{16,24},{20,28},{9,1},{13,5},{17,25},{21,29},{10,2},{... | collective-permute-start | bytes 1572872 | tf_op jit(solution)/shard_map/ppermute | solution.py:331
  107.5 10.1 %collective-permute-start.21 = (f32[512,256]{1,0:T(8,128)S(1)}, f32[512,256]{1,0:T(8,128)S(1)}, u32[]{:S(2)}, u32[]{:S(2)}) collective-permute-start(f32[512,256]{1,0:T(8,128)S(1)} %g4.1.refs_3_.refs_1_), channel_id=1, source_target_pairs={{0,1},{1,0},{2,3},{3,2},{4,5},{5,4},{6,7},{7,6},{8,9},{9,8},{10,11... | collective-permute-start | bytes 1572872 | tf_op jit(solution)/shard_map/ppermute | solution.py:49
  109.3 14.4 %collective-permute-start.25 = (f32[256,512]{1,0:T(8,128)S(1)}, f32[256,512]{1,0:T(8,128)S(1)}, u32[]{:S(2)}, u32[]{:S(2)}) collective-permute-start(f32[256,512]{1,0:T(8,128)S(1)} %zm5.1.refs_3_.refs_1_), channel_id=1, source_target_pairs={{8,16},{12,20},{16,8},{20,12},{9,17},{13,21},{17,9},{21,13},{10,18... | collective-permute-start | bytes 1572872 | tf_op jit(solution)/shard_map/ppermute | solution.py:328
  110.0 14.9 %collective-permute-start.26 = (f32[256,512]{1,0:T(8,128)S(1)}, f32[256,512]{1,0:T(8,128)S(1)}, u32[]{:S(2)}, u32[]{:S(2)}) collective-permute-start(f32[256,512]{1,0:T(8,128)S(1)} %ag1.1.refs_3_.refs_4_), channel_id=1, source_target_pairs={{0,4},{4,0},{8,12},{12,8},{16,20},{20,16},{24,28},{28,24},{1,5},{5... | collective-permute-start | bytes 1572872 | tf_op jit(solution)/shard_map/ppermute | solution.py:49
  112.2 17.7 %collective-permute-start.27 = (f32[256,512]{1,0:T(8,128)S(1)}, f32[256,512]{1,0:T(8,128)S(1)}, u32[]{:S(2)}, u32[]{:S(2)}) collective-permute-start(f32[256,512]{1,0:T(8,128)S(1)} %zo4.1.refs_3_.refs_1_), channel_id=1, source_target_pairs={{8,0},{12,4},{16,24},{20,28},{9,1},{13,5},{17,25},{21,29},{10,2},{... | collective-permute-start | bytes 1572872 | tf_op jit(solution)/shard_map/ppermute | solution.py:331
  118.2 17.9 %collective-permute-start.29 = (f32[256,512]{1,0:T(8,128)S(1)}, f32[256,512]{1,0:T(8,128)S(1)}, u32[]{:S(2)}, u32[]{:S(2)}) collective-permute-start(f32[256,512]{1,0:T(8,128)S(1)} %ag2.1.refs_3_.refs_4_), channel_id=1, source_target_pairs={{0,4},{4,0},{8,12},{12,8},{16,20},{20,16},{24,28},{28,24},{1,5},{5... | collective-permute-start | bytes 1572872 | tf_op jit(solution)/shard_map/ppermute | solution.py:49
  125.5 14.7 %collective-permute-start.28 = (f32[256,512]{1,0:T(8,128)S(1)}, f32[256,512]{1,0:T(8,128)S(1)}, u32[]{:S(2)}, u32[]{:S(2)}) collective-permute-start(f32[256,512]{1,0:T(8,128)S(1)} %zo5.1.refs_3_.refs_1_), channel_id=1, source_target_pairs={{8,0},{12,4},{16,24},{20,28},{9,1},{13,5},{17,25},{21,29},{10,2},{... | collective-permute-start | bytes 1572872 | tf_op jit(solution)/shard_map/ppermute | solution.py:331
  130.5 20.5 %collective-permute-start.30 = (f32[256,512]{1,0:T(8,128)S(1)}, f32[256,512]{1,0:T(8,128)S(1)}, u32[]{:S(2)}, u32[]{:S(2)}) collective-permute-start(f32[256,512]{1,0:T(8,128)S(1)} %ag3.1.refs_3_.refs_4_), channel_id=1, source_target_pairs={{0,4},{4,0},{8,12},{12,8},{16,20},{20,16},{24,28},{28,24},{1,5},{5... | collective-permute-start | bytes 1572872 | tf_op jit(solution)/shard_map/ppermute | solution.py:49
  136.7 22.9 %collective-permute-start.31 = (f32[256,512]{1,0:T(8,128)S(1)}, f32[256,512]{1,0:T(8,128)S(1)}, u32[]{:S(2)}, u32[]{:S(2)}) collective-permute-start(f32[256,512]{1,0:T(8,128)S(1)} %ag4.1.refs_3_.refs_4_), channel_id=1, source_target_pairs={{0,4},{4,0},{8,12},{12,8},{16,20},{20,16},{24,28},{28,24},{1,5},{5... | collective-permute-start | bytes 1572872 | tf_op jit(solution)/shard_map/ppermute | solution.py:49
  141.0 27.2 %collective-permute-start.32 = (f32[256,512]{1,0:T(8,128)S(1)}, f32[256,512]{1,0:T(8,128)S(1)}, u32[]{:S(2)}, u32[]{:S(2)}) collective-permute-start(f32[256,512]{1,0:T(8,128)S(1)} %ag5.1.refs_3_.refs_4_), channel_id=1, source_target_pairs={{0,4},{4,0},{8,12},{12,8},{16,20},{20,16},{24,28},{28,24},{1,5},{5... | collective-permute-start | bytes 1572872 | tf_op jit(solution)/shard_map/ppermute | solution.py:49

commit v3 on v2

--- a/solution.py
+++ b/solution.py
@@ -15,7 +15,7 @@
 ORDER = (
     "panels send0 send1 send2", "send3 keep0 send4 send5", "keep1 zm0 keep2 zm1", "zo0 keep3 zm2 zo1",
     "~zo0 keep4 zm3 zo2", "~zo1 ag0 keep5 zm4", "zo3 ~zo2 ag1 g4", "zm5 zo4 ~zo3 ag2",
-    "g6 ch0 ~ag1 zo5", "~zo4 ag3 ch1 ~ag2", "ag4 ~zo5 ag5 ch2", "ch3 ~ag3 weights fin0",
+    "g6 ~ag1 ch0 zo5", "~zo4 ag3 ch1 ~ag2", "ag4 ~zo5 ag5 ch2", "ch3 ~ag3 weights fin0",
     "fin1 fin2 fin3 fin4", "fin5",
 )
 

time: 175 us -> 172 us (0.983)
    ppermute x14, waiting for transfers between devices: 30.4 us -> 28.2 us  [flip(): return lax.ppermute(value, axis, [(i, i ^ bit) for i in range(n)])]
    ppermute x6, waiting for transfers between devices: 15.8 us -> 17.9 us  [out_hop(): lax.ppermute(value, 'prow', [(2, 0), (3, 1), (4, 6), (5, 7)])]
  transfers between devices with their start and end apart: 33 -> 33, of which waited for: 18 -> 16; matrix products, arithmetic and copies ran while one was open for 0% -> 0% of each run, Pallas kernels for 32% -> 32%
where the time goes in v3:
time: 172 us
  Pallas kernels  63.3 us (37%)
  waiting for transfers between devices  52.2 us (30%)
  starting transfers between devices  50.6 us (29%)
  local copies, waits for them, and re-layouts  4.16 us (2%)
    pallas_call x46, Pallas kernels, __call__(): pl.pallas_call(body, out_shape=[jax.ShapeDtypeStruct(*(o if isinstance(o[...  60.2 us
    ppermute x14, waiting for transfers between devices, flip(): return lax.ppermute(value, axis, [(i, i ^ bit) for i in range(n)])  28.2 us
    ppermute x6, starting transfers between devices, in_hop(): lax.ppermute(value, 'prow', [(0, 2), (1, 3), (6, 4), (7, 5)])  20.4 us
    ppermute x6, waiting for transfers between devices, out_hop(): lax.ppermute(value, 'prow', [(2, 0), (3, 1), (4, 6), (5, 7)])  17.9 us
    ppermute x14, starting transfers between devices, flip(): return lax.ppermute(value, axis, [(i, i ^ bit) for i in range(n)])  13.4 us
    ppermute x6, starting transfers between devices, out_hop(): lax.ppermute(value, 'prow', [(2, 0), (3, 1), (4, 6), (5, 7)])  7.75 us
    ppermute x1, waiting for transfers between devices, local(): came = lax.ppermute(held, 'pcol', [(0, 2), (1, 3)]) if n_col > 2 else held  6 us
    ppermute x1, starting transfers between devices, local(): came = lax.ppermute(held, 'pcol', [(0, 2), (1, 3)]) if n_col > 2 else held  4.88 us
  transfers between devices with their start and end apart: 33, of which 16 were waited for; matrix products, arithmetic and copies ran while one was open for 0% of the time, Pallas kernels for 32%

profile of v3, /device:TPU:0, one launch (start us, length us, event | category | flops | bytes accessed | tf_op | source)
XLA Modules:
  0.0 171.6 jit_solution(3903996875378781308)
XLA Ops:
  0.6 1.4 slice.3
  2.1 4.9 %collective-permute-start = (f32[512,256]{1,0:T(8,128)S(1)}, f32[512,256]{1,0:T(8,128)S(1)}, u32[]{:S(2)}, u32[]{:S(2)}) collective-permute-start(f32[512,256]{1,0:T(8,128)S(1)} %bitcast.13), channel_id=1, source_target_pairs={{0,2},{1,3},{4,6},{5,7},{8,10},{9,11},{12,14},{13,15},{16,18},{17,... | collective-permute-start | bytes 1572872 | tf_op jit(solution)/shard_map/ppermute | solution.py:307
  7.1 2.6 %copy-done = f32[512,11,1,256]{3,2,1,0:T(1,128)S(1)} copy-done((f32[512,11,1,256]{3,2,1,0:T(1,128)S(1)}, f32[512,11,1,256]{3,2,1,0:T(1,128)}, u32[]{:S(2)}) %copy-start) | copy-done | bytes 5767192
  9.7 2.4 %rows_to_tiles.1 = (f32[512,256]{1,0:T(8,128)S(1)}, bf16[512,256]{1,0:T(8,128)(2,1)S(1)}, bf16[512,256]{1,0:T(8,128)(2,1)S(1)}, f32[512,512]{1,0:T(8,128)S(1)}, ...) custom-call(s32[6]{0:T(128)S(1)} %stack.43.refs_0_, ...), custom_call_target="tpu_custom_call" | custom-call | flops 1000 | bytes 1000 | tf_op jit(solution)/shard_map/rows_to_tiles/pallas_call | solution.py:66
  12.1 6.0 %collective-permute-done.refs_1_ = f32[512,256]{1,0:T(8,128)S(1)} collective-permute-done((f32[512,256]{1,0:T(8,128)S(1)}, f32[512,256]{1,0:T(8,128)S(1)}, u32[]{:S(2)}, u32[]{:S(2)}) %collective-permute-start) | collective-permute-done | bytes 524320 | tf_op jit(solution)/shard_map/ppermute | solution.py:307
  18.8 1.9 %collective-permute-done.1.refs_2_ = f32[512,256]{1,0:T(8,128)S(1)} collective-permute-done((f32[512,256]{1,0:T(8,128)S(1)}, f32[512,256]{1,0:T(8,128)S(1)}, u32[]{:S(2)}, u32[]{:S(2)}) %collective-permute-start.1) | collective-permute-done | bytes 524320 | tf_op jit(solution)/shard_map/ppermute | solution.py:49
  21.6 1.3 send0.1.refs_5_
  23.0 1.6 collective-permute-start.2
  28.5 9.3 %collective-permute-done.2.refs_5_ = f32[256,512]{1,0:T(8,128)S(1)} collective-permute-done((f32[256,512]{1,0:T(8,128)S(1)}, f32[256,512]{1,0:T(8,128)S(1)}, u32[]{:S(2)}, u32[]{:S(2)}) %collective-permute-start.2) | collective-permute-done | bytes 524320 | tf_op jit(solution)/shard_map/ppermute | solution.py:49
  37.8 1.4 keep0.1.refs_5_.refs_1_
  39.2 3.5 %collective-permute-start.3 = (f32[256,512]{1,0:T(8,128)S(1)}, f32[256,512]{1,0:T(8,128)S(1)}, u32[]{:S(2)}, u32[]{:S(2)}) collective-permute-start(f32[256,512]{1,0:T(8,128)S(1)} %keep0.1.refs_5_.refs_1_), channel_id=1, source_target_pairs={{0,8},{4,12},{24,16},{28,20},{1,9},{5,13},{25,17},{29,21},{2,10},{... | collective-permute-start | bytes 1572872 | tf_op jit(solution)/shard_map/ppermute | solution.py:325
  42.7 1.6 collective-permute-start.7
  46.5 2.5 %collective-permute-done.4.refs_5_ = f32[256,512]{1,0:T(8,128)S(1)} collective-permute-done((f32[256,512]{1,0:T(8,128)S(1)}, f32[256,512]{1,0:T(8,128)S(1)}, u32[]{:S(2)}, u32[]{:S(2)}) %collective-permute-start.4) | collective-permute-done | bytes 524320 | tf_op jit(solution)/shard_map/ppermute | solution.py:49
  50.2 3.5 %collective-permute-start.6 = (f32[256,512]{1,0:T(8,128)S(1)}, f32[256,512]{1,0:T(8,128)S(1)}, u32[]{:S(2)}, u32[]{:S(2)}) collective-permute-start(f32[256,512]{1,0:T(8,128)S(1)} %keep1.1.refs_3_.refs_1_), channel_id=1, source_target_pairs={{0,8},{4,12},{24,16},{28,20},{1,9},{5,13},{25,17},{29,21},{2,10},{... | collective-permute-start | bytes 1572872 | tf_op jit(solution)/shard_map/ppermute | solution.py:325
  55.0 1.6 collective-permute-start.10
  56.6 3.7 %collective-permute-done.7.refs_5_ = f32[256,512]{1,0:T(8,128)S(1)} collective-permute-done((f32[256,512]{1,0:T(8,128)S(1)}, f32[256,512]{1,0:T(8,128)S(1)}, u32[]{:S(2)}, u32[]{:S(2)}) %collective-permute-start.7) | collective-permute-done | bytes 524320 | tf_op jit(solution)/shard_map/ppermute | solution.py:49
  61.4 3.5 %collective-permute-start.9 = (f32[256,512]{1,0:T(8,128)S(1)}, f32[256,512]{1,0:T(8,128)S(1)}, u32[]{:S(2)}, u32[]{:S(2)}) collective-permute-start(f32[256,512]{1,0:T(8,128)S(1)} %keep2.1.refs_3_.refs_1_), channel_id=1, source_target_pairs={{0,8},{4,12},{24,16},{28,20},{1,9},{5,13},{25,17},{29,21},{2,10},{... | collective-permute-start | bytes 1572872 | tf_op jit(solution)/shard_map/ppermute | solution.py:325
  66.2 1.6 collective-permute-start.13
  68.4 1.3 collective-permute-start.8
  69.7 1.8 %collective-permute-done.10.refs_5_ = f32[256,512]{1,0:T(8,128)S(1)} collective-permute-done((f32[256,512]{1,0:T(8,128)S(1)}, f32[256,512]{1,0:T(8,128)S(1)}, u32[]{:S(2)}, u32[]{:S(2)}) %collective-permute-start.10) | collective-permute-done | bytes 524320 | tf_op jit(solution)/shard_map/ppermute | solution.py:49
  72.6 4.4 %collective-permute-start.12 = (f32[256,512]{1,0:T(8,128)S(1)}, f32[256,512]{1,0:T(8,128)S(1)}, u32[]{:S(2)}, u32[]{:S(2)}) collective-permute-start(f32[256,512]{1,0:T(8,128)S(1)} %keep3.1.refs_3_.refs_1_), channel_id=1, source_target_pairs={{0,8},{4,12},{24,16},{28,20},{1,9},{5,13},{25,17},{29,21},{2,10},{... | collective-permute-start | bytes 1572872 | tf_op jit(solution)/shard_map/ppermute | solution.py:325
  79.0 1.3 collective-permute-start.15
  80.3 1.6 collective-permute-done.13.refs_5_
  82.0 1.5 collective-permute-start.19
  85.5 2.8 %collective-permute-start.18 = (f32[256,512]{1,0:T(8,128)S(1)}, f32[256,512]{1,0:T(8,128)S(1)}, u32[]{:S(2)}, u32[]{:S(2)}) collective-permute-start(f32[256,512]{1,0:T(8,128)S(1)} %keep4.1.refs_3_.refs_1_), channel_id=1, source_target_pairs={{0,8},{4,12},{24,16},{28,20},{1,9},{5,13},{25,17},{29,21},{2,10},{... | collective-permute-start | bytes 1572872 | tf_op jit(solution)/shard_map/ppermute | solution.py:325
  90.3 1.3 collective-permute-start.20
  91.6 4.0 %collective-permute-done.15.refs_4_.refs_2_ = f32[256,512]{1,0:T(8,128)S(1)} collective-permute-done((f32[256,512]{1,0:T(8,128)S(1)}, f32[256,512]{1,0:T(8,128)S(1)}, u32[]{:S(2)}, u32[]{:S(2)}) %collective-permute-start.15) | collective-permute-done | bytes 524320 | tf_op jit(solution)/shard_map/ppermute | solution.py:331
  97.4 2.6 %collective-permute-start.23 = (f32[256,512]{1,0:T(8,128)S(1)}, f32[256,512]{1,0:T(8,128)S(1)}, u32[]{:S(2)}, u32[]{:S(2)}) collective-permute-start(f32[256,512]{1,0:T(8,128)S(1)} %keep5.1.refs_3_.refs_1_), channel_id=1, source_target_pairs={{0,8},{4,12},{24,16},{28,20},{1,9},{5,13},{25,17},{29,21},{2,10},{... | collective-permute-start | bytes 1572872 | tf_op jit(solution)/shard_map/ppermute | solution.py:325
  101.9 1.3 collective-permute-start.24
  103.2 2.5 %collective-permute-done.20.refs_4_.refs_2_ = f32[256,512]{1,0:T(8,128)S(1)} collective-permute-done((f32[256,512]{1,0:T(8,128)S(1)}, f32[256,512]{1,0:T(8,128)S(1)}, u32[]{:S(2)}, u32[]{:S(2)}) %collective-permute-start.20) | collective-permute-done | bytes 524320 | tf_op jit(solution)/shard_map/ppermute | solution.py:331
  110.6 1.3 collective-permute-start.27
  111.9 4.9 %collective-permute-done.24.refs_4_.refs_2_ = f32[256,512]{1,0:T(8,128)S(1)} collective-permute-done((f32[256,512]{1,0:T(8,128)S(1)}, f32[256,512]{1,0:T(8,128)S(1)}, u32[]{:S(2)}, u32[]{:S(2)}) %collective-permute-start.24) | collective-permute-done | bytes 524320 | tf_op jit(solution)/shard_map/ppermute | solution.py:331
  118.8 3.5 %collective-permute-done.25.refs_3_.refs_5_ = f32[256,512]{1,0:T(8,128)S(1)} collective-permute-done((f32[256,512]{1,0:T(8,128)S(1)}, f32[256,512]{1,0:T(8,128)S(1)}, u32[]{:S(2)}, u32[]{:S(2)}) %collective-permute-start.25) | collective-permute-done | bytes 524320 | tf_op jit(solution)/shard_map/ppermute | solution.py:49
  122.3 4.9 %factor0.1 = (f32[512,512]{1,0:T(8,128)S(1)}, f32[512,512]{1,0:T(8,128)S(1)}) custom-call(s32[6]{0:T(128)S(1)} %stack.43.refs_0_, f32[512,512]{1,0:T(8,128)S(1)} %g6.1.refs_1_.refs_2_, f32[512,512]{1,0:T(8,128)S(1)} %g6.1.refs_1_.refs_2_, f32[256,512]{1,0:T(8,128)S(1)} %collective-permute-done.25.refs_3_.refs_5_), custom_call_target="tpu_custom_call" | custom-call | flops 1000 | bytes 1000 | tf_op jit(solution)/shard_map/factor0/pallas_call | solution.py:66
  127.8 1.3 collective-permute-start.28
  130.7 4.7 %factor1.1 = (f32[512,512]{1,0:T(8,128)S(1)}, f32[512,512]{1,0:T(8,128)S(1)}) custom-call(s32[6]{0:T(128)S(1)} %stack.43.refs_0_, f32[512,512]{1,0:T(8,128)S(1)} %get-tuple-element.71.refs_3_.refs_1_, f32[512,512]{1,0:T(8,128)S(1)} %get-tuple-element.72.refs_2_, f32[256,512]{1,0:T(8,128)S(1)} %ag3.1.refs_3_.refs_4_), custom_call_target="tpu_custom_call" | custom-call | flops 1000 | bytes 1000 | tf_op jit(solution)/shard_map/factor1/pallas_call | solution.py:66
  137.2 5.5 %collective-permute-done.28.refs_2_.refs_4_ = f32[256,512]{1,0:T(8,128)S(1)} collective-permute-done((f32[256,512]{1,0:T(8,128)S(1)}, f32[256,512]{1,0:T(8,128)S(1)}, u32[]{:S(2)}, u32[]{:S(2)}) %collective-permute-start.28) | collective-permute-done | bytes 524320 | tf_op jit(solution)/shard_map/ppermute | solution.py:331
  144.6 4.7 %factor2.1 = (f32[512,512]{1,0:T(8,128)S(1)}, f32[512,512]{1,0:T(8,128)S(1)}) custom-call(s32[6]{0:T(128)S(1)} %stack.43.refs_0_, f32[512,512]{1,0:T(8,128)S(1)} %get-tuple-element.73.refs_3_.refs_1_, f32[512,512]{1,0:T(8,128)S(1)} %get-tuple-element.74.refs_2_, f32[256,512]{1,0:T(8,128)S(1)} %ag5.1.refs_3_.refs_4_), custom_call_target="tpu_custom_call" | custom-call | flops 1000 | bytes 1000 | tf_op jit(solution)/shard_map/factor2/pallas_call | solution.py:66
  149.3 4.0 %factor3.1 = (f32[512,512]{1,0:T(8,128)S(1)}, f32[512,512]{1,0:T(8,128)S(1)}) custom-call(s32[6]{0:T(128)S(1)} %stack.43.refs_0_, f32[512,512]{1,0:T(8,128)S(1)} %get-tuple-element.75.refs_1_.refs_3_, f32[512,512]{1,0:T(8,128)S(1)} %get-tuple-element.76.refs_2_, f32[512,512]{1,0:T(8,128)S(1)} %get-tuple-element.75.refs_1_.refs_3_), custom_call_target="tpu_custom_call" | custom-call | flops 1000 | bytes 1000 | tf_op jit(solution)/shard_map/factor3/pallas_call | solution.py:66
  153.4 2.6 %weights.1 = (bf16[576,512]{1,0:T(8,128)(2,1)S(1)}, bf16[576,512]{1,0:T(8,128)(2,1)S(1)}) custom-call(s32[6]{0:T(128)S(1)} %stack.43.refs_0_, f32[512,512]{1,0:T(8,128)S(1)} %get-tuple-element.52.refs_7_.refs_1_, f32[512,512]{1,0:T(8,128)S(1)} %get-tuple-element.77.refs_2_, f32[512,512]{1,0:T(8,128)S(1)} %get-tuple-element.78.refs_3_, ...), custom_call_target="tpu_custom_call" | custom-call | flops 1000 | bytes 1000 | tf_op jit(solution)/shard_map/weights/pallas_call | solution.py:66
  156.0 1.2 fin0.1
  157.2 1.6 fin1.1
  158.8 1.6 fin2.1
  160.4 1.6 fin3.1
  162.1 1.6 fin4.1
  163.7 3.1 %collective-permute-done.32.refs_5_ = f32[256,512]{1,0:T(8,128)S(1)} collective-permute-done((f32[256,512]{1,0:T(8,128)S(1)}, f32[256,512]{1,0:T(8,128)S(1)}, u32[]{:S(2)}, u32[]{:S(2)}) %collective-permute-start.32) | collective-permute-done | bytes 524320 | tf_op jit(solution)/shard_map/ppermute | solution.py:49
  166.8 1.6 fin5.1
  168.5 3.1 %tiles_to_rows.1 = (f32[11264,128]{1,0:T(8,128)}, f32[1408,128]{1,0:T(8,128)}) custom-call(f32[512,256]{1,0:T(8,128)S(1)} %get-tuple-element.81.refs_6_.refs_0_, f32[512,512]{1,0:T(8,128)S(1)} %get-tuple-element.83.refs_6_.refs_1_, f32[512,512]{1,0:T(8,128)S(1)} %get-tuple-element.85.refs_6_.refs_2_, f32[512,512]{1,0:T(8,128)S(1)} %get-tuple-element.87.refs_6_.refs_3_, ...), custom_call_target="tpu_custom_call" | custom-call | tf_op jit(solution)/shard_map/tiles_to_rows/pallas_call | solution.py:272
  (70 shorter events, 36.3 us)
Async XLA Ops:
  2.1 16.0 %collective-permute-start = (f32[512,256]{1,0:T(8,128)S(1)}, f32[512,256]{1,0:T(8,128)S(1)}, u32[]{:S(2)}, u32[]{:S(2)}) collective-permute-start(f32[512,256]{1,0:T(8,128)S(1)} %bitcast.13), channel_id=1, source_target_pairs={{0,2},{1,3},{4,6},{5,7},{8,10},{9,11},{12,14},{13,15},{16,18},{17,... | collective-permute-start | bytes 1572872 | tf_op jit(solution)/shard_map/ppermute | solution.py:307
  7.1 2.6 %copy-start = (f32[512,11,1,256]{3,2,1,0:T(1,128)S(1)}, f32[512,11,1,256]{3,2,1,0:T(1,128)}, u32[]{:S(2)}) copy-start(f32[512,11,1,256]{3,2,1,0:T(1,128)} %param.1) | copy-start | bytes 17301508
  18.7 2.0 %collective-permute-start.1 = (f32[512,256]{1,0:T(8,128)S(1)}, f32[512,256]{1,0:T(8,128)S(1)}, u32[]{:S(2)}, u32[]{:S(2)}) collective-permute-start(f32[512,256]{1,0:T(8,128)S(1)} %pick.1.refs_1_.refs_3_.refs_6_.refs_7_), channel_id=1, source_target_pairs={{0,1},{1,0},{2,3},{3,2},{4,5},{5,4},{6,7},{7,6},{8,9},{9,8},{10,11... | collective-permute-start | bytes 1572872 | tf_op jit(solution)/shard_map/ppermute | solution.py:49
  23.0 14.8 %collective-permute-start.2 = (f32[256,512]{1,0:T(8,128)S(1)}, f32[256,512]{1,0:T(8,128)S(1)}, u32[]{:S(2)}, u32[]{:S(2)}) collective-permute-start(f32[256,512]{1,0:T(8,128)S(1)} %send0.1.refs_5_), channel_id=1, source_target_pairs={{0,4},{4,0},{8,12},{12,8},{16,20},{20,16},{24,28},{28,24},{1,5},{5... | collective-permute-start | bytes 1572872 | tf_op jit(solution)/shard_map/ppermute | solution.py:49
  25.7 23.4 %collective-permute-start.4 = (f32[256,512]{1,0:T(8,128)S(1)}, f32[256,512]{1,0:T(8,128)S(1)}, u32[]{:S(2)}, u32[]{:S(2)}) collective-permute-start(f32[256,512]{1,0:T(8,128)S(1)} %send1.1.refs_5_), channel_id=1, source_target_pairs={{0,4},{4,0},{8,12},{12,8},{16,20},{20,16},{24,28},{28,24},{1,5},{5... | collective-permute-start | bytes 1572872 | tf_op jit(solution)/shard_map/ppermute | solution.py:49
  39.2 14.5 %collective-permute-start.3 = (f32[256,512]{1,0:T(8,128)S(1)}, f32[256,512]{1,0:T(8,128)S(1)}, u32[]{:S(2)}, u32[]{:S(2)}) collective-permute-start(f32[256,512]{1,0:T(8,128)S(1)} %keep0.1.refs_5_.refs_1_), channel_id=1, source_target_pairs={{0,8},{4,12},{24,16},{28,20},{1,9},{5,13},{25,17},{29,21},{2,10},{... | collective-permute-start | bytes 1572872 | tf_op jit(solution)/shard_map/ppermute | solution.py:325
  42.7 17.6 %collective-permute-start.7 = (f32[256,512]{1,0:T(8,128)S(1)}, f32[256,512]{1,0:T(8,128)S(1)}, u32[]{:S(2)}, u32[]{:S(2)}) collective-permute-start(f32[256,512]{1,0:T(8,128)S(1)} %send2.1.refs_5_), channel_id=1, source_target_pairs={{0,4},{4,0},{8,12},{12,8},{16,20},{20,16},{24,28},{28,24},{1,5},{5... | collective-permute-start | bytes 1572872 | tf_op jit(solution)/shard_map/ppermute | solution.py:49
  50.2 14.8 %collective-permute-start.6 = (f32[256,512]{1,0:T(8,128)S(1)}, f32[256,512]{1,0:T(8,128)S(1)}, u32[]{:S(2)}, u32[]{:S(2)}) collective-permute-start(f32[256,512]{1,0:T(8,128)S(1)} %keep1.1.refs_3_.refs_1_), channel_id=1, source_target_pairs={{0,8},{4,12},{24,16},{28,20},{1,9},{5,13},{25,17},{29,21},{2,10},{... | collective-permute-start | bytes 1572872 | tf_op jit(solution)/shard_map/ppermute | solution.py:325
  54.3 13.5 %collective-permute-start.5 = (f32[256,512]{1,0:T(8,128)S(1)}, f32[256,512]{1,0:T(8,128)S(1)}, u32[]{:S(2)}, u32[]{:S(2)}) collective-permute-start(f32[256,512]{1,0:T(8,128)S(1)} %zm0.1.refs_6_.refs_1_), channel_id=1, source_target_pairs={{8,16},{12,20},{16,8},{20,12},{9,17},{13,21},{17,9},{21,13},{10,18... | collective-permute-start | bytes 1572872 | tf_op jit(solution)/shard_map/ppermute | solution.py:328
  55.0 16.5 %collective-permute-start.10 = (f32[256,512]{1,0:T(8,128)S(1)}, f32[256,512]{1,0:T(8,128)S(1)}, u32[]{:S(2)}, u32[]{:S(2)}) collective-permute-start(f32[256,512]{1,0:T(8,128)S(1)} %send3.1.refs_8_), channel_id=1, source_target_pairs={{0,4},{4,0},{8,12},{12,8},{16,20},{20,16},{24,28},{28,24},{1,5},{5... | collective-permute-start | bytes 1572872 | tf_op jit(solution)/shard_map/ppermute | solution.py:49
  61.4 15.7 %collective-permute-start.9 = (f32[256,512]{1,0:T(8,128)S(1)}, f32[256,512]{1,0:T(8,128)S(1)}, u32[]{:S(2)}, u32[]{:S(2)}) collective-permute-start(f32[256,512]{1,0:T(8,128)S(1)} %keep2.1.refs_3_.refs_1_), channel_id=1, source_target_pairs={{0,8},{4,12},{24,16},{28,20},{1,9},{5,13},{25,17},{29,21},{2,10},{... | collective-permute-start | bytes 1572872 | tf_op jit(solution)/shard_map/ppermute | solution.py:325
  65.5 12.9 %collective-permute-start.14 = (f32[256,512]{1,0:T(8,128)S(1)}, f32[256,512]{1,0:T(8,128)S(1)}, u32[]{:S(2)}, u32[]{:S(2)}) collective-permute-start(f32[256,512]{1,0:T(8,128)S(1)} %zm1.1.refs_3_.refs_1_), channel_id=1, source_target_pairs={{8,16},{12,20},{16,8},{20,12},{9,17},{13,21},{17,9},{21,13},{10,18... | collective-permute-start | bytes 1572872 | tf_op jit(solution)/shard_map/ppermute | solution.py:328
  66.2 15.7 %collective-permute-start.13 = (f32[256,512]{1,0:T(8,128)S(1)}, f32[256,512]{1,0:T(8,128)S(1)}, u32[]{:S(2)}, u32[]{:S(2)}) collective-permute-start(f32[256,512]{1,0:T(8,128)S(1)} %send4.1.refs_5_), channel_id=1, source_target_pairs={{0,4},{4,0},{8,12},{12,8},{16,20},{20,16},{24,28},{28,24},{1,5},{5... | collective-permute-start | bytes 1572872 | tf_op jit(solution)/shard_map/ppermute | solution.py:49
  68.4 15.9 %collective-permute-start.8 = (f32[256,512]{1,0:T(8,128)S(1)}, f32[256,512]{1,0:T(8,128)S(1)}, u32[]{:S(2)}, u32[]{:S(2)}) collective-permute-start(f32[256,512]{1,0:T(8,128)S(1)} %zo0.1.refs_6_.refs_1_), channel_id=1, source_target_pairs={{8,0},{12,4},{16,24},{20,28},{9,1},{13,5},{17,25},{21,29},{10,2},{... | collective-permute-start | bytes 1572872 | tf_op jit(solution)/shard_map/ppermute | solution.py:331
  72.6 15.7 %collective-permute-start.12 = (f32[256,512]{1,0:T(8,128)S(1)}, f32[256,512]{1,0:T(8,128)S(1)}, u32[]{:S(2)}, u32[]{:S(2)}) collective-permute-start(f32[256,512]{1,0:T(8,128)S(1)} %keep3.1.refs_3_.refs_1_), channel_id=1, source_target_pairs={{0,8},{4,12},{24,16},{28,20},{1,9},{5,13},{25,17},{29,21},{2,10},{... | collective-permute-start | bytes 1572872 | tf_op jit(solution)/shard_map/ppermute | solution.py:325
  77.7 11.9 %collective-permute-start.11 = (f32[256,512]{1,0:T(8,128)S(1)}, f32[256,512]{1,0:T(8,128)S(1)}, u32[]{:S(2)}, u32[]{:S(2)}) collective-permute-start(f32[256,512]{1,0:T(8,128)S(1)} %zm2.1.refs_3_.refs_1_), channel_id=1, source_target_pairs={{8,16},{12,20},{16,8},{20,12},{9,17},{13,21},{17,9},{21,13},{10,18... | collective-permute-start | bytes 1572872 | tf_op jit(solution)/shard_map/ppermute | solution.py:328
  79.0 16.6 %collective-permute-start.15 = (f32[256,512]{1,0:T(8,128)S(1)}, f32[256,512]{1,0:T(8,128)S(1)}, u32[]{:S(2)}, u32[]{:S(2)}) collective-permute-start(f32[256,512]{1,0:T(8,128)S(1)} %zo1.1.refs_6_.refs_1_), channel_id=1, source_target_pairs={{8,0},{12,4},{16,24},{20,28},{9,1},{13,5},{17,25},{21,29},{10,2},{... | collective-permute-start | bytes 1572872 | tf_op jit(solution)/shard_map/ppermute | solution.py:331
  82.0 14.3 %collective-permute-start.19 = (f32[256,512]{1,0:T(8,128)S(1)}, f32[256,512]{1,0:T(8,128)S(1)}, u32[]{:S(2)}, u32[]{:S(2)}) collective-permute-start(f32[256,512]{1,0:T(8,128)S(1)} %send5.1.refs_6_), channel_id=1, source_target_pairs={{0,4},{4,0},{8,12},{12,8},{16,20},{20,16},{24,28},{28,24},{1,5},{5... | collective-permute-start | bytes 1572872 | tf_op jit(solution)/shard_map/ppermute | solution.py:49
  85.5 14.5 %collective-permute-start.18 = (f32[256,512]{1,0:T(8,128)S(1)}, f32[256,512]{1,0:T(8,128)S(1)}, u32[]{:S(2)}, u32[]{:S(2)}) collective-permute-start(f32[256,512]{1,0:T(8,128)S(1)} %keep4.1.refs_3_.refs_1_), channel_id=1, source_target_pairs={{0,8},{4,12},{24,16},{28,20},{1,9},{5,13},{25,17},{29,21},{2,10},{... | collective-permute-start | bytes 1572872 | tf_op jit(solution)/shard_map/ppermute | solution.py:325
  88.9 12.4 %collective-permute-start.17 = (f32[256,512]{1,0:T(8,128)S(1)}, f32[256,512]{1,0:T(8,128)S(1)}, u32[]{:S(2)}, u32[]{:S(2)}) collective-permute-start(f32[256,512]{1,0:T(8,128)S(1)} %zm3.1.refs_3_.refs_1_), channel_id=1, source_target_pairs={{8,16},{12,20},{16,8},{20,12},{9,17},{13,21},{17,9},{21,13},{10,18... | collective-permute-start | bytes 1572872 | tf_op jit(solution)/shard_map/ppermute | solution.py:328
  90.3 15.5 %collective-permute-start.20 = (f32[256,512]{1,0:T(8,128)S(1)}, f32[256,512]{1,0:T(8,128)S(1)}, u32[]{:S(2)}, u32[]{:S(2)}) collective-permute-start(f32[256,512]{1,0:T(8,128)S(1)} %zo2.1.refs_3_.refs_1_), channel_id=1, source_target_pairs={{8,0},{12,4},{16,24},{20,28},{9,1},{13,5},{17,25},{21,29},{10,2},{... | collective-permute-start | bytes 1572872 | tf_op jit(solution)/shard_map/ppermute | solution.py:331
  96.2 10.7 %collective-permute-start.16 = (f32[256,512]{1,0:T(8,128)S(1)}, f32[256,512]{1,0:T(8,128)S(1)}, u32[]{:S(2)}, u32[]{:S(2)}) collective-permute-start(f32[256,512]{1,0:T(8,128)S(1)} %ag0.1.refs_6_.refs_1_.refs_4_), channel_id=1, source_target_pairs={{0,4},{4,0},{8,12},{12,8},{16,20},{20,16},{24,28},{28,24},{1,5},{5... | collective-permute-start | bytes 1572872 | tf_op jit(solution)/shard_map/ppermute | solution.py:49
  97.4 11.3 %collective-permute-start.23 = (f32[256,512]{1,0:T(8,128)S(1)}, f32[256,512]{1,0:T(8,128)S(1)}, u32[]{:S(2)}, u32[]{:S(2)}) collective-permute-start(f32[256,512]{1,0:T(8,128)S(1)} %keep5.1.refs_3_.refs_1_), channel_id=1, source_target_pairs={{0,8},{4,12},{24,16},{28,20},{1,9},{5,13},{25,17},{29,21},{2,10},{... | collective-permute-start | bytes 1572872 | tf_op jit(solution)/shard_map/ppermute | solution.py:325
  100.6 9.4 %collective-permute-start.22 = (f32[256,512]{1,0:T(8,128)S(1)}, f32[256,512]{1,0:T(8,128)S(1)}, u32[]{:S(2)}, u32[]{:S(2)}) collective-permute-start(f32[256,512]{1,0:T(8,128)S(1)} %zm4.1.refs_3_.refs_1_), channel_id=1, source_target_pairs={{8,16},{12,20},{16,8},{20,12},{9,17},{13,21},{17,9},{21,13},{10,18... | collective-permute-start | bytes 1572872 | tf_op jit(solution)/shard_map/ppermute | solution.py:328
  101.9 14.9 %collective-permute-start.24 = (f32[256,512]{1,0:T(8,128)S(1)}, f32[256,512]{1,0:T(8,128)S(1)}, u32[]{:S(2)}, u32[]{:S(2)}) collective-permute-start(f32[256,512]{1,0:T(8,128)S(1)} %zo3.1.refs_3_.refs_1_), channel_id=1, source_target_pairs={{8,0},{12,4},{16,24},{20,28},{9,1},{13,5},{17,25},{21,29},{10,2},{... | collective-permute-start | bytes 1572872 | tf_op jit(solution)/shard_map/ppermute | solution.py:331
  107.5 10.7 %collective-permute-start.21 = (f32[512,256]{1,0:T(8,128)S(1)}, f32[512,256]{1,0:T(8,128)S(1)}, u32[]{:S(2)}, u32[]{:S(2)}) collective-permute-start(f32[512,256]{1,0:T(8,128)S(1)} %g4.1.refs_3_.refs_1_), channel_id=1, source_target_pairs={{0,1},{1,0},{2,3},{3,2},{4,5},{5,4},{6,7},{7,6},{8,9},{9,8},{10,11... | collective-permute-start | bytes 1572872 | tf_op jit(solution)/shard_map/ppermute | solution.py:49
  107.5 14.8 %collective-permute-start.25 = (f32[256,512]{1,0:T(8,128)S(1)}, f32[256,512]{1,0:T(8,128)S(1)}, u32[]{:S(2)}, u32[]{:S(2)}) collective-permute-start(f32[256,512]{1,0:T(8,128)S(1)} %ag1.1.refs_3_.refs_4_), channel_id=1, source_target_pairs={{0,4},{4,0},{8,12},{12,8},{16,20},{20,16},{24,28},{28,24},{1,5},{5... | collective-permute-start | bytes 1572872 | tf_op jit(solution)/shard_map/ppermute | solution.py:49
  109.3 17.9 %collective-permute-start.26 = (f32[256,512]{1,0:T(8,128)S(1)}, f32[256,512]{1,0:T(8,128)S(1)}, u32[]{:S(2)}, u32[]{:S(2)}) collective-permute-start(f32[256,512]{1,0:T(8,128)S(1)} %zm5.1.refs_3_.refs_1_), channel_id=1, source_target_pairs={{8,16},{12,20},{16,8},{20,12},{9,17},{13,21},{17,9},{21,13},{10,18... | collective-permute-start | bytes 1572872 | tf_op jit(solution)/shard_map/ppermute | solution.py:328
  110.6 18.5 %collective-permute-start.27 = (f32[256,512]{1,0:T(8,128)S(1)}, f32[256,512]{1,0:T(8,128)S(1)}, u32[]{:S(2)}, u32[]{:S(2)}) collective-permute-start(f32[256,512]{1,0:T(8,128)S(1)} %zo4.1.refs_3_.refs_1_), channel_id=1, source_target_pairs={{8,0},{12,4},{16,24},{20,28},{9,1},{13,5},{17,25},{21,29},{10,2},{... | collective-permute-start | bytes 1572872 | tf_op jit(solution)/shard_map/ppermute | solution.py:331
  117.6 17.9 %collective-permute-start.29 = (f32[256,512]{1,0:T(8,128)S(1)}, f32[256,512]{1,0:T(8,128)S(1)}, u32[]{:S(2)}, u32[]{:S(2)}) collective-permute-start(f32[256,512]{1,0:T(8,128)S(1)} %ag2.1.refs_3_.refs_4_), channel_id=1, source_target_pairs={{0,4},{4,0},{8,12},{12,8},{16,20},{20,16},{24,28},{28,24},{1,5},{5... | collective-permute-start | bytes 1572872 | tf_op jit(solution)/shard_map/ppermute | solution.py:49
  127.8 14.9 %collective-permute-start.28 = (f32[256,512]{1,0:T(8,128)S(1)}, f32[256,512]{1,0:T(8,128)S(1)}, u32[]{:S(2)}, u32[]{:S(2)}) collective-permute-start(f32[256,512]{1,0:T(8,128)S(1)} %zo5.1.refs_3_.refs_1_), channel_id=1, source_target_pairs={{8,0},{12,4},{16,24},{20,28},{9,1},{13,5},{17,25},{21,29},{10,2},{... | collective-permute-start | bytes 1572872 | tf_op jit(solution)/shard_map/ppermute | solution.py:331
  129.7 23.6 %collective-permute-start.30 = (f32[256,512]{1,0:T(8,128)S(1)}, f32[256,512]{1,0:T(8,128)S(1)}, u32[]{:S(2)}, u32[]{:S(2)}) collective-permute-start(f32[256,512]{1,0:T(8,128)S(1)} %ag3.1.refs_3_.refs_4_), channel_id=1, source_target_pairs={{0,4},{4,0},{8,12},{12,8},{16,20},{20,16},{24,28},{28,24},{1,5},{5... | collective-permute-start | bytes 1572872 | tf_op jit(solution)/shard_map/ppermute | solution.py:49
  136.1 26.0 %collective-permute-start.31 = (f32[256,512]{1,0:T(8,128)S(1)}, f32[256,512]{1,0:T(8,128)S(1)}, u32[]{:S(2)}, u32[]{:S(2)}) collective-permute-start(f32[256,512]{1,0:T(8,128)S(1)} %ag4.1.refs_3_.refs_4_), channel_id=1, source_target_pairs={{0,4},{4,0},{8,12},{12,8},{16,20},{20,16},{24,28},{28,24},{1,5},{5... | collective-permute-start | bytes 1572872 | tf_op jit(solution)/shard_map/ppermute | solution.py:49
  143.6 23.3 %collective-permute-start.32 = (f32[256,512]{1,0:T(8,128)S(1)}, f32[256,512]{1,0:T(8,128)S(1)}, u32[]{:S(2)}, u32[]{:S(2)}) collective-permute-start(f32[256,512]{1,0:T(8,128)S(1)} %ag5.1.refs_3_.refs_4_), channel_id=1, source_target_pairs={{0,4},{4,0},{8,12},{12,8},{16,20},{20,16},{24,28},{28,24},{1,5},{5... | collective-permute-start | bytes 1572872 | tf_op jit(solution)/shard_map/ppermute | solution.py:49

commit v4 on v3

--- a/solution.py
+++ b/solution.py
@@ -11,12 +11,15 @@
 f32 = jnp.float32
 bf16 = jnp.bfloat16
 TILE = 128
-SIZES = (1, 2, 2, 2, 2, 2)
+EXTRA = 32
+PIECES = 1
+GROUPS = (4, 1, 2, 2, 2)
+GROUP_OF = (0, 1, 0, 2, 3, 4)
 ORDER = (
-    "panels send0 send1 send2", "send3 keep0 send4 send5", "keep1 zm0 keep2 zm1", "zo0 keep3 zm2 zo1",
-    "~zo0 keep4 zm3 zo2", "~zo1 ag0 keep5 zm4", "zo3 ~zo2 ag1 g4", "zm5 zo4 ~zo3 ag2",
-    "g6 ~ag1 ch0 zo5", "~zo4 ag3 ch1 ~ag2", "ag4 ~zo5 ag5 ch2", "ch3 ~ag3 weights fin0",
-    "fin1 fin2 fin3 fin4", "fin5",
+    "ka pa send0 kb", "pb send1 send2 send3", "keep0 send4 send5 keep1", "zm0 keep2 zm1 zo0",
+    "keep3 zm2 zo1 ~zo0", "keep4 zm3 zo2 ~zo1", "ag0 keep5 zm4 zo3", "~zo2 ~ag0 ag1 zm5",
+    "zo4 ~zo3 ag2 g4", "~zo4 ag3 zo5 g6", "ch0 ~ag2 ag4 ch1", "~zo5 ag5 ch2 ch3",
+    "weights fin1 fin0 ~ag3", "fin3 ~ag4 fin4",
 )
 
 
@@ -60,20 +63,19 @@
         vmem = pl.BlockSpec(memory_space=pltpu.VMEM)
 
         def body(*refs):
-            skip = 1 + n_in
-            kernel(*refs[:skip], *refs[skip + n_after:])
+            kernel(refs[0], *refs[1 + n_after:])
 
         result = pl.pallas_call(
             body,
             out_shape=[jax.ShapeDtypeStruct(*(o if isinstance(o[0], tuple) else (o, f32))) for o in outs],
-            in_specs=[pl.BlockSpec(memory_space=pltpu.SMEM)] + [vmem] * n_in
-            + [pl.BlockSpec(memory_space=pl.ANY)] * n_after,
+            in_specs=[pl.BlockSpec(memory_space=pltpu.SMEM)] + [pl.BlockSpec(memory_space=pl.ANY)] * n_after
+            + [vmem] * n_in,
             out_specs=[vmem] * len(outs),
             scratch_shapes=list(scratch),
             name=name,
             compiler_params=pltpu.CompilerParams(vmem_limit_bytes=24 * 2**20),
             cost_estimate=pl.CostEstimate(flops=1000, bytes_accessed=1000, transcendentals=0),
-        )(flags, *operands, *after)
+        )(flags, *after, *operands)
         self.last = [result[0]]
         self.waits = []
         return result
@@ -91,46 +93,44 @@
             part += 1
 
 
-def pick_kernel(which, flags, a_ref, b_ref, out_ref):
-    @pl.when(flags[which] != 0)
-    def _():
-        out_ref[...] = a_ref[...]
-
-    @pl.when(flags[which] == 0)
-    def _():
-        out_ref[...] = b_ref[...]
-
-
-def panels_kernel(
-    flags, held_ref, other_ref, both_ref, keep_ref, send_ref, keep_high, keep_low, send_high, send_low
-):
-    width = held_ref.shape[1]
-    held, other = held_ref[...], other_ref[...]
-    low = flags[1] != 0
-    p0, p1 = jnp.where(low, held, other), jnp.where(low, other, held)
-    both_ref[:, :width] = p0
-    both_ref[:, width:] = p1
-    t0, t1 = p0.T, p1.T
-    first = flags[2] != 0
-    keep, send = jnp.where(first, t0, t1), jnp.where(first, t1, t0)
-    keep_ref[...], send_ref[...] = keep, send
-    keep_high[...], keep_low[...] = split(keep)
-    send_high[...], send_low[...] = split(send)
-
-
-def product_kernel(flags, panel_high, panel_low, a_high, a_low, *refs):
-    columns, out_ref = a_high.shape[1], refs[-1]
-    out_ref[:, :columns] = dot3((panel_high[...], panel_low[...]), (a_high[...], a_low[...]))
-    if len(refs) > 1:
-        out_ref[:, columns:] = dot(refs[0][...], refs[1][...])
-
-
-def product_add_kernel(flags, panel_high, panel_low, a_high, a_low, came_ref, *refs):
-    columns, out_ref = a_high.shape[1], refs[-1]
-    product = dot3((panel_high[...], panel_low[...]), (a_high[...], a_low[...]))
-    out_ref[:, :columns] = product + came_ref[:, :columns]
-    if len(refs) > 1:
-        out_ref[:, columns:] = dot(refs[0][...], refs[1][...]) + came_ref[:, columns:]
+def pick_kernel(which, flags, a_ref, b_ref, *out_refs):
+    for choice, ref in enumerate((b_ref, a_ref)):
+        @pl.when(flags[which] == choice)
+        def _():
+            at = 0
+            for out_ref in out_refs:
+                out_ref[...] = ref[at:at + out_ref.shape[0]]
+                at += out_ref.shape[0]
+
+
+def half_panels_kernel(flags, *refs):
+    pieces, (keep_high, keep_low, send_high, send_low) = refs[:-4], refs[-4:]
+    count = len(pieces) // 2
+    held, other = (jnp.concatenate([r[...] for r in part], 0).T for part in (pieces[:count], pieces[count:]))
+    same = flags[1] == flags[2]
+    keep_high[...], keep_low[...] = split(jnp.where(same, held, other))
+    send_high[...], send_low[...] = split(jnp.where(same, other, held))
+
+
+def joined(refs):
+    later = [jnp.concatenate([r[...] for r in part], 0) for part in (refs[2:2 + PIECES], refs[2 + PIECES:])]
+    return [jnp.concatenate([r[...], v], 1) for r, v in zip(refs, later)]
+
+
+def product_kernel(count, kept, flags, *refs):
+    highs, lows, (a_high, a_low) = refs[:count], refs[count:2 * count], refs[2 * count:2 * count + 2]
+    rest, out_ref = refs[2 * count + 2:-1], refs[-1]
+    columns = a_high.shape[1]
+    came = rest[0][...] if kept else None
+    panel = [jnp.concatenate([r[...] for r in part], 0) for part in (highs, lows)]
+    product = dot3(panel, (a_high[...], a_low[...]))
+    out_ref[:, :columns] = product + came[:, :columns] if kept else product
+    halves = rest[1 if kept else 0:]
+    if halves:
+        held, other = joined(halves)
+        mine = (flags[1] == flags[2]) == kept
+        product = dot_t(jnp.where(mine, held, other), held)
+        out_ref[:, columns:] = product + came[:, columns:] if kept else product
 
 
 def share_kernel(flags, keep_ref, other_ref, out_ref):
@@ -220,13 +220,16 @@
         out_inv_ref[hi:, :hi] = out_inv_ref[hi:, :hi] - dot(below, done)
 
 
-def weights_kernel(flags, both_ref, inv_ref, high_ref, low_ref):
-    rows = both_ref.shape[0]
-    width = both_ref.shape[1] // 2
+def weights_kernel(flags, *refs):
+    inv_ref, high_ref, low_ref = refs[-3:]
+    held, other = joined(refs[:-3])
+    rows, width = held.shape
+    low_core = flags[1] != 0
+    panels = jnp.concatenate([jnp.where(low_core, held, other), jnp.where(low_core, other, held)], 1)
     per_device = high_ref.shape[0] - rows
     inverse = inv_ref[...]
     high, low = split(inverse)
-    ortho = split(dot3(split(both_ref[...]), split(inverse.T)))
+    ortho = split(dot3(split(panels), split(inverse.T)))
     first = flags[2] != 0
     mine = inv_ref[pl.ds(pl.multiple_of(flags[5] * per_device, 8), per_device), :]
 
@@ -239,17 +242,32 @@
     put(slice(rows, rows + per_device), mine[:, :width], mine[:, width:])
 
 
-def finish_kernel(flags, a_ref, high_ref, low_ref, first_ref, second_ref, rest_ref, factor_ref):
+def finish_kernel(flags, a_ref, high_ref, low_ref, *refs):
+    (rest_ref, factor_ref), sums = refs[-2:], refs[:-2]
     rows, columns = a_ref.shape
-    width = first_ref.shape[0]
-    change = dot3((high_ref[:, :width], low_ref[:, :width]), split(first_ref[:, :columns]))
-    change += dot3((high_ref[:, width:], low_ref[:, width:]), split(second_ref[:, :columns]))
+    count = len(sums) // 2
+    first, second = (
+        split(jnp.concatenate([r[:, :columns] for r in part], 0)) for part in (sums[:count], sums[count:])
+    )
+    width = first[0].shape[0]
+    change = dot3((high_ref[:, :width], low_ref[:, :width]), first)
+    change += dot3((high_ref[:, width:], low_ref[:, width:]), second)
     rest_ref[...] = a_ref[...] - change[:rows]
     factor_ref[...] = change[rows:]
 
 
-def rows_kernel(parts, n, *refs):
-    rests, factors, (rest_ref, factor_ref) = refs[:n], refs[n:2 * n], refs[2 * n:]
+def rows_kernel(parts, n, a_ref, high_ref, low_ref, mine_high, mine_low, first_ref, second_ref, *refs):
+    rests, factors, (rest_ref, factor_ref, *sums) = refs[:n], refs[n:2 * n], refs[2 * n:]
+    width = first_ref.shape[0]
+
+    @pl.when(pl.program_id(0) == 0)
+    def _():
+        sums[0][...], sums[1][...] = split(first_ref[...])
+        sums[2][...], sums[3][...] = split(second_ref[...])
+
+    def update(high, low):
+        change = dot3((high[:, :width], low[:, :width]), (sums[0][...], sums[1][...]))
+        return change + dot3((high[:, width:], low[:, width:]), (sums[2][...], sums[3][...]))
 
     def lay(pieces, out_ref):
         part = 0
@@ -259,16 +277,19 @@
                 out_ref[pl.ds(part, rows, stride=parts), :] = piece[:, at:at + TILE]
                 part += 1
 
-    lay(rests, rest_ref)
+    lay([*rests, a_ref[...] - update(high_ref, low_ref)], rest_ref)
 
     @pl.when(pl.program_id(0) == 0)
     def _():
-        lay(factors, factor_ref)
-
-
-def in_rows(rests, factors, parts):
-    rows, own_rows = rests[0].shape[0], factors[0].shape[0]
+        lay([*factors, update(mine_high, mine_low)], factor_ref)
+
+
+def in_rows(last, weights, first, second, rests, factors, parts):
+    rows, own_rows = last.shape[0], factors[0].shape[0]
     step = min(rows, 128)
+    by_rows = lambda v: pl.BlockSpec((step, v.shape[1]), lambda i: (i, 0))
+    whole = lambda v: pl.BlockSpec(v.shape, lambda i: (0, 0))
+    mine = pl.BlockSpec((own_rows, weights[0].shape[1]), lambda i: (rows // own_rows, 0))
     return pl.pallas_call(
         functools.partial(rows_kernel, parts, len(rests)),
         grid=(rows // step,),
@@ -276,15 +297,16 @@
             jax.ShapeDtypeStruct((rows * parts, TILE), f32),
             jax.ShapeDtypeStruct((own_rows * parts, TILE), f32),
         ],
-        in_specs=[pl.BlockSpec((step, v.shape[1]), lambda i: (i, 0)) for v in rests]
-        + [pl.BlockSpec(v.shape, lambda i: (0, 0)) for v in factors],
+        in_specs=[by_rows(last), by_rows(weights[0]), by_rows(weights[1]), mine, mine, whole(first), whole(second)]
+        + [by_rows(v) for v in rests] + [whole(v) for v in factors],
         out_specs=[
             pl.BlockSpec((step * parts, TILE), lambda i: (i, 0)),
             pl.BlockSpec((own_rows * parts, TILE), lambda i: (0, 0)),
         ],
+        scratch_shapes=[pltpu.VMEM(first.shape, bf16)] * 4,
         name="tiles_to_rows",
         compiler_params=pltpu.CompilerParams(vmem_limit_bytes=24 * 2**20),
-    )(*rests, *factors)
+    )(last, *weights, *weights, first, second, *rests, *factors)
 
 
 def local(matrix):
@@ -295,29 +317,35 @@
     row, col = lax.axis_index("prow"), lax.axis_index("pcol")
     place = row // 2
     line = n_row == 8
-    sizes = SIZES if sum(SIZES) == blocks else (blocks,)
     flags = jnp.stack([
         col >= 2, col % 2 == 0, row % 2 == 0, (place == 1) | (place == 2), col, row,
     ]).astype(jnp.int32)
     chain = Chain()
     flat = matrix.reshape(rows * parts, TILE)
 
-    held = matrix[:, 0, 0, :]
-    reach = 2
-    came = lax.ppermute(held, "pcol", [(0, 2), (1, 3)]) if n_col > 2 else held
+    own = [matrix[:, 0, 0, :width // 2], matrix[:, 0, 0, width // 2:]]
+    own[1] = jnp.concatenate([own[1], own[1][:EXTRA]], 0)
+    came = [lax.ppermute(v, "pcol", [(0, 2), (1, 3)]) for v in own]
     shapes = []
-    for count in sizes:
+    for count in GROUPS:
         shape = (rows, count * width)
         shapes += [shape, (shape, bf16), (shape, bf16)]
     cuts = chain(functools.partial(spread_kernel, parts), "rows_to_tiles", shapes, flags, flat)
-    cuts = [cuts[3 * k:3 * k + 3] for k in range(len(sizes))]
-    held, = chain(functools.partial(pick_kernel, 0), "pick", [held.shape], flags, came, held)
-    reach = 4
-    while reach < n_col:
-        came = lax.ppermute(held, "pcol", [(i, i + reach) for i in range(reach) if i + reach < n_col])
-        held = jnp.where((col >= reach) & (col < 2 * reach), came, held)
-        reach *= 2
-    beside = flip(held, "pcol", 1)
+    cuts = [cuts[3 * k:3 * k + 3] for k in range(len(GROUPS))]
+
+    def bring(which, name):
+        pieces = (1, PIECES)[which]
+        held = chain(
+            functools.partial(pick_kernel, 0), name, [(rows // pieces, width // 2)] * pieces, flags,
+            came[which], own[which],
+        )
+        reach = 4
+        while reach < n_col:
+            pairs = [(i, i + reach) for i in range(reach) if i + reach < n_col]
+            at = (col >= reach) & (col < 2 * reach)
+            held = [jnp.where(at, lax.ppermute(v, "pcol", pairs), v) for v in held]
+            reach *= 2
+        return [*held, *[flip(v, "pcol", 1) for v in held]]
 
     state = {}
 
@@ -345,14 +373,13 @@
         return chain(functools.partial(pick_kernel, 3), name, [a.shape], flags, a, b)[0]
 
     def run(task):
-        if task == "panels":
-            cut = (width, rows)
-            both, keep, send, *parted = chain(
-                panels_kernel, task, [(rows, depth), cut, cut] + [(cut, bf16)] * 4, flags, held, beside
-            )
-            state.update(both=both, keep=parted[:2], send=parted[2:], keep_more=[keep, held], send_more=[send, held])
+        if task == "ka" or task == "kb":
+            state[task] = bring("ab".index(task[1]), task)
+        elif task == "pa" or task == "pb":
+            half = ((width // 2, rows), bf16)
+            state[task] = chain(half_panels_kernel, task, [half] * 4, flags, *state["k" + task[1]])
         elif task == "g4":
-            share, = chain(share_kernel, task, [(depth, width)], flags, state["s", 0], state["r", 0])
+            share, = chain(share_kernel, task, [(depth, width)], flags, state["s", 1], state["r", 1])
             state["gr"] = share, flip(share, "pcol", 1)
         elif task == "g6":
             state["gram"], = chain(gather_kernel, task, [(depth, depth)], flags, *state["gr"])
@@ -365,20 +392,23 @@
             )
         elif task == "weights":
             cut = ((rows + depth // n_row, depth), bf16)
-            state["weights"] = chain(weights_kernel, task, [cut] * 2, flags, state["both"], state["factor"][1])
+            state["weights"] = chain(weights_kernel, task, [cut] * 2, flags, *state["ka"], *state["kb"], state["factor"][1])
         else:
             kind, k = task.rstrip("0123456789"), int(task.lstrip("abcdefghijklmnopqrstuvwxyz"))
-            if k >= len(sizes):
-                return
-            count = (sizes[k] + (k == 0)) * width
+            group = GROUP_OF[k]
+            lines = width if GROUP_OF.count(group) == 1 else width // 2
+            halves = [state[p] for p in (("pa",), ("pa", "pb"), ("pb",))[min(k, 1) if k != 2 else 2]]
+            shape = (lines, GROUPS[group] * width + (k == 1) * width)
+            more = [*state["ka"], *state["kb"]] if k == 1 else []
             if kind == "send":
-                more = state["send_more"] if k == 0 else []
-                out, = chain(product_kernel, task, [(width, count)], flags, *state["send"], *cuts[k][1:], *more)
+                pieces = [p[2] for p in halves] + [p[3] for p in halves]
+                out, = chain(functools.partial(product_kernel, len(halves), False), task, [shape],
+                             flags, *pieces, *cuts[group][1:], *more)
                 state["r", k] = flip(out, "prow", 1)
             elif kind == "keep":
-                more = state["keep_more"] if k == 0 else []
-                out, = chain(product_add_kernel, task, [(width, count)],
-                             flags, *state["keep"], *cuts[k][1:], state["r", k], *more)
+                pieces = [p[0] for p in halves] + [p[1] for p in halves]
+                out, = chain(functools.partial(product_kernel, len(halves), True), task, [shape],
+                             flags, *pieces, *cuts[group][1:], state["r", k], *more)
                 state["s", k], state["r", k] = out, in_hop(out)
             elif kind == "zm":
                 out = add(task, state["s", k], state["r", k])
@@ -390,9 +420,11 @@
                 out = pick_inner(task, state["s", k], state["r", k])
                 state["s", k], state["r", k] = out, flip(out, "prow", 1)
             elif kind == "fin":
-                state["out", k] = chain(
-                    finish_kernel, task, [(rows, sizes[k] * width), (depth // n_row, sizes[k] * width)],
-                    flags, cuts[k][0], *state["weights"], state["s", k], state["r", k],
+                pieces = [j for j, g in enumerate(GROUP_OF) if g == group]
+                state["out", group] = chain(
+                    finish_kernel, task, [(rows, GROUPS[group] * width), (depth // n_row, GROUPS[group] * width)],
+                    flags, cuts[group][0], *state["weights"],
+                    *[state["s", j] for j in pieces], *[state["r", j] for j in pieces],
                 )
 
     for task in " ".join(ORDER).split():
@@ -400,8 +432,13 @@
             run(task)
         elif line and ("r", int(task[-1])) in state:
             chain.waits.append(state["r", int(task[-1])])
-    outs = [state["out", k] for k in range(len(sizes))]
-    rest, factor = in_rows([o[0] for o in outs], [o[1] for o in outs], parts)
+    end = len(GROUPS) - 1
+    outs = [state["out", k] for k in range(end)]
+    k = GROUP_OF.index(end)
+    rest, factor = in_rows(
+        cuts[end][0], state["weights"], state["s", k], state["r", k],
+        [o[0] for o in outs], [o[1] for o in outs], parts,
+    )
     return (
         factor.reshape(depth // n_row, blocks, 1, width),
         rest.reshape(rows, blocks, 1, width),

time: 172 us -> 170 us (0.988)
  waiting for transfers between devices: 52.2 us -> 42.8 us
  starting transfers between devices: 50.6 us -> 57.4 us
    ppermute x14 -> x15, waiting for transfers between devices: 28.2 us -> 18.5 us  [flip(): return lax.ppermute(value, axis, [(i, i ^ bit) for i in range(n)])]
    ppermute x1 -> x2, starting transfers between devices: 4.88 us -> 9.26 us  [local(): came = [lax.ppermute(v, 'pcol', [(0, 2), (1, 3)]) for v in own]]
    ppermute x6, waiting for transfers between devices: 17.9 us -> 20.7 us  [out_hop(): lax.ppermute(value, 'prow', [(2, 0), (3, 1), (4, 6), (5, 7)])]
    ppermute x1 -> x2, waiting for transfers between devices: 6 us -> 3.27 us  [local(): came = [lax.ppermute(v, 'pcol', [(0, 2), (1, 3)]) for v in own]]
    ppermute x14 -> x15, starting transfers between devices: 13.4 us -> 14.8 us  [flip(): return lax.ppermute(value, axis, [(i, i ^ bit) for i in range(n)])]
  transfers between devices with their start and end apart: 33 -> 35, of which waited for: 16 -> 16; matrix products, arithmetic and copies ran while one was open for 0% -> 0% of each run, Pallas kernels for 32% -> 35%
where the time goes in v4:
time: 170 us
  Pallas kernels  63.6 us (37%)
  starting transfers between devices  57.4 us (34%)
  waiting for transfers between devices  42.8 us (25%)
  local copies, waits for them, and re-layouts  4.53 us (3%)
    pallas_call x46, Pallas kernels, __call__(): pl.pallas_call(body, out_shape=[jax.ShapeDtypeStruct(*(o if isinstance(o[...  59.4 us
    ppermute x6, starting transfers between devices, in_hop(): lax.ppermute(value, 'prow', [(0, 2), (1, 3), (6, 4), (7, 5)])  21.4 us
    ppermute x6, waiting for transfers between devices, out_hop(): lax.ppermute(value, 'prow', [(2, 0), (3, 1), (4, 6), (5, 7)])  20.7 us
    ppermute x15, waiting for transfers between devices, flip(): return lax.ppermute(value, axis, [(i, i ^ bit) for i in range(n)])  18.5 us
    ppermute x15, starting transfers between devices, flip(): return lax.ppermute(value, axis, [(i, i ^ bit) for i in range(n)])  14.8 us
    ppermute x2, starting transfers between devices, local(): came = [lax.ppermute(v, 'pcol', [(0, 2), (1, 3)]) for v in own]  9.26 us
    ppermute x6, starting transfers between devices, out_hop(): lax.ppermute(value, 'prow', [(2, 0), (3, 1), (4, 6), (5, 7)])  7.75 us
    pallas_call x1, Pallas kernels, in_rows(): pl.pallas_call(functools.partial(rows_kernel, parts, len(rests)), grid=(r...  4.22 us
  transfers between devices with their start and end apart: 35, of which 16 were waited for; matrix products, arithmetic and copies ran while one was open for 0% of the time, Pallas kernels for 35%

profile of v4, /device:TPU:0, one launch (start us, length us, event | category | flops | bytes accessed | tf_op | source)
XLA Modules:
  0.0 169.8 jit_solution(15495106273961898408)
XLA Ops:
  1.7 4.9 %collective-permute-start = (f32[512,128]{1,0:T(8,128)S(1)}, f32[512,128]{1,0:T(8,128)S(1)}, u32[]{:S(2)}, u32[]{:S(2)}) collective-permute-start(f32[512,128]{1,0:T(8,128)S(1)} %bitcast.19), channel_id=1, source_target_pairs={{0,2},{1,3},{4,6},{5,7},{8,10},{9,11},{12,14},{13,15},{16,18},{17,... | collective-permute-start | bytes 786440 | tf_op jit(solution)/shard_map/ppermute | solution.py:328
  6.7 2.6 %copy-done = f32[512,11,1,256]{3,2,1,0:T(1,128)S(1)} copy-done((f32[512,11,1,256]{3,2,1,0:T(1,128)S(1)}, f32[512,11,1,256]{3,2,1,0:T(1,128)}, u32[]{:S(2)}) %copy-start) | copy-done | bytes 5767192
  9.3 2.5 %rows_to_tiles.1 = (f32[512,1024]{1,0:T(8,128)S(1)}, bf16[512,1024]{1,0:T(8,128)(2,1)S(1)}, bf16[512,1024]{1,0:T(8,128)(2,1)S(1)}, f32[512,256]{1,0:T(8,128)S(1)...) custom-call(s32[6]{0:T(128)S(1)} %stack.43.refs_0_, ...), custom_call_target="tpu_custom_call" | custom-call | flops 1000 | bytes 1000 | tf_op jit(solution)/shard_map/rows_to_tiles/pallas_call | solution.py:68
  13.5 4.4 %collective-permute-start.2 = (f32[544,128]{1,0:T(8,128)S(1)}, f32[544,128]{1,0:T(8,128)S(1)}, u32[]{:S(2)}, u32[]{:S(2)}) collective-permute-start(f32[544,128]{1,0:T(8,128)S(1)} %pad_maximum_fusion.refs_3_), channel_id=1, source_target_pairs={{0,2},{1,3},{4,6},{5,7},{8,10},{9,11},{12,14},{13,15},{16,18},{17,... | collective-permute-start | bytes 835592 | tf_op jit(solution)/shard_map/ppermute | solution.py:328
  19.8 1.6 collective-permute-start.4
  21.4 3.0 %collective-permute-done.2.refs_2_ = f32[544,128]{1,0:T(8,128)S(1)} collective-permute-done((f32[544,128]{1,0:T(8,128)S(1)}, f32[544,128]{1,0:T(8,128)S(1)}, u32[]{:S(2)}, u32[]{:S(2)}) %collective-permute-start.2) | collective-permute-done | bytes 278560 | tf_op jit(solution)/shard_map/ppermute | solution.py:328
  25.1 1.5 collective-permute-done.3.refs_3_.refs_11_.refs_12_.refs_5_
  27.4 1.4 send1.1.refs_1_
  28.8 1.6 collective-permute-start.5
  32.6 2.0 %collective-permute-done.4.refs_6_ = f32[128,1024]{1,0:T(8,128)S(1)} collective-permute-done((f32[128,1024]{1,0:T(8,128)S(1)}, f32[128,1024]{1,0:T(8,128)S(1)}, u32[]{:S(2)}, u32[]{:S(2)}) %collective-permute-start.4) | collective-permute-done | bytes 524320 | tf_op jit(solution)/shard_map/ppermute | solution.py:52
  35.8 3.5 %collective-permute-start.6 = (f32[128,1024]{1,0:T(8,128)S(1)}, f32[128,1024]{1,0:T(8,128)S(1)}, u32[]{:S(2)}, u32[]{:S(2)}) collective-permute-start(f32[128,1024]{1,0:T(8,128)S(1)} %keep0.1.refs_1_.refs_2_), channel_id=1, source_target_pairs={{0,8},{4,12},{24,16},{28,20},{1,9},{5,13},{25,17},{29,21},{2,10},{... | collective-permute-start | bytes 1572872 | tf_op jit(solution)/shard_map/ppermute | solution.py:353
  39.3 1.6 collective-permute-start.7
  43.1 2.8 %collective-permute-done.5.refs_8_ = f32[256,512]{1,0:T(8,128)S(1)} collective-permute-done((f32[256,512]{1,0:T(8,128)S(1)}, f32[256,512]{1,0:T(8,128)S(1)}, u32[]{:S(2)}, u32[]{:S(2)}) %collective-permute-start.5) | collective-permute-done | bytes 524320 | tf_op jit(solution)/shard_map/ppermute | solution.py:52
  45.9 1.4 keep1.1.refs_1_.refs_2_
  47.3 3.5 %collective-permute-start.8 = (f32[256,512]{1,0:T(8,128)S(1)}, f32[256,512]{1,0:T(8,128)S(1)}, u32[]{:S(2)}, u32[]{:S(2)}) collective-permute-start(f32[256,512]{1,0:T(8,128)S(1)} %keep1.1.refs_1_.refs_2_), channel_id=1, source_target_pairs={{0,8},{4,12},{24,16},{28,20},{1,9},{5,13},{25,17},{29,21},{2,10},{... | collective-permute-start | bytes 1572872 | tf_op jit(solution)/shard_map/ppermute | solution.py:353
  52.1 1.6 collective-permute-start.10
  53.7 3.4 %collective-permute-done.7.refs_6_ = f32[128,1024]{1,0:T(8,128)S(1)} collective-permute-done((f32[128,1024]{1,0:T(8,128)S(1)}, f32[128,1024]{1,0:T(8,128)S(1)}, u32[]{:S(2)}, u32[]{:S(2)}) %collective-permute-start.7) | collective-permute-done | bytes 524320 | tf_op jit(solution)/shard_map/ppermute | solution.py:52
  58.3 3.5 %collective-permute-start.11 = (f32[128,1024]{1,0:T(8,128)S(1)}, f32[128,1024]{1,0:T(8,128)S(1)}, u32[]{:S(2)}, u32[]{:S(2)}) collective-permute-start(f32[128,1024]{1,0:T(8,128)S(1)} %keep2.1.refs_1_.refs_2_), channel_id=1, source_target_pairs={{0,8},{4,12},{24,16},{28,20},{1,9},{5,13},{25,17},{29,21},{2,10},{... | collective-permute-start | bytes 1572872 | tf_op jit(solution)/shard_map/ppermute | solution.py:353
  63.1 1.6 collective-permute-start.14
  65.3 1.3 collective-permute-start.13
  66.6 1.8 %collective-permute-done.10.refs_8_ = f32[256,512]{1,0:T(8,128)S(1)} collective-permute-done((f32[256,512]{1,0:T(8,128)S(1)}, f32[256,512]{1,0:T(8,128)S(1)}, u32[]{:S(2)}, u32[]{:S(2)}) %collective-permute-start.10) | collective-permute-done | bytes 524320 | tf_op jit(solution)/shard_map/ppermute | solution.py:52
  69.5 4.7 %collective-permute-start.15 = (f32[256,512]{1,0:T(8,128)S(1)}, f32[256,512]{1,0:T(8,128)S(1)}, u32[]{:S(2)}, u32[]{:S(2)}) collective-permute-start(f32[256,512]{1,0:T(8,128)S(1)} %keep3.1.refs_1_.refs_2_), channel_id=1, source_target_pairs={{0,8},{4,12},{24,16},{28,20},{1,9},{5,13},{25,17},{29,21},{2,10},{... | collective-permute-start | bytes 1572872 | tf_op jit(solution)/shard_map/ppermute | solution.py:353
  76.1 1.3 collective-permute-start.17
  77.4 1.5 collective-permute-done.14.refs_9_
  78.9 1.5 collective-permute-start.18
  82.3 3.2 %collective-permute-start.19 = (f32[256,512]{1,0:T(8,128)S(1)}, f32[256,512]{1,0:T(8,128)S(1)}, u32[]{:S(2)}, u32[]{:S(2)}) collective-permute-start(f32[256,512]{1,0:T(8,128)S(1)} %keep4.1.refs_1_.refs_2_), channel_id=1, source_target_pairs={{0,8},{4,12},{24,16},{28,20},{1,9},{5,13},{25,17},{29,21},{2,10},{... | collective-permute-start | bytes 1572872 | tf_op jit(solution)/shard_map/ppermute | solution.py:353
  87.4 1.3 collective-permute-start.21
  88.7 3.7 %collective-permute-done.17.refs_2_.refs_5_ = f32[256,512]{1,0:T(8,128)S(1)} collective-permute-done((f32[256,512]{1,0:T(8,128)S(1)}, f32[256,512]{1,0:T(8,128)S(1)}, u32[]{:S(2)}, u32[]{:S(2)}) %collective-permute-start.17) | collective-permute-done | bytes 524320 | tf_op jit(solution)/shard_map/ppermute | solution.py:359
  94.2 3.0 %collective-permute-start.23 = (f32[256,512]{1,0:T(8,128)S(1)}, f32[256,512]{1,0:T(8,128)S(1)}, u32[]{:S(2)}, u32[]{:S(2)}) collective-permute-start(f32[256,512]{1,0:T(8,128)S(1)} %keep5.1.refs_1_.refs_2_), channel_id=1, source_target_pairs={{0,8},{4,12},{24,16},{28,20},{1,9},{5,13},{25,17},{29,21},{2,10},{... | collective-permute-start | bytes 1572872 | tf_op jit(solution)/shard_map/ppermute | solution.py:353
  99.2 1.3 collective-permute-start.25
  100.5 2.5 %collective-permute-done.21.refs_2_.refs_4_ = f32[128,1024]{1,0:T(8,128)S(1)} collective-permute-done((f32[128,1024]{1,0:T(8,128)S(1)}, f32[128,1024]{1,0:T(8,128)S(1)}, u32[]{:S(2)}, u32[]{:S(2)}) %collective-permute-start.21) | collective-permute-done | bytes 524320 | tf_op jit(solution)/shard_map/ppermute | solution.py:359
  104.4 1.1 collective-permute-start.26
  107.1 1.3 collective-permute-start.27
  109.1 7.1 %collective-permute-done.25.refs_2_.refs_4_ = f32[256,512]{1,0:T(8,128)S(1)} collective-permute-done((f32[256,512]{1,0:T(8,128)S(1)}, f32[256,512]{1,0:T(8,128)S(1)}, u32[]{:S(2)}, u32[]{:S(2)}) %collective-permute-start.25) | collective-permute-done | bytes 524320 | tf_op jit(solution)/shard_map/ppermute | solution.py:359
  118.5 6.6 %collective-permute-done.27.refs_2_.refs_4_ = f32[256,512]{1,0:T(8,128)S(1)} collective-permute-done((f32[256,512]{1,0:T(8,128)S(1)}, f32[256,512]{1,0:T(8,128)S(1)}, u32[]{:S(2)}, u32[]{:S(2)}) %collective-permute-start.27) | collective-permute-done | bytes 524320 | tf_op jit(solution)/shard_map/ppermute | solution.py:359
  126.5 1.3 collective-permute-start.31
  129.2 4.8 %factor0.1 = (f32[512,512]{1,0:T(8,128)S(1)}, f32[512,512]{1,0:T(8,128)S(1)}) custom-call(s32[6]{0:T(128)S(1)} %stack.43.refs_0_, f32[512,512]{1,0:T(8,128)S(1)} %g6.1.refs_1_.refs_2_, f32[512,512]{1,0:T(8,128)S(1)} %g6.1.refs_1_.refs_2_), custom_call_target="tpu_custom_call" | custom-call | flops 1000 | bytes 1000 | tf_op jit(solution)/shard_map/factor0/pallas_call | solution.py:68
  134.7 1.4 collective-permute-start.34
  136.0 4.7 %factor1.1 = (f32[512,512]{1,0:T(8,128)S(1)}, f32[512,512]{1,0:T(8,128)S(1)}) custom-call(s32[6]{0:T(128)S(1)} %stack.43.refs_0_, f32[256,512]{1,0:T(8,128)S(1)} %ag4.1.refs_1_.refs_6_, f32[512,512]{1,0:T(8,128)S(1)} %get-tuple-element.65.refs_1_.refs_2_, f32[512,512]{1,0:T(8,128)S(1)} %get-tuple-element.66.refs_3_), custom_call_target="tpu_custom_call" | custom-call | flops 1000 | bytes 1000 | tf_op jit(solution)/shard_map/factor1/pallas_call | solution.py:68
  142.4 4.7 %factor2.1 = (f32[512,512]{1,0:T(8,128)S(1)}, f32[512,512]{1,0:T(8,128)S(1)}) custom-call(s32[6]{0:T(128)S(1)} %stack.43.refs_0_, f32[256,512]{1,0:T(8,128)S(1)} %ag5.1.refs_1_.first_ref, f32[512,512]{1,0:T(8,128)S(1)} %get-tuple-element.67.refs_1_.refs_2_, f32[512,512]{1,0:T(8,128)S(1)} %get-tuple-element.68.refs_3_), custom_call_target="tpu_custom_call" | custom-call | flops 1000 | bytes 1000 | tf_op jit(solution)/shard_map/factor2/pallas_call | solution.py:68
  147.1 4.0 %factor3.1 = (f32[512,512]{1,0:T(8,128)S(1)}, f32[512,512]{1,0:T(8,128)S(1)}) custom-call(s32[6]{0:T(128)S(1)} %stack.43.refs_0_, f32[512,512]{1,0:T(8,128)S(1)} %get-tuple-element.69.refs_1_.refs_2_, f32[512,512]{1,0:T(8,128)S(1)} %get-tuple-element.69.refs_1_.refs_2_, f32[512,512]{1,0:T(8,128)S(1)} %get-tuple-element.70.refs_3_), custom_call_target="tpu_custom_call" | custom-call | flops 1000 | bytes 1000 | tf_op jit(solution)/shard_map/factor3/pallas_call | solution.py:68
  151.1 2.6 %weights.1 = (bf16[576,512]{1,0:T(8,128)(2,1)S(1)}, bf16[576,512]{1,0:T(8,128)(2,1)S(1)}) custom-call(s32[6]{0:T(128)S(1)} %stack.43.refs_0_, f32[512,512]{1,0:T(8,128)S(1)} %get-tuple-element.71.refs_1_, f32[512,128]{1,0:T(8,128)S(1)} %ka.1.refs_1_.refs_2_.refs_8_.refs_9_, f32[512,128]{1,0:T(8,128)S(1)} %collective-permute-done.1.refs_3_.refs_9_.refs_10_, ...), custom_call_target="tpu_custom_call" | custom-call | flops 1000 | bytes 1000 | tf_op jit(solution)/shard_map/weights/pallas_call | solution.py:68
  153.8 1.2 fin1.1
  155.0 2.6 %fin0.1 = (f32[512,1024]{1,0:T(8,128)S(1)}, f32[64,1024]{1,0:T(8,128)S(1)}) custom-call(s32[6]{0:T(128)S(1)} %stack.43.refs_0_, f32[512,256]{1,0:T(8,128)S(1)} %get-tuple-element.76.refs_1_, f32[512,1024]{1,0:T(8,128)S(1)} %get-tuple-element.46.refs_1_.refs_2_, bf16[576,512]{1,0:T(8,128)(2,1)S(1)} %get-tuple-element.73.refs_1_.refs_3_.refs_4_.high_ref.mine_high, ...), custom_call_target="tpu_custom_call" | custom-call | flops 1000 | bytes 1000 | tf_op jit(solution)/shard_map/fin0/pallas_call | solution.py:68
  157.6 1.6 fin3.1
  159.2 1.6 fin4.1
  160.9 4.7 %collective-permute-done.32.second_ref = f32[256,512]{1,0:T(8,128)S(1)} collective-permute-done((f32[256,512]{1,0:T(8,128)S(1)}, f32[256,512]{1,0:T(8,128)S(1)}, u32[]{:S(2)}, u32[]{:S(2)}) %collective-permute-start.32) | collective-permute-done | bytes 524320 | tf_op jit(solution)/shard_map/ppermute | solution.py:52
  165.5 4.2 %tiles_to_rows.1 = (f32[11264,128]{1,0:T(8,128)}, f32[1408,128]{1,0:T(8,128)}) custom-call(f32[512,512]{1,0:T(8,128)S(1)} %get-tuple-element.45.a_ref, bf16[576,512]{1,0:T(8,128)(2,1)S(1)} %get-tuple-element.73.refs_1_.refs_3_.refs_4_.high_ref.mine_high, bf16[576,512]{1,0:T(8,128)(2,1)S(1)} %get-tuple-element.74.refs_4_.refs_5_.low_ref.mine_low, ...), custom_call_target="tpu_custom_call" | custom-call | tf_op jit(solution)/shard_map/tiles_to_rows/pallas_call | solution.py:293
  (75 shorter events, 37.2 us)
Async XLA Ops:
  1.7 10.4 %collective-permute-start = (f32[512,128]{1,0:T(8,128)S(1)}, f32[512,128]{1,0:T(8,128)S(1)}, u32[]{:S(2)}, u32[]{:S(2)}) collective-permute-start(f32[512,128]{1,0:T(8,128)S(1)} %bitcast.19), channel_id=1, source_target_pairs={{0,2},{1,3},{4,6},{5,7},{8,10},{9,11},{12,14},{13,15},{16,18},{17,... | collective-permute-start | bytes 786440 | tf_op jit(solution)/shard_map/ppermute | solution.py:328
  6.7 2.6 %copy-start = (f32[512,11,1,256]{3,2,1,0:T(1,128)S(1)}, f32[512,11,1,256]{3,2,1,0:T(1,128)}, u32[]{:S(2)}) copy-start(f32[512,11,1,256]{3,2,1,0:T(1,128)} %param.1) | copy-start | bytes 17301508
  12.7 5.2 %collective-permute-start.1 = (f32[512,128]{1,0:T(8,128)S(1)}, f32[512,128]{1,0:T(8,128)S(1)}, u32[]{:S(2)}, u32[]{:S(2)}) collective-permute-start(f32[512,128]{1,0:T(8,128)S(1)} %ka.1.refs_1_.refs_2_.refs_8_.refs_9_), channel_id=1, source_target_pairs={{0,1},{1,0},{2,3},{3,2},{4,5},{5,4},{6,7},{7,6},{8,9},{9,8},{10,11... | collective-permute-start | bytes 786440 | tf_op jit(solution)/shard_map/ppermute | solution.py:52
  13.5 10.9 %collective-permute-start.2 = (f32[544,128]{1,0:T(8,128)S(1)}, f32[544,128]{1,0:T(8,128)S(1)}, u32[]{:S(2)}, u32[]{:S(2)}) collective-permute-start(f32[544,128]{1,0:T(8,128)S(1)} %pad_maximum_fusion.refs_3_), channel_id=1, source_target_pairs={{0,2},{1,3},{4,6},{5,7},{8,10},{9,11},{12,14},{13,15},{16,18},{17,... | collective-permute-start | bytes 835592 | tf_op jit(solution)/shard_map/ppermute | solution.py:328
  19.8 14.8 %collective-permute-start.4 = (f32[128,1024]{1,0:T(8,128)S(1)}, f32[128,1024]{1,0:T(8,128)S(1)}, u32[]{:S(2)}, u32[]{:S(2)}) collective-permute-start(f32[128,1024]{1,0:T(8,128)S(1)} %send0.1.refs_1_), channel_id=1, source_target_pairs={{0,4},{4,0},{8,12},{12,8},{16,20},{20,16},{24,28},{28,24},{1,5},{5... | collective-permute-start | bytes 1572872 | tf_op jit(solution)/shard_map/ppermute | solution.py:52
  25.0 1.6 collective-permute-start.3
  28.8 17.1 %collective-permute-start.5 = (f32[256,512]{1,0:T(8,128)S(1)}, f32[256,512]{1,0:T(8,128)S(1)}, u32[]{:S(2)}, u32[]{:S(2)}) collective-permute-start(f32[256,512]{1,0:T(8,128)S(1)} %send1.1.refs_1_), channel_id=1, source_target_pairs={{0,4},{4,0},{8,12},{12,8},{16,20},{20,16},{24,28},{28,24},{1,5},{5... | collective-permute-start | bytes 1572872 | tf_op jit(solution)/shard_map/ppermute | solution.py:52
  35.8 15.0 %collective-permute-start.6 = (f32[128,1024]{1,0:T(8,128)S(1)}, f32[128,1024]{1,0:T(8,128)S(1)}, u32[]{:S(2)}, u32[]{:S(2)}) collective-permute-start(f32[128,1024]{1,0:T(8,128)S(1)} %keep0.1.refs_1_.refs_2_), channel_id=1, source_target_pairs={{0,8},{4,12},{24,16},{28,20},{1,9},{5,13},{25,17},{29,21},{2,10},{... | collective-permute-start | bytes 1572872 | tf_op jit(solution)/shard_map/ppermute | solution.py:353
  39.3 17.8 %collective-permute-start.7 = (f32[128,1024]{1,0:T(8,128)S(1)}, f32[128,1024]{1,0:T(8,128)S(1)}, u32[]{:S(2)}, u32[]{:S(2)}) collective-permute-start(f32[128,1024]{1,0:T(8,128)S(1)} %send2.1.refs_1_), channel_id=1, source_target_pairs={{0,4},{4,0},{8,12},{12,8},{16,20},{20,16},{24,28},{28,24},{1,5},{5... | collective-permute-start | bytes 1572872 | tf_op jit(solution)/shard_map/ppermute | solution.py:52
  47.3 14.5 %collective-permute-start.8 = (f32[256,512]{1,0:T(8,128)S(1)}, f32[256,512]{1,0:T(8,128)S(1)}, u32[]{:S(2)}, u32[]{:S(2)}) collective-permute-start(f32[256,512]{1,0:T(8,128)S(1)} %keep1.1.refs_1_.refs_2_), channel_id=1, source_target_pairs={{0,8},{4,12},{24,16},{28,20},{1,9},{5,13},{25,17},{29,21},{2,10},{... | collective-permute-start | bytes 1572872 | tf_op jit(solution)/shard_map/ppermute | solution.py:353
  51.4 13.3 %collective-permute-start.9 = (f32[128,1024]{1,0:T(8,128)S(1)}, f32[128,1024]{1,0:T(8,128)S(1)}, u32[]{:S(2)}, u32[]{:S(2)}) collective-permute-start(f32[128,1024]{1,0:T(8,128)S(1)} %zm0.1.refs_1_.refs_2_), channel_id=1, source_target_pairs={{8,16},{12,20},{16,8},{20,12},{9,17},{13,21},{17,9},{21,13},{10,18... | collective-permute-start | bytes 1572872 | tf_op jit(solution)/shard_map/ppermute | solution.py:356
  52.1 16.2 %collective-permute-start.10 = (f32[256,512]{1,0:T(8,128)S(1)}, f32[256,512]{1,0:T(8,128)S(1)}, u32[]{:S(2)}, u32[]{:S(2)}) collective-permute-start(f32[256,512]{1,0:T(8,128)S(1)} %send3.1.refs_1_), channel_id=1, source_target_pairs={{0,4},{4,0},{8,12},{12,8},{16,20},{20,16},{24,28},{28,24},{1,5},{5... | collective-permute-start | bytes 1572872 | tf_op jit(solution)/shard_map/ppermute | solution.py:52
  58.3 15.9 %collective-permute-start.11 = (f32[128,1024]{1,0:T(8,128)S(1)}, f32[128,1024]{1,0:T(8,128)S(1)}, u32[]{:S(2)}, u32[]{:S(2)}) collective-permute-start(f32[128,1024]{1,0:T(8,128)S(1)} %keep2.1.refs_1_.refs_2_), channel_id=1, source_target_pairs={{0,8},{4,12},{24,16},{28,20},{1,9},{5,13},{25,17},{29,21},{2,10},{... | collective-permute-start | bytes 1572872 | tf_op jit(solution)/shard_map/ppermute | solution.py:353
  62.4 13.1 %collective-permute-start.12 = (f32[256,512]{1,0:T(8,128)S(1)}, f32[256,512]{1,0:T(8,128)S(1)}, u32[]{:S(2)}, u32[]{:S(2)}) collective-permute-start(f32[256,512]{1,0:T(8,128)S(1)} %zm1.1.refs_1_.refs_2_), channel_id=1, source_target_pairs={{8,16},{12,20},{16,8},{20,12},{9,17},{13,21},{17,9},{21,13},{10,18... | collective-permute-start | bytes 1572872 | tf_op jit(solution)/shard_map/ppermute | solution.py:356
  63.1 15.8 %collective-permute-start.14 = (f32[256,512]{1,0:T(8,128)S(1)}, f32[256,512]{1,0:T(8,128)S(1)}, u32[]{:S(2)}, u32[]{:S(2)}) collective-permute-start(f32[256,512]{1,0:T(8,128)S(1)} %send4.1.refs_1_), channel_id=1, source_target_pairs={{0,4},{4,0},{8,12},{12,8},{16,20},{20,16},{24,28},{28,24},{1,5},{5... | collective-permute-start | bytes 1572872 | tf_op jit(solution)/shard_map/ppermute | solution.py:52
  65.3 15.8 %collective-permute-start.13 = (f32[128,1024]{1,0:T(8,128)S(1)}, f32[128,1024]{1,0:T(8,128)S(1)}, u32[]{:S(2)}, u32[]{:S(2)}) collective-permute-start(f32[128,1024]{1,0:T(8,128)S(1)} %zo0.1.refs_1_.refs_3_), channel_id=1, source_target_pairs={{8,0},{12,4},{16,24},{20,28},{9,1},{13,5},{17,25},{21,29},{10,2},{... | collective-permute-start | bytes 1572872 | tf_op jit(solution)/shard_map/ppermute | solution.py:359
  69.5 16.0 %collective-permute-start.15 = (f32[256,512]{1,0:T(8,128)S(1)}, f32[256,512]{1,0:T(8,128)S(1)}, u32[]{:S(2)}, u32[]{:S(2)}) collective-permute-start(f32[256,512]{1,0:T(8,128)S(1)} %keep3.1.refs_1_.refs_2_), channel_id=1, source_target_pairs={{0,8},{4,12},{24,16},{28,20},{1,9},{5,13},{25,17},{29,21},{2,10},{... | collective-permute-start | bytes 1572872 | tf_op jit(solution)/shard_map/ppermute | solution.py:353
  74.8 12.0 %collective-permute-start.16 = (f32[128,1024]{1,0:T(8,128)S(1)}, f32[128,1024]{1,0:T(8,128)S(1)}, u32[]{:S(2)}, u32[]{:S(2)}) collective-permute-start(f32[128,1024]{1,0:T(8,128)S(1)} %zm2.1.refs_1_.refs_2_), channel_id=1, source_target_pairs={{8,16},{12,20},{16,8},{20,12},{9,17},{13,21},{17,9},{21,13},{10,18... | collective-permute-start | bytes 1572872 | tf_op jit(solution)/shard_map/ppermute | solution.py:356
  76.1 16.3 %collective-permute-start.17 = (f32[256,512]{1,0:T(8,128)S(1)}, f32[256,512]{1,0:T(8,128)S(1)}, u32[]{:S(2)}, u32[]{:S(2)}) collective-permute-start(f32[256,512]{1,0:T(8,128)S(1)} %zo1.1.refs_1_.refs_4_), channel_id=1, source_target_pairs={{8,0},{12,4},{16,24},{20,28},{9,1},{13,5},{17,25},{21,29},{10,2},{... | collective-permute-start | bytes 1572872 | tf_op jit(solution)/shard_map/ppermute | solution.py:359
  78.9 14.2 %collective-permute-start.18 = (f32[256,512]{1,0:T(8,128)S(1)}, f32[256,512]{1,0:T(8,128)S(1)}, u32[]{:S(2)}, u32[]{:S(2)}) collective-permute-start(f32[256,512]{1,0:T(8,128)S(1)} %send5.1.refs_1_), channel_id=1, source_target_pairs={{0,4},{4,0},{8,12},{12,8},{16,20},{20,16},{24,28},{28,24},{1,5},{5... | collective-permute-start | bytes 1572872 | tf_op jit(solution)/shard_map/ppermute | solution.py:52
  82.3 15.0 %collective-permute-start.19 = (f32[256,512]{1,0:T(8,128)S(1)}, f32[256,512]{1,0:T(8,128)S(1)}, u32[]{:S(2)}, u32[]{:S(2)}) collective-permute-start(f32[256,512]{1,0:T(8,128)S(1)} %keep4.1.refs_1_.refs_2_), channel_id=1, source_target_pairs={{0,8},{4,12},{24,16},{28,20},{1,9},{5,13},{25,17},{29,21},{2,10},{... | collective-permute-start | bytes 1572872 | tf_op jit(solution)/shard_map/ppermute | solution.py:353
  86.1 12.5 %collective-permute-start.20 = (f32[256,512]{1,0:T(8,128)S(1)}, f32[256,512]{1,0:T(8,128)S(1)}, u32[]{:S(2)}, u32[]{:S(2)}) collective-permute-start(f32[256,512]{1,0:T(8,128)S(1)} %zm3.1.refs_1_.refs_2_), channel_id=1, source_target_pairs={{8,16},{12,20},{16,8},{20,12},{9,17},{13,21},{17,9},{21,13},{10,18... | collective-permute-start | bytes 1572872 | tf_op jit(solution)/shard_map/ppermute | solution.py:356
  87.4 15.6 %collective-permute-start.21 = (f32[128,1024]{1,0:T(8,128)S(1)}, f32[128,1024]{1,0:T(8,128)S(1)}, u32[]{:S(2)}, u32[]{:S(2)}) collective-permute-start(f32[128,1024]{1,0:T(8,128)S(1)} %zo2.1.refs_1_.refs_3_), channel_id=1, source_target_pairs={{8,0},{12,4},{16,24},{20,28},{9,1},{13,5},{17,25},{21,29},{10,2},{... | collective-permute-start | bytes 1572872 | tf_op jit(solution)/shard_map/ppermute | solution.py:359
  93.0 10.8 %collective-permute-start.22 = (f32[128,1024]{1,0:T(8,128)S(1)}, f32[128,1024]{1,0:T(8,128)S(1)}, u32[]{:S(2)}, u32[]{:S(2)}) collective-permute-start(f32[128,1024]{1,0:T(8,128)S(1)} %ag0.1.refs_1_.refs_5_), channel_id=1, source_target_pairs={{0,4},{4,0},{8,12},{12,8},{16,20},{20,16},{24,28},{28,24},{1,5},{5... | collective-permute-start | bytes 1572872 | tf_op jit(solution)/shard_map/ppermute | solution.py:52
  94.2 11.7 %collective-permute-start.23 = (f32[256,512]{1,0:T(8,128)S(1)}, f32[256,512]{1,0:T(8,128)S(1)}, u32[]{:S(2)}, u32[]{:S(2)}) collective-permute-start(f32[256,512]{1,0:T(8,128)S(1)} %keep5.1.refs_1_.refs_2_), channel_id=1, source_target_pairs={{0,8},{4,12},{24,16},{28,20},{1,9},{5,13},{25,17},{29,21},{2,10},{... | collective-permute-start | bytes 1572872 | tf_op jit(solution)/shard_map/ppermute | solution.py:353
  97.9 8.6 %collective-permute-start.24 = (f32[256,512]{1,0:T(8,128)S(1)}, f32[256,512]{1,0:T(8,128)S(1)}, u32[]{:S(2)}, u32[]{:S(2)}) collective-permute-start(f32[256,512]{1,0:T(8,128)S(1)} %zm4.1.refs_1_.refs_2_), channel_id=1, source_target_pairs={{8,16},{12,20},{16,8},{20,12},{9,17},{13,21},{17,9},{21,13},{10,18... | collective-permute-start | bytes 1572872 | tf_op jit(solution)/shard_map/ppermute | solution.py:356
  99.2 17.0 %collective-permute-start.25 = (f32[256,512]{1,0:T(8,128)S(1)}, f32[256,512]{1,0:T(8,128)S(1)}, u32[]{:S(2)}, u32[]{:S(2)}) collective-permute-start(f32[256,512]{1,0:T(8,128)S(1)} %zo3.1.refs_1_.refs_3_), channel_id=1, source_target_pairs={{8,0},{12,4},{16,24},{20,28},{9,1},{13,5},{17,25},{21,29},{10,2},{... | collective-permute-start | bytes 1572872 | tf_op jit(solution)/shard_map/ppermute | solution.py:359
  104.4 12.4 %collective-permute-start.26 = (f32[256,512]{1,0:T(8,128)S(1)}, f32[256,512]{1,0:T(8,128)S(1)}, u32[]{:S(2)}, u32[]{:S(2)}) collective-permute-start(f32[256,512]{1,0:T(8,128)S(1)} %ag1.1.refs_1_.refs_2_.refs_5_), channel_id=1, source_target_pairs={{0,4},{4,0},{8,12},{12,8},{16,20},{20,16},{24,28},{28,24},{1,5},{5... | collective-permute-start | bytes 1572872 | tf_op jit(solution)/shard_map/ppermute | solution.py:52
  107.1 18.0 %collective-permute-start.27 = (f32[256,512]{1,0:T(8,128)S(1)}, f32[256,512]{1,0:T(8,128)S(1)}, u32[]{:S(2)}, u32[]{:S(2)}) collective-permute-start(f32[256,512]{1,0:T(8,128)S(1)} %zo4.1.refs_1_.refs_3_), channel_id=1, source_target_pairs={{8,0},{12,4},{16,24},{20,28},{9,1},{13,5},{17,25},{21,29},{10,2},{... | collective-permute-start | bytes 1572872 | tf_op jit(solution)/shard_map/ppermute | solution.py:359
  108.4 17.5 %collective-permute-start.28 = (f32[256,512]{1,0:T(8,128)S(1)}, f32[256,512]{1,0:T(8,128)S(1)}, u32[]{:S(2)}, u32[]{:S(2)}) collective-permute-start(f32[256,512]{1,0:T(8,128)S(1)} %zm5.1.refs_1_.refs_2_), channel_id=1, source_target_pairs={{8,16},{12,20},{16,8},{20,12},{9,17},{13,21},{17,9},{21,13},{10,18... | collective-permute-start | bytes 1572872 | tf_op jit(solution)/shard_map/ppermute | solution.py:356
  117.4 10.4 %collective-permute-start.29 = (f32[512,256]{1,0:T(8,128)S(1)}, f32[512,256]{1,0:T(8,128)S(1)}, u32[]{:S(2)}, u32[]{:S(2)}) collective-permute-start(f32[512,256]{1,0:T(8,128)S(1)} %g4.1.refs_1_.refs_2_), channel_id=1, source_target_pairs={{0,1},{1,0},{2,3},{3,2},{4,5},{5,4},{6,7},{7,6},{8,9},{9,8},{10,11... | collective-permute-start | bytes 1572872 | tf_op jit(solution)/shard_map/ppermute | solution.py:52
  117.5 16.6 %collective-permute-start.30 = (f32[128,1024]{1,0:T(8,128)S(1)}, f32[128,1024]{1,0:T(8,128)S(1)}, u32[]{:S(2)}, u32[]{:S(2)}) collective-permute-start(f32[128,1024]{1,0:T(8,128)S(1)} %ag2.1.refs_1_.refs_6_), channel_id=1, source_target_pairs={{0,4},{4,0},{8,12},{12,8},{16,20},{20,16},{24,28},{28,24},{1,5},{5... | collective-permute-start | bytes 1572872 | tf_op jit(solution)/shard_map/ppermute | solution.py:52
  126.5 14.3 %collective-permute-start.31 = (f32[256,512]{1,0:T(8,128)S(1)}, f32[256,512]{1,0:T(8,128)S(1)}, u32[]{:S(2)}, u32[]{:S(2)}) collective-permute-start(f32[256,512]{1,0:T(8,128)S(1)} %zo5.1.refs_1_.refs_3_), channel_id=1, source_target_pairs={{8,0},{12,4},{16,24},{20,28},{9,1},{13,5},{17,25},{21,29},{10,2},{... | collective-permute-start | bytes 1572872 | tf_op jit(solution)/shard_map/ppermute | solution.py:359
  128.4 29.1 %collective-permute-start.33 = (f32[256,512]{1,0:T(8,128)S(1)}, f32[256,512]{1,0:T(8,128)S(1)}, u32[]{:S(2)}, u32[]{:S(2)}) collective-permute-start(f32[256,512]{1,0:T(8,128)S(1)} %ag3.1.refs_1_.refs_6_), channel_id=1, source_target_pairs={{0,4},{4,0},{8,12},{12,8},{16,20},{20,16},{24,28},{28,24},{1,5},{5... | collective-permute-start | bytes 1572872 | tf_op jit(solution)/shard_map/ppermute | solution.py:52
  134.7 24.6 %collective-permute-start.34 = (f32[256,512]{1,0:T(8,128)S(1)}, f32[256,512]{1,0:T(8,128)S(1)}, u32[]{:S(2)}, u32[]{:S(2)}) collective-permute-start(f32[256,512]{1,0:T(8,128)S(1)} %ag4.1.refs_1_.refs_6_), channel_id=1, source_target_pairs={{0,4},{4,0},{8,12},{12,8},{16,20},{20,16},{24,28},{28,24},{1,5},{5... | collective-permute-start | bytes 1572872 | tf_op jit(solution)/shard_map/ppermute | solution.py:52
  141.6 23.9 %collective-permute-start.32 = (f32[256,512]{1,0:T(8,128)S(1)}, f32[256,512]{1,0:T(8,128)S(1)}, u32[]{:S(2)}, u32[]{:S(2)}) collective-permute-start(f32[256,512]{1,0:T(8,128)S(1)} %ag5.1.refs_1_.first_ref), channel_id=1, source_target_pairs={{0,4},{4,0},{8,12},{12,8},{16,20},{20,16},{24,28},{28,24},{1,5},{5... | collective-permute-start | bytes 1572872 | tf_op jit(solution)/shard_map/ppermute | solution.py:52

commit v5 on v4

--- a/solution.py
+++ b/solution.py
@@ -17,9 +17,9 @@
 GROUP_OF = (0, 1, 0, 2, 3, 4)
 ORDER = (
     "ka pa send0 kb", "pb send1 send2 send3", "keep0 send4 send5 keep1", "zm0 keep2 zm1 zo0",
-    "keep3 zm2 zo1 ~zo0", "keep4 zm3 zo2 ~zo1", "ag0 keep5 zm4 zo3", "~zo2 ~ag0 ag1 zm5",
-    "zo4 ~zo3 ag2 g4", "~zo4 ag3 zo5 g6", "ch0 ~ag2 ag4 ch1", "~zo5 ag5 ch2 ch3",
-    "weights fin1 fin0 ~ag3", "fin3 ~ag4 fin4",
+    "keep3 zm2 zo1 ~zo0", "keep4 zm3 zo2 ~zo1", "ag0 keep5 zm4 zo3", "~zo2 ag1 ~ag0 zm5",
+    "zo4 ~zo3 ag2 g4", "zo5 ~zo4 ag3 g6", "ch0 ~ag2 ag4 ch1", "~zo5 ag5 ~ag3 ch2",
+    "ch3 weights fin1 fin0", "fin3 ~ag4 fin4",
 )
 
 

time: 170 us -> 171 us (level)
  starting transfers between devices: 57.4 us -> 52.1 us
  waiting for transfers between devices: 42.8 us -> 47.5 us
    ppermute x15, waiting for transfers between devices: 18.5 us -> 23.2 us  [flip(): return lax.ppermute(value, axis, [(i, i ^ bit) for i in range(n)])]
    ppermute x2, waiting for transfers between devices: 3.27 us -> 0.01 us  [local(): came = [lax.ppermute(v, 'pcol', [(0, 2), (1, 3)]) for v in own]]
    ppermute x2, starting transfers between devices: 9.26 us -> 6.17 us  [local(): came = [lax.ppermute(v, 'pcol', [(0, 2), (1, 3)]) for v in own]]
    ppermute x6, waiting for transfers between devices: 20.7 us -> 23.5 us  [out_hop(): lax.ppermute(value, 'prow', [(2, 0), (3, 1), (4, 6), (5, 7)])]
    ppermute x15, starting transfers between devices: 14.8 us -> 12.5 us  [flip(): return lax.ppermute(value, axis, [(i, i ^ bit) for i in range(n)])]
    unnamed x2 -> x6, local copies, waits for them, and re-layouts: 2.64 us -> 4.28 us
  transfers between devices with their start and end apart: 35 -> 35, of which waited for: 16 -> 14; matrix products, arithmetic and copies ran while one was open for 0% -> 0% of each run, Pallas kernels for 35% -> 34%
where the time goes in v5:
time: 171 us
  Pallas kernels  63.5 us (37%)
  starting transfers between devices  52.1 us (30%)
  waiting for transfers between devices  47.5 us (28%)
  local copies, waits for them, and re-layouts  6.18 us (4%)
    pallas_call x46, Pallas kernels, __call__(): pl.pallas_call(body, out_shape=[jax.ShapeDtypeStruct(*(o if isinstance(o[...  59.2 us
    ppermute x6, waiting for transfers between devices, out_hop(): lax.ppermute(value, 'prow', [(2, 0), (3, 1), (4, 6), (5, 7)])  23.5 us
    ppermute x15, waiting for transfers between devices, flip(): return lax.ppermute(value, axis, [(i, i ^ bit) for i in range(n)])  23.2 us
    ppermute x6, starting transfers between devices, in_hop(): lax.ppermute(value, 'prow', [(0, 2), (1, 3), (6, 4), (7, 5)])  21.3 us
    ppermute x15, starting transfers between devices, flip(): return lax.ppermute(value, axis, [(i, i ^ bit) for i in range(n)])  12.5 us
    ppermute x6, starting transfers between devices, out_hop(): lax.ppermute(value, 'prow', [(2, 0), (3, 1), (4, 6), (5, 7)])  7.93 us
    ppermute x2, starting transfers between devices, local(): came = [lax.ppermute(v, 'pcol', [(0, 2), (1, 3)]) for v in own]  6.17 us
    unnamed x6, local copies, waits for them, and re-layouts  4.28 us
  transfers between devices with their start and end apart: 35, of which 14 were waited for; matrix products, arithmetic and copies ran while one was open for 0% of the time, Pallas kernels for 34%

profile of v5, /device:TPU:0, one launch (start us, length us, event | category | flops | bytes accessed | tf_op | source)
XLA Modules:
  0.0 170.6 jit_solution(4328743713094703914)
XLA Ops:
  1.7 4.9 %collective-permute-start = (f32[512,128]{1,0:T(8,128)S(1)}, f32[512,128]{1,0:T(8,128)S(1)}, u32[]{:S(2)}, u32[]{:S(2)}) collective-permute-start(f32[512,128]{1,0:T(8,128)S(1)} %bitcast.19), channel_id=1, source_target_pairs={{0,2},{1,3},{4,6},{5,7},{8,10},{9,11},{12,14},{13,15},{16,18},{17,... | collective-permute-start | bytes 786440 | tf_op jit(solution)/shard_map/ppermute | solution.py:328
  7.3 1.3 collective-permute-start.2
  8.8 2.6 %copy-done = f32[512,11,1,256]{3,2,1,0:T(1,128)S(1)} copy-done((f32[512,11,1,256]{3,2,1,0:T(1,128)S(1)}, f32[512,11,1,256]{3,2,1,0:T(1,128)}, u32[]{:S(2)}) %copy-start) | copy-done | bytes 5767192
  11.4 2.5 %rows_to_tiles.1 = (f32[512,1024]{1,0:T(8,128)S(1)}, bf16[512,1024]{1,0:T(8,128)(2,1)S(1)}, bf16[512,1024]{1,0:T(8,128)(2,1)S(1)}, f32[512,256]{1,0:T(8,128)S(1)...) custom-call(s32[6]{0:T(128)S(1)} %stack.43.refs_0_, ...), custom_call_target="tpu_custom_call" | custom-call | flops 1000 | bytes 1000 | tf_op jit(solution)/shard_map/rows_to_tiles/pallas_call | solution.py:68
  16.3 1.5 collective-permute-done.1.refs_3_.refs_9_.refs_10_
  20.5 1.5 collective-permute-start.4
  22.8 1.4 send1.1.refs_1_
  24.2 1.4 collective-permute-start.5
  27.9 7.3 %collective-permute-done.4.refs_6_ = f32[128,1024]{1,0:T(8,128)S(1)} collective-permute-done((f32[128,1024]{1,0:T(8,128)S(1)}, f32[128,1024]{1,0:T(8,128)S(1)}, u32[]{:S(2)}, u32[]{:S(2)}) %collective-permute-start.4) | collective-permute-done | bytes 524320 | tf_op jit(solution)/shard_map/ppermute | solution.py:52
  36.4 3.5 %collective-permute-start.6 = (f32[128,1024]{1,0:T(8,128)S(1)}, f32[128,1024]{1,0:T(8,128)S(1)}, u32[]{:S(2)}, u32[]{:S(2)}) collective-permute-start(f32[128,1024]{1,0:T(8,128)S(1)} %keep0.1.refs_1_.refs_2_), channel_id=1, source_target_pairs={{0,8},{4,12},{24,16},{28,20},{1,9},{5,13},{25,17},{29,21},{2,10},{... | collective-permute-start | bytes 1572872 | tf_op jit(solution)/shard_map/ppermute | solution.py:353
  39.9 1.6 collective-permute-start.7
  43.7 2.8 %collective-permute-done.5.refs_8_ = f32[256,512]{1,0:T(8,128)S(1)} collective-permute-done((f32[256,512]{1,0:T(8,128)S(1)}, f32[256,512]{1,0:T(8,128)S(1)}, u32[]{:S(2)}, u32[]{:S(2)}) %collective-permute-start.5) | collective-permute-done | bytes 524320 | tf_op jit(solution)/shard_map/ppermute | solution.py:52
  46.5 1.4 keep1.1.refs_1_.refs_2_
  47.9 3.5 %collective-permute-start.8 = (f32[256,512]{1,0:T(8,128)S(1)}, f32[256,512]{1,0:T(8,128)S(1)}, u32[]{:S(2)}, u32[]{:S(2)}) collective-permute-start(f32[256,512]{1,0:T(8,128)S(1)} %keep1.1.refs_1_.refs_2_), channel_id=1, source_target_pairs={{0,8},{4,12},{24,16},{28,20},{1,9},{5,13},{25,17},{29,21},{2,10},{... | collective-permute-start | bytes 1572872 | tf_op jit(solution)/shard_map/ppermute | solution.py:353
  52.7 1.6 collective-permute-start.10
  54.3 3.4 %collective-permute-done.7.refs_6_ = f32[128,1024]{1,0:T(8,128)S(1)} collective-permute-done((f32[128,1024]{1,0:T(8,128)S(1)}, f32[128,1024]{1,0:T(8,128)S(1)}, u32[]{:S(2)}, u32[]{:S(2)}) %collective-permute-start.7) | collective-permute-done | bytes 524320 | tf_op jit(solution)/shard_map/ppermute | solution.py:52
  58.9 3.5 %collective-permute-start.11 = (f32[128,1024]{1,0:T(8,128)S(1)}, f32[128,1024]{1,0:T(8,128)S(1)}, u32[]{:S(2)}, u32[]{:S(2)}) collective-permute-start(f32[128,1024]{1,0:T(8,128)S(1)} %keep2.1.refs_1_.refs_2_), channel_id=1, source_target_pairs={{0,8},{4,12},{24,16},{28,20},{1,9},{5,13},{25,17},{29,21},{2,10},{... | collective-permute-start | bytes 1572872 | tf_op jit(solution)/shard_map/ppermute | solution.py:353
  63.7 1.6 collective-permute-start.14
  65.9 1.3 collective-permute-start.13
  67.2 1.8 %collective-permute-done.10.refs_8_ = f32[256,512]{1,0:T(8,128)S(1)} collective-permute-done((f32[256,512]{1,0:T(8,128)S(1)}, f32[256,512]{1,0:T(8,128)S(1)}, u32[]{:S(2)}, u32[]{:S(2)}) %collective-permute-start.10) | collective-permute-done | bytes 524320 | tf_op jit(solution)/shard_map/ppermute | solution.py:52
  70.1 5.0 %collective-permute-start.15 = (f32[256,512]{1,0:T(8,128)S(1)}, f32[256,512]{1,0:T(8,128)S(1)}, u32[]{:S(2)}, u32[]{:S(2)}) collective-permute-start(f32[256,512]{1,0:T(8,128)S(1)} %keep3.1.refs_1_.refs_2_), channel_id=1, source_target_pairs={{0,8},{4,12},{24,16},{28,20},{1,9},{5,13},{25,17},{29,21},{2,10},{... | collective-permute-start | bytes 1572872 | tf_op jit(solution)/shard_map/ppermute | solution.py:353
  77.0 1.3 collective-permute-start.17
  78.3 1.3 collective-permute-done.14.refs_9_
  79.6 1.5 collective-permute-start.18
  81.1 1.2 collective-permute-done.13.refs_2_.refs_4_
  83.4 3.0 %collective-permute-start.19 = (f32[256,512]{1,0:T(8,128)S(1)}, f32[256,512]{1,0:T(8,128)S(1)}, u32[]{:S(2)}, u32[]{:S(2)}) collective-permute-start(f32[256,512]{1,0:T(8,128)S(1)} %keep4.1.refs_1_.refs_2_), channel_id=1, source_target_pairs={{0,8},{4,12},{24,16},{28,20},{1,9},{5,13},{25,17},{29,21},{2,10},{... | collective-permute-start | bytes 1572872 | tf_op jit(solution)/shard_map/ppermute | solution.py:353
  88.3 1.3 collective-permute-start.21
  89.6 4.2 %collective-permute-done.17.refs_2_.refs_4_ = f32[256,512]{1,0:T(8,128)S(1)} collective-permute-done((f32[256,512]{1,0:T(8,128)S(1)}, f32[256,512]{1,0:T(8,128)S(1)}, u32[]{:S(2)}, u32[]{:S(2)}) %collective-permute-start.17) | collective-permute-done | bytes 524320 | tf_op jit(solution)/shard_map/ppermute | solution.py:359
  95.7 2.8 %collective-permute-start.23 = (f32[256,512]{1,0:T(8,128)S(1)}, f32[256,512]{1,0:T(8,128)S(1)}, u32[]{:S(2)}, u32[]{:S(2)}) collective-permute-start(f32[256,512]{1,0:T(8,128)S(1)} %keep5.1.refs_1_.refs_3_), channel_id=1, source_target_pairs={{0,8},{4,12},{24,16},{28,20},{1,9},{5,13},{25,17},{29,21},{2,10},{... | collective-permute-start | bytes 1572872 | tf_op jit(solution)/shard_map/ppermute | solution.py:353
  100.4 1.3 collective-permute-start.25
  101.7 3.8 %collective-permute-done.21.refs_2_.refs_4_ = f32[128,1024]{1,0:T(8,128)S(1)} collective-permute-done((f32[128,1024]{1,0:T(8,128)S(1)}, f32[128,1024]{1,0:T(8,128)S(1)}, u32[]{:S(2)}, u32[]{:S(2)}) %collective-permute-start.21) | collective-permute-done | bytes 524320 | tf_op jit(solution)/shard_map/ppermute | solution.py:359
  108.9 1.3 collective-permute-start.28
  110.2 6.9 %collective-permute-done.25.refs_2_.refs_4_ = f32[256,512]{1,0:T(8,128)S(1)} collective-permute-done((f32[256,512]{1,0:T(8,128)S(1)}, f32[256,512]{1,0:T(8,128)S(1)}, u32[]{:S(2)}, u32[]{:S(2)}) %collective-permute-start.25) | collective-permute-done | bytes 524320 | tf_op jit(solution)/shard_map/ppermute | solution.py:359
  119.5 1.5 collective-permute-start.31
  121.0 7.4 %collective-permute-done.28.refs_2_.refs_4_ = f32[256,512]{1,0:T(8,128)S(1)} collective-permute-done((f32[256,512]{1,0:T(8,128)S(1)}, f32[256,512]{1,0:T(8,128)S(1)}, u32[]{:S(2)}, u32[]{:S(2)}) %collective-permute-start.28) | collective-permute-done | bytes 524320 | tf_op jit(solution)/shard_map/ppermute | solution.py:359
  129.7 4.9 %factor0.1 = (f32[512,512]{1,0:T(8,128)S(1)}, f32[512,512]{1,0:T(8,128)S(1)}) custom-call(s32[6]{0:T(128)S(1)} %stack.43.refs_0_, f32[512,512]{1,0:T(8,128)S(1)} %g6.1.refs_1_.refs_2_, f32[512,512]{1,0:T(8,128)S(1)} %g6.1.refs_1_.refs_2_), custom_call_target="tpu_custom_call" | custom-call | flops 1000 | bytes 1000 | tf_op jit(solution)/shard_map/factor0/pallas_call | solution.py:68
  135.2 2.1 %collective-permute-start.34 = (f32[256,512]{1,0:T(8,128)S(1)}, f32[256,512]{1,0:T(8,128)S(1)}, u32[]{:S(2)}, u32[]{:S(2)}) collective-permute-start(f32[256,512]{1,0:T(8,128)S(1)} %ag4.1.refs_1_.refs_6_), channel_id=1, source_target_pairs={{0,4},{4,0},{8,12},{12,8},{16,20},{20,16},{24,28},{28,24},{1,5},{5... | collective-permute-start | bytes 1572872 | tf_op jit(solution)/shard_map/ppermute | solution.py:52
  137.3 4.7 %factor1.1 = (f32[512,512]{1,0:T(8,128)S(1)}, f32[512,512]{1,0:T(8,128)S(1)}) custom-call(s32[6]{0:T(128)S(1)} %stack.43.refs_0_, f32[256,512]{1,0:T(8,128)S(1)} %ag4.1.refs_1_.refs_6_, f32[512,512]{1,0:T(8,128)S(1)} %get-tuple-element.65.refs_1_.refs_2_, f32[512,512]{1,0:T(8,128)S(1)} %get-tuple-element.66.refs_3_), custom_call_target="tpu_custom_call" | custom-call | flops 1000 | bytes 1000 | tf_op jit(solution)/shard_map/factor1/pallas_call | solution.py:68
  142.9 1.5 collective-permute-done.32.refs_2_.refs_6_
  144.4 4.7 %factor2.1 = (f32[512,512]{1,0:T(8,128)S(1)}, f32[512,512]{1,0:T(8,128)S(1)}) custom-call(s32[6]{0:T(128)S(1)} %stack.43.refs_0_, f32[256,512]{1,0:T(8,128)S(1)} %ag5.1.refs_1_.first_ref, f32[256,512]{1,0:T(8,128)S(1)} %collective-permute-done.32.refs_2_.refs_6_, f32[512,512]{1,0:T(8,128)S(1)} %get-tuple-element.67.refs_1_.refs_3_, ...), custom_call_target="tpu_custom_call" | custom-call | flops 1000 | bytes 1000 | tf_op jit(solution)/shard_map/factor2/pallas_call | solution.py:68
  149.1 4.0 %factor3.1 = (f32[512,512]{1,0:T(8,128)S(1)}, f32[512,512]{1,0:T(8,128)S(1)}) custom-call(s32[6]{0:T(128)S(1)} %stack.43.refs_0_, f32[512,512]{1,0:T(8,128)S(1)} %get-tuple-element.69.refs_1_.refs_2_, f32[512,512]{1,0:T(8,128)S(1)} %get-tuple-element.69.refs_1_.refs_2_, f32[512,512]{1,0:T(8,128)S(1)} %get-tuple-element.70.refs_3_), custom_call_target="tpu_custom_call" | custom-call | flops 1000 | bytes 1000 | tf_op jit(solution)/shard_map/factor3/pallas_call | solution.py:68
  153.1 2.6 %weights.1 = (bf16[576,512]{1,0:T(8,128)(2,1)S(1)}, bf16[576,512]{1,0:T(8,128)(2,1)S(1)}) custom-call(s32[6]{0:T(128)S(1)} %stack.43.refs_0_, f32[512,512]{1,0:T(8,128)S(1)} %get-tuple-element.71.refs_1_, f32[512,128]{1,0:T(8,128)S(1)} %ka.1.refs_1_.refs_2_.refs_8_.refs_9_, f32[512,128]{1,0:T(8,128)S(1)} %collective-permute-done.1.refs_3_.refs_9_.refs_10_, ...), custom_call_target="tpu_custom_call" | custom-call | flops 1000 | bytes 1000 | tf_op jit(solution)/shard_map/weights/pallas_call | solution.py:68
  155.8 1.2 fin1.1
  157.0 2.6 %fin0.1 = (f32[512,1024]{1,0:T(8,128)S(1)}, f32[64,1024]{1,0:T(8,128)S(1)}) custom-call(s32[6]{0:T(128)S(1)} %stack.43.refs_0_, f32[512,256]{1,0:T(8,128)S(1)} %get-tuple-element.76.refs_1_, f32[512,1024]{1,0:T(8,128)S(1)} %get-tuple-element.46.refs_1_.refs_2_, bf16[576,512]{1,0:T(8,128)(2,1)S(1)} %get-tuple-element.73.refs_1_.refs_3_.refs_4_.high_ref.mine_high, ...), custom_call_target="tpu_custom_call" | custom-call | flops 1000 | bytes 1000 | tf_op jit(solution)/shard_map/fin0/pallas_call | solution.py:68
  159.6 1.6 fin3.1
  161.2 1.6 fin4.1
  162.8 3.6 %collective-permute-done.33.second_ref = f32[256,512]{1,0:T(8,128)S(1)} collective-permute-done((f32[256,512]{1,0:T(8,128)S(1)}, f32[256,512]{1,0:T(8,128)S(1)}, u32[]{:S(2)}, u32[]{:S(2)}) %collective-permute-start.33) | collective-permute-done | bytes 524320 | tf_op jit(solution)/shard_map/ppermute | solution.py:52
  166.4 4.2 %tiles_to_rows.1 = (f32[11264,128]{1,0:T(8,128)}, f32[1408,128]{1,0:T(8,128)}) custom-call(f32[512,512]{1,0:T(8,128)S(1)} %get-tuple-element.45.a_ref, bf16[576,512]{1,0:T(8,128)(2,1)S(1)} %get-tuple-element.73.refs_1_.refs_3_.refs_4_.high_ref.mine_high, bf16[576,512]{1,0:T(8,128)(2,1)S(1)} %get-tuple-element.74.refs_4_.refs_5_.low_ref.mine_low, ...), custom_call_target="tpu_custom_call" | custom-call | tf_op jit(solution)/shard_map/tiles_to_rows/pallas_call | solution.py:293
  (79 shorter events, 35.7 us)
Async XLA Ops:
  1.7 12.2 %collective-permute-start = (f32[512,128]{1,0:T(8,128)S(1)}, f32[512,128]{1,0:T(8,128)S(1)}, u32[]{:S(2)}, u32[]{:S(2)}) collective-permute-start(f32[512,128]{1,0:T(8,128)S(1)} %bitcast.19), channel_id=1, source_target_pairs={{0,2},{1,3},{4,6},{5,7},{8,10},{9,11},{12,14},{13,15},{16,18},{17,... | collective-permute-start | bytes 786440 | tf_op jit(solution)/shard_map/ppermute | solution.py:328
  7.3 12.4 %collective-permute-start.2 = (f32[544,128]{1,0:T(8,128)S(1)}, f32[544,128]{1,0:T(8,128)S(1)}, u32[]{:S(2)}, u32[]{:S(2)}) collective-permute-start(f32[544,128]{1,0:T(8,128)S(1)} %pad_maximum_fusion.refs_3_), channel_id=1, source_target_pairs={{0,2},{1,3},{4,6},{5,7},{8,10},{9,11},{12,14},{13,15},{16,18},{17,... | collective-permute-start | bytes 835592 | tf_op jit(solution)/shard_map/ppermute | solution.py:328
  8.8 2.6 %copy-start = (f32[512,11,1,256]{3,2,1,0:T(1,128)S(1)}, f32[512,11,1,256]{3,2,1,0:T(1,128)}, u32[]{:S(2)}) copy-start(f32[512,11,1,256]{3,2,1,0:T(1,128)} %param.1) | copy-start | bytes 17301508
  13.9 0.7 copy-start.1
  14.7 0.9 copy-start.2
  16.2 1.6 collective-permute-start.1
  20.3 1.7 %collective-permute-start.3 = (f32[512,128]{1,0:T(8,128)S(1)}, f32[512,128]{1,0:T(8,128)S(1)}, u32[]{:S(2)}, u32[]{:S(2)}) collective-permute-start(f32[512,128]{1,0:T(8,128)S(1)} %kb.1.refs_1_.refs_2_.refs_10_.refs_11_.refs_4_), channel_id=1, source_target_pairs={{0,1},{1,0},{2,3},{3,2},{4,5},{5,4},{6,7},{7,6},{8,9},{9,8},{10,11... | collective-permute-start | bytes 786440 | tf_op jit(solution)/shard_map/ppermute | solution.py:52
  20.5 14.8 %collective-permute-start.4 = (f32[128,1024]{1,0:T(8,128)S(1)}, f32[128,1024]{1,0:T(8,128)S(1)}, u32[]{:S(2)}, u32[]{:S(2)}) collective-permute-start(f32[128,1024]{1,0:T(8,128)S(1)} %send0.1.refs_1_), channel_id=1, source_target_pairs={{0,4},{4,0},{8,12},{12,8},{16,20},{20,16},{24,28},{28,24},{1,5},{5... | collective-permute-start | bytes 1572872 | tf_op jit(solution)/shard_map/ppermute | solution.py:52
  24.2 22.3 %collective-permute-start.5 = (f32[256,512]{1,0:T(8,128)S(1)}, f32[256,512]{1,0:T(8,128)S(1)}, u32[]{:S(2)}, u32[]{:S(2)}) collective-permute-start(f32[256,512]{1,0:T(8,128)S(1)} %send1.1.refs_1_), channel_id=1, source_target_pairs={{0,4},{4,0},{8,12},{12,8},{16,20},{20,16},{24,28},{28,24},{1,5},{5... | collective-permute-start | bytes 1572872 | tf_op jit(solution)/shard_map/ppermute | solution.py:52
  36.4 15.0 %collective-permute-start.6 = (f32[128,1024]{1,0:T(8,128)S(1)}, f32[128,1024]{1,0:T(8,128)S(1)}, u32[]{:S(2)}, u32[]{:S(2)}) collective-permute-start(f32[128,1024]{1,0:T(8,128)S(1)} %keep0.1.refs_1_.refs_2_), channel_id=1, source_target_pairs={{0,8},{4,12},{24,16},{28,20},{1,9},{5,13},{25,17},{29,21},{2,10},{... | collective-permute-start | bytes 1572872 | tf_op jit(solution)/shard_map/ppermute | solution.py:353
  39.9 17.8 %collective-permute-start.7 = (f32[128,1024]{1,0:T(8,128)S(1)}, f32[128,1024]{1,0:T(8,128)S(1)}, u32[]{:S(2)}, u32[]{:S(2)}) collective-permute-start(f32[128,1024]{1,0:T(8,128)S(1)} %send2.1.refs_1_), channel_id=1, source_target_pairs={{0,4},{4,0},{8,12},{12,8},{16,20},{20,16},{24,28},{28,24},{1,5},{5... | collective-permute-start | bytes 1572872 | tf_op jit(solution)/shard_map/ppermute | solution.py:52
  47.9 14.5 %collective-permute-start.8 = (f32[256,512]{1,0:T(8,128)S(1)}, f32[256,512]{1,0:T(8,128)S(1)}, u32[]{:S(2)}, u32[]{:S(2)}) collective-permute-start(f32[256,512]{1,0:T(8,128)S(1)} %keep1.1.refs_1_.refs_2_), channel_id=1, source_target_pairs={{0,8},{4,12},{24,16},{28,20},{1,9},{5,13},{25,17},{29,21},{2,10},{... | collective-permute-start | bytes 1572872 | tf_op jit(solution)/shard_map/ppermute | solution.py:353
  52.0 13.3 %collective-permute-start.9 = (f32[128,1024]{1,0:T(8,128)S(1)}, f32[128,1024]{1,0:T(8,128)S(1)}, u32[]{:S(2)}, u32[]{:S(2)}) collective-permute-start(f32[128,1024]{1,0:T(8,128)S(1)} %zm0.1.refs_1_.refs_2_), channel_id=1, source_target_pairs={{8,16},{12,20},{16,8},{20,12},{9,17},{13,21},{17,9},{21,13},{10,18... | collective-permute-start | bytes 1572872 | tf_op jit(solution)/shard_map/ppermute | solution.py:356
  52.7 16.2 %collective-permute-start.10 = (f32[256,512]{1,0:T(8,128)S(1)}, f32[256,512]{1,0:T(8,128)S(1)}, u32[]{:S(2)}, u32[]{:S(2)}) collective-permute-start(f32[256,512]{1,0:T(8,128)S(1)} %send3.1.refs_1_), channel_id=1, source_target_pairs={{0,4},{4,0},{8,12},{12,8},{16,20},{20,16},{24,28},{28,24},{1,5},{5... | collective-permute-start | bytes 1572872 | tf_op jit(solution)/shard_map/ppermute | solution.py:52
  58.9 16.2 %collective-permute-start.11 = (f32[128,1024]{1,0:T(8,128)S(1)}, f32[128,1024]{1,0:T(8,128)S(1)}, u32[]{:S(2)}, u32[]{:S(2)}) collective-permute-start(f32[128,1024]{1,0:T(8,128)S(1)} %keep2.1.refs_1_.refs_2_), channel_id=1, source_target_pairs={{0,8},{4,12},{24,16},{28,20},{1,9},{5,13},{25,17},{29,21},{2,10},{... | collective-permute-start | bytes 1572872 | tf_op jit(solution)/shard_map/ppermute | solution.py:353
  63.0 13.4 %collective-permute-start.12 = (f32[256,512]{1,0:T(8,128)S(1)}, f32[256,512]{1,0:T(8,128)S(1)}, u32[]{:S(2)}, u32[]{:S(2)}) collective-permute-start(f32[256,512]{1,0:T(8,128)S(1)} %zm1.1.refs_1_.refs_2_), channel_id=1, source_target_pairs={{8,16},{12,20},{16,8},{20,12},{9,17},{13,21},{17,9},{21,13},{10,18... | collective-permute-start | bytes 1572872 | tf_op jit(solution)/shard_map/ppermute | solution.py:356
  63.7 15.9 %collective-permute-start.14 = (f32[256,512]{1,0:T(8,128)S(1)}, f32[256,512]{1,0:T(8,128)S(1)}, u32[]{:S(2)}, u32[]{:S(2)}) collective-permute-start(f32[256,512]{1,0:T(8,128)S(1)} %send4.1.refs_1_), channel_id=1, source_target_pairs={{0,4},{4,0},{8,12},{12,8},{16,20},{20,16},{24,28},{28,24},{1,5},{5... | collective-permute-start | bytes 1572872 | tf_op jit(solution)/shard_map/ppermute | solution.py:52
  65.9 16.4 %collective-permute-start.13 = (f32[128,1024]{1,0:T(8,128)S(1)}, f32[128,1024]{1,0:T(8,128)S(1)}, u32[]{:S(2)}, u32[]{:S(2)}) collective-permute-start(f32[128,1024]{1,0:T(8,128)S(1)} %zo0.1.refs_1_.refs_3_), channel_id=1, source_target_pairs={{8,0},{12,4},{16,24},{20,28},{9,1},{13,5},{17,25},{21,29},{10,2},{... | collective-permute-start | bytes 1572872 | tf_op jit(solution)/shard_map/ppermute | solution.py:359
  70.1 16.4 %collective-permute-start.15 = (f32[256,512]{1,0:T(8,128)S(1)}, f32[256,512]{1,0:T(8,128)S(1)}, u32[]{:S(2)}, u32[]{:S(2)}) collective-permute-start(f32[256,512]{1,0:T(8,128)S(1)} %keep3.1.refs_1_.refs_2_), channel_id=1, source_target_pairs={{0,8},{4,12},{24,16},{28,20},{1,9},{5,13},{25,17},{29,21},{2,10},{... | collective-permute-start | bytes 1572872 | tf_op jit(solution)/shard_map/ppermute | solution.py:353
  75.7 12.1 %collective-permute-start.16 = (f32[128,1024]{1,0:T(8,128)S(1)}, f32[128,1024]{1,0:T(8,128)S(1)}, u32[]{:S(2)}, u32[]{:S(2)}) collective-permute-start(f32[128,1024]{1,0:T(8,128)S(1)} %zm2.1.refs_1_.refs_2_), channel_id=1, source_target_pairs={{8,16},{12,20},{16,8},{20,12},{9,17},{13,21},{17,9},{21,13},{10,18... | collective-permute-start | bytes 1572872 | tf_op jit(solution)/shard_map/ppermute | solution.py:356
  77.0 16.9 %collective-permute-start.17 = (f32[256,512]{1,0:T(8,128)S(1)}, f32[256,512]{1,0:T(8,128)S(1)}, u32[]{:S(2)}, u32[]{:S(2)}) collective-permute-start(f32[256,512]{1,0:T(8,128)S(1)} %zo1.1.refs_1_.refs_3_), channel_id=1, source_target_pairs={{8,0},{12,4},{16,24},{20,28},{9,1},{13,5},{17,25},{21,29},{10,2},{... | collective-permute-start | bytes 1572872 | tf_op jit(solution)/shard_map/ppermute | solution.py:359
  79.6 14.9 %collective-permute-start.18 = (f32[256,512]{1,0:T(8,128)S(1)}, f32[256,512]{1,0:T(8,128)S(1)}, u32[]{:S(2)}, u32[]{:S(2)}) collective-permute-start(f32[256,512]{1,0:T(8,128)S(1)} %send5.1.refs_1_), channel_id=1, source_target_pairs={{0,4},{4,0},{8,12},{12,8},{16,20},{20,16},{24,28},{28,24},{1,5},{5... | collective-permute-start | bytes 1572872 | tf_op jit(solution)/shard_map/ppermute | solution.py:52
  83.4 15.0 %collective-permute-start.19 = (f32[256,512]{1,0:T(8,128)S(1)}, f32[256,512]{1,0:T(8,128)S(1)}, u32[]{:S(2)}, u32[]{:S(2)}) collective-permute-start(f32[256,512]{1,0:T(8,128)S(1)} %keep4.1.refs_1_.refs_2_), channel_id=1, source_target_pairs={{0,8},{4,12},{24,16},{28,20},{1,9},{5,13},{25,17},{29,21},{2,10},{... | collective-permute-start | bytes 1572872 | tf_op jit(solution)/shard_map/ppermute | solution.py:353
  87.0 12.7 %collective-permute-start.20 = (f32[256,512]{1,0:T(8,128)S(1)}, f32[256,512]{1,0:T(8,128)S(1)}, u32[]{:S(2)}, u32[]{:S(2)}) collective-permute-start(f32[256,512]{1,0:T(8,128)S(1)} %zm3.1.refs_1_.refs_2_), channel_id=1, source_target_pairs={{8,16},{12,20},{16,8},{20,12},{9,17},{13,21},{17,9},{21,13},{10,18... | collective-permute-start | bytes 1572872 | tf_op jit(solution)/shard_map/ppermute | solution.py:356
  88.3 17.1 %collective-permute-start.21 = (f32[128,1024]{1,0:T(8,128)S(1)}, f32[128,1024]{1,0:T(8,128)S(1)}, u32[]{:S(2)}, u32[]{:S(2)}) collective-permute-start(f32[128,1024]{1,0:T(8,128)S(1)} %zo2.1.refs_1_.refs_3_), channel_id=1, source_target_pairs={{8,0},{12,4},{16,24},{20,28},{9,1},{13,5},{17,25},{21,29},{10,2},{... | collective-permute-start | bytes 1572872 | tf_op jit(solution)/shard_map/ppermute | solution.py:359
  94.5 11.7 %collective-permute-start.22 = (f32[128,1024]{1,0:T(8,128)S(1)}, f32[128,1024]{1,0:T(8,128)S(1)}, u32[]{:S(2)}, u32[]{:S(2)}) collective-permute-start(f32[128,1024]{1,0:T(8,128)S(1)} %ag0.1.refs_1_.refs_5_), channel_id=1, source_target_pairs={{0,4},{4,0},{8,12},{12,8},{16,20},{20,16},{24,28},{28,24},{1,5},{5... | collective-permute-start | bytes 1572872 | tf_op jit(solution)/shard_map/ppermute | solution.py:52
  95.7 11.3 %collective-permute-start.23 = (f32[256,512]{1,0:T(8,128)S(1)}, f32[256,512]{1,0:T(8,128)S(1)}, u32[]{:S(2)}, u32[]{:S(2)}) collective-permute-start(f32[256,512]{1,0:T(8,128)S(1)} %keep5.1.refs_1_.refs_3_), channel_id=1, source_target_pairs={{0,8},{4,12},{24,16},{28,20},{1,9},{5,13},{25,17},{29,21},{2,10},{... | collective-permute-start | bytes 1572872 | tf_op jit(solution)/shard_map/ppermute | solution.py:353
  99.1 9.2 %collective-permute-start.24 = (f32[256,512]{1,0:T(8,128)S(1)}, f32[256,512]{1,0:T(8,128)S(1)}, u32[]{:S(2)}, u32[]{:S(2)}) collective-permute-start(f32[256,512]{1,0:T(8,128)S(1)} %zm4.1.refs_1_.refs_2_), channel_id=1, source_target_pairs={{8,16},{12,20},{16,8},{20,12},{9,17},{13,21},{17,9},{21,13},{10,18... | collective-permute-start | bytes 1572872 | tf_op jit(solution)/shard_map/ppermute | solution.py:356
  100.4 16.7 %collective-permute-start.25 = (f32[256,512]{1,0:T(8,128)S(1)}, f32[256,512]{1,0:T(8,128)S(1)}, u32[]{:S(2)}, u32[]{:S(2)}) collective-permute-start(f32[256,512]{1,0:T(8,128)S(1)} %zo3.1.refs_1_.refs_3_), channel_id=1, source_target_pairs={{8,0},{12,4},{16,24},{20,28},{9,1},{13,5},{17,25},{21,29},{10,2},{... | collective-permute-start | bytes 1572872 | tf_op jit(solution)/shard_map/ppermute | solution.py:359
  106.1 11.6 %collective-permute-start.26 = (f32[256,512]{1,0:T(8,128)S(1)}, f32[256,512]{1,0:T(8,128)S(1)}, u32[]{:S(2)}, u32[]{:S(2)}) collective-permute-start(f32[256,512]{1,0:T(8,128)S(1)} %ag1.1.refs_1_.refs_2_.refs_5_), channel_id=1, source_target_pairs={{0,4},{4,0},{8,12},{12,8},{16,20},{20,16},{24,28},{28,24},{1,5},{5... | collective-permute-start | bytes 1572872 | tf_op jit(solution)/shard_map/ppermute | solution.py:52
  107.6 11.3 %collective-permute-start.27 = (f32[256,512]{1,0:T(8,128)S(1)}, f32[256,512]{1,0:T(8,128)S(1)}, u32[]{:S(2)}, u32[]{:S(2)}) collective-permute-start(f32[256,512]{1,0:T(8,128)S(1)} %zm5.1.refs_1_.refs_2_), channel_id=1, source_target_pairs={{8,16},{12,20},{16,8},{20,12},{9,17},{13,21},{17,9},{21,13},{10,18... | collective-permute-start | bytes 1572872 | tf_op jit(solution)/shard_map/ppermute | solution.py:356
  108.9 19.5 %collective-permute-start.28 = (f32[256,512]{1,0:T(8,128)S(1)}, f32[256,512]{1,0:T(8,128)S(1)}, u32[]{:S(2)}, u32[]{:S(2)}) collective-permute-start(f32[256,512]{1,0:T(8,128)S(1)} %zo4.1.refs_1_.refs_3_), channel_id=1, source_target_pairs={{8,0},{12,4},{16,24},{20,28},{9,1},{13,5},{17,25},{21,29},{10,2},{... | collective-permute-start | bytes 1572872 | tf_op jit(solution)/shard_map/ppermute | solution.py:359
  118.3 10.8 %collective-permute-start.29 = (f32[512,256]{1,0:T(8,128)S(1)}, f32[512,256]{1,0:T(8,128)S(1)}, u32[]{:S(2)}, u32[]{:S(2)}) collective-permute-start(f32[512,256]{1,0:T(8,128)S(1)} %g4.1.refs_1_.refs_2_), channel_id=1, source_target_pairs={{0,1},{1,0},{2,3},{3,2},{4,5},{5,4},{6,7},{7,6},{8,9},{9,8},{10,11... | collective-permute-start | bytes 1572872 | tf_op jit(solution)/shard_map/ppermute | solution.py:52
  118.4 16.2 %collective-permute-start.30 = (f32[128,1024]{1,0:T(8,128)S(1)}, f32[128,1024]{1,0:T(8,128)S(1)}, u32[]{:S(2)}, u32[]{:S(2)}) collective-permute-start(f32[128,1024]{1,0:T(8,128)S(1)} %ag2.1.refs_1_.refs_6_), channel_id=1, source_target_pairs={{0,4},{4,0},{8,12},{12,8},{16,20},{20,16},{24,28},{28,24},{1,5},{5... | collective-permute-start | bytes 1572872 | tf_op jit(solution)/shard_map/ppermute | solution.py:52
  119.5 22.5 %collective-permute-start.31 = (f32[256,512]{1,0:T(8,128)S(1)}, f32[256,512]{1,0:T(8,128)S(1)}, u32[]{:S(2)}, u32[]{:S(2)}) collective-permute-start(f32[256,512]{1,0:T(8,128)S(1)} %zo5.1.refs_1_.refs_3_), channel_id=1, source_target_pairs={{8,0},{12,4},{16,24},{20,28},{9,1},{13,5},{17,25},{21,29},{10,2},{... | collective-permute-start | bytes 1572872 | tf_op jit(solution)/shard_map/ppermute | solution.py:359
  129.0 15.4 %collective-permute-start.32 = (f32[256,512]{1,0:T(8,128)S(1)}, f32[256,512]{1,0:T(8,128)S(1)}, u32[]{:S(2)}, u32[]{:S(2)}) collective-permute-start(f32[256,512]{1,0:T(8,128)S(1)} %ag3.1.refs_1_.refs_5_), channel_id=1, source_target_pairs={{0,4},{4,0},{8,12},{12,8},{16,20},{20,16},{24,28},{28,24},{1,5},{5... | collective-permute-start | bytes 1572872 | tf_op jit(solution)/shard_map/ppermute | solution.py:52
  135.2 26.0 %collective-permute-start.34 = (f32[256,512]{1,0:T(8,128)S(1)}, f32[256,512]{1,0:T(8,128)S(1)}, u32[]{:S(2)}, u32[]{:S(2)}) collective-permute-start(f32[256,512]{1,0:T(8,128)S(1)} %ag4.1.refs_1_.refs_6_), channel_id=1, source_target_pairs={{0,4},{4,0},{8,12},{12,8},{16,20},{20,16},{24,28},{28,24},{1,5},{5... | collective-permute-start | bytes 1572872 | tf_op jit(solution)/shard_map/ppermute | solution.py:52
  142.8 23.6 %collective-permute-start.33 = (f32[256,512]{1,0:T(8,128)S(1)}, f32[256,512]{1,0:T(8,128)S(1)}, u32[]{:S(2)}, u32[]{:S(2)}) collective-permute-start(f32[256,512]{1,0:T(8,128)S(1)} %ag5.1.refs_1_.first_ref), channel_id=1, source_target_pairs={{0,4},{4,0},{8,12},{12,8},{16,20},{20,16},{24,28},{28,24},{1,5},{5... | collective-permute-start | bytes 1572872 | tf_op jit(solution)/shard_map/ppermute | solution.py:52

commit v6 on v5

--- a/solution.py
+++ b/solution.py
@@ -57,7 +57,7 @@
         self.last = []
         self.waits = []
 
-    def __call__(self, kernel, name, outs, flags, *operands, scratch=()):
+    def __call__(self, kernel, name, outs, flags, *operands, scratch=(), limit=12):
         after = self.last + self.waits
         n_in, n_after = len(operands), len(after)
         vmem = pl.BlockSpec(memory_space=pltpu.VMEM)
@@ -73,7 +73,7 @@
             out_specs=[vmem] * len(outs),
             scratch_shapes=list(scratch),
             name=name,
-            compiler_params=pltpu.CompilerParams(vmem_limit_bytes=24 * 2**20),
+            compiler_params=pltpu.CompilerParams(vmem_limit_bytes=limit * 2**20),
             cost_estimate=pl.CostEstimate(flops=1000, bytes_accessed=1000, transcendentals=0),
         )(flags, *after, *operands)
         self.last = [result[0]]
@@ -330,7 +330,7 @@
     for count in GROUPS:
         shape = (rows, count * width)
         shapes += [shape, (shape, bf16), (shape, bf16)]
-    cuts = chain(functools.partial(spread_kernel, parts), "rows_to_tiles", shapes, flags, flat)
+    cuts = chain(functools.partial(spread_kernel, parts), "rows_to_tiles", shapes, flags, flat, limit=24)
     cuts = [cuts[3 * k:3 * k + 3] for k in range(len(GROUPS))]
 
     def bring(which, name):

time: 171 us -> 171 us (level)
  no operation moved by 1% of the time
where the time goes in v6:
time: 171 us; the launch traced here: 170 us
  Pallas kernels  63.3 us (37%)
  starting transfers between devices  52 us (30%)
  waiting for transfers between devices  47.6 us (28%)
  local copies, waits for them, and re-layouts  6.18 us (4%)
    pallas_call x46, Pallas kernels, __call__(): pl.pallas_call(body, out_shape=[jax.ShapeDtypeStruct(*(o if isinstance(o[...  59.1 us
    ppermute x15, waiting for transfers between devices, flip(): return lax.ppermute(value, axis, [(i, i ^ bit) for i in range(n)])  23.4 us
    ppermute x6, waiting for transfers between devices, out_hop(): lax.ppermute(value, 'prow', [(2, 0), (3, 1), (4, 6), (5, 7)])  23.2 us
    ppermute x6, starting transfers between devices, in_hop(): lax.ppermute(value, 'prow', [(0, 2), (1, 3), (6, 4), (7, 5)])  21.1 us
    ppermute x15, starting transfers between devices, flip(): return lax.ppermute(value, axis, [(i, i ^ bit) for i in range(n)])  12.6 us
    ppermute x6, starting transfers between devices, out_hop(): lax.ppermute(value, 'prow', [(2, 0), (3, 1), (4, 6), (5, 7)])  7.93 us
    ppermute x2, starting transfers between devices, local(): came = [lax.ppermute(v, 'pcol', [(0, 2), (1, 3)]) for v in own]  6.17 us
    unnamed x6, local copies, waits for them, and re-layouts  4.28 us
  transfers between devices with their start and end apart: 35, of which 14 were waited for; matrix products, arithmetic and copies ran while one was open for 0% of the time, Pallas kernels for 34%

profile of v6, /device:TPU:0, one launch (start us, length us, event | category | flops | bytes accessed | tf_op | source)
XLA Modules:
  0.0 170.5 jit_solution(10803068726554727200)
XLA Ops:
  1.7 4.9 %collective-permute-start = (f32[512,128]{1,0:T(8,128)S(1)}, f32[512,128]{1,0:T(8,128)S(1)}, u32[]{:S(2)}, u32[]{:S(2)}) collective-permute-start(f32[512,128]{1,0:T(8,128)S(1)} %bitcast.19), channel_id=1, source_target_pairs={{0,2},{1,3},{4,6},{5,7},{8,10},{9,11},{12,14},{13,15},{16,18},{17,... | collective-permute-start | bytes 786440 | tf_op jit(solution)/shard_map/ppermute | solution.py:328
  7.3 1.3 collective-permute-start.2
  8.8 2.6 %copy-done = f32[512,11,1,256]{3,2,1,0:T(1,128)S(1)} copy-done((f32[512,11,1,256]{3,2,1,0:T(1,128)S(1)}, f32[512,11,1,256]{3,2,1,0:T(1,128)}, u32[]{:S(2)}) %copy-start) | copy-done | bytes 5767192
  11.4 2.5 %rows_to_tiles.1 = (f32[512,1024]{1,0:T(8,128)S(1)}, bf16[512,1024]{1,0:T(8,128)(2,1)S(1)}, bf16[512,1024]{1,0:T(8,128)(2,1)S(1)}, f32[512,256]{1,0:T(8,128)S(1)...) custom-call(s32[6]{0:T(128)S(1)} %stack.43.refs_0_, ...), custom_call_target="tpu_custom_call" | custom-call | flops 1000 | bytes 1000 | tf_op jit(solution)/shard_map/rows_to_tiles/pallas_call | solution.py:68
  16.3 1.5 collective-permute-done.1.refs_3_.refs_9_.refs_10_
  20.5 1.5 collective-permute-start.4
  22.8 1.4 send1.1.refs_1_
  24.2 1.4 collective-permute-start.5
  27.9 7.4 %collective-permute-done.4.refs_6_ = f32[128,1024]{1,0:T(8,128)S(1)} collective-permute-done((f32[128,1024]{1,0:T(8,128)S(1)}, f32[128,1024]{1,0:T(8,128)S(1)}, u32[]{:S(2)}, u32[]{:S(2)}) %collective-permute-start.4) | collective-permute-done | bytes 524320 | tf_op jit(solution)/shard_map/ppermute | solution.py:52
  36.4 3.5 %collective-permute-start.6 = (f32[128,1024]{1,0:T(8,128)S(1)}, f32[128,1024]{1,0:T(8,128)S(1)}, u32[]{:S(2)}, u32[]{:S(2)}) collective-permute-start(f32[128,1024]{1,0:T(8,128)S(1)} %keep0.1.refs_1_.refs_2_), channel_id=1, source_target_pairs={{0,8},{4,12},{24,16},{28,20},{1,9},{5,13},{25,17},{29,21},{2,10},{... | collective-permute-start | bytes 1572872 | tf_op jit(solution)/shard_map/ppermute | solution.py:353
  39.9 1.6 collective-permute-start.7
  43.7 2.8 %collective-permute-done.5.refs_8_ = f32[256,512]{1,0:T(8,128)S(1)} collective-permute-done((f32[256,512]{1,0:T(8,128)S(1)}, f32[256,512]{1,0:T(8,128)S(1)}, u32[]{:S(2)}, u32[]{:S(2)}) %collective-permute-start.5) | collective-permute-done | bytes 524320 | tf_op jit(solution)/shard_map/ppermute | solution.py:52
  46.5 1.4 keep1.1.refs_1_.refs_2_
  47.8 3.5 %collective-permute-start.8 = (f32[256,512]{1,0:T(8,128)S(1)}, f32[256,512]{1,0:T(8,128)S(1)}, u32[]{:S(2)}, u32[]{:S(2)}) collective-permute-start(f32[256,512]{1,0:T(8,128)S(1)} %keep1.1.refs_1_.refs_2_), channel_id=1, source_target_pairs={{0,8},{4,12},{24,16},{28,20},{1,9},{5,13},{25,17},{29,21},{2,10},{... | collective-permute-start | bytes 1572872 | tf_op jit(solution)/shard_map/ppermute | solution.py:353
  52.7 1.6 collective-permute-start.10
  54.3 3.4 %collective-permute-done.7.refs_6_ = f32[128,1024]{1,0:T(8,128)S(1)} collective-permute-done((f32[128,1024]{1,0:T(8,128)S(1)}, f32[128,1024]{1,0:T(8,128)S(1)}, u32[]{:S(2)}, u32[]{:S(2)}) %collective-permute-start.7) | collective-permute-done | bytes 524320 | tf_op jit(solution)/shard_map/ppermute | solution.py:52
  58.8 3.5 %collective-permute-start.11 = (f32[128,1024]{1,0:T(8,128)S(1)}, f32[128,1024]{1,0:T(8,128)S(1)}, u32[]{:S(2)}, u32[]{:S(2)}) collective-permute-start(f32[128,1024]{1,0:T(8,128)S(1)} %keep2.1.refs_1_.refs_2_), channel_id=1, source_target_pairs={{0,8},{4,12},{24,16},{28,20},{1,9},{5,13},{25,17},{29,21},{2,10},{... | collective-permute-start | bytes 1572872 | tf_op jit(solution)/shard_map/ppermute | solution.py:353
  63.7 1.6 collective-permute-start.14
  65.9 1.3 collective-permute-start.13
  67.2 1.8 %collective-permute-done.10.refs_8_ = f32[256,512]{1,0:T(8,128)S(1)} collective-permute-done((f32[256,512]{1,0:T(8,128)S(1)}, f32[256,512]{1,0:T(8,128)S(1)}, u32[]{:S(2)}, u32[]{:S(2)}) %collective-permute-start.10) | collective-permute-done | bytes 524320 | tf_op jit(solution)/shard_map/ppermute | solution.py:52
  70.1 4.9 %collective-permute-start.15 = (f32[256,512]{1,0:T(8,128)S(1)}, f32[256,512]{1,0:T(8,128)S(1)}, u32[]{:S(2)}, u32[]{:S(2)}) collective-permute-start(f32[256,512]{1,0:T(8,128)S(1)} %keep3.1.refs_1_.refs_2_), channel_id=1, source_target_pairs={{0,8},{4,12},{24,16},{28,20},{1,9},{5,13},{25,17},{29,21},{2,10},{... | collective-permute-start | bytes 1572872 | tf_op jit(solution)/shard_map/ppermute | solution.py:353
  76.9 1.3 collective-permute-start.17
  78.2 1.4 collective-permute-done.14.refs_9_
  79.6 1.5 collective-permute-start.18
  81.1 1.2 collective-permute-done.13.refs_2_.refs_4_
  83.4 2.9 %collective-permute-start.19 = (f32[256,512]{1,0:T(8,128)S(1)}, f32[256,512]{1,0:T(8,128)S(1)}, u32[]{:S(2)}, u32[]{:S(2)}) collective-permute-start(f32[256,512]{1,0:T(8,128)S(1)} %keep4.1.refs_1_.refs_2_), channel_id=1, source_target_pairs={{0,8},{4,12},{24,16},{28,20},{1,9},{5,13},{25,17},{29,21},{2,10},{... | collective-permute-start | bytes 1572872 | tf_op jit(solution)/shard_map/ppermute | solution.py:353
  88.2 1.3 collective-permute-start.21
  89.5 4.3 %collective-permute-done.17.refs_2_.refs_4_ = f32[256,512]{1,0:T(8,128)S(1)} collective-permute-done((f32[256,512]{1,0:T(8,128)S(1)}, f32[256,512]{1,0:T(8,128)S(1)}, u32[]{:S(2)}, u32[]{:S(2)}) %collective-permute-start.17) | collective-permute-done | bytes 524320 | tf_op jit(solution)/shard_map/ppermute | solution.py:359
  95.6 2.7 %collective-permute-start.23 = (f32[256,512]{1,0:T(8,128)S(1)}, f32[256,512]{1,0:T(8,128)S(1)}, u32[]{:S(2)}, u32[]{:S(2)}) collective-permute-start(f32[256,512]{1,0:T(8,128)S(1)} %keep5.1.refs_1_.refs_3_), channel_id=1, source_target_pairs={{0,8},{4,12},{24,16},{28,20},{1,9},{5,13},{25,17},{29,21},{2,10},{... | collective-permute-start | bytes 1572872 | tf_op jit(solution)/shard_map/ppermute | solution.py:353
  100.3 1.3 collective-permute-start.25
  101.6 3.7 %collective-permute-done.21.refs_2_.refs_4_ = f32[128,1024]{1,0:T(8,128)S(1)} collective-permute-done((f32[128,1024]{1,0:T(8,128)S(1)}, f32[128,1024]{1,0:T(8,128)S(1)}, u32[]{:S(2)}, u32[]{:S(2)}) %collective-permute-start.21) | collective-permute-done | bytes 524320 | tf_op jit(solution)/shard_map/ppermute | solution.py:359
  108.9 1.3 collective-permute-start.28
  110.2 6.8 %collective-permute-done.25.refs_2_.refs_4_ = f32[256,512]{1,0:T(8,128)S(1)} collective-permute-done((f32[256,512]{1,0:T(8,128)S(1)}, f32[256,512]{1,0:T(8,128)S(1)}, u32[]{:S(2)}, u32[]{:S(2)}) %collective-permute-start.25) | collective-permute-done | bytes 524320 | tf_op jit(solution)/shard_map/ppermute | solution.py:359
  119.5 1.5 collective-permute-start.31
  121.0 7.2 %collective-permute-done.28.refs_2_.refs_4_ = f32[256,512]{1,0:T(8,128)S(1)} collective-permute-done((f32[256,512]{1,0:T(8,128)S(1)}, f32[256,512]{1,0:T(8,128)S(1)}, u32[]{:S(2)}, u32[]{:S(2)}) %collective-permute-start.28) | collective-permute-done | bytes 524320 | tf_op jit(solution)/shard_map/ppermute | solution.py:359
  129.6 4.9 %factor0.1 = (f32[512,512]{1,0:T(8,128)S(1)}, f32[512,512]{1,0:T(8,128)S(1)}) custom-call(s32[6]{0:T(128)S(1)} %stack.43.refs_0_, f32[512,512]{1,0:T(8,128)S(1)} %g6.1.refs_1_.refs_2_, f32[512,512]{1,0:T(8,128)S(1)} %g6.1.refs_1_.refs_2_), custom_call_target="tpu_custom_call" | custom-call | flops 1000 | bytes 1000 | tf_op jit(solution)/shard_map/factor0/pallas_call | solution.py:68
  135.0 2.1 %collective-permute-start.34 = (f32[256,512]{1,0:T(8,128)S(1)}, f32[256,512]{1,0:T(8,128)S(1)}, u32[]{:S(2)}, u32[]{:S(2)}) collective-permute-start(f32[256,512]{1,0:T(8,128)S(1)} %ag4.1.refs_1_.refs_6_), channel_id=1, source_target_pairs={{0,4},{4,0},{8,12},{12,8},{16,20},{20,16},{24,28},{28,24},{1,5},{5... | collective-permute-start | bytes 1572872 | tf_op jit(solution)/shard_map/ppermute | solution.py:52
  137.1 4.7 %factor1.1 = (f32[512,512]{1,0:T(8,128)S(1)}, f32[512,512]{1,0:T(8,128)S(1)}) custom-call(s32[6]{0:T(128)S(1)} %stack.43.refs_0_, f32[256,512]{1,0:T(8,128)S(1)} %ag4.1.refs_1_.refs_6_, f32[512,512]{1,0:T(8,128)S(1)} %get-tuple-element.65.refs_1_.refs_2_, f32[512,512]{1,0:T(8,128)S(1)} %get-tuple-element.66.refs_3_), custom_call_target="tpu_custom_call" | custom-call | flops 1000 | bytes 1000 | tf_op jit(solution)/shard_map/factor1/pallas_call | solution.py:68
  142.8 1.5 collective-permute-done.32.refs_2_.refs_6_
  144.3 4.7 %factor2.1 = (f32[512,512]{1,0:T(8,128)S(1)}, f32[512,512]{1,0:T(8,128)S(1)}) custom-call(s32[6]{0:T(128)S(1)} %stack.43.refs_0_, f32[256,512]{1,0:T(8,128)S(1)} %ag5.1.refs_1_.first_ref, f32[256,512]{1,0:T(8,128)S(1)} %collective-permute-done.32.refs_2_.refs_6_, f32[512,512]{1,0:T(8,128)S(1)} %get-tuple-element.67.refs_1_.refs_3_, ...), custom_call_target="tpu_custom_call" | custom-call | flops 1000 | bytes 1000 | tf_op jit(solution)/shard_map/factor2/pallas_call | solution.py:68
  149.0 4.0 %factor3.1 = (f32[512,512]{1,0:T(8,128)S(1)}, f32[512,512]{1,0:T(8,128)S(1)}) custom-call(s32[6]{0:T(128)S(1)} %stack.43.refs_0_, f32[512,512]{1,0:T(8,128)S(1)} %get-tuple-element.69.refs_1_.refs_2_, f32[512,512]{1,0:T(8,128)S(1)} %get-tuple-element.69.refs_1_.refs_2_, f32[512,512]{1,0:T(8,128)S(1)} %get-tuple-element.70.refs_3_), custom_call_target="tpu_custom_call" | custom-call | flops 1000 | bytes 1000 | tf_op jit(solution)/shard_map/factor3/pallas_call | solution.py:68
  153.0 2.6 %weights.1 = (bf16[576,512]{1,0:T(8,128)(2,1)S(1)}, bf16[576,512]{1,0:T(8,128)(2,1)S(1)}) custom-call(s32[6]{0:T(128)S(1)} %stack.43.refs_0_, f32[512,512]{1,0:T(8,128)S(1)} %get-tuple-element.71.refs_1_, f32[512,128]{1,0:T(8,128)S(1)} %ka.1.refs_1_.refs_2_.refs_8_.refs_9_, f32[512,128]{1,0:T(8,128)S(1)} %collective-permute-done.1.refs_3_.refs_9_.refs_10_, ...), custom_call_target="tpu_custom_call" | custom-call | flops 1000 | bytes 1000 | tf_op jit(solution)/shard_map/weights/pallas_call | solution.py:68
  155.6 1.2 fin1.1
  156.8 2.6 %fin0.1 = (f32[512,1024]{1,0:T(8,128)S(1)}, f32[64,1024]{1,0:T(8,128)S(1)}) custom-call(s32[6]{0:T(128)S(1)} %stack.43.refs_0_, f32[512,256]{1,0:T(8,128)S(1)} %get-tuple-element.76.refs_1_, f32[512,1024]{1,0:T(8,128)S(1)} %get-tuple-element.46.refs_1_.refs_2_, bf16[576,512]{1,0:T(8,128)(2,1)S(1)} %get-tuple-element.73.refs_1_.refs_3_.refs_4_.high_ref.mine_high, ...), custom_call_target="tpu_custom_call" | custom-call | flops 1000 | bytes 1000 | tf_op jit(solution)/shard_map/fin0/pallas_call | solution.py:68
  159.4 1.6 fin3.1
  161.0 1.6 fin4.1
  162.7 3.6 %collective-permute-done.33.second_ref = f32[256,512]{1,0:T(8,128)S(1)} collective-permute-done((f32[256,512]{1,0:T(8,128)S(1)}, f32[256,512]{1,0:T(8,128)S(1)}, u32[]{:S(2)}, u32[]{:S(2)}) %collective-permute-start.33) | collective-permute-done | bytes 524320 | tf_op jit(solution)/shard_map/ppermute | solution.py:52
  166.3 4.2 %tiles_to_rows.1 = (f32[11264,128]{1,0:T(8,128)}, f32[1408,128]{1,0:T(8,128)}) custom-call(f32[512,512]{1,0:T(8,128)S(1)} %get-tuple-element.45.a_ref, bf16[576,512]{1,0:T(8,128)(2,1)S(1)} %get-tuple-element.73.refs_1_.refs_3_.refs_4_.high_ref.mine_high, bf16[576,512]{1,0:T(8,128)(2,1)S(1)} %get-tuple-element.74.refs_4_.refs_5_.low_ref.mine_low, ...), custom_call_target="tpu_custom_call" | custom-call | tf_op jit(solution)/shard_map/tiles_to_rows/pallas_call | solution.py:293
  (79 shorter events, 36.1 us)
Async XLA Ops:
  1.7 12.2 %collective-permute-start = (f32[512,128]{1,0:T(8,128)S(1)}, f32[512,128]{1,0:T(8,128)S(1)}, u32[]{:S(2)}, u32[]{:S(2)}) collective-permute-start(f32[512,128]{1,0:T(8,128)S(1)} %bitcast.19), channel_id=1, source_target_pairs={{0,2},{1,3},{4,6},{5,7},{8,10},{9,11},{12,14},{13,15},{16,18},{17,... | collective-permute-start | bytes 786440 | tf_op jit(solution)/shard_map/ppermute | solution.py:328
  7.3 12.4 %collective-permute-start.2 = (f32[544,128]{1,0:T(8,128)S(1)}, f32[544,128]{1,0:T(8,128)S(1)}, u32[]{:S(2)}, u32[]{:S(2)}) collective-permute-start(f32[544,128]{1,0:T(8,128)S(1)} %pad_maximum_fusion.refs_3_), channel_id=1, source_target_pairs={{0,2},{1,3},{4,6},{5,7},{8,10},{9,11},{12,14},{13,15},{16,18},{17,... | collective-permute-start | bytes 835592 | tf_op jit(solution)/shard_map/ppermute | solution.py:328
  8.8 2.6 %copy-start = (f32[512,11,1,256]{3,2,1,0:T(1,128)S(1)}, f32[512,11,1,256]{3,2,1,0:T(1,128)}, u32[]{:S(2)}) copy-start(f32[512,11,1,256]{3,2,1,0:T(1,128)} %param.1) | copy-start | bytes 17301508
  13.9 0.7 copy-start.1
  14.7 0.9 copy-start.2
  16.2 1.6 collective-permute-start.1
  20.3 1.7 %collective-permute-start.3 = (f32[512,128]{1,0:T(8,128)S(1)}, f32[512,128]{1,0:T(8,128)S(1)}, u32[]{:S(2)}, u32[]{:S(2)}) collective-permute-start(f32[512,128]{1,0:T(8,128)S(1)} %kb.1.refs_1_.refs_2_.refs_10_.refs_11_.refs_4_), channel_id=1, source_target_pairs={{0,1},{1,0},{2,3},{3,2},{4,5},{5,4},{6,7},{7,6},{8,9},{9,8},{10,11... | collective-permute-start | bytes 786440 | tf_op jit(solution)/shard_map/ppermute | solution.py:52
  20.5 14.8 %collective-permute-start.4 = (f32[128,1024]{1,0:T(8,128)S(1)}, f32[128,1024]{1,0:T(8,128)S(1)}, u32[]{:S(2)}, u32[]{:S(2)}) collective-permute-start(f32[128,1024]{1,0:T(8,128)S(1)} %send0.1.refs_1_), channel_id=1, source_target_pairs={{0,4},{4,0},{8,12},{12,8},{16,20},{20,16},{24,28},{28,24},{1,5},{5... | collective-permute-start | bytes 1572872 | tf_op jit(solution)/shard_map/ppermute | solution.py:52
  24.2 22.3 %collective-permute-start.5 = (f32[256,512]{1,0:T(8,128)S(1)}, f32[256,512]{1,0:T(8,128)S(1)}, u32[]{:S(2)}, u32[]{:S(2)}) collective-permute-start(f32[256,512]{1,0:T(8,128)S(1)} %send1.1.refs_1_), channel_id=1, source_target_pairs={{0,4},{4,0},{8,12},{12,8},{16,20},{20,16},{24,28},{28,24},{1,5},{5... | collective-permute-start | bytes 1572872 | tf_op jit(solution)/shard_map/ppermute | solution.py:52
  36.4 15.0 %collective-permute-start.6 = (f32[128,1024]{1,0:T(8,128)S(1)}, f32[128,1024]{1,0:T(8,128)S(1)}, u32[]{:S(2)}, u32[]{:S(2)}) collective-permute-start(f32[128,1024]{1,0:T(8,128)S(1)} %keep0.1.refs_1_.refs_2_), channel_id=1, source_target_pairs={{0,8},{4,12},{24,16},{28,20},{1,9},{5,13},{25,17},{29,21},{2,10},{... | collective-permute-start | bytes 1572872 | tf_op jit(solution)/shard_map/ppermute | solution.py:353
  39.9 17.8 %collective-permute-start.7 = (f32[128,1024]{1,0:T(8,128)S(1)}, f32[128,1024]{1,0:T(8,128)S(1)}, u32[]{:S(2)}, u32[]{:S(2)}) collective-permute-start(f32[128,1024]{1,0:T(8,128)S(1)} %send2.1.refs_1_), channel_id=1, source_target_pairs={{0,4},{4,0},{8,12},{12,8},{16,20},{20,16},{24,28},{28,24},{1,5},{5... | collective-permute-start | bytes 1572872 | tf_op jit(solution)/shard_map/ppermute | solution.py:52
  47.8 14.5 %collective-permute-start.8 = (f32[256,512]{1,0:T(8,128)S(1)}, f32[256,512]{1,0:T(8,128)S(1)}, u32[]{:S(2)}, u32[]{:S(2)}) collective-permute-start(f32[256,512]{1,0:T(8,128)S(1)} %keep1.1.refs_1_.refs_2_), channel_id=1, source_target_pairs={{0,8},{4,12},{24,16},{28,20},{1,9},{5,13},{25,17},{29,21},{2,10},{... | collective-permute-start | bytes 1572872 | tf_op jit(solution)/shard_map/ppermute | solution.py:353
  52.0 13.3 %collective-permute-start.9 = (f32[128,1024]{1,0:T(8,128)S(1)}, f32[128,1024]{1,0:T(8,128)S(1)}, u32[]{:S(2)}, u32[]{:S(2)}) collective-permute-start(f32[128,1024]{1,0:T(8,128)S(1)} %zm0.1.refs_1_.refs_2_), channel_id=1, source_target_pairs={{8,16},{12,20},{16,8},{20,12},{9,17},{13,21},{17,9},{21,13},{10,18... | collective-permute-start | bytes 1572872 | tf_op jit(solution)/shard_map/ppermute | solution.py:356
  52.7 16.3 %collective-permute-start.10 = (f32[256,512]{1,0:T(8,128)S(1)}, f32[256,512]{1,0:T(8,128)S(1)}, u32[]{:S(2)}, u32[]{:S(2)}) collective-permute-start(f32[256,512]{1,0:T(8,128)S(1)} %send3.1.refs_1_), channel_id=1, source_target_pairs={{0,4},{4,0},{8,12},{12,8},{16,20},{20,16},{24,28},{28,24},{1,5},{5... | collective-permute-start | bytes 1572872 | tf_op jit(solution)/shard_map/ppermute | solution.py:52
  58.8 16.2 %collective-permute-start.11 = (f32[128,1024]{1,0:T(8,128)S(1)}, f32[128,1024]{1,0:T(8,128)S(1)}, u32[]{:S(2)}, u32[]{:S(2)}) collective-permute-start(f32[128,1024]{1,0:T(8,128)S(1)} %keep2.1.refs_1_.refs_2_), channel_id=1, source_target_pairs={{0,8},{4,12},{24,16},{28,20},{1,9},{5,13},{25,17},{29,21},{2,10},{... | collective-permute-start | bytes 1572872 | tf_op jit(solution)/shard_map/ppermute | solution.py:353
  63.0 13.3 %collective-permute-start.12 = (f32[256,512]{1,0:T(8,128)S(1)}, f32[256,512]{1,0:T(8,128)S(1)}, u32[]{:S(2)}, u32[]{:S(2)}) collective-permute-start(f32[256,512]{1,0:T(8,128)S(1)} %zm1.1.refs_1_.refs_2_), channel_id=1, source_target_pairs={{8,16},{12,20},{16,8},{20,12},{9,17},{13,21},{17,9},{21,13},{10,18... | collective-permute-start | bytes 1572872 | tf_op jit(solution)/shard_map/ppermute | solution.py:356
  63.7 15.9 %collective-permute-start.14 = (f32[256,512]{1,0:T(8,128)S(1)}, f32[256,512]{1,0:T(8,128)S(1)}, u32[]{:S(2)}, u32[]{:S(2)}) collective-permute-start(f32[256,512]{1,0:T(8,128)S(1)} %send4.1.refs_1_), channel_id=1, source_target_pairs={{0,4},{4,0},{8,12},{12,8},{16,20},{20,16},{24,28},{28,24},{1,5},{5... | collective-permute-start | bytes 1572872 | tf_op jit(solution)/shard_map/ppermute | solution.py:52
  65.9 16.4 %collective-permute-start.13 = (f32[128,1024]{1,0:T(8,128)S(1)}, f32[128,1024]{1,0:T(8,128)S(1)}, u32[]{:S(2)}, u32[]{:S(2)}) collective-permute-start(f32[128,1024]{1,0:T(8,128)S(1)} %zo0.1.refs_1_.refs_3_), channel_id=1, source_target_pairs={{8,0},{12,4},{16,24},{20,28},{9,1},{13,5},{17,25},{21,29},{10,2},{... | collective-permute-start | bytes 1572872 | tf_op jit(solution)/shard_map/ppermute | solution.py:359
  70.1 16.2 %collective-permute-start.15 = (f32[256,512]{1,0:T(8,128)S(1)}, f32[256,512]{1,0:T(8,128)S(1)}, u32[]{:S(2)}, u32[]{:S(2)}) collective-permute-start(f32[256,512]{1,0:T(8,128)S(1)} %keep3.1.refs_1_.refs_2_), channel_id=1, source_target_pairs={{0,8},{4,12},{24,16},{28,20},{1,9},{5,13},{25,17},{29,21},{2,10},{... | collective-permute-start | bytes 1572872 | tf_op jit(solution)/shard_map/ppermute | solution.py:353
  75.6 12.0 %collective-permute-start.16 = (f32[128,1024]{1,0:T(8,128)S(1)}, f32[128,1024]{1,0:T(8,128)S(1)}, u32[]{:S(2)}, u32[]{:S(2)}) collective-permute-start(f32[128,1024]{1,0:T(8,128)S(1)} %zm2.1.refs_1_.refs_2_), channel_id=1, source_target_pairs={{8,16},{12,20},{16,8},{20,12},{9,17},{13,21},{17,9},{21,13},{10,18... | collective-permute-start | bytes 1572872 | tf_op jit(solution)/shard_map/ppermute | solution.py:356
  76.9 16.9 %collective-permute-start.17 = (f32[256,512]{1,0:T(8,128)S(1)}, f32[256,512]{1,0:T(8,128)S(1)}, u32[]{:S(2)}, u32[]{:S(2)}) collective-permute-start(f32[256,512]{1,0:T(8,128)S(1)} %zo1.1.refs_1_.refs_3_), channel_id=1, source_target_pairs={{8,0},{12,4},{16,24},{20,28},{9,1},{13,5},{17,25},{21,29},{10,2},{... | collective-permute-start | bytes 1572872 | tf_op jit(solution)/shard_map/ppermute | solution.py:359
  79.6 14.9 %collective-permute-start.18 = (f32[256,512]{1,0:T(8,128)S(1)}, f32[256,512]{1,0:T(8,128)S(1)}, u32[]{:S(2)}, u32[]{:S(2)}) collective-permute-start(f32[256,512]{1,0:T(8,128)S(1)} %send5.1.refs_1_), channel_id=1, source_target_pairs={{0,4},{4,0},{8,12},{12,8},{16,20},{20,16},{24,28},{28,24},{1,5},{5... | collective-permute-start | bytes 1572872 | tf_op jit(solution)/shard_map/ppermute | solution.py:52
  83.4 14.9 %collective-permute-start.19 = (f32[256,512]{1,0:T(8,128)S(1)}, f32[256,512]{1,0:T(8,128)S(1)}, u32[]{:S(2)}, u32[]{:S(2)}) collective-permute-start(f32[256,512]{1,0:T(8,128)S(1)} %keep4.1.refs_1_.refs_2_), channel_id=1, source_target_pairs={{0,8},{4,12},{24,16},{28,20},{1,9},{5,13},{25,17},{29,21},{2,10},{... | collective-permute-start | bytes 1572872 | tf_op jit(solution)/shard_map/ppermute | solution.py:353
  86.9 12.8 %collective-permute-start.20 = (f32[256,512]{1,0:T(8,128)S(1)}, f32[256,512]{1,0:T(8,128)S(1)}, u32[]{:S(2)}, u32[]{:S(2)}) collective-permute-start(f32[256,512]{1,0:T(8,128)S(1)} %zm3.1.refs_1_.refs_2_), channel_id=1, source_target_pairs={{8,16},{12,20},{16,8},{20,12},{9,17},{13,21},{17,9},{21,13},{10,18... | collective-permute-start | bytes 1572872 | tf_op jit(solution)/shard_map/ppermute | solution.py:356
  88.2 17.1 %collective-permute-start.21 = (f32[128,1024]{1,0:T(8,128)S(1)}, f32[128,1024]{1,0:T(8,128)S(1)}, u32[]{:S(2)}, u32[]{:S(2)}) collective-permute-start(f32[128,1024]{1,0:T(8,128)S(1)} %zo2.1.refs_1_.refs_3_), channel_id=1, source_target_pairs={{8,0},{12,4},{16,24},{20,28},{9,1},{13,5},{17,25},{21,29},{10,2},{... | collective-permute-start | bytes 1572872 | tf_op jit(solution)/shard_map/ppermute | solution.py:359
  94.4 11.5 %collective-permute-start.22 = (f32[128,1024]{1,0:T(8,128)S(1)}, f32[128,1024]{1,0:T(8,128)S(1)}, u32[]{:S(2)}, u32[]{:S(2)}) collective-permute-start(f32[128,1024]{1,0:T(8,128)S(1)} %ag0.1.refs_1_.refs_5_), channel_id=1, source_target_pairs={{0,4},{4,0},{8,12},{12,8},{16,20},{20,16},{24,28},{28,24},{1,5},{5... | collective-permute-start | bytes 1572872 | tf_op jit(solution)/shard_map/ppermute | solution.py:52
  95.6 11.4 %collective-permute-start.23 = (f32[256,512]{1,0:T(8,128)S(1)}, f32[256,512]{1,0:T(8,128)S(1)}, u32[]{:S(2)}, u32[]{:S(2)}) collective-permute-start(f32[256,512]{1,0:T(8,128)S(1)} %keep5.1.refs_1_.refs_3_), channel_id=1, source_target_pairs={{0,8},{4,12},{24,16},{28,20},{1,9},{5,13},{25,17},{29,21},{2,10},{... | collective-permute-start | bytes 1572872 | tf_op jit(solution)/shard_map/ppermute | solution.py:353
  98.9 9.4 %collective-permute-start.24 = (f32[256,512]{1,0:T(8,128)S(1)}, f32[256,512]{1,0:T(8,128)S(1)}, u32[]{:S(2)}, u32[]{:S(2)}) collective-permute-start(f32[256,512]{1,0:T(8,128)S(1)} %zm4.1.refs_1_.refs_2_), channel_id=1, source_target_pairs={{8,16},{12,20},{16,8},{20,12},{9,17},{13,21},{17,9},{21,13},{10,18... | collective-permute-start | bytes 1572872 | tf_op jit(solution)/shard_map/ppermute | solution.py:356
  100.3 16.7 %collective-permute-start.25 = (f32[256,512]{1,0:T(8,128)S(1)}, f32[256,512]{1,0:T(8,128)S(1)}, u32[]{:S(2)}, u32[]{:S(2)}) collective-permute-start(f32[256,512]{1,0:T(8,128)S(1)} %zo3.1.refs_1_.refs_3_), channel_id=1, source_target_pairs={{8,0},{12,4},{16,24},{20,28},{9,1},{13,5},{17,25},{21,29},{10,2},{... | collective-permute-start | bytes 1572872 | tf_op jit(solution)/shard_map/ppermute | solution.py:359
  105.9 11.7 %collective-permute-start.26 = (f32[256,512]{1,0:T(8,128)S(1)}, f32[256,512]{1,0:T(8,128)S(1)}, u32[]{:S(2)}, u32[]{:S(2)}) collective-permute-start(f32[256,512]{1,0:T(8,128)S(1)} %ag1.1.refs_1_.refs_2_.refs_5_), channel_id=1, source_target_pairs={{0,4},{4,0},{8,12},{12,8},{16,20},{20,16},{24,28},{28,24},{1,5},{5... | collective-permute-start | bytes 1572872 | tf_op jit(solution)/shard_map/ppermute | solution.py:52
  107.6 11.3 %collective-permute-start.27 = (f32[256,512]{1,0:T(8,128)S(1)}, f32[256,512]{1,0:T(8,128)S(1)}, u32[]{:S(2)}, u32[]{:S(2)}) collective-permute-start(f32[256,512]{1,0:T(8,128)S(1)} %zm5.1.refs_1_.refs_2_), channel_id=1, source_target_pairs={{8,16},{12,20},{16,8},{20,12},{9,17},{13,21},{17,9},{21,13},{10,18... | collective-permute-start | bytes 1572872 | tf_op jit(solution)/shard_map/ppermute | solution.py:356
  108.9 19.4 %collective-permute-start.28 = (f32[256,512]{1,0:T(8,128)S(1)}, f32[256,512]{1,0:T(8,128)S(1)}, u32[]{:S(2)}, u32[]{:S(2)}) collective-permute-start(f32[256,512]{1,0:T(8,128)S(1)} %zo4.1.refs_1_.refs_3_), channel_id=1, source_target_pairs={{8,0},{12,4},{16,24},{20,28},{9,1},{13,5},{17,25},{21,29},{10,2},{... | collective-permute-start | bytes 1572872 | tf_op jit(solution)/shard_map/ppermute | solution.py:359
  118.2 10.8 %collective-permute-start.29 = (f32[512,256]{1,0:T(8,128)S(1)}, f32[512,256]{1,0:T(8,128)S(1)}, u32[]{:S(2)}, u32[]{:S(2)}) collective-permute-start(f32[512,256]{1,0:T(8,128)S(1)} %g4.1.refs_1_.refs_2_), channel_id=1, source_target_pairs={{0,1},{1,0},{2,3},{3,2},{4,5},{5,4},{6,7},{7,6},{8,9},{9,8},{10,11... | collective-permute-start | bytes 1572872 | tf_op jit(solution)/shard_map/ppermute | solution.py:52
  118.2 16.2 %collective-permute-start.30 = (f32[128,1024]{1,0:T(8,128)S(1)}, f32[128,1024]{1,0:T(8,128)S(1)}, u32[]{:S(2)}, u32[]{:S(2)}) collective-permute-start(f32[128,1024]{1,0:T(8,128)S(1)} %ag2.1.refs_1_.refs_6_), channel_id=1, source_target_pairs={{0,4},{4,0},{8,12},{12,8},{16,20},{20,16},{24,28},{28,24},{1,5},{5... | collective-permute-start | bytes 1572872 | tf_op jit(solution)/shard_map/ppermute | solution.py:52
  119.5 22.3 %collective-permute-start.31 = (f32[256,512]{1,0:T(8,128)S(1)}, f32[256,512]{1,0:T(8,128)S(1)}, u32[]{:S(2)}, u32[]{:S(2)}) collective-permute-start(f32[256,512]{1,0:T(8,128)S(1)} %zo5.1.refs_1_.refs_3_), channel_id=1, source_target_pairs={{8,0},{12,4},{16,24},{20,28},{9,1},{13,5},{17,25},{21,29},{10,2},{... | collective-permute-start | bytes 1572872 | tf_op jit(solution)/shard_map/ppermute | solution.py:359
  128.9 15.4 %collective-permute-start.32 = (f32[256,512]{1,0:T(8,128)S(1)}, f32[256,512]{1,0:T(8,128)S(1)}, u32[]{:S(2)}, u32[]{:S(2)}) collective-permute-start(f32[256,512]{1,0:T(8,128)S(1)} %ag3.1.refs_1_.refs_5_), channel_id=1, source_target_pairs={{0,4},{4,0},{8,12},{12,8},{16,20},{20,16},{24,28},{28,24},{1,5},{5... | collective-permute-start | bytes 1572872 | tf_op jit(solution)/shard_map/ppermute | solution.py:52
  135.0 26.0 %collective-permute-start.34 = (f32[256,512]{1,0:T(8,128)S(1)}, f32[256,512]{1,0:T(8,128)S(1)}, u32[]{:S(2)}, u32[]{:S(2)}) collective-permute-start(f32[256,512]{1,0:T(8,128)S(1)} %ag4.1.refs_1_.refs_6_), channel_id=1, source_target_pairs={{0,4},{4,0},{8,12},{12,8},{16,20},{20,16},{24,28},{28,24},{1,5},{5... | collective-permute-start | bytes 1572872 | tf_op jit(solution)/shard_map/ppermute | solution.py:52
  142.7 23.6 %collective-permute-start.33 = (f32[256,512]{1,0:T(8,128)S(1)}, f32[256,512]{1,0:T(8,128)S(1)}, u32[]{:S(2)}, u32[]{:S(2)}) collective-permute-start(f32[256,512]{1,0:T(8,128)S(1)} %ag5.1.refs_1_.first_ref), channel_id=1, source_target_pairs={{0,4},{4,0},{8,12},{12,8},{16,20},{20,16},{24,28},{28,24},{1,5},{5... | collective-permute-start | bytes 1572872 | tf_op jit(solution)/shard_map/ppermute | solution.py:52

commit v7 on v5

--- a/solution.py
+++ b/solution.py
@@ -16,10 +16,10 @@
 GROUPS = (4, 1, 2, 2, 2)
 GROUP_OF = (0, 1, 0, 2, 3, 4)
 ORDER = (
-    "ka pa send0 kb", "pb send1 send2 send3", "keep0 send4 send5 keep1", "zm0 keep2 zm1 zo0",
-    "keep3 zm2 zo1 ~zo0", "keep4 zm3 zo2 ~zo1", "ag0 keep5 zm4 zo3", "~zo2 ag1 ~ag0 zm5",
-    "zo4 ~zo3 ag2 g4", "zo5 ~zo4 ag3 g6", "ch0 ~ag2 ag4 ch1", "~zo5 ag5 ~ag3 ch2",
-    "ch3 weights fin1 fin0", "fin3 ~ag4 fin4",
+    "ka pa send0 kb", "pb send1 send2 send3", "keep0 send4 send5 keep1", "zm0 keep2 zm1 ~send3",
+    "zo0 keep3 zm2 zo1", "~zo0 keep4 zm3 zo2", "~zo1 ag0 keep5 zm4", "zo3 ~zo2 ag1 ~ag0",
+    "zm5 zo4 ~zo3 ag2", "g4 ~zo4 ag3 zo5", "g6 ch0 ~ag2 ag4", "ch1 ~zo5 ag5 ch2",
+    "~ag3 ch3 weights fin1", "fin0 fin3 ~ag4 fin4",
 )
 
 

time: 171 us -> 175 us (1.023)
  starting transfers between devices: 52.1 us -> 58.9 us
    ppermute x15, starting transfers between devices: 12.5 us -> 17.7 us  [flip(): return lax.ppermute(value, axis, [(i, i ^ bit) for i in range(n)])]
    ppermute x15, waiting for transfers between devices: 23.2 us -> 19 us  [flip(): return lax.ppermute(value, axis, [(i, i ^ bit) for i in range(n)])]
    ppermute x2, waiting for transfers between devices: 0.01 us -> 3.27 us  [local(): came = [lax.ppermute(v, 'pcol', [(0, 2), (1, 3)]) for v in own]]
    ppermute x2, starting transfers between devices: 6.17 us -> 9.26 us  [local(): came = [lax.ppermute(v, 'pcol', [(0, 2), (1, 3)]) for v in own]]
    unnamed x6 -> x2, local copies, waits for them, and re-layouts: 4.28 us -> 2.64 us
  transfers between devices with their start and end apart: 35 -> 35, of which waited for: 14 -> 13; matrix products, arithmetic and copies ran while one was open for 0% -> 0% of each run, Pallas kernels for 34% -> 34%
where the time goes in v7:
time: 175 us
  Pallas kernels  63.4 us (36%)
  starting transfers between devices  58.9 us (34%)
  waiting for transfers between devices  46.4 us (27%)
  local copies, waits for them, and re-layouts  4.53 us (3%)
    pallas_call x46, Pallas kernels, __call__(): pl.pallas_call(body, out_shape=[jax.ShapeDtypeStruct(*(o if isinstance(o[...  59.2 us
    ppermute x6, waiting for transfers between devices, out_hop(): lax.ppermute(value, 'prow', [(2, 0), (3, 1), (4, 6), (5, 7)])  24.1 us
    ppermute x6, starting transfers between devices, in_hop(): lax.ppermute(value, 'prow', [(0, 2), (1, 3), (6, 4), (7, 5)])  19.8 us
    ppermute x15, waiting for transfers between devices, flip(): return lax.ppermute(value, axis, [(i, i ^ bit) for i in range(n)])  19 us
    ppermute x15, starting transfers between devices, flip(): return lax.ppermute(value, axis, [(i, i ^ bit) for i in range(n)])  17.7 us
    ppermute x2, starting transfers between devices, local(): came = [lax.ppermute(v, 'pcol', [(0, 2), (1, 3)]) for v in own]  9.26 us
    ppermute x6, starting transfers between devices, out_hop(): lax.ppermute(value, 'prow', [(2, 0), (3, 1), (4, 6), (5, 7)])  7.93 us
    pallas_call x1, Pallas kernels, in_rows(): pl.pallas_call(functools.partial(rows_kernel, parts, len(rests)), grid=(r...  4.21 us
  transfers between devices with their start and end apart: 35, of which 13 were waited for; matrix products, arithmetic and copies ran while one was open for 0% of the time, Pallas kernels for 34%

profile of v7, /device:TPU:0, one launch (start us, length us, event | category | flops | bytes accessed | tf_op | source)
XLA Modules:
  0.0 174.6 jit_solution(13733439707686591589)
XLA Ops:
  1.7 4.9 %collective-permute-start = (f32[512,128]{1,0:T(8,128)S(1)}, f32[512,128]{1,0:T(8,128)S(1)}, u32[]{:S(2)}, u32[]{:S(2)}) collective-permute-start(f32[512,128]{1,0:T(8,128)S(1)} %bitcast.19), channel_id=1, source_target_pairs={{0,2},{1,3},{4,6},{5,7},{8,10},{9,11},{12,14},{13,15},{16,18},{17,... | collective-permute-start | bytes 786440 | tf_op jit(solution)/shard_map/ppermute | solution.py:328
  6.7 2.6 %copy-done = f32[512,11,1,256]{3,2,1,0:T(1,128)S(1)} copy-done((f32[512,11,1,256]{3,2,1,0:T(1,128)S(1)}, f32[512,11,1,256]{3,2,1,0:T(1,128)}, u32[]{:S(2)}) %copy-start) | copy-done | bytes 5767192
  9.3 2.5 %rows_to_tiles.1 = (f32[512,1024]{1,0:T(8,128)S(1)}, bf16[512,1024]{1,0:T(8,128)(2,1)S(1)}, bf16[512,1024]{1,0:T(8,128)(2,1)S(1)}, f32[512,256]{1,0:T(8,128)S(1)...) custom-call(s32[6]{0:T(128)S(1)} %stack.43.refs_0_, ...), custom_call_target="tpu_custom_call" | custom-call | flops 1000 | bytes 1000 | tf_op jit(solution)/shard_map/rows_to_tiles/pallas_call | solution.py:68
  13.5 4.4 %collective-permute-start.2 = (f32[544,128]{1,0:T(8,128)S(1)}, f32[544,128]{1,0:T(8,128)S(1)}, u32[]{:S(2)}, u32[]{:S(2)}) collective-permute-start(f32[544,128]{1,0:T(8,128)S(1)} %pad_maximum_fusion.refs_3_), channel_id=1, source_target_pairs={{0,2},{1,3},{4,6},{5,7},{8,10},{9,11},{12,14},{13,15},{16,18},{17,... | collective-permute-start | bytes 835592 | tf_op jit(solution)/shard_map/ppermute | solution.py:328
  19.8 1.6 collective-permute-start.4
  21.4 3.0 %collective-permute-done.2.refs_2_ = f32[544,128]{1,0:T(8,128)S(1)} collective-permute-done((f32[544,128]{1,0:T(8,128)S(1)}, f32[544,128]{1,0:T(8,128)S(1)}, u32[]{:S(2)}, u32[]{:S(2)}) %collective-permute-start.2) | collective-permute-done | bytes 278560 | tf_op jit(solution)/shard_map/ppermute | solution.py:328
  25.1 1.5 collective-permute-done.3.refs_3_.refs_11_.refs_12_.refs_5_
  27.4 1.4 send1.1.refs_1_
  28.8 1.6 collective-permute-start.5
  32.6 2.0 %collective-permute-done.4.refs_6_ = f32[128,1024]{1,0:T(8,128)S(1)} collective-permute-done((f32[128,1024]{1,0:T(8,128)S(1)}, f32[128,1024]{1,0:T(8,128)S(1)}, u32[]{:S(2)}, u32[]{:S(2)}) %collective-permute-start.4) | collective-permute-done | bytes 524320 | tf_op jit(solution)/shard_map/ppermute | solution.py:52
  35.8 3.5 %collective-permute-start.6 = (f32[128,1024]{1,0:T(8,128)S(1)}, f32[128,1024]{1,0:T(8,128)S(1)}, u32[]{:S(2)}, u32[]{:S(2)}) collective-permute-start(f32[128,1024]{1,0:T(8,128)S(1)} %keep0.1.refs_1_.refs_2_), channel_id=1, source_target_pairs={{0,8},{4,12},{24,16},{28,20},{1,9},{5,13},{25,17},{29,21},{2,10},{... | collective-permute-start | bytes 1572872 | tf_op jit(solution)/shard_map/ppermute | solution.py:353
  39.3 1.6 collective-permute-start.7
  43.1 2.8 %collective-permute-done.5.refs_8_ = f32[256,512]{1,0:T(8,128)S(1)} collective-permute-done((f32[256,512]{1,0:T(8,128)S(1)}, f32[256,512]{1,0:T(8,128)S(1)}, u32[]{:S(2)}, u32[]{:S(2)}) %collective-permute-start.5) | collective-permute-done | bytes 524320 | tf_op jit(solution)/shard_map/ppermute | solution.py:52
  45.9 1.4 keep1.1.refs_1_.refs_2_
  47.3 3.5 %collective-permute-start.8 = (f32[256,512]{1,0:T(8,128)S(1)}, f32[256,512]{1,0:T(8,128)S(1)}, u32[]{:S(2)}, u32[]{:S(2)}) collective-permute-start(f32[256,512]{1,0:T(8,128)S(1)} %keep1.1.refs_1_.refs_2_), channel_id=1, source_target_pairs={{0,8},{4,12},{24,16},{28,20},{1,9},{5,13},{25,17},{29,21},{2,10},{... | collective-permute-start | bytes 1572872 | tf_op jit(solution)/shard_map/ppermute | solution.py:353
  50.8 1.6 collective-permute-start.9
  53.7 3.4 %collective-permute-done.7.refs_6_ = f32[128,1024]{1,0:T(8,128)S(1)} collective-permute-done((f32[128,1024]{1,0:T(8,128)S(1)}, f32[128,1024]{1,0:T(8,128)S(1)}, u32[]{:S(2)}, u32[]{:S(2)}) %collective-permute-start.7) | collective-permute-done | bytes 524320 | tf_op jit(solution)/shard_map/ppermute | solution.py:52
  58.3 3.5 %collective-permute-start.11 = (f32[128,1024]{1,0:T(8,128)S(1)}, f32[128,1024]{1,0:T(8,128)S(1)}, u32[]{:S(2)}, u32[]{:S(2)}) collective-permute-start(f32[128,1024]{1,0:T(8,128)S(1)} %keep2.1.refs_1_.refs_2_), channel_id=1, source_target_pairs={{0,8},{4,12},{24,16},{28,20},{1,9},{5,13},{25,17},{29,21},{2,10},{... | collective-permute-start | bytes 1572872 | tf_op jit(solution)/shard_map/ppermute | solution.py:353
  63.1 1.6 collective-permute-start.14
  64.7 3.7 %collective-permute-done.9.refs_2_.refs_8_ = f32[256,512]{1,0:T(8,128)S(1)} collective-permute-done((f32[256,512]{1,0:T(8,128)S(1)}, f32[256,512]{1,0:T(8,128)S(1)}, u32[]{:S(2)}, u32[]{:S(2)}) %collective-permute-start.9) | collective-permute-done | bytes 524320 | tf_op jit(solution)/shard_map/ppermute | solution.py:52
  69.0 1.3 collective-permute-start.13
  71.4 4.6 %collective-permute-start.15 = (f32[256,512]{1,0:T(8,128)S(1)}, f32[256,512]{1,0:T(8,128)S(1)}, u32[]{:S(2)}, u32[]{:S(2)}) collective-permute-start(f32[256,512]{1,0:T(8,128)S(1)} %keep3.1.refs_1_.refs_2_), channel_id=1, source_target_pairs={{0,8},{4,12},{24,16},{28,20},{1,9},{5,13},{25,17},{29,21},{2,10},{... | collective-permute-start | bytes 1572872 | tf_op jit(solution)/shard_map/ppermute | solution.py:353
  77.9 1.3 collective-permute-start.17
  79.3 1.6 collective-permute-start.18
  80.8 4.4 %collective-permute-done.13.refs_2_.refs_4_ = f32[128,1024]{1,0:T(8,128)S(1)} collective-permute-done((f32[128,1024]{1,0:T(8,128)S(1)}, f32[128,1024]{1,0:T(8,128)S(1)}, u32[]{:S(2)}, u32[]{:S(2)}) %collective-permute-start.13) | collective-permute-done | bytes 524320 | tf_op jit(solution)/shard_map/ppermute | solution.py:359
  86.4 1.5 collective-permute-start.19
  89.8 1.3 collective-permute-start.21
  91.1 4.7 %collective-permute-done.17.refs_2_.refs_4_ = f32[256,512]{1,0:T(8,128)S(1)} collective-permute-done((f32[256,512]{1,0:T(8,128)S(1)}, f32[256,512]{1,0:T(8,128)S(1)}, u32[]{:S(2)}, u32[]{:S(2)}) %collective-permute-start.17) | collective-permute-done | bytes 524320 | tf_op jit(solution)/shard_map/ppermute | solution.py:359
  96.4 1.6 collective-permute-start.22
  99.1 3.2 %collective-permute-start.23 = (f32[256,512]{1,0:T(8,128)S(1)}, f32[256,512]{1,0:T(8,128)S(1)}, u32[]{:S(2)}, u32[]{:S(2)}) collective-permute-start(f32[256,512]{1,0:T(8,128)S(1)} %keep5.1.refs_1_.refs_3_), channel_id=1, source_target_pairs={{0,8},{4,12},{24,16},{28,20},{1,9},{5,13},{25,17},{29,21},{2,10},{... | collective-permute-start | bytes 1572872 | tf_op jit(solution)/shard_map/ppermute | solution.py:353
  104.3 1.3 collective-permute-start.25
  105.6 2.2 %collective-permute-done.21.refs_2_.refs_4_ = f32[128,1024]{1,0:T(8,128)S(1)} collective-permute-done((f32[128,1024]{1,0:T(8,128)S(1)}, f32[128,1024]{1,0:T(8,128)S(1)}, u32[]{:S(2)}, u32[]{:S(2)}) %collective-permute-start.21) | collective-permute-done | bytes 524320 | tf_op jit(solution)/shard_map/ppermute | solution.py:359
  108.4 2.0 %collective-permute-start.26 = (f32[256,512]{1,0:T(8,128)S(1)}, f32[256,512]{1,0:T(8,128)S(1)}, u32[]{:S(2)}, u32[]{:S(2)}) collective-permute-start(f32[256,512]{1,0:T(8,128)S(1)} %ag1.1.refs_1_.refs_2_.refs_5_), channel_id=1, source_target_pairs={{0,4},{4,0},{8,12},{12,8},{16,20},{20,16},{24,28},{28,24},{1,5},{5... | collective-permute-start | bytes 1572872 | tf_op jit(solution)/shard_map/ppermute | solution.py:52
  113.6 7.5 %collective-permute-done.25.refs_2_.refs_4_ = f32[256,512]{1,0:T(8,128)S(1)} collective-permute-done((f32[256,512]{1,0:T(8,128)S(1)}, f32[256,512]{1,0:T(8,128)S(1)}, u32[]{:S(2)}, u32[]{:S(2)}) %collective-permute-start.25) | collective-permute-done | bytes 524320 | tf_op jit(solution)/shard_map/ppermute | solution.py:359
  123.0 5.3 %collective-permute-done.27.refs_2_.refs_4_ = f32[256,512]{1,0:T(8,128)S(1)} collective-permute-done((f32[256,512]{1,0:T(8,128)S(1)}, f32[256,512]{1,0:T(8,128)S(1)}, u32[]{:S(2)}, u32[]{:S(2)}) %collective-permute-start.27) | collective-permute-done | bytes 524320 | tf_op jit(solution)/shard_map/ppermute | solution.py:359
  129.5 1.5 collective-permute-start.31
  131.0 1.6 collective-permute-start.32
  133.2 4.9 %factor0.1 = (f32[512,512]{1,0:T(8,128)S(1)}, f32[512,512]{1,0:T(8,128)S(1)}) custom-call(s32[6]{0:T(128)S(1)} %stack.43.refs_0_, f32[512,512]{1,0:T(8,128)S(1)} %g6.1.refs_1_.refs_2_, f32[512,512]{1,0:T(8,128)S(1)} %g6.1.refs_1_.refs_2_), custom_call_target="tpu_custom_call" | custom-call | flops 1000 | bytes 1000 | tf_op jit(solution)/shard_map/factor0/pallas_call | solution.py:68
  139.3 4.7 %factor1.1 = (f32[512,512]{1,0:T(8,128)S(1)}, f32[512,512]{1,0:T(8,128)S(1)}) custom-call(s32[6]{0:T(128)S(1)} %stack.43.refs_0_, f32[256,512]{1,0:T(8,128)S(1)} %ag4.1.refs_1_.refs_6_, f32[512,512]{1,0:T(8,128)S(1)} %get-tuple-element.65.refs_1_.refs_2_, f32[512,512]{1,0:T(8,128)S(1)} %get-tuple-element.66.refs_3_), custom_call_target="tpu_custom_call" | custom-call | flops 1000 | bytes 1000 | tf_op jit(solution)/shard_map/factor1/pallas_call | solution.py:68
  144.8 1.6 collective-permute-start.33
  146.4 4.7 %factor2.1 = (f32[512,512]{1,0:T(8,128)S(1)}, f32[512,512]{1,0:T(8,128)S(1)}) custom-call(s32[6]{0:T(128)S(1)} %stack.43.refs_0_, f32[256,512]{1,0:T(8,128)S(1)} %ag5.1.refs_1_.first_ref, f32[512,512]{1,0:T(8,128)S(1)} %get-tuple-element.67.refs_1_.refs_2_, f32[512,512]{1,0:T(8,128)S(1)} %get-tuple-element.68.refs_3_), custom_call_target="tpu_custom_call" | custom-call | flops 1000 | bytes 1000 | tf_op jit(solution)/shard_map/factor2/pallas_call | solution.py:68
  151.2 4.0 %factor3.1 = (f32[512,512]{1,0:T(8,128)S(1)}, f32[512,512]{1,0:T(8,128)S(1)}) custom-call(s32[6]{0:T(128)S(1)} %stack.43.refs_0_, f32[512,512]{1,0:T(8,128)S(1)} %get-tuple-element.69.refs_1_.refs_3_, f32[256,512]{1,0:T(8,128)S(1)} %collective-permute-done.32.refs_2_.refs_6_, f32[512,512]{1,0:T(8,128)S(1)} %get-tuple-element.69.refs_1_.refs_3_, ...), custom_call_target="tpu_custom_call" | custom-call | flops 1000 | bytes 1000 | tf_op jit(solution)/shard_map/factor3/pallas_call | solution.py:68
  155.2 2.6 %weights.1 = (bf16[576,512]{1,0:T(8,128)(2,1)S(1)}, bf16[576,512]{1,0:T(8,128)(2,1)S(1)}) custom-call(s32[6]{0:T(128)S(1)} %stack.43.refs_0_, f32[512,512]{1,0:T(8,128)S(1)} %get-tuple-element.71.refs_1_, f32[512,128]{1,0:T(8,128)S(1)} %ka.1.refs_1_.refs_2_.refs_8_.refs_9_, f32[512,128]{1,0:T(8,128)S(1)} %collective-permute-done.1.refs_3_.refs_9_.refs_10_, ...), custom_call_target="tpu_custom_call" | custom-call | flops 1000 | bytes 1000 | tf_op jit(solution)/shard_map/weights/pallas_call | solution.py:68
  159.0 2.6 %fin0.1 = (f32[512,1024]{1,0:T(8,128)S(1)}, f32[64,1024]{1,0:T(8,128)S(1)}) custom-call(s32[6]{0:T(128)S(1)} %stack.43.refs_0_, f32[512,256]{1,0:T(8,128)S(1)} %get-tuple-element.76.refs_1_, f32[512,1024]{1,0:T(8,128)S(1)} %get-tuple-element.46.refs_1_.refs_2_, bf16[576,512]{1,0:T(8,128)(2,1)S(1)} %get-tuple-element.73.refs_1_.refs_3_.refs_4_.high_ref.mine_high, ...), custom_call_target="tpu_custom_call" | custom-call | flops 1000 | bytes 1000 | tf_op jit(solution)/shard_map/fin0/pallas_call | solution.py:68
  161.6 1.6 fin3.1
  163.2 1.6 fin4.1
  164.9 5.5 %collective-permute-done.33.second_ref = f32[256,512]{1,0:T(8,128)S(1)} collective-permute-done((f32[256,512]{1,0:T(8,128)S(1)}, f32[256,512]{1,0:T(8,128)S(1)}, u32[]{:S(2)}, u32[]{:S(2)}) %collective-permute-start.33) | collective-permute-done | bytes 524320 | tf_op jit(solution)/shard_map/ppermute | solution.py:52
  170.4 4.2 %tiles_to_rows.1 = (f32[11264,128]{1,0:T(8,128)}, f32[1408,128]{1,0:T(8,128)}) custom-call(f32[512,512]{1,0:T(8,128)S(1)} %get-tuple-element.45.a_ref, bf16[576,512]{1,0:T(8,128)(2,1)S(1)} %get-tuple-element.73.refs_1_.refs_3_.refs_4_.high_ref.mine_high, bf16[576,512]{1,0:T(8,128)(2,1)S(1)} %get-tuple-element.74.refs_4_.refs_5_.low_ref.mine_low, ...), custom_call_target="tpu_custom_call" | custom-call | tf_op jit(solution)/shard_map/tiles_to_rows/pallas_call | solution.py:293
  (75 shorter events, 36.2 us)
Async XLA Ops:
  1.7 10.4 %collective-permute-start = (f32[512,128]{1,0:T(8,128)S(1)}, f32[512,128]{1,0:T(8,128)S(1)}, u32[]{:S(2)}, u32[]{:S(2)}) collective-permute-start(f32[512,128]{1,0:T(8,128)S(1)} %bitcast.19), channel_id=1, source_target_pairs={{0,2},{1,3},{4,6},{5,7},{8,10},{9,11},{12,14},{13,15},{16,18},{17,... | collective-permute-start | bytes 786440 | tf_op jit(solution)/shard_map/ppermute | solution.py:328
  6.7 2.6 %copy-start = (f32[512,11,1,256]{3,2,1,0:T(1,128)S(1)}, f32[512,11,1,256]{3,2,1,0:T(1,128)}, u32[]{:S(2)}) copy-start(f32[512,11,1,256]{3,2,1,0:T(1,128)} %param.1) | copy-start | bytes 17301508
  12.7 5.2 %collective-permute-start.1 = (f32[512,128]{1,0:T(8,128)S(1)}, f32[512,128]{1,0:T(8,128)S(1)}, u32[]{:S(2)}, u32[]{:S(2)}) collective-permute-start(f32[512,128]{1,0:T(8,128)S(1)} %ka.1.refs_1_.refs_2_.refs_8_.refs_9_), channel_id=1, source_target_pairs={{0,1},{1,0},{2,3},{3,2},{4,5},{5,4},{6,7},{7,6},{8,9},{9,8},{10,11... | collective-permute-start | bytes 786440 | tf_op jit(solution)/shard_map/ppermute | solution.py:52
  13.5 10.9 %collective-permute-start.2 = (f32[544,128]{1,0:T(8,128)S(1)}, f32[544,128]{1,0:T(8,128)S(1)}, u32[]{:S(2)}, u32[]{:S(2)}) collective-permute-start(f32[544,128]{1,0:T(8,128)S(1)} %pad_maximum_fusion.refs_3_), channel_id=1, source_target_pairs={{0,2},{1,3},{4,6},{5,7},{8,10},{9,11},{12,14},{13,15},{16,18},{17,... | collective-permute-start | bytes 835592 | tf_op jit(solution)/shard_map/ppermute | solution.py:328
  19.8 14.8 %collective-permute-start.4 = (f32[128,1024]{1,0:T(8,128)S(1)}, f32[128,1024]{1,0:T(8,128)S(1)}, u32[]{:S(2)}, u32[]{:S(2)}) collective-permute-start(f32[128,1024]{1,0:T(8,128)S(1)} %send0.1.refs_1_), channel_id=1, source_target_pairs={{0,4},{4,0},{8,12},{12,8},{16,20},{20,16},{24,28},{28,24},{1,5},{5... | collective-permute-start | bytes 1572872 | tf_op jit(solution)/shard_map/ppermute | solution.py:52
  25.0 1.6 collective-permute-start.3
  28.8 17.1 %collective-permute-start.5 = (f32[256,512]{1,0:T(8,128)S(1)}, f32[256,512]{1,0:T(8,128)S(1)}, u32[]{:S(2)}, u32[]{:S(2)}) collective-permute-start(f32[256,512]{1,0:T(8,128)S(1)} %send1.1.refs_1_), channel_id=1, source_target_pairs={{0,4},{4,0},{8,12},{12,8},{16,20},{20,16},{24,28},{28,24},{1,5},{5... | collective-permute-start | bytes 1572872 | tf_op jit(solution)/shard_map/ppermute | solution.py:52
  35.8 16.6 %collective-permute-start.6 = (f32[128,1024]{1,0:T(8,128)S(1)}, f32[128,1024]{1,0:T(8,128)S(1)}, u32[]{:S(2)}, u32[]{:S(2)}) collective-permute-start(f32[128,1024]{1,0:T(8,128)S(1)} %keep0.1.refs_1_.refs_2_), channel_id=1, source_target_pairs={{0,8},{4,12},{24,16},{28,20},{1,9},{5,13},{25,17},{29,21},{2,10},{... | collective-permute-start | bytes 1572872 | tf_op jit(solution)/shard_map/ppermute | solution.py:353
  39.3 17.8 %collective-permute-start.7 = (f32[128,1024]{1,0:T(8,128)S(1)}, f32[128,1024]{1,0:T(8,128)S(1)}, u32[]{:S(2)}, u32[]{:S(2)}) collective-permute-start(f32[128,1024]{1,0:T(8,128)S(1)} %send2.1.refs_1_), channel_id=1, source_target_pairs={{0,4},{4,0},{8,12},{12,8},{16,20},{20,16},{24,28},{28,24},{1,5},{5... | collective-permute-start | bytes 1572872 | tf_op jit(solution)/shard_map/ppermute | solution.py:52
  47.3 14.5 %collective-permute-start.8 = (f32[256,512]{1,0:T(8,128)S(1)}, f32[256,512]{1,0:T(8,128)S(1)}, u32[]{:S(2)}, u32[]{:S(2)}) collective-permute-start(f32[256,512]{1,0:T(8,128)S(1)} %keep1.1.refs_1_.refs_2_), channel_id=1, source_target_pairs={{0,8},{4,12},{24,16},{28,20},{1,9},{5,13},{25,17},{29,21},{2,10},{... | collective-permute-start | bytes 1572872 | tf_op jit(solution)/shard_map/ppermute | solution.py:353
  50.8 17.6 %collective-permute-start.9 = (f32[256,512]{1,0:T(8,128)S(1)}, f32[256,512]{1,0:T(8,128)S(1)}, u32[]{:S(2)}, u32[]{:S(2)}) collective-permute-start(f32[256,512]{1,0:T(8,128)S(1)} %send3.1.refs_1_), channel_id=1, source_target_pairs={{0,4},{4,0},{8,12},{12,8},{16,20},{20,16},{24,28},{28,24},{1,5},{5... | collective-permute-start | bytes 1572872 | tf_op jit(solution)/shard_map/ppermute | solution.py:52
  53.0 15.4 %collective-permute-start.10 = (f32[128,1024]{1,0:T(8,128)S(1)}, f32[128,1024]{1,0:T(8,128)S(1)}, u32[]{:S(2)}, u32[]{:S(2)}) collective-permute-start(f32[128,1024]{1,0:T(8,128)S(1)} %zm0.1.refs_1_.refs_3_), channel_id=1, source_target_pairs={{8,16},{12,20},{16,8},{20,12},{9,17},{13,21},{17,9},{21,13},{10,18... | collective-permute-start | bytes 1572872 | tf_op jit(solution)/shard_map/ppermute | solution.py:356
  58.3 17.7 %collective-permute-start.11 = (f32[128,1024]{1,0:T(8,128)S(1)}, f32[128,1024]{1,0:T(8,128)S(1)}, u32[]{:S(2)}, u32[]{:S(2)}) collective-permute-start(f32[128,1024]{1,0:T(8,128)S(1)} %keep2.1.refs_1_.refs_2_), channel_id=1, source_target_pairs={{0,8},{4,12},{24,16},{28,20},{1,9},{5,13},{25,17},{29,21},{2,10},{... | collective-permute-start | bytes 1572872 | tf_op jit(solution)/shard_map/ppermute | solution.py:353
  62.4 14.9 %collective-permute-start.12 = (f32[256,512]{1,0:T(8,128)S(1)}, f32[256,512]{1,0:T(8,128)S(1)}, u32[]{:S(2)}, u32[]{:S(2)}) collective-permute-start(f32[256,512]{1,0:T(8,128)S(1)} %zm1.1.refs_1_.refs_2_), channel_id=1, source_target_pairs={{8,16},{12,20},{16,8},{20,12},{9,17},{13,21},{17,9},{21,13},{10,18... | collective-permute-start | bytes 1572872 | tf_op jit(solution)/shard_map/ppermute | solution.py:356
  63.1 16.1 %collective-permute-start.14 = (f32[256,512]{1,0:T(8,128)S(1)}, f32[256,512]{1,0:T(8,128)S(1)}, u32[]{:S(2)}, u32[]{:S(2)}) collective-permute-start(f32[256,512]{1,0:T(8,128)S(1)} %send4.1.refs_1_), channel_id=1, source_target_pairs={{0,4},{4,0},{8,12},{12,8},{16,20},{20,16},{24,28},{28,24},{1,5},{5... | collective-permute-start | bytes 1572872 | tf_op jit(solution)/shard_map/ppermute | solution.py:52
  69.0 16.3 %collective-permute-start.13 = (f32[128,1024]{1,0:T(8,128)S(1)}, f32[128,1024]{1,0:T(8,128)S(1)}, u32[]{:S(2)}, u32[]{:S(2)}) collective-permute-start(f32[128,1024]{1,0:T(8,128)S(1)} %zo0.1.refs_1_.refs_3_), channel_id=1, source_target_pairs={{8,0},{12,4},{16,24},{20,28},{9,1},{13,5},{17,25},{21,29},{10,2},{... | collective-permute-start | bytes 1572872 | tf_op jit(solution)/shard_map/ppermute | solution.py:359
  71.4 16.4 %collective-permute-start.15 = (f32[256,512]{1,0:T(8,128)S(1)}, f32[256,512]{1,0:T(8,128)S(1)}, u32[]{:S(2)}, u32[]{:S(2)}) collective-permute-start(f32[256,512]{1,0:T(8,128)S(1)} %keep3.1.refs_1_.refs_2_), channel_id=1, source_target_pairs={{0,8},{4,12},{24,16},{28,20},{1,9},{5,13},{25,17},{29,21},{2,10},{... | collective-permute-start | bytes 1572872 | tf_op jit(solution)/shard_map/ppermute | solution.py:353
  76.6 12.5 %collective-permute-start.16 = (f32[128,1024]{1,0:T(8,128)S(1)}, f32[128,1024]{1,0:T(8,128)S(1)}, u32[]{:S(2)}, u32[]{:S(2)}) collective-permute-start(f32[128,1024]{1,0:T(8,128)S(1)} %zm2.1.refs_1_.refs_2_), channel_id=1, source_target_pairs={{8,16},{12,20},{16,8},{20,12},{9,17},{13,21},{17,9},{21,13},{10,18... | collective-permute-start | bytes 1572872 | tf_op jit(solution)/shard_map/ppermute | solution.py:356
  77.9 17.9 %collective-permute-start.17 = (f32[256,512]{1,0:T(8,128)S(1)}, f32[256,512]{1,0:T(8,128)S(1)}, u32[]{:S(2)}, u32[]{:S(2)}) collective-permute-start(f32[256,512]{1,0:T(8,128)S(1)} %zo1.1.refs_1_.refs_3_), channel_id=1, source_target_pairs={{8,0},{12,4},{16,24},{20,28},{9,1},{13,5},{17,25},{21,29},{10,2},{... | collective-permute-start | bytes 1572872 | tf_op jit(solution)/shard_map/ppermute | solution.py:359
  79.3 18.8 %collective-permute-start.18 = (f32[256,512]{1,0:T(8,128)S(1)}, f32[256,512]{1,0:T(8,128)S(1)}, u32[]{:S(2)}, u32[]{:S(2)}) collective-permute-start(f32[256,512]{1,0:T(8,128)S(1)} %send5.1.refs_1_), channel_id=1, source_target_pairs={{0,4},{4,0},{8,12},{12,8},{16,20},{20,16},{24,28},{28,24},{1,5},{5... | collective-permute-start | bytes 1572872 | tf_op jit(solution)/shard_map/ppermute | solution.py:52
  86.4 16.0 %collective-permute-start.19 = (f32[256,512]{1,0:T(8,128)S(1)}, f32[256,512]{1,0:T(8,128)S(1)}, u32[]{:S(2)}, u32[]{:S(2)}) collective-permute-start(f32[256,512]{1,0:T(8,128)S(1)} %keep4.1.refs_1_.refs_2_), channel_id=1, source_target_pairs={{0,8},{4,12},{24,16},{28,20},{1,9},{5,13},{25,17},{29,21},{2,10},{... | collective-permute-start | bytes 1572872 | tf_op jit(solution)/shard_map/ppermute | solution.py:353
  88.5 15.2 %collective-permute-start.20 = (f32[256,512]{1,0:T(8,128)S(1)}, f32[256,512]{1,0:T(8,128)S(1)}, u32[]{:S(2)}, u32[]{:S(2)}) collective-permute-start(f32[256,512]{1,0:T(8,128)S(1)} %zm3.1.refs_1_.refs_2_), channel_id=1, source_target_pairs={{8,16},{12,20},{16,8},{20,12},{9,17},{13,21},{17,9},{21,13},{10,18... | collective-permute-start | bytes 1572872 | tf_op jit(solution)/shard_map/ppermute | solution.py:356
  89.8 18.0 %collective-permute-start.21 = (f32[128,1024]{1,0:T(8,128)S(1)}, f32[128,1024]{1,0:T(8,128)S(1)}, u32[]{:S(2)}, u32[]{:S(2)}) collective-permute-start(f32[128,1024]{1,0:T(8,128)S(1)} %zo2.1.refs_1_.refs_3_), channel_id=1, source_target_pairs={{8,0},{12,4},{16,24},{20,28},{9,1},{13,5},{17,25},{21,29},{10,2},{... | collective-permute-start | bytes 1572872 | tf_op jit(solution)/shard_map/ppermute | solution.py:359
  96.4 13.9 %collective-permute-start.22 = (f32[128,1024]{1,0:T(8,128)S(1)}, f32[128,1024]{1,0:T(8,128)S(1)}, u32[]{:S(2)}, u32[]{:S(2)}) collective-permute-start(f32[128,1024]{1,0:T(8,128)S(1)} %ag0.1.refs_1_.refs_5_), channel_id=1, source_target_pairs={{0,4},{4,0},{8,12},{12,8},{16,20},{20,16},{24,28},{28,24},{1,5},{5... | collective-permute-start | bytes 1572872 | tf_op jit(solution)/shard_map/ppermute | solution.py:52
  99.1 11.2 %collective-permute-start.23 = (f32[256,512]{1,0:T(8,128)S(1)}, f32[256,512]{1,0:T(8,128)S(1)}, u32[]{:S(2)}, u32[]{:S(2)}) collective-permute-start(f32[256,512]{1,0:T(8,128)S(1)} %keep5.1.refs_1_.refs_3_), channel_id=1, source_target_pairs={{0,8},{4,12},{24,16},{28,20},{1,9},{5,13},{25,17},{29,21},{2,10},{... | collective-permute-start | bytes 1572872 | tf_op jit(solution)/shard_map/ppermute | solution.py:353
  103.0 8.0 %collective-permute-start.24 = (f32[256,512]{1,0:T(8,128)S(1)}, f32[256,512]{1,0:T(8,128)S(1)}, u32[]{:S(2)}, u32[]{:S(2)}) collective-permute-start(f32[256,512]{1,0:T(8,128)S(1)} %zm4.1.refs_1_.refs_2_), channel_id=1, source_target_pairs={{8,16},{12,20},{16,8},{20,12},{9,17},{13,21},{17,9},{21,13},{10,18... | collective-permute-start | bytes 1572872 | tf_op jit(solution)/shard_map/ppermute | solution.py:356
  104.3 16.8 %collective-permute-start.25 = (f32[256,512]{1,0:T(8,128)S(1)}, f32[256,512]{1,0:T(8,128)S(1)}, u32[]{:S(2)}, u32[]{:S(2)}) collective-permute-start(f32[256,512]{1,0:T(8,128)S(1)} %zo3.1.refs_1_.refs_3_), channel_id=1, source_target_pairs={{8,0},{12,4},{16,24},{20,28},{9,1},{13,5},{17,25},{21,29},{10,2},{... | collective-permute-start | bytes 1572872 | tf_op jit(solution)/shard_map/ppermute | solution.py:359
  108.4 13.3 %collective-permute-start.26 = (f32[256,512]{1,0:T(8,128)S(1)}, f32[256,512]{1,0:T(8,128)S(1)}, u32[]{:S(2)}, u32[]{:S(2)}) collective-permute-start(f32[256,512]{1,0:T(8,128)S(1)} %ag1.1.refs_1_.refs_2_.refs_5_), channel_id=1, source_target_pairs={{0,4},{4,0},{8,12},{12,8},{16,20},{20,16},{24,28},{28,24},{1,5},{5... | collective-permute-start | bytes 1572872 | tf_op jit(solution)/shard_map/ppermute | solution.py:52
  111.6 16.7 %collective-permute-start.27 = (f32[256,512]{1,0:T(8,128)S(1)}, f32[256,512]{1,0:T(8,128)S(1)}, u32[]{:S(2)}, u32[]{:S(2)}) collective-permute-start(f32[256,512]{1,0:T(8,128)S(1)} %zo4.1.refs_1_.refs_3_), channel_id=1, source_target_pairs={{8,0},{12,4},{16,24},{20,28},{9,1},{13,5},{17,25},{21,29},{10,2},{... | collective-permute-start | bytes 1572872 | tf_op jit(solution)/shard_map/ppermute | solution.py:359
  112.9 16.0 %collective-permute-start.28 = (f32[256,512]{1,0:T(8,128)S(1)}, f32[256,512]{1,0:T(8,128)S(1)}, u32[]{:S(2)}, u32[]{:S(2)}) collective-permute-start(f32[256,512]{1,0:T(8,128)S(1)} %zm5.1.refs_1_.refs_2_), channel_id=1, source_target_pairs={{8,16},{12,20},{16,8},{20,12},{9,17},{13,21},{17,9},{21,13},{10,18... | collective-permute-start | bytes 1572872 | tf_op jit(solution)/shard_map/ppermute | solution.py:356
  122.3 10.3 %collective-permute-start.29 = (f32[512,256]{1,0:T(8,128)S(1)}, f32[512,256]{1,0:T(8,128)S(1)}, u32[]{:S(2)}, u32[]{:S(2)}) collective-permute-start(f32[512,256]{1,0:T(8,128)S(1)} %g4.1.refs_1_.refs_2_), channel_id=1, source_target_pairs={{0,1},{1,0},{2,3},{3,2},{4,5},{5,4},{6,7},{7,6},{8,9},{9,8},{10,11... | collective-permute-start | bytes 1572872 | tf_op jit(solution)/shard_map/ppermute | solution.py:52
  122.4 15.7 %collective-permute-start.30 = (f32[128,1024]{1,0:T(8,128)S(1)}, f32[128,1024]{1,0:T(8,128)S(1)}, u32[]{:S(2)}, u32[]{:S(2)}) collective-permute-start(f32[128,1024]{1,0:T(8,128)S(1)} %ag2.1.refs_1_.refs_6_), channel_id=1, source_target_pairs={{0,4},{4,0},{8,12},{12,8},{16,20},{20,16},{24,28},{28,24},{1,5},{5... | collective-permute-start | bytes 1572872 | tf_op jit(solution)/shard_map/ppermute | solution.py:52
  129.5 14.5 %collective-permute-start.31 = (f32[256,512]{1,0:T(8,128)S(1)}, f32[256,512]{1,0:T(8,128)S(1)}, u32[]{:S(2)}, u32[]{:S(2)}) collective-permute-start(f32[256,512]{1,0:T(8,128)S(1)} %zo5.1.refs_1_.refs_3_), channel_id=1, source_target_pairs={{8,0},{12,4},{16,24},{20,28},{9,1},{13,5},{17,25},{21,29},{10,2},{... | collective-permute-start | bytes 1572872 | tf_op jit(solution)/shard_map/ppermute | solution.py:359
  131.0 20.1 %collective-permute-start.32 = (f32[256,512]{1,0:T(8,128)S(1)}, f32[256,512]{1,0:T(8,128)S(1)}, u32[]{:S(2)}, u32[]{:S(2)}) collective-permute-start(f32[256,512]{1,0:T(8,128)S(1)} %ag3.1.refs_1_.refs_5_), channel_id=1, source_target_pairs={{0,4},{4,0},{8,12},{12,8},{16,20},{20,16},{24,28},{28,24},{1,5},{5... | collective-permute-start | bytes 1572872 | tf_op jit(solution)/shard_map/ppermute | solution.py:52
  138.7 24.5 %collective-permute-start.34 = (f32[256,512]{1,0:T(8,128)S(1)}, f32[256,512]{1,0:T(8,128)S(1)}, u32[]{:S(2)}, u32[]{:S(2)}) collective-permute-start(f32[256,512]{1,0:T(8,128)S(1)} %ag4.1.refs_1_.refs_6_), channel_id=1, source_target_pairs={{0,4},{4,0},{8,12},{12,8},{16,20},{20,16},{24,28},{28,24},{1,5},{5... | collective-permute-start | bytes 1572872 | tf_op jit(solution)/shard_map/ppermute | solution.py:52
  144.8 25.6 %collective-permute-start.33 = (f32[256,512]{1,0:T(8,128)S(1)}, f32[256,512]{1,0:T(8,128)S(1)}, u32[]{:S(2)}, u32[]{:S(2)}) collective-permute-start(f32[256,512]{1,0:T(8,128)S(1)} %ag5.1.refs_1_.first_ref), channel_id=1, source_target_pairs={{0,4},{4,0},{8,12},{12,8},{16,20},{20,16},{24,28},{28,24},{1,5},{5... | collective-permute-start | bytes 1572872 | tf_op jit(solution)/shard_map/ppermute | solution.py:52

commit v8 on v5

--- a/solution.py
+++ b/solution.py
@@ -18,7 +18,7 @@
 ORDER = (
     "ka pa send0 kb", "pb send1 send2 send3", "keep0 send4 send5 keep1", "zm0 keep2 zm1 zo0",
     "keep3 zm2 zo1 ~zo0", "keep4 zm3 zo2 ~zo1", "ag0 keep5 zm4 zo3", "~zo2 ag1 ~ag0 zm5",
-    "zo4 ~zo3 ag2 g4", "zo5 ~zo4 ag3 g6", "ch0 ~ag2 ag4 ch1", "~zo5 ag5 ~ag3 ch2",
+    "zo4 ~zo3 ag2 g4", "~zo4 ag3 zo5 g6", "ch0 ~ag2 ag4 ch1", "~zo5 ag5 ch2 ~ag3",
     "ch3 weights fin1 fin0", "fin3 ~ag4 fin4",
 )
 

time: 171 us -> 170 us (level)
  starting transfers between devices: 52.1 us -> 56.7 us
  waiting for transfers between devices: 47.5 us -> 43.5 us
    ppermute x15, waiting for transfers between devices: 23.2 us -> 17.6 us  [flip(): return lax.ppermute(value, axis, [(i, i ^ bit) for i in range(n)])]
    ppermute x2, waiting for transfers between devices: 0.01 us -> 3.27 us  [local(): came = [lax.ppermute(v, 'pcol', [(0, 2), (1, 3)]) for v in own]]
    ppermute x2, starting transfers between devices: 6.17 us -> 9.26 us  [local(): came = [lax.ppermute(v, 'pcol', [(0, 2), (1, 3)]) for v in own]]
    ppermute x6, waiting for transfers between devices: 23.5 us -> 20.6 us  [out_hop(): lax.ppermute(value, 'prow', [(2, 0), (3, 1), (4, 6), (5, 7)])]
    unnamed x6 -> x2, local copies, waits for them, and re-layouts: 4.28 us -> 2.64 us
  transfers between devices with their start and end apart: 35 -> 35, of which waited for: 14 -> 15; matrix products, arithmetic and copies ran while one was open for 0% -> 0% of each run, Pallas kernels for 34% -> 35%
where the time goes in v8:
time: 170 us
  Pallas kernels  63.4 us (37%)
  starting transfers between devices  56.7 us (33%)
  waiting for transfers between devices  43.5 us (26%)
  local copies, waits for them, and re-layouts  4.53 us (3%)
    pallas_call x46, Pallas kernels, __call__(): pl.pallas_call(body, out_shape=[jax.ShapeDtypeStruct(*(o if isinstance(o[...  59.2 us
    ppermute x6, starting transfers between devices, in_hop(): lax.ppermute(value, 'prow', [(0, 2), (1, 3), (6, 4), (7, 5)])  21.4 us
    ppermute x6, waiting for transfers between devices, out_hop(): lax.ppermute(value, 'prow', [(2, 0), (3, 1), (4, 6), (5, 7)])  20.6 us
    ppermute x15, waiting for transfers between devices, flip(): return lax.ppermute(value, axis, [(i, i ^ bit) for i in range(n)])  17.6 us
    ppermute x15, starting transfers between devices, flip(): return lax.ppermute(value, axis, [(i, i ^ bit) for i in range(n)])  14 us
    ppermute x2, starting transfers between devices, local(): came = [lax.ppermute(v, 'pcol', [(0, 2), (1, 3)]) for v in own]  9.26 us
    ppermute x6, starting transfers between devices, out_hop(): lax.ppermute(value, 'prow', [(2, 0), (3, 1), (4, 6), (5, 7)])  7.93 us
    pallas_call x1, Pallas kernels, in_rows(): pl.pallas_call(functools.partial(rows_kernel, parts, len(rests)), grid=(r...  4.22 us
  transfers between devices with their start and end apart: 35, of which 15 were waited for; matrix products, arithmetic and copies ran while one was open for 0% of the time, Pallas kernels for 35%

profile of v8, /device:TPU:0, one launch (start us, length us, event | category | flops | bytes accessed | tf_op | source)
XLA Modules:
  0.0 169.6 jit_solution(635580536275372851)
XLA Ops:
  1.7 4.9 %collective-permute-start = (f32[512,128]{1,0:T(8,128)S(1)}, f32[512,128]{1,0:T(8,128)S(1)}, u32[]{:S(2)}, u32[]{:S(2)}) collective-permute-start(f32[512,128]{1,0:T(8,128)S(1)} %bitcast.19), channel_id=1, source_target_pairs={{0,2},{1,3},{4,6},{5,7},{8,10},{9,11},{12,14},{13,15},{16,18},{17,... | collective-permute-start | bytes 786440 | tf_op jit(solution)/shard_map/ppermute | solution.py:328
  6.7 2.6 %copy-done = f32[512,11,1,256]{3,2,1,0:T(1,128)S(1)} copy-done((f32[512,11,1,256]{3,2,1,0:T(1,128)S(1)}, f32[512,11,1,256]{3,2,1,0:T(1,128)}, u32[]{:S(2)}) %copy-start) | copy-done | bytes 5767192
  9.3 2.5 %rows_to_tiles.1 = (f32[512,1024]{1,0:T(8,128)S(1)}, bf16[512,1024]{1,0:T(8,128)(2,1)S(1)}, bf16[512,1024]{1,0:T(8,128)(2,1)S(1)}, f32[512,256]{1,0:T(8,128)S(1)...) custom-call(s32[6]{0:T(128)S(1)} %stack.43.refs_0_, ...), custom_call_target="tpu_custom_call" | custom-call | flops 1000 | bytes 1000 | tf_op jit(solution)/shard_map/rows_to_tiles/pallas_call | solution.py:68
  13.5 4.4 %collective-permute-start.2 = (f32[544,128]{1,0:T(8,128)S(1)}, f32[544,128]{1,0:T(8,128)S(1)}, u32[]{:S(2)}, u32[]{:S(2)}) collective-permute-start(f32[544,128]{1,0:T(8,128)S(1)} %pad_maximum_fusion.refs_3_), channel_id=1, source_target_pairs={{0,2},{1,3},{4,6},{5,7},{8,10},{9,11},{12,14},{13,15},{16,18},{17,... | collective-permute-start | bytes 835592 | tf_op jit(solution)/shard_map/ppermute | solution.py:328
  19.8 1.6 collective-permute-start.4
  21.4 3.0 %collective-permute-done.2.refs_2_ = f32[544,128]{1,0:T(8,128)S(1)} collective-permute-done((f32[544,128]{1,0:T(8,128)S(1)}, f32[544,128]{1,0:T(8,128)S(1)}, u32[]{:S(2)}, u32[]{:S(2)}) %collective-permute-start.2) | collective-permute-done | bytes 278560 | tf_op jit(solution)/shard_map/ppermute | solution.py:328
  25.1 1.5 collective-permute-done.3.refs_3_.refs_11_.refs_12_.refs_5_
  27.4 1.4 send1.1.refs_1_
  28.8 1.6 collective-permute-start.5
  32.6 2.0 %collective-permute-done.4.refs_6_ = f32[128,1024]{1,0:T(8,128)S(1)} collective-permute-done((f32[128,1024]{1,0:T(8,128)S(1)}, f32[128,1024]{1,0:T(8,128)S(1)}, u32[]{:S(2)}, u32[]{:S(2)}) %collective-permute-start.4) | collective-permute-done | bytes 524320 | tf_op jit(solution)/shard_map/ppermute | solution.py:52
  35.8 3.5 %collective-permute-start.6 = (f32[128,1024]{1,0:T(8,128)S(1)}, f32[128,1024]{1,0:T(8,128)S(1)}, u32[]{:S(2)}, u32[]{:S(2)}) collective-permute-start(f32[128,1024]{1,0:T(8,128)S(1)} %keep0.1.refs_1_.refs_2_), channel_id=1, source_target_pairs={{0,8},{4,12},{24,16},{28,20},{1,9},{5,13},{25,17},{29,21},{2,10},{... | collective-permute-start | bytes 1572872 | tf_op jit(solution)/shard_map/ppermute | solution.py:353
  39.3 1.6 collective-permute-start.7
  43.1 2.8 %collective-permute-done.5.refs_8_ = f32[256,512]{1,0:T(8,128)S(1)} collective-permute-done((f32[256,512]{1,0:T(8,128)S(1)}, f32[256,512]{1,0:T(8,128)S(1)}, u32[]{:S(2)}, u32[]{:S(2)}) %collective-permute-start.5) | collective-permute-done | bytes 524320 | tf_op jit(solution)/shard_map/ppermute | solution.py:52
  45.9 1.4 keep1.1.refs_1_.refs_2_
  47.3 3.5 %collective-permute-start.8 = (f32[256,512]{1,0:T(8,128)S(1)}, f32[256,512]{1,0:T(8,128)S(1)}, u32[]{:S(2)}, u32[]{:S(2)}) collective-permute-start(f32[256,512]{1,0:T(8,128)S(1)} %keep1.1.refs_1_.refs_2_), channel_id=1, source_target_pairs={{0,8},{4,12},{24,16},{28,20},{1,9},{5,13},{25,17},{29,21},{2,10},{... | collective-permute-start | bytes 1572872 | tf_op jit(solution)/shard_map/ppermute | solution.py:353
  52.1 1.6 collective-permute-start.10
  53.7 3.4 %collective-permute-done.7.refs_6_ = f32[128,1024]{1,0:T(8,128)S(1)} collective-permute-done((f32[128,1024]{1,0:T(8,128)S(1)}, f32[128,1024]{1,0:T(8,128)S(1)}, u32[]{:S(2)}, u32[]{:S(2)}) %collective-permute-start.7) | collective-permute-done | bytes 524320 | tf_op jit(solution)/shard_map/ppermute | solution.py:52
  58.3 3.5 %collective-permute-start.11 = (f32[128,1024]{1,0:T(8,128)S(1)}, f32[128,1024]{1,0:T(8,128)S(1)}, u32[]{:S(2)}, u32[]{:S(2)}) collective-permute-start(f32[128,1024]{1,0:T(8,128)S(1)} %keep2.1.refs_1_.refs_2_), channel_id=1, source_target_pairs={{0,8},{4,12},{24,16},{28,20},{1,9},{5,13},{25,17},{29,21},{2,10},{... | collective-permute-start | bytes 1572872 | tf_op jit(solution)/shard_map/ppermute | solution.py:353
  63.1 1.6 collective-permute-start.14
  65.3 1.3 collective-permute-start.13
  66.6 1.8 %collective-permute-done.10.refs_8_ = f32[256,512]{1,0:T(8,128)S(1)} collective-permute-done((f32[256,512]{1,0:T(8,128)S(1)}, f32[256,512]{1,0:T(8,128)S(1)}, u32[]{:S(2)}, u32[]{:S(2)}) %collective-permute-start.10) | collective-permute-done | bytes 524320 | tf_op jit(solution)/shard_map/ppermute | solution.py:52
  69.5 4.7 %collective-permute-start.15 = (f32[256,512]{1,0:T(8,128)S(1)}, f32[256,512]{1,0:T(8,128)S(1)}, u32[]{:S(2)}, u32[]{:S(2)}) collective-permute-start(f32[256,512]{1,0:T(8,128)S(1)} %keep3.1.refs_1_.refs_2_), channel_id=1, source_target_pairs={{0,8},{4,12},{24,16},{28,20},{1,9},{5,13},{25,17},{29,21},{2,10},{... | collective-permute-start | bytes 1572872 | tf_op jit(solution)/shard_map/ppermute | solution.py:353
  76.1 1.3 collective-permute-start.17
  77.4 1.5 collective-permute-done.14.refs_9_
  78.9 1.5 collective-permute-start.18
  82.3 3.1 %collective-permute-start.19 = (f32[256,512]{1,0:T(8,128)S(1)}, f32[256,512]{1,0:T(8,128)S(1)}, u32[]{:S(2)}, u32[]{:S(2)}) collective-permute-start(f32[256,512]{1,0:T(8,128)S(1)} %keep4.1.refs_1_.refs_2_), channel_id=1, source_target_pairs={{0,8},{4,12},{24,16},{28,20},{1,9},{5,13},{25,17},{29,21},{2,10},{... | collective-permute-start | bytes 1572872 | tf_op jit(solution)/shard_map/ppermute | solution.py:353
  87.4 1.3 collective-permute-start.21
  88.7 3.7 %collective-permute-done.17.refs_2_.refs_4_ = f32[256,512]{1,0:T(8,128)S(1)} collective-permute-done((f32[256,512]{1,0:T(8,128)S(1)}, f32[256,512]{1,0:T(8,128)S(1)}, u32[]{:S(2)}, u32[]{:S(2)}) %collective-permute-start.17) | collective-permute-done | bytes 524320 | tf_op jit(solution)/shard_map/ppermute | solution.py:359
  94.2 3.0 %collective-permute-start.23 = (f32[256,512]{1,0:T(8,128)S(1)}, f32[256,512]{1,0:T(8,128)S(1)}, u32[]{:S(2)}, u32[]{:S(2)}) collective-permute-start(f32[256,512]{1,0:T(8,128)S(1)} %keep5.1.refs_1_.refs_3_), channel_id=1, source_target_pairs={{0,8},{4,12},{24,16},{28,20},{1,9},{5,13},{25,17},{29,21},{2,10},{... | collective-permute-start | bytes 1572872 | tf_op jit(solution)/shard_map/ppermute | solution.py:353
  99.1 1.3 collective-permute-start.25
  100.4 2.5 %collective-permute-done.21.refs_2_.refs_4_ = f32[128,1024]{1,0:T(8,128)S(1)} collective-permute-done((f32[128,1024]{1,0:T(8,128)S(1)}, f32[128,1024]{1,0:T(8,128)S(1)}, u32[]{:S(2)}, u32[]{:S(2)}) %collective-permute-start.21) | collective-permute-done | bytes 524320 | tf_op jit(solution)/shard_map/ppermute | solution.py:359
  103.8 2.0 %collective-permute-done.23.refs_4_ = f32[256,512]{1,0:T(8,128)S(1)} collective-permute-done((f32[256,512]{1,0:T(8,128)S(1)}, f32[256,512]{1,0:T(8,128)S(1)}, u32[]{:S(2)}, u32[]{:S(2)}) %collective-permute-start.23) | collective-permute-done | bytes 524320 | tf_op jit(solution)/shard_map/ppermute | solution.py:353
  107.0 1.3 collective-permute-start.27
  109.0 7.0 %collective-permute-done.25.refs_2_.refs_4_ = f32[256,512]{1,0:T(8,128)S(1)} collective-permute-done((f32[256,512]{1,0:T(8,128)S(1)}, f32[256,512]{1,0:T(8,128)S(1)}, u32[]{:S(2)}, u32[]{:S(2)}) %collective-permute-start.25) | collective-permute-done | bytes 524320 | tf_op jit(solution)/shard_map/ppermute | solution.py:359
  118.5 6.6 %collective-permute-done.27.refs_2_.refs_4_ = f32[256,512]{1,0:T(8,128)S(1)} collective-permute-done((f32[256,512]{1,0:T(8,128)S(1)}, f32[256,512]{1,0:T(8,128)S(1)}, u32[]{:S(2)}, u32[]{:S(2)}) %collective-permute-start.27) | collective-permute-done | bytes 524320 | tf_op jit(solution)/shard_map/ppermute | solution.py:359
  126.3 1.5 collective-permute-start.31
  129.2 4.9 %factor0.1 = (f32[512,512]{1,0:T(8,128)S(1)}, f32[512,512]{1,0:T(8,128)S(1)}) custom-call(s32[6]{0:T(128)S(1)} %stack.43.refs_0_, f32[512,512]{1,0:T(8,128)S(1)} %g6.1.refs_1_.refs_2_, f32[512,512]{1,0:T(8,128)S(1)} %g6.1.refs_1_.refs_2_), custom_call_target="tpu_custom_call" | custom-call | flops 1000 | bytes 1000 | tf_op jit(solution)/shard_map/factor0/pallas_call | solution.py:68
  134.6 1.4 collective-permute-start.34
  136.0 4.7 %factor1.1 = (f32[512,512]{1,0:T(8,128)S(1)}, f32[512,512]{1,0:T(8,128)S(1)}) custom-call(s32[6]{0:T(128)S(1)} %stack.43.refs_0_, f32[256,512]{1,0:T(8,128)S(1)} %ag4.1.refs_1_.refs_6_, f32[512,512]{1,0:T(8,128)S(1)} %get-tuple-element.65.refs_1_.refs_2_, f32[512,512]{1,0:T(8,128)S(1)} %get-tuple-element.66.refs_3_), custom_call_target="tpu_custom_call" | custom-call | flops 1000 | bytes 1000 | tf_op jit(solution)/shard_map/factor1/pallas_call | solution.py:68
  142.4 4.7 %factor2.1 = (f32[512,512]{1,0:T(8,128)S(1)}, f32[512,512]{1,0:T(8,128)S(1)}) custom-call(s32[6]{0:T(128)S(1)} %stack.43.refs_0_, f32[256,512]{1,0:T(8,128)S(1)} %ag5.1.refs_1_.first_ref, f32[512,512]{1,0:T(8,128)S(1)} %get-tuple-element.67.refs_1_.refs_2_, f32[512,512]{1,0:T(8,128)S(1)} %get-tuple-element.68.refs_3_), custom_call_target="tpu_custom_call" | custom-call | flops 1000 | bytes 1000 | tf_op jit(solution)/shard_map/factor2/pallas_call | solution.py:68
  147.1 4.0 %factor3.1 = (f32[512,512]{1,0:T(8,128)S(1)}, f32[512,512]{1,0:T(8,128)S(1)}) custom-call(s32[6]{0:T(128)S(1)} %stack.43.refs_0_, f32[512,512]{1,0:T(8,128)S(1)} %get-tuple-element.69.refs_1_.refs_3_, f32[256,512]{1,0:T(8,128)S(1)} %collective-permute-done.32.refs_2_.refs_6_, f32[512,512]{1,0:T(8,128)S(1)} %get-tuple-element.69.refs_1_.refs_3_, ...), custom_call_target="tpu_custom_call" | custom-call | flops 1000 | bytes 1000 | tf_op jit(solution)/shard_map/factor3/pallas_call | solution.py:68
  151.1 2.6 %weights.1 = (bf16[576,512]{1,0:T(8,128)(2,1)S(1)}, bf16[576,512]{1,0:T(8,128)(2,1)S(1)}) custom-call(s32[6]{0:T(128)S(1)} %stack.43.refs_0_, f32[512,512]{1,0:T(8,128)S(1)} %get-tuple-element.71.refs_1_, f32[512,128]{1,0:T(8,128)S(1)} %ka.1.refs_1_.refs_2_.refs_8_.refs_9_, f32[512,128]{1,0:T(8,128)S(1)} %collective-permute-done.1.refs_3_.refs_9_.refs_10_, ...), custom_call_target="tpu_custom_call" | custom-call | flops 1000 | bytes 1000 | tf_op jit(solution)/shard_map/weights/pallas_call | solution.py:68
  153.7 1.2 fin1.1
  154.9 2.6 %fin0.1 = (f32[512,1024]{1,0:T(8,128)S(1)}, f32[64,1024]{1,0:T(8,128)S(1)}) custom-call(s32[6]{0:T(128)S(1)} %stack.43.refs_0_, f32[512,256]{1,0:T(8,128)S(1)} %get-tuple-element.76.refs_1_, f32[512,1024]{1,0:T(8,128)S(1)} %get-tuple-element.46.refs_1_.refs_2_, bf16[576,512]{1,0:T(8,128)(2,1)S(1)} %get-tuple-element.73.refs_1_.refs_3_.refs_4_.high_ref.mine_high, ...), custom_call_target="tpu_custom_call" | custom-call | flops 1000 | bytes 1000 | tf_op jit(solution)/shard_map/fin0/pallas_call | solution.py:68
  157.5 1.6 fin3.1
  159.2 1.6 fin4.1
  160.8 4.6 %collective-permute-done.33.second_ref = f32[256,512]{1,0:T(8,128)S(1)} collective-permute-done((f32[256,512]{1,0:T(8,128)S(1)}, f32[256,512]{1,0:T(8,128)S(1)}, u32[]{:S(2)}, u32[]{:S(2)}) %collective-permute-start.33) | collective-permute-done | bytes 524320 | tf_op jit(solution)/shard_map/ppermute | solution.py:52
  165.4 4.2 %tiles_to_rows.1 = (f32[11264,128]{1,0:T(8,128)}, f32[1408,128]{1,0:T(8,128)}) custom-call(f32[512,512]{1,0:T(8,128)S(1)} %get-tuple-element.45.a_ref, bf16[576,512]{1,0:T(8,128)(2,1)S(1)} %get-tuple-element.73.refs_1_.refs_3_.refs_4_.high_ref.mine_high, bf16[576,512]{1,0:T(8,128)(2,1)S(1)} %get-tuple-element.74.refs_4_.refs_5_.low_ref.mine_low, ...), custom_call_target="tpu_custom_call" | custom-call | tf_op jit(solution)/shard_map/tiles_to_rows/pallas_call | solution.py:293
  (75 shorter events, 36.3 us)
Async XLA Ops:
  1.7 10.4 %collective-permute-start = (f32[512,128]{1,0:T(8,128)S(1)}, f32[512,128]{1,0:T(8,128)S(1)}, u32[]{:S(2)}, u32[]{:S(2)}) collective-permute-start(f32[512,128]{1,0:T(8,128)S(1)} %bitcast.19), channel_id=1, source_target_pairs={{0,2},{1,3},{4,6},{5,7},{8,10},{9,11},{12,14},{13,15},{16,18},{17,... | collective-permute-start | bytes 786440 | tf_op jit(solution)/shard_map/ppermute | solution.py:328
  6.7 2.6 %copy-start = (f32[512,11,1,256]{3,2,1,0:T(1,128)S(1)}, f32[512,11,1,256]{3,2,1,0:T(1,128)}, u32[]{:S(2)}) copy-start(f32[512,11,1,256]{3,2,1,0:T(1,128)} %param.1) | copy-start | bytes 17301508
  12.7 5.2 %collective-permute-start.1 = (f32[512,128]{1,0:T(8,128)S(1)}, f32[512,128]{1,0:T(8,128)S(1)}, u32[]{:S(2)}, u32[]{:S(2)}) collective-permute-start(f32[512,128]{1,0:T(8,128)S(1)} %ka.1.refs_1_.refs_2_.refs_8_.refs_9_), channel_id=1, source_target_pairs={{0,1},{1,0},{2,3},{3,2},{4,5},{5,4},{6,7},{7,6},{8,9},{9,8},{10,11... | collective-permute-start | bytes 786440 | tf_op jit(solution)/shard_map/ppermute | solution.py:52
  13.5 10.9 %collective-permute-start.2 = (f32[544,128]{1,0:T(8,128)S(1)}, f32[544,128]{1,0:T(8,128)S(1)}, u32[]{:S(2)}, u32[]{:S(2)}) collective-permute-start(f32[544,128]{1,0:T(8,128)S(1)} %pad_maximum_fusion.refs_3_), channel_id=1, source_target_pairs={{0,2},{1,3},{4,6},{5,7},{8,10},{9,11},{12,14},{13,15},{16,18},{17,... | collective-permute-start | bytes 835592 | tf_op jit(solution)/shard_map/ppermute | solution.py:328
  19.8 14.8 %collective-permute-start.4 = (f32[128,1024]{1,0:T(8,128)S(1)}, f32[128,1024]{1,0:T(8,128)S(1)}, u32[]{:S(2)}, u32[]{:S(2)}) collective-permute-start(f32[128,1024]{1,0:T(8,128)S(1)} %send0.1.refs_1_), channel_id=1, source_target_pairs={{0,4},{4,0},{8,12},{12,8},{16,20},{20,16},{24,28},{28,24},{1,5},{5... | collective-permute-start | bytes 1572872 | tf_op jit(solution)/shard_map/ppermute | solution.py:52
  25.0 1.6 collective-permute-start.3
  28.8 17.1 %collective-permute-start.5 = (f32[256,512]{1,0:T(8,128)S(1)}, f32[256,512]{1,0:T(8,128)S(1)}, u32[]{:S(2)}, u32[]{:S(2)}) collective-permute-start(f32[256,512]{1,0:T(8,128)S(1)} %send1.1.refs_1_), channel_id=1, source_target_pairs={{0,4},{4,0},{8,12},{12,8},{16,20},{20,16},{24,28},{28,24},{1,5},{5... | collective-permute-start | bytes 1572872 | tf_op jit(solution)/shard_map/ppermute | solution.py:52
  35.8 15.0 %collective-permute-start.6 = (f32[128,1024]{1,0:T(8,128)S(1)}, f32[128,1024]{1,0:T(8,128)S(1)}, u32[]{:S(2)}, u32[]{:S(2)}) collective-permute-start(f32[128,1024]{1,0:T(8,128)S(1)} %keep0.1.refs_1_.refs_2_), channel_id=1, source_target_pairs={{0,8},{4,12},{24,16},{28,20},{1,9},{5,13},{25,17},{29,21},{2,10},{... | collective-permute-start | bytes 1572872 | tf_op jit(solution)/shard_map/ppermute | solution.py:353
  39.3 17.8 %collective-permute-start.7 = (f32[128,1024]{1,0:T(8,128)S(1)}, f32[128,1024]{1,0:T(8,128)S(1)}, u32[]{:S(2)}, u32[]{:S(2)}) collective-permute-start(f32[128,1024]{1,0:T(8,128)S(1)} %send2.1.refs_1_), channel_id=1, source_target_pairs={{0,4},{4,0},{8,12},{12,8},{16,20},{20,16},{24,28},{28,24},{1,5},{5... | collective-permute-start | bytes 1572872 | tf_op jit(solution)/shard_map/ppermute | solution.py:52
  47.3 14.5 %collective-permute-start.8 = (f32[256,512]{1,0:T(8,128)S(1)}, f32[256,512]{1,0:T(8,128)S(1)}, u32[]{:S(2)}, u32[]{:S(2)}) collective-permute-start(f32[256,512]{1,0:T(8,128)S(1)} %keep1.1.refs_1_.refs_2_), channel_id=1, source_target_pairs={{0,8},{4,12},{24,16},{28,20},{1,9},{5,13},{25,17},{29,21},{2,10},{... | collective-permute-start | bytes 1572872 | tf_op jit(solution)/shard_map/ppermute | solution.py:353
  51.4 13.3 %collective-permute-start.9 = (f32[128,1024]{1,0:T(8,128)S(1)}, f32[128,1024]{1,0:T(8,128)S(1)}, u32[]{:S(2)}, u32[]{:S(2)}) collective-permute-start(f32[128,1024]{1,0:T(8,128)S(1)} %zm0.1.refs_1_.refs_2_), channel_id=1, source_target_pairs={{8,16},{12,20},{16,8},{20,12},{9,17},{13,21},{17,9},{21,13},{10,18... | collective-permute-start | bytes 1572872 | tf_op jit(solution)/shard_map/ppermute | solution.py:356
  52.1 16.2 %collective-permute-start.10 = (f32[256,512]{1,0:T(8,128)S(1)}, f32[256,512]{1,0:T(8,128)S(1)}, u32[]{:S(2)}, u32[]{:S(2)}) collective-permute-start(f32[256,512]{1,0:T(8,128)S(1)} %send3.1.refs_1_), channel_id=1, source_target_pairs={{0,4},{4,0},{8,12},{12,8},{16,20},{20,16},{24,28},{28,24},{1,5},{5... | collective-permute-start | bytes 1572872 | tf_op jit(solution)/shard_map/ppermute | solution.py:52
  58.3 15.9 %collective-permute-start.11 = (f32[128,1024]{1,0:T(8,128)S(1)}, f32[128,1024]{1,0:T(8,128)S(1)}, u32[]{:S(2)}, u32[]{:S(2)}) collective-permute-start(f32[128,1024]{1,0:T(8,128)S(1)} %keep2.1.refs_1_.refs_2_), channel_id=1, source_target_pairs={{0,8},{4,12},{24,16},{28,20},{1,9},{5,13},{25,17},{29,21},{2,10},{... | collective-permute-start | bytes 1572872 | tf_op jit(solution)/shard_map/ppermute | solution.py:353
  62.4 13.1 %collective-permute-start.12 = (f32[256,512]{1,0:T(8,128)S(1)}, f32[256,512]{1,0:T(8,128)S(1)}, u32[]{:S(2)}, u32[]{:S(2)}) collective-permute-start(f32[256,512]{1,0:T(8,128)S(1)} %zm1.1.refs_1_.refs_2_), channel_id=1, source_target_pairs={{8,16},{12,20},{16,8},{20,12},{9,17},{13,21},{17,9},{21,13},{10,18... | collective-permute-start | bytes 1572872 | tf_op jit(solution)/shard_map/ppermute | solution.py:356
  63.1 15.8 %collective-permute-start.14 = (f32[256,512]{1,0:T(8,128)S(1)}, f32[256,512]{1,0:T(8,128)S(1)}, u32[]{:S(2)}, u32[]{:S(2)}) collective-permute-start(f32[256,512]{1,0:T(8,128)S(1)} %send4.1.refs_1_), channel_id=1, source_target_pairs={{0,4},{4,0},{8,12},{12,8},{16,20},{20,16},{24,28},{28,24},{1,5},{5... | collective-permute-start | bytes 1572872 | tf_op jit(solution)/shard_map/ppermute | solution.py:52
  65.3 15.8 %collective-permute-start.13 = (f32[128,1024]{1,0:T(8,128)S(1)}, f32[128,1024]{1,0:T(8,128)S(1)}, u32[]{:S(2)}, u32[]{:S(2)}) collective-permute-start(f32[128,1024]{1,0:T(8,128)S(1)} %zo0.1.refs_1_.refs_3_), channel_id=1, source_target_pairs={{8,0},{12,4},{16,24},{20,28},{9,1},{13,5},{17,25},{21,29},{10,2},{... | collective-permute-start | bytes 1572872 | tf_op jit(solution)/shard_map/ppermute | solution.py:359
  69.5 15.9 %collective-permute-start.15 = (f32[256,512]{1,0:T(8,128)S(1)}, f32[256,512]{1,0:T(8,128)S(1)}, u32[]{:S(2)}, u32[]{:S(2)}) collective-permute-start(f32[256,512]{1,0:T(8,128)S(1)} %keep3.1.refs_1_.refs_2_), channel_id=1, source_target_pairs={{0,8},{4,12},{24,16},{28,20},{1,9},{5,13},{25,17},{29,21},{2,10},{... | collective-permute-start | bytes 1572872 | tf_op jit(solution)/shard_map/ppermute | solution.py:353
  74.8 12.0 %collective-permute-start.16 = (f32[128,1024]{1,0:T(8,128)S(1)}, f32[128,1024]{1,0:T(8,128)S(1)}, u32[]{:S(2)}, u32[]{:S(2)}) collective-permute-start(f32[128,1024]{1,0:T(8,128)S(1)} %zm2.1.refs_1_.refs_2_), channel_id=1, source_target_pairs={{8,16},{12,20},{16,8},{20,12},{9,17},{13,21},{17,9},{21,13},{10,18... | collective-permute-start | bytes 1572872 | tf_op jit(solution)/shard_map/ppermute | solution.py:356
  76.1 16.3 %collective-permute-start.17 = (f32[256,512]{1,0:T(8,128)S(1)}, f32[256,512]{1,0:T(8,128)S(1)}, u32[]{:S(2)}, u32[]{:S(2)}) collective-permute-start(f32[256,512]{1,0:T(8,128)S(1)} %zo1.1.refs_1_.refs_3_), channel_id=1, source_target_pairs={{8,0},{12,4},{16,24},{20,28},{9,1},{13,5},{17,25},{21,29},{10,2},{... | collective-permute-start | bytes 1572872 | tf_op jit(solution)/shard_map/ppermute | solution.py:359
  78.9 14.2 %collective-permute-start.18 = (f32[256,512]{1,0:T(8,128)S(1)}, f32[256,512]{1,0:T(8,128)S(1)}, u32[]{:S(2)}, u32[]{:S(2)}) collective-permute-start(f32[256,512]{1,0:T(8,128)S(1)} %send5.1.refs_1_), channel_id=1, source_target_pairs={{0,4},{4,0},{8,12},{12,8},{16,20},{20,16},{24,28},{28,24},{1,5},{5... | collective-permute-start | bytes 1572872 | tf_op jit(solution)/shard_map/ppermute | solution.py:52
  82.3 14.9 %collective-permute-start.19 = (f32[256,512]{1,0:T(8,128)S(1)}, f32[256,512]{1,0:T(8,128)S(1)}, u32[]{:S(2)}, u32[]{:S(2)}) collective-permute-start(f32[256,512]{1,0:T(8,128)S(1)} %keep4.1.refs_1_.refs_2_), channel_id=1, source_target_pairs={{0,8},{4,12},{24,16},{28,20},{1,9},{5,13},{25,17},{29,21},{2,10},{... | collective-permute-start | bytes 1572872 | tf_op jit(solution)/shard_map/ppermute | solution.py:353
  86.0 12.5 %collective-permute-start.20 = (f32[256,512]{1,0:T(8,128)S(1)}, f32[256,512]{1,0:T(8,128)S(1)}, u32[]{:S(2)}, u32[]{:S(2)}) collective-permute-start(f32[256,512]{1,0:T(8,128)S(1)} %zm3.1.refs_1_.refs_2_), channel_id=1, source_target_pairs={{8,16},{12,20},{16,8},{20,12},{9,17},{13,21},{17,9},{21,13},{10,18... | collective-permute-start | bytes 1572872 | tf_op jit(solution)/shard_map/ppermute | solution.py:356
  87.4 15.6 %collective-permute-start.21 = (f32[128,1024]{1,0:T(8,128)S(1)}, f32[128,1024]{1,0:T(8,128)S(1)}, u32[]{:S(2)}, u32[]{:S(2)}) collective-permute-start(f32[128,1024]{1,0:T(8,128)S(1)} %zo2.1.refs_1_.refs_3_), channel_id=1, source_target_pairs={{8,0},{12,4},{16,24},{20,28},{9,1},{13,5},{17,25},{21,29},{10,2},{... | collective-permute-start | bytes 1572872 | tf_op jit(solution)/shard_map/ppermute | solution.py:359
  93.0 10.8 %collective-permute-start.22 = (f32[128,1024]{1,0:T(8,128)S(1)}, f32[128,1024]{1,0:T(8,128)S(1)}, u32[]{:S(2)}, u32[]{:S(2)}) collective-permute-start(f32[128,1024]{1,0:T(8,128)S(1)} %ag0.1.refs_1_.refs_5_), channel_id=1, source_target_pairs={{0,4},{4,0},{8,12},{12,8},{16,20},{20,16},{24,28},{28,24},{1,5},{5... | collective-permute-start | bytes 1572872 | tf_op jit(solution)/shard_map/ppermute | solution.py:52
  94.2 11.7 %collective-permute-start.23 = (f32[256,512]{1,0:T(8,128)S(1)}, f32[256,512]{1,0:T(8,128)S(1)}, u32[]{:S(2)}, u32[]{:S(2)}) collective-permute-start(f32[256,512]{1,0:T(8,128)S(1)} %keep5.1.refs_1_.refs_3_), channel_id=1, source_target_pairs={{0,8},{4,12},{24,16},{28,20},{1,9},{5,13},{25,17},{29,21},{2,10},{... | collective-permute-start | bytes 1572872 | tf_op jit(solution)/shard_map/ppermute | solution.py:353
  97.8 8.6 %collective-permute-start.24 = (f32[256,512]{1,0:T(8,128)S(1)}, f32[256,512]{1,0:T(8,128)S(1)}, u32[]{:S(2)}, u32[]{:S(2)}) collective-permute-start(f32[256,512]{1,0:T(8,128)S(1)} %zm4.1.refs_1_.refs_2_), channel_id=1, source_target_pairs={{8,16},{12,20},{16,8},{20,12},{9,17},{13,21},{17,9},{21,13},{10,18... | collective-permute-start | bytes 1572872 | tf_op jit(solution)/shard_map/ppermute | solution.py:356
  99.1 16.9 %collective-permute-start.25 = (f32[256,512]{1,0:T(8,128)S(1)}, f32[256,512]{1,0:T(8,128)S(1)}, u32[]{:S(2)}, u32[]{:S(2)}) collective-permute-start(f32[256,512]{1,0:T(8,128)S(1)} %zo3.1.refs_1_.refs_3_), channel_id=1, source_target_pairs={{8,0},{12,4},{16,24},{20,28},{9,1},{13,5},{17,25},{21,29},{10,2},{... | collective-permute-start | bytes 1572872 | tf_op jit(solution)/shard_map/ppermute | solution.py:359
  103.5 13.2 %collective-permute-start.26 = (f32[256,512]{1,0:T(8,128)S(1)}, f32[256,512]{1,0:T(8,128)S(1)}, u32[]{:S(2)}, u32[]{:S(2)}) collective-permute-start(f32[256,512]{1,0:T(8,128)S(1)} %ag1.1.refs_1_.refs_2_.refs_5_), channel_id=1, source_target_pairs={{0,4},{4,0},{8,12},{12,8},{16,20},{20,16},{24,28},{28,24},{1,5},{5... | collective-permute-start | bytes 1572872 | tf_op jit(solution)/shard_map/ppermute | solution.py:52
  107.0 18.0 %collective-permute-start.27 = (f32[256,512]{1,0:T(8,128)S(1)}, f32[256,512]{1,0:T(8,128)S(1)}, u32[]{:S(2)}, u32[]{:S(2)}) collective-permute-start(f32[256,512]{1,0:T(8,128)S(1)} %zo4.1.refs_1_.refs_3_), channel_id=1, source_target_pairs={{8,0},{12,4},{16,24},{20,28},{9,1},{13,5},{17,25},{21,29},{10,2},{... | collective-permute-start | bytes 1572872 | tf_op jit(solution)/shard_map/ppermute | solution.py:359
  108.3 17.3 %collective-permute-start.28 = (f32[256,512]{1,0:T(8,128)S(1)}, f32[256,512]{1,0:T(8,128)S(1)}, u32[]{:S(2)}, u32[]{:S(2)}) collective-permute-start(f32[256,512]{1,0:T(8,128)S(1)} %zm5.1.refs_1_.refs_2_), channel_id=1, source_target_pairs={{8,16},{12,20},{16,8},{20,12},{9,17},{13,21},{17,9},{21,13},{10,18... | collective-permute-start | bytes 1572872 | tf_op jit(solution)/shard_map/ppermute | solution.py:356
  117.3 11.3 %collective-permute-start.29 = (f32[512,256]{1,0:T(8,128)S(1)}, f32[512,256]{1,0:T(8,128)S(1)}, u32[]{:S(2)}, u32[]{:S(2)}) collective-permute-start(f32[512,256]{1,0:T(8,128)S(1)} %g4.1.refs_1_.refs_2_), channel_id=1, source_target_pairs={{0,1},{1,0},{2,3},{3,2},{4,5},{5,4},{6,7},{7,6},{8,9},{9,8},{10,11... | collective-permute-start | bytes 1572872 | tf_op jit(solution)/shard_map/ppermute | solution.py:52
  117.4 16.7 %collective-permute-start.30 = (f32[128,1024]{1,0:T(8,128)S(1)}, f32[128,1024]{1,0:T(8,128)S(1)}, u32[]{:S(2)}, u32[]{:S(2)}) collective-permute-start(f32[128,1024]{1,0:T(8,128)S(1)} %ag2.1.refs_1_.refs_6_), channel_id=1, source_target_pairs={{0,4},{4,0},{8,12},{12,8},{16,20},{20,16},{24,28},{28,24},{1,5},{5... | collective-permute-start | bytes 1572872 | tf_op jit(solution)/shard_map/ppermute | solution.py:52
  126.3 14.5 %collective-permute-start.31 = (f32[256,512]{1,0:T(8,128)S(1)}, f32[256,512]{1,0:T(8,128)S(1)}, u32[]{:S(2)}, u32[]{:S(2)}) collective-permute-start(f32[256,512]{1,0:T(8,128)S(1)} %zo5.1.refs_1_.refs_3_), channel_id=1, source_target_pairs={{8,0},{12,4},{16,24},{20,28},{9,1},{13,5},{17,25},{21,29},{10,2},{... | collective-permute-start | bytes 1572872 | tf_op jit(solution)/shard_map/ppermute | solution.py:359
  127.8 19.3 %collective-permute-start.32 = (f32[256,512]{1,0:T(8,128)S(1)}, f32[256,512]{1,0:T(8,128)S(1)}, u32[]{:S(2)}, u32[]{:S(2)}) collective-permute-start(f32[256,512]{1,0:T(8,128)S(1)} %ag3.1.refs_1_.refs_5_), channel_id=1, source_target_pairs={{0,4},{4,0},{8,12},{12,8},{16,20},{20,16},{24,28},{28,24},{1,5},{5... | collective-permute-start | bytes 1572872 | tf_op jit(solution)/shard_map/ppermute | solution.py:52
  134.6 24.6 %collective-permute-start.34 = (f32[256,512]{1,0:T(8,128)S(1)}, f32[256,512]{1,0:T(8,128)S(1)}, u32[]{:S(2)}, u32[]{:S(2)}) collective-permute-start(f32[256,512]{1,0:T(8,128)S(1)} %ag4.1.refs_1_.refs_6_), channel_id=1, source_target_pairs={{0,4},{4,0},{8,12},{12,8},{16,20},{20,16},{24,28},{28,24},{1,5},{5... | collective-permute-start | bytes 1572872 | tf_op jit(solution)/shard_map/ppermute | solution.py:52
  141.6 23.8 %collective-permute-start.33 = (f32[256,512]{1,0:T(8,128)S(1)}, f32[256,512]{1,0:T(8,128)S(1)}, u32[]{:S(2)}, u32[]{:S(2)}) collective-permute-start(f32[256,512]{1,0:T(8,128)S(1)} %ag5.1.refs_1_.first_ref), channel_id=1, source_target_pairs={{0,4},{4,0},{8,12},{12,8},{16,20},{20,16},{24,28},{28,24},{1,5},{5... | collective-permute-start | bytes 1572872 | tf_op jit(solution)/shard_map/ppermute | solution.py:52
